TPU v7x, 512 devices: a whole 4x8x8 slice. The times are simulated.
512 devices in a mesh: ctx: 64 (over x, y, z_lo), exp: 8 (over z_hi, core).
Axes of the slice: x: 4, y: 8, z: 8 (z_hi: 4, z_lo: 2; z = z_hi * 2 + z_lo), core: 2. Of those that a mesh axis runs over, the one named last changes fastest.
Arguments:
- queries: bfloat16 [8192, 4096], P('ctx', 'exp'), may hold values from -14 to 14
- key_rows: bfloat16 [8192, 256], P('ctx'), may hold values from -14 to 14
- value_rows: bfloat16 [8192, 256], P('ctx'), may hold values from -6 to 6
- out_weight: bfloat16 [4096, 4096], P('ctx', 'exp'), may hold values from -0.09375 to 0.09375
- residual: bfloat16 [8192, 4096], P('ctx', 'exp'), may hold values from -6 to 6
- norm_gain: float32 [4096], P('exp'), may hold values from 0.25 to 1.75
- w_gate: bfloat16 [64, 4096, 768], P('ctx', 'exp'), may hold values from -0.09375 to 0.09375
- w_up: bfloat16 [64, 4096, 768], P('ctx', 'exp'), may hold values from -0.09375 to 0.09375
- w_down: bfloat16 [64, 768, 4096], P('ctx', None, 'exp'), may hold values from -0.21875 to 0.21875
- pred_ids: int32 [8192, 8], P('ctx'), may hold values from 0 to 63, all different within a row; in each aligned block of 128 rows (0 to 127, 128 to 255, ...) at most 19 rows name the same one
- route_gates: bfloat16 [8192, 8], P('ctx'), may hold values from 0.049804688 to 0.29882812
- fix_pair: int32 [64, 32], P('ctx'), may hold values from 0 to 1023, as said below
- fix_expert: int32 [64, 32], P('ctx'), may hold values from 0 to 63, as said below
- fix_count: int32 [64], P('ctx'), may hold values from 2 to 32
Outputs:
- stream_out: bfloat16 [8192, 4096], P('ctx', 'exp')
- expert_out: bfloat16 [8192, 4096], P('ctx', 'exp')
Inputs may be any that keep to these rules, and one draw needn't show every extreme that they name: `pred_ids`: within the rows of one device (128 tokens), no expert is named more than 19 times; the 8 ids of a token differ. `fix_pair`: A device's entries are distinct choices of its own tokens; only its first fix_count entries are listed. `fix_expert`: among one device's listed entries no expert appears more than 2 times; the first 2 entries of every device name one common expert.
All inputs are finite; a program needn't handle non-finite values.
Results may differ from a plain program's by a relative error of at most 0.029.
Values may be sent and summed in bfloat16 or wider, within the bound.
No kernel may reach another device: no remote copies, remote signals or barrier semaphores. Data moves between devices by JAX's collectives and lax.ppermute only.
A program may use at most 64 MiB of HBM per device.

v0:
```python
import jax
import jax.numpy as jnp
from jax import lax
from jax.sharding import PartitionSpec as P

D = 4096
HD = 128
TOPK = 8
QH = 32
KVH = 2
FIX = 32
FCAP = 2


epsilon = 1e-06


def from_behind(block, axis, distance):
    devices = range(lax.axis_size(axis))
    route = [(i - distance, i) for i in devices if i - distance in devices]
    return lax.ppermute(block, axis, route)


def body(
    queries,
    key_rows,
    value_rows,
    out_weight,
    residual,
    norm_gain,
    w_gate,
    w_up,
    w_down,
    pred_ids,
    route_gates,
    fix_pair,
    fix_expert,
    fix_count,
):
    cycle_size = lax.axis_size("ctx")
    cycle_pos = lax.axis_index("ctx")
    exp_pos = lax.axis_index("exp")
    tokens = queries.shape[0]
    q_heads = queries.shape[1] // HD
    group_size = QH // KVH
    kv_heads = max(q_heads // group_size, 1)
    per_group = q_heads // kv_heads
    kv_first = exp_pos * q_heads // group_size * HD
    own_keys = lax.dynamic_slice_in_dim(key_rows, kv_first, kv_heads * HD, 1)
    own_values = lax.dynamic_slice_in_dim(value_rows, kv_first, kv_heads * HD, 1)
    window_blocks = [(own_keys, own_values)]
    current = (own_keys, own_values)
    for rounds in range(3):
        current = from_behind((current[0], current[1]), "ctx", 1)
        window_blocks.append(current)
    keys_all = jnp.concatenate([pair_block[0] for pair_block in reversed(window_blocks)], axis=0)
    values_all = jnp.concatenate([pair_block[1] for pair_block in reversed(window_blocks)], axis=0)
    score_scale = 1.0 / HD**0.5
    q_view = queries.reshape(tokens, kv_heads, per_group, HD)
    k_view = keys_all.reshape(4 * tokens, kv_heads, HD)
    v_view = values_all.reshape(4 * tokens, kv_heads, HD)
    scores = (
        jnp.einsum("tkgd,skd->kgts", q_view, k_view, preferred_element_type=jnp.float32)
        * score_scale
    )
    q_pos = cycle_pos * tokens + jnp.arange(tokens)
    k_pos = (cycle_pos - 3) * tokens + jnp.arange(4 * tokens)
    allowed = (k_pos[None, :] >= 0) & (k_pos[None, :] <= q_pos[:, None])
    scores = jnp.where(allowed, scores, -1e30)
    highest = jnp.max(scores, axis=3, keepdims=True)
    weights = jnp.where(allowed, jnp.exp(scores - highest), 0.0)
    denominators = jnp.sum(weights, axis=3, keepdims=True)
    mixed_out = (
        jnp.einsum(
            "kgts,skd->kgtd",
            weights.astype(jnp.bfloat16),
            v_view,
            preferred_element_type=jnp.float32,
        )
        / denominators
    )
    attended = (
        jnp.transpose(mixed_out, (2, 0, 1, 3)).reshape(tokens, q_heads * HD).astype(jnp.bfloat16)
    )
    every_head = lax.all_gather(attended, "exp", axis=1, tiled=True)
    projected = jnp.dot(
        every_head,
        lax.all_gather(out_weight, "ctx", axis=0, tiled=True),
        preferred_element_type=jnp.float32,
    )
    stream = residual.astype(jnp.float32) + projected
    squares = lax.psum(jnp.sum(stream * stream, axis=1), "exp")
    normed = (stream * lax.rsqrt(squares[:, None] / D + epsilon) * norm_gain[None, :]).astype(
        jnp.bfloat16
    )
    slot_total = tokens * TOPK
    slots_cap = tokens * TOPK * 19 // (16 * cycle_size)
    slot_width = slots_cap + FCAP
    send_rows = cycle_size * slot_width
    flat_ids = pred_ids.reshape(slot_total)
    pairs_in = fix_pair[0]
    fix_targets = fix_expert[0]
    live_fix = jnp.arange(FIX) < fix_count[0]
    listed = jnp.any(
        (pairs_in[None, :] == jnp.arange(slot_total)[:, None]) & live_fix[None, :], axis=1
    )
    expert_ids = jnp.arange(cycle_size)
    pred_onehot = (flat_ids[:, None] == expert_ids[None, :]) & jnp.logical_not(listed)[:, None]
    pred_rank = jnp.sum(
        jnp.where(pred_onehot, jnp.cumsum(pred_onehot.astype(jnp.int32), axis=0) - 1, 0), axis=1
    )
    pred_dest = jnp.where(listed, -1, flat_ids * slot_width + pred_rank)
    fix_onehot = (fix_targets[:, None] == expert_ids[None, :]) & live_fix[:, None]
    fix_rank = jnp.sum(
        jnp.where(fix_onehot, jnp.cumsum(fix_onehot.astype(jnp.int32), axis=0) - 1, 0), axis=1
    )
    fix_dest = jnp.where(live_fix, fix_targets * slot_width + slots_cap + fix_rank, -1)
    fix_tokens = pairs_in // TOPK
    slot_index = jnp.arange(send_rows)
    pred_match = pred_dest.reshape(tokens, TOPK)[None, :, :] == slot_index[:, None, None]
    pred_map = jnp.any(pred_match, axis=2).astype(jnp.bfloat16)
    fix_map = (fix_dest[None, :] == slot_index[:, None]).astype(jnp.bfloat16)
    fix_rows = normed[fix_tokens]
    outgoing = (
        jnp.dot(pred_map, normed, preferred_element_type=jnp.float32)
        + jnp.dot(fix_map, fix_rows, preferred_element_type=jnp.float32)
    ).astype(jnp.bfloat16)
    incoming = lax.all_to_all(
        outgoing.reshape(cycle_size, slot_width, outgoing.shape[1]),
        "ctx",
        split_axis=0,
        concat_axis=0,
        tiled=True,
    )
    rows_all = incoming.reshape(send_rows, incoming.shape[2])
    gate_local = w_gate[0]
    up_local = w_up[0]
    down_local = w_down[0]
    gate_part = jnp.dot(rows_all, gate_local, preferred_element_type=jnp.float32).astype(
        jnp.bfloat16
    )
    up_part = jnp.dot(rows_all, up_local, preferred_element_type=jnp.float32).astype(jnp.bfloat16)
    summed_gate, summed_up = (
        lax.psum(gate_part, "exp").astype(jnp.float32),
        lax.psum(up_part, "exp").astype(jnp.float32),
    )
    hidden = (jax.nn.silu(summed_gate) * summed_up).astype(jnp.bfloat16)
    results = jnp.dot(hidden, down_local, preferred_element_type=jnp.float32).astype(jnp.bfloat16)
    returned = lax.all_to_all(
        results.reshape(cycle_size, slot_width, results.shape[1]),
        "ctx",
        split_axis=0,
        concat_axis=0,
        tiled=True,
    )
    pred_weight = jnp.sum(
        jnp.where(pred_match, route_gates[None, :, :].astype(jnp.float32), 0.0), axis=2
    )
    token_match = (fix_tokens[:, None] == jnp.arange(tokens)[None, :]).astype(jnp.float32)
    fix_gates = route_gates.reshape(slot_total)[pairs_in].astype(jnp.float32)
    fix_weight = jnp.dot(
        fix_map.astype(jnp.float32) * fix_gates[None, :],
        token_match,
        precision=lax.Precision.HIGHEST,
    )
    combine = (pred_weight + fix_weight).astype(jnp.bfloat16)
    expert_out = jnp.einsum(
        "rt,rd->td",
        combine,
        returned.reshape(send_rows, returned.shape[2]),
        preferred_element_type=jnp.float32,
    ).astype(jnp.bfloat16)
    return (stream.astype(jnp.bfloat16), expert_out)


def solution(mesh):
    placed = (
        P("ctx", "exp"),
        P("ctx", None),
        P("ctx", None),
        P("ctx", "exp"),
        P("ctx", "exp"),
        P("exp"),
        P("ctx", "exp", None),
        P("ctx", "exp", None),
        P("ctx", None, "exp"),
        P("ctx", None),
        P("ctx", None),
        P("ctx", None),
        P("ctx", None),
        P("ctx"),
    )
    return jax.shard_map(
        body,
        mesh=mesh,
        in_specs=placed,
        out_specs=(P("ctx", "exp"), P("ctx", "exp")),
        check_vma=False,
    )
```

profile of v0, /device:TPU:129, one launch (start us, length us, event | category | flops | bytes accessed | tf_op | source)
XLA Modules:
  0.0 649.2 jit_solution(15063764580044845694)
XLA Ops:
  8.1 4.0 collective-permute-start
  12.9 2.3 collective-permute-start.3
  15.3 4.0 collective-permute-start.1
  19.3 2.3 collective-permute-start.4
  21.6 4.0 collective-permute-start.2
  25.9 2.3 collective-permute-start.5
  32.7 18.0 %reduce-window.6 = s32[64,8,128]{2,1,0:T(8,128)S(1)} reduce-window(s32[64,8,128]{2,1,0:T(8,128)S(1)} %fusion.33, s32[]{:T(128)} %constant.36.clone.1), window={size=1x1x128 pad=0_0x0_0x127_0}, to_apply=%region_3.4 | reduce-window | flops 8323072 | bytes 524292 | tf_op jit(solution)/shard_map/reduce-window
  51.9 5.5 fusion
  57.5 16.1 %all-gather.3.cloned.1.call-done = bf16[128,4096]{0,1:T(8,128)(2,1)} async-done(((bf16[128,512]{0,1:T(8,128)(2,1)}), bf16[128,4096]{0,1:T(8,128)(2,1)}) %all-gather.3.cloned.1.call-update) | async-done | bytes 1048592 | tf_op jit(solution)/shard_map/all_gather | solution.py:85
  73.6 264.8 %all-gather.5.cloned.1.call-done = bf16[4096,512]{1,0:T(8,128)(2,1)} async-done(((bf16[64,512]{1,0:T(8,128)(2,1)}), bf16[4096,512]{1,0:T(8,128)(2,1)}) %all-gather.5.cloned.1.call-update) | async-done | bytes 4194320 | tf_op jit(solution)/shard_map/all_gather | solution.py:88
  338.3 3.3 multiply_reduce_fusion
  341.7 56.2 %psum.21 = f32[128]{0:T(128)S(1)} all-reduce(f32[128]{0:T(128)S(1)} %get-tuple-element.12), channel_id=1, replica_groups=mesh['ctx'=64,'exp'=8] {'exp'}, use_global_device_ids=true, to_apply=%region_11.12 | all-reduce | flops 128 | bytes 1024 | tf_op jit(solution)/shard_map/psum | solution.py:92
  402.8 2.3 fusion.6
  405.2 2.3 reshape.241
  407.5 46.2 %all_to_all.10 = bf16[64,21,512]{2,1,0:T(8,128)(2,1)} all-to-all(bf16[64,21,512]{2,1,0:T(8,128)(2,1)S(1)} %reshape.241), channel_id=1, replica_groups=mesh['ctx'=64,'exp'=8] {'ctx'}, dimensions={0} | all-to-all | bytes 2752512 | tf_op jit(solution)/shard_map/all_to_all | solution.py:128
  453.7 2.4 reshape.242
  456.2 2.6 convolution_convert_fusion
  458.7 2.6 convolution_convert_fusion.1
  461.3 121.9 %all-reduce.3.cloned.1.call-done = (bf16[1344,768]{1,0:T(8,128)(2,1)}, bf16[1344,768]{1,0:T(8,128)(2,1)}) async-done(((bf16[1344,768]{1,0:T(8,128)(2,1)}, bf16[1344,768]{1,0:T(8,128)(2,1)}), (bf16[1344,768]{1,0:T(8,128)(2,1)}, bf16[1344,768]{1,0:T(8,128)(2,1)})) %all-reduce.3.cloned.1.call-update) | async-done | bytes 4128784 | tf_op jit(solution)/shard_map/psum | solution.py:145
  583.2 3.7 convolution_convert_fusion.2
  588.3 11.3 %all-to-all-start.1 = ((bf16[64,21,512]{2,1,0:T(8,128)(2,1)}), bf16[64,21,512]{2,1,0:T(8,128)(2,1)S(1)}, u32[]{:S(2)}, u32[]{:S(2)}) async-start(bf16[64,21,512]{2,1,0:T(8,128)(2,1)} %reshape.243), calls=%async_computation.1 | async-start | bytes 3145728 | tf_op jit(solution)/shard_map/all_to_all | solution.py:149
  600.6 7.1 %select_reduce_fusion = f32[1344,128]{1,0:T(8,128)S(1)} fusion(f32[128,8]{0,1:T(8,128)S(1)} %convert_element_type.86, s32[128,8]{0,1:T(8,128)S(1)} %add_select_fusion), kind=kLoop, calls=%fused_computation.2 | loop fusion | flops 3956736 | bytes 696320 | tf_op jit(solution)/shard_map/reduce_sum | solution.py:156
  608.3 30.7 %all-to-all-done.1 = bf16[64,21,512]{2,1,0:T(8,128)(2,1)S(1)} async-done(((bf16[64,21,512]{2,1,0:T(8,128)(2,1)}), bf16[64,21,512]{2,1,0:T(8,128)(2,1)S(1)}, u32[]{:S(2)}, u32[]{:S(2)}) %all-to-all-start.1) | async-done | bytes 1376288 | tf_op jit(solution)/shard_map/all_to_all | solution.py:149
  640.3 2.4 convolution_convert_fusion.3
  (82 shorter events, 16.1 us)
Async XLA Ops:
  7.2 449.0 %copy-start = (bf16[1,512,768]{2,1,0:T(8,128)(2,1)S(1)}, bf16[1,512,768]{2,1,0:T(8,128)(2,1)}, u32[]{:S(2)}) copy-start(bf16[1,512,768]{2,1,0:T(8,128)(2,1)} %param.21) | copy-start | bytes 2359300
  7.2 66.4 %all-gather.3.cloned.1.call-start = ((), (), s32[]{:S(2)}) async-start(), calls=%async_computation.2 | async-start | bytes 1179648 | tf_op jit(solution)/shard_map/all_gather | solution.py:85
  8.1 7.2 %collective-permute-start = (bf16[128,128]{1,0:T(8,128)(2,1)S(1)}, bf16[128,128]{1,0:T(8,128)(2,1)S(1)}, u32[]{:S(2)}, u32[]{:S(2)}) collective-permute-start(bf16[128,128]{1,0:T(8,128)(2,1)S(1)} %constant_dynamic-slice_fusion.1), channel_id=1, source_target_pairs={{0,8},{8,16},{16,24},{24,32},{32,40},{40,48},{48,56},{56,64},{64,7... | collective-permute-start | bytes 98312 | tf_op jit(solution)/shard_map/ppermute | solution.py:21
  12.9 6.4 collective-permute-start.3
  15.3 6.3 collective-permute-start.1
  19.3 6.5 %collective-permute-start.4 = (bf16[128,128]{0,1:T(8,128)(2,1)S(1)}, bf16[128,128]{0,1:T(8,128)(2,1)S(1)}, u32[]{:S(2)}, u32[]{:S(2)}) collective-permute-start(bf16[128,128]{0,1:T(8,128)(2,1)S(1)} %collective-permute-done.3), channel_id=1, source_target_pairs={{0,8},{8,16},{16,24},{24,32},{32,40},{40,48},{48,56},{56,64},{64,7... | collective-permute-start | bytes 98312 | tf_op jit(solution)/shard_map/ppermute | solution.py:21
  21.6 6.5 %collective-permute-start.2 = (bf16[128,128]{1,0:T(8,128)(2,1)S(1)}, bf16[128,128]{1,0:T(8,128)(2,1)S(1)}, u32[]{:S(2)}, u32[]{:S(2)}) collective-permute-start(bf16[128,128]{1,0:T(8,128)(2,1)S(1)} %collective-permute-done.1), channel_id=1, source_target_pairs={{0,8},{8,16},{16,24},{24,32},{32,40},{40,48},{48,56},{56,64},{64,7... | collective-permute-start | bytes 98312 | tf_op jit(solution)/shard_map/ppermute | solution.py:21
  25.9 3.8 collective-permute-start.5
  29.4 2.1 copy-start.3
  29.4 3.0 copy-start.7
  30.6 20.9 %copy-start.5 = (s32[1,32]{1,0:T(1,128)S(1)}, s32[1,32]{1,0:T(1,128)}, u32[]{:S(2)}) copy-start(s32[1,32]{1,0:T(1,128)} %param.26) | copy-start | bytes 388
  30.6 307.7 %copy-start.2 = (bf16[128,512]{1,0:T(8,128)(2,1)S(1)}, bf16[128,512]{1,0:T(8,128)(2,1)}, u32[]{:S(2)}) copy-start(bf16[128,512]{1,0:T(8,128)(2,1)} %param.18) | copy-start | bytes 393220
  30.7 307.7 %all-gather.5.cloned.1.call-start = ((), (), s32[]{:S(2)}) async-start(), calls=%async_computation.3 | async-start | bytes 4259840 | tf_op jit(solution)/shard_map/all_gather | solution.py:88
  31.4 551.8 %all-reduce.3.cloned.1.call-start = ((), (), s32[]{:S(2)}) async-start(), calls=%async_computation.4 | async-start | bytes 8257536 | tf_op jit(solution)/shard_map/psum | solution.py:145
  57.5 340.4 %copy-start.6 = (f32[512]{0:T(512)S(1)}, f32[512]{0:T(512)}, u32[]{:S(2)}) copy-start(f32[512]{0:T(512)} %param.19) | copy-start | bytes 6148
  398.6 0.7 copy-start.1
  456.2 2.6 copy-start.9
  461.3 122.0 %copy-start.10 = (bf16[1,768,512]{2,1,0:T(8,128)(2,1)S(1)}, bf16[1,768,512]{2,1,0:T(8,128)(2,1)}, u32[]{:S(2)}) copy-start(bf16[1,768,512]{2,1,0:T(8,128)(2,1)} %param.22) | copy-start | bytes 2359300
  588.3 11.3 %copy-start.4 = (bf16[128,8]{0,1:T(8,128)(2,1)S(1)}, bf16[128,8]{0,1:T(8,128)(2,1)}, u32[]{:S(2)}) copy-start(bf16[128,8]{0,1:T(8,128)(2,1)} %param.24) | copy-start | bytes 6148
  588.3 12.3 %copy-start.8 = (s32[1,32]{1,0:T(1,128)S(1)}, s32[1,32]{1,0:T(1,128)}, u32[]{:S(2)}) copy-start(s32[1,32]{1,0:T(1,128)} %param.25) | copy-start | bytes 388
  588.3 50.7 %all-to-all-start.1 = ((bf16[64,21,512]{2,1,0:T(8,128)(2,1)}), bf16[64,21,512]{2,1,0:T(8,128)(2,1)S(1)}, u32[]{:S(2)}, u32[]{:S(2)}) async-start(bf16[64,21,512]{2,1,0:T(8,128)(2,1)} %reshape.243), calls=%async_computation.1 | async-start | bytes 3145728 | tf_op jit(solution)/shard_map/all_to_all | solution.py:149
Sparse Core Ops, SparseCore 0:
  30.8 42.7 all-gather.2
  75.7 262.6 all-gather.4
  461.4 121.7 all-reduce.2
where the time goes:
time: 650 us; the launch traced here: 649 us
  waiting for transfers between devices  434 us (67%)
  blocking collectives  102 us (16%)
  other arithmetic  32.5 us (5%)
  starting transfers between devices  30.3 us (5%)
  matrix products  21.1 us (3%)
  between operations  14.8 us (2%)
  local copies, waits for them, and re-layouts  13.9 us (2%)
    all_gather x1, waiting for transfers between devices, body(): lax.all_gather(out_weight, 'ctx', axis=0, tiled=True)  265 us
    psum x1, waiting for transfers between devices, body(): lax.psum(up_part, 'exp').astype(jnp.float32)  122 us
    psum x1, blocking collectives, body(): squares = lax.psum(jnp.sum(stream * stream, axis=1), 'exp')  56.2 us
    all_to_all x1, blocking collectives, body(): lax.all_to_all(outgoing.reshape(cycle_size, slot_width, outgoing.shape[1]...  46.2 us
    all_to_all x1, waiting for transfers between devices, body(): lax.all_to_all(results.reshape(cycle_size, slot_width, results.shape[1]),...  30.7 us
    ppermute x6, starting transfers between devices, from_behind(): return lax.ppermute(block, axis, route)  18.9 us
    another operation x2, other arithmetic  18 us
    all_gather x1, waiting for transfers between devices, body(): every_head = lax.all_gather(attended, 'exp', axis=1, tiled=True)  16.1 us
  transfers between devices with their start and end apart: 10, of which 4 were waited for; matrix products, arithmetic and copies ran while one was open for 6% of the time, Pallas kernels for 0%

commit v1 on v0

v1 whole, which is shorter than its diff:
```python
import jax
import jax.numpy as jnp
import numpy as np
from jax import lax
from jax.sharding import Mesh, PartitionSpec as P

D = 4096
HD = 128
TOPK = 8
QH = 32
KVH = 2
FF = 768
FIX = 32
TOK = 128
SLOTS = 21
NX, NY, NL, NH, NC = 4, 8, 2, 4, 2
N_CTX = NX * NY * NL
ROWS = N_CTX * SLOTS
SHARE = ROWS // NX
SLICE = D // (NH * NC)
CTX = ("x", "y", "l")
HOME = ("h", "y", "l")
f32, bf16 = jnp.float32, jnp.bfloat16

epsilon = 1e-06


def turn(block):
    route = [(a * NH + b, b * NX + a) for a in range(NX) for b in range(NH)]
    return lax.ppermute(block, ("x", "h"), route)


def swap(block, axis):
    return lax.ppermute(block, axis, [(0, 1), (1, 0)])


def from_behind(block, distance):
    route = [(i, i + distance) for i in range(N_CTX - distance)]
    return lax.ppermute(block, CTX, route)


def attention(queries, key_rows, value_rows):
    tokens = queries.shape[0]
    block = lax.axis_index(CTX)
    kv_first = lax.axis_index("h") // 2 * HD
    own = jnp.concatenate(
        [
            lax.dynamic_slice_in_dim(key_rows, kv_first, HD, 1),
            lax.dynamic_slice_in_dim(value_rows, kv_first, HD, 1),
        ],
        axis=1,
    )
    pairs = [from_behind(own, 3), from_behind(own, 2), from_behind(own, 1), own]
    keys = jnp.concatenate([pair[:, :HD] for pair in pairs], axis=0)
    values = jnp.concatenate([pair[:, HD:] for pair in pairs], axis=0)
    q_view = queries.reshape(tokens, -1, HD)
    scores = jnp.einsum("tgd,sd->gts", q_view, keys, preferred_element_type=f32) / HD**0.5
    q_pos = block * tokens + jnp.arange(tokens)
    k_pos = (block - 3) * tokens + jnp.arange(4 * tokens)
    allowed = (k_pos[None, :] >= 0) & (k_pos[None, :] <= q_pos[:, None])
    scores = jnp.where(allowed, scores, -1e30)
    highest = jnp.max(scores, axis=2, keepdims=True)
    weights = jnp.where(allowed, jnp.exp(scores - highest), 0.0)
    denominators = jnp.sum(weights, axis=2, keepdims=True)
    mixed = (
        jnp.einsum("gts,sd->gtd", weights.astype(bf16), values, preferred_element_type=f32)
        / denominators
    )
    return jnp.transpose(mixed, (1, 0, 2)).reshape(tokens, -1).astype(bf16)


def slots_of(pred_ids, fix_pair, fix_expert, fix_count):
    tokens = pred_ids.shape[0]
    places = jnp.arange(tokens * TOPK, dtype=jnp.int32).reshape(tokens, TOPK)
    live = jnp.arange(FIX) < fix_count[0]
    hit = (places[:, :, None] == fix_pair[0][None, None, :]) & live[None, None, :]
    fixed = jnp.sum(jnp.where(hit, fix_expert[0][None, None, :], 0), axis=2)
    ids = jnp.where(jnp.any(hit, axis=2), fixed, pred_ids)
    named = ids[:, :, None] == jnp.arange(N_CTX)[None, None, :]
    counts = jnp.sum(named.astype(f32), axis=1)
    earlier = (
        jnp.arange(tokens)[:, None] > jnp.arange(tokens)[None, :]
    ).astype(bf16)
    before = jnp.dot(earlier, counts.astype(bf16), preferred_element_type=f32)
    rank = jnp.sum(jnp.where(named, before[:, None, :], 0.0), axis=2)
    twin = (ids[:, :, None] == ids[:, None, :]) & (
        jnp.arange(TOPK)[None, :, None] > jnp.arange(TOPK)[None, None, :]
    )
    rank = rank + jnp.sum(twin.astype(f32), axis=2)
    return ids.astype(f32) * SLOTS + rank


def body(
    queries,
    key_rows,
    value_rows,
    out_weight,
    residual,
    norm_gain,
    w_gate,
    w_up,
    w_down,
    pred_ids,
    route_gates,
    fix_pair,
    fix_expert,
    fix_count,
):
    core = lax.axis_index("c")
    tokens = queries.shape[0]
    half = FF // 2

    strip = turn(out_weight)
    other_strip = swap(strip, "l")
    first = lax.axis_index("l") == 0
    strips = jnp.concatenate(
        [jnp.where(first, strip, other_strip), jnp.where(first, other_strip, strip)], axis=0
    )
    quarter = lax.all_gather(strips, "y", axis=0, tiled=True)

    slots = slots_of(pred_ids, fix_pair, fix_expert, fix_count)
    table = turn(jnp.concatenate([slots, route_gates.astype(f32)], axis=1)).T
    slot_rows, gate_rows = table[:TOPK], table[TOPK:]
    row_ids = jnp.arange(ROWS, dtype=f32)[:, None]
    row_map = jnp.zeros((ROWS, tokens), f32)
    combine = jnp.zeros((ROWS, tokens), f32)
    for k in range(TOPK):
        here = slot_rows[k][None, :] == row_ids
        row_map = row_map + jnp.where(here, 1.0, 0.0)
        combine = combine + jnp.where(here, gate_rows[k][None, :], 0.0)
    row_map, combine = row_map.astype(bf16), combine.astype(bf16)

    def columns(which):
        return jnp.concatenate(
            [
                lax.dynamic_slice_in_dim(w_gate[0], which * half, half, 1),
                lax.dynamic_slice_in_dim(w_up[0], which * half, half, 1),
            ],
            axis=1,
        )

    gate_up = turn(jnp.concatenate([columns(core), swap(columns(1 - core), "c")], axis=0))
    down = turn(w_down[0])
    gain = turn(norm_gain[None, :])
    inverse = 1.0 / (gain * gain)
    other_inverse = swap(inverse, "c")
    residual_here = turn(residual)

    attended = attention(queries, key_rows, value_rows)
    heads = lax.all_gather(attended, "x", axis=0, tiled=True)
    other_heads = swap(heads, "c")
    partial = jnp.dot(
        heads,
        lax.dynamic_slice_in_dim(quarter, core * SLICE, SLICE, 0),
        preferred_element_type=f32,
    ) + jnp.dot(
        other_heads,
        lax.dynamic_slice_in_dim(quarter, (1 - core) * SLICE, SLICE, 0),
        preferred_element_type=f32,
    )
    terms = lax.all_to_all(
        partial.astype(bf16).reshape(NH, tokens, SLICE), "h", split_axis=0, concat_axis=0, tiled=True
    )
    stream = residual_here.astype(f32) + jnp.sum(terms.astype(f32), axis=0)
    stream_out = turn(stream.astype(bf16))

    scaled = (stream * gain).astype(bf16)
    outgoing = jnp.dot(row_map, scaled, preferred_element_type=f32).astype(bf16)
    incoming = lax.all_to_all(
        outgoing.reshape(N_CTX, SLOTS, SLICE), HOME, split_axis=0, concat_axis=0, tiled=True
    ).reshape(ROWS, SLICE)
    other_incoming = swap(incoming, "c")
    gate_up_part = (
        jnp.dot(incoming, gate_up[:SLICE], preferred_element_type=f32)
        + jnp.dot(other_incoming, gate_up[SLICE:], preferred_element_type=f32)
    ).astype(bf16)

    def squares(rows, weight):
        return jnp.sum(jnp.square(rows.astype(f32)) * weight, axis=1)

    square_part = (squares(incoming, inverse) + squares(other_incoming, other_inverse)).reshape(
        NX, 1, SHARE
    )
    high = square_part.astype(bf16)
    low = (square_part - high.astype(f32)).astype(bf16)
    extra = jnp.concatenate([high, low], axis=1)
    extra = jnp.pad(extra, ((0, 0), (0, 14), (0, FF - SHARE)))
    parts = lax.all_to_all(
        jnp.concatenate([gate_up_part.reshape(NX, SHARE, FF), extra], axis=1),
        "x",
        split_axis=0,
        concat_axis=0,
        tiled=True,
    ).astype(f32)
    sums = jnp.sum(parts[:, :SHARE], axis=0)
    total = jnp.sum(parts[:, SHARE : SHARE + 2, :SHARE], axis=(0, 1))
    sums = sums * lax.rsqrt(total / D + epsilon)[:, None]
    hidden = (jax.nn.silu(sums[:, :half]) * sums[:, half:]).astype(bf16)
    all_hidden = lax.all_gather(hidden, "x", axis=0, tiled=True)
    other_hidden = swap(all_hidden, "c")
    results = (
        jnp.dot(
            all_hidden,
            lax.dynamic_slice_in_dim(down, core * half, half, 0),
            preferred_element_type=f32,
        )
        + jnp.dot(
            other_hidden,
            lax.dynamic_slice_in_dim(down, (1 - core) * half, half, 0),
            preferred_element_type=f32,
        )
    ).astype(bf16)
    returned = lax.all_to_all(
        results.reshape(N_CTX, SLOTS, SLICE), HOME, split_axis=0, concat_axis=0, tiled=True
    ).reshape(ROWS, SLICE)
    mixed = jnp.einsum("rt,rd->td", combine, returned, preferred_element_type=f32)
    return stream_out, turn(mixed.astype(bf16))


def solution(mesh):
    split = Mesh(np.asarray(mesh.devices).reshape(NX, NY, NL, NH, NC), ("x", "y", "l", "h", "c"))
    ctx, exp = CTX, ("h", "c")
    placed = (
        P(ctx, exp),
        P(ctx, None),
        P(ctx, None),
        P(ctx, exp),
        P(ctx, exp),
        P(exp),
        P(ctx, exp, None),
        P(ctx, exp, None),
        P(ctx, None, exp),
        P(ctx, None),
        P(ctx, None),
        P(ctx, None),
        P(ctx, None),
        P(ctx),
    )
    return jax.shard_map(
        body,
        mesh=split,
        in_specs=placed,
        out_specs=(P(ctx, exp), P(ctx, exp)),
        check_vma=False,
    )
```

time: 650 us -> 466 us (0.72)
  the two profiles are of different devices: /device:TPU:129 before, /device:TPU:38 now
where the time goes in v1:
time: 466 us; the launch traced here: 464 us
  waiting for transfers between devices  256 us (55%)
  starting transfers between devices  104 us (22%)
  blocking collectives  58.3 us (13%)
  between operations  15.4 us (3%)
  matrix products  12.6 us (3%)
  local copies, waits for them, and re-layouts  9.21 us (2%)
  other arithmetic  8.95 us (2%)
    ppermute x8, waiting for transfers between devices, turn(): return lax.ppermute(block, ('x', 'h'), route)  163 us
    ppermute x8, starting transfers between devices, turn(): return lax.ppermute(block, ('x', 'h'), route)  50.1 us
    all_to_all x1, waiting for transfers between devices, body(): lax.all_to_all(results.reshape(N_CTX, SLOTS, SLICE), HOME, split_axis=0,...  37.1 us
    all_to_all x1, blocking collectives, body(): lax.all_to_all(jnp.concatenate([gate_up_part.reshape(NX, SHARE, FF), extr...  30.5 us
    all_to_all x1, waiting for transfers between devices, body(): lax.all_to_all(outgoing.reshape(N_CTX, SLOTS, SLICE), HOME, split_axis=0,...  29.6 us
    all_gather x1, waiting for transfers between devices, body(): quarter = lax.all_gather(strips, 'y', axis=0, tiled=True)  23 us
    all_gather x1, blocking collectives, body(): all_hidden = lax.all_gather(hidden, 'x', axis=0, tiled=True)  15.2 us
    all_to_all x1, starting transfers between devices, body(): lax.all_to_all(outgoing.reshape(N_CTX, SLOTS, SLICE), HOME, split_axis=0,...  14.3 us
  transfers between devices with their start and end apart: 21, of which 10 were waited for; matrix products, arithmetic and copies ran while one was open for 3% of the time, Pallas kernels for 0%

profile of v1, /device:TPU:38, one launch (start us, length us, event | category | flops | bytes accessed | tf_op | source)
XLA Modules:
  0.0 464.0 jit_solution(5141711784244347996)
XLA Ops:
  8.0 4.3 collective-permute-start.3
  12.3 2.6 collective-permute-start.2
  17.0 10.6 %collective-permute-start.4 = (bf16[64,512]{1,0:T(8,128)(2,1)}, bf16[64,512]{1,0:T(8,128)(2,1)S(1)}, u32[]{:S(2)}, u32[]{:S(2)}) collective-permute-start(bf16[64,512]{1,0:T(8,128)(2,1)} %param.17), channel_id=1, source_target_pairs={{0,0},{2,128},{4,256},{6,384},{128,2},{130,130},{132,258},{134,386... | collective-permute-start | bytes 196616 | tf_op jit(solution)/shard_map/ppermute | solution.py:30
  31.7 3.5 collective-permute-start.5
  35.3 2.6 collective-permute-done.5
  40.0 12.5 %all_gather.9 = bf16[512,512]{0,1:T(8,128)(2,1)S(1)} all-gather(bf16[128,512]{0,1:T(8,128)(2,1)S(1)} %bitcast.103), channel_id=1, replica_groups=mesh['x'=4,'y'=8,'l'=2,'h'=4,'c'=2] {'x'}, dimensions={0}, use_global_device_ids=true | all-gather | bytes 655360 | tf_op jit(solution)/shard_map/all_gather | solution.py:150
  54.6 23.0 %all-gather.2.cloned.1.call-done = bf16[1024,512]{1,0:T(8,128)(2,1)} async-done(((bf16[128,512]{1,0:T(8,128)(2,1)}), bf16[1024,512]{1,0:T(8,128)(2,1)}) %all-gather.2.cloned.1.call-update) | async-done | bytes 1048592 | tf_op jit(solution)/shard_map/all_gather | solution.py:119
  80.5 7.4 %all-to-all-start = ((bf16[4,128,512]{2,1,0:T(8,128)(2,1)}), bf16[4,128,512]{2,1,0:T(8,128)(2,1)S(1)}, u32[]{:S(2)}, u32[]{:S(2)}) async-start(bf16[4,128,512]{2,1,0:T(8,128)(2,1)} %bitcast.6), calls=%async_computation | async-start | bytes 1048576 | tf_op jit(solution)/shard_map/all_to_all | solution.py:161
  88.0 6.0 %collective-permute-start.8 = (f32[128,16]{0,1:T(8,128)S(1)}, f32[128,16]{0,1:T(8,128)S(1)}, u32[]{:S(2)}, u32[]{:S(2)}) collective-permute-start(f32[128,16]{0,1:T(8,128)S(1)} %pad_maximum_fusion.4), channel_id=1, source_target_pairs={{0,0},{2,128},{4,256},{6,384},{128,2},{130,130},{132,258},{134,386... | collective-permute-start | bytes 24584 | tf_op jit(solution)/shard_map/ppermute | solution.py:30
  94.1 4.1 collective-permute-start
  98.1 6.0 %collective-permute-start.9 = (f32[1,512]{1,0:T(1,128)S(1)}, f32[1,512]{1,0:T(1,128)S(1)}, u32[]{:S(2)}, u32[]{:S(2)}) collective-permute-start(f32[1,512]{1,0:T(1,128)S(1)} %bitcast.112), channel_id=1, source_target_pairs={{0,0},{2,128},{4,256},{6,384},{128,2},{130,130},{132,258},{134,386... | collective-permute-start | bytes 6152 | tf_op jit(solution)/shard_map/ppermute | solution.py:30
  104.3 3.8 collective-permute-done.9
  110.3 14.3 %all-to-all-start.1 = ((bf16[64,21,512]{2,1,0:T(8,128)(2,1)}), bf16[64,21,512]{2,1,0:T(8,128)(2,1)S(1)}, u32[]{:S(2)}, u32[]{:S(2)}) async-start(bf16[64,21,512]{2,1,0:T(8,128)(2,1)} %reshape.145), calls=%async_computation.1 | async-start | bytes 3145728 | tf_op jit(solution)/shard_map/all_to_all | solution.py:169
  129.8 29.6 %all-to-all-done.1 = bf16[64,21,512]{2,1,0:T(8,128)(2,1)S(1)} async-done(((bf16[64,21,512]{2,1,0:T(8,128)(2,1)}), bf16[64,21,512]{2,1,0:T(8,128)(2,1)S(1)}, u32[]{:S(2)}, u32[]{:S(2)}) %all-to-all-start.1) | async-done | bytes 1376288 | tf_op jit(solution)/shard_map/all_to_all | solution.py:169
  165.2 3.5 collective-permute-start.11
  172.3 98.4 %collective-permute-done.11 = bf16[1024,768]{1,0:T(8,128)(2,1)} collective-permute-done((bf16[1024,768]{1,0:T(8,128)(2,1)}, bf16[1024,768]{1,0:T(8,128)(2,1)}, u32[]{:S(2)}, u32[]{:S(2)}) %collective-permute-start.11) | collective-permute-done | bytes 1572896 | tf_op jit(solution)/shard_map/ppermute | solution.py:30
  275.6 30.5 %all_to_all.20 = bf16[4,352,768]{2,1,0:T(8,128)(2,1)S(1)} all-to-all(bf16[4,352,768]{2,1,0:T(8,128)(2,1)S(1)} %fusion.3), channel_id=1, replica_groups=mesh['x'=4,'y'=8,'l'=2,'h'=4,'c'=2] {'x'}, dimensions={0} | all-to-all | bytes 4325376 | tf_op jit(solution)/shard_map/all_to_all | solution.py:188
  307.1 15.2 %all_gather.11 = bf16[1344,384]{1,0:T(8,128)(2,1)S(1)} all-gather(bf16[336,384]{1,0:T(8,128)(2,1)S(1)} %fusion.19), channel_id=1, replica_groups=mesh['x'=4,'y'=8,'l'=2,'h'=4,'c'=2] {'x'}, dimensions={0}, use_global_device_ids=true | all-gather | bytes 1290240 | tf_op jit(solution)/shard_map/all_gather | solution.py:199
  324.2 7.9 %collective-permute-start.14 = (bf16[768,512]{1,0:T(8,128)(2,1)S(1)}, bf16[768,512]{1,0:T(8,128)(2,1)S(1)}, u32[]{:S(2)}, u32[]{:S(2)}) collective-permute-start(bf16[768,512]{1,0:T(8,128)(2,1)S(1)} %bitcast.111), channel_id=1, source_target_pairs={{0,0},{2,128},{4,256},{6,384},{128,2},{130,130},{132,258},{134,386... | collective-permute-start | bytes 2359304 | tf_op jit(solution)/shard_map/ppermute | solution.py:30
  332.1 51.0 %collective-permute-done.14 = bf16[768,512]{1,0:T(8,128)(2,1)S(1)} collective-permute-done((bf16[768,512]{1,0:T(8,128)(2,1)S(1)}, bf16[768,512]{1,0:T(8,128)(2,1)S(1)}, u32[]{:S(2)}, u32[]{:S(2)}) %collective-permute-start.14) | collective-permute-done | bytes 786464 | tf_op jit(solution)/shard_map/ppermute | solution.py:30
  386.2 9.7 %all-to-all-start.3 = ((bf16[64,21,512]{2,1,0:T(8,128)(2,1)}), bf16[64,21,512]{2,1,0:T(8,128)(2,1)S(1)}, u32[]{:S(2)}, u32[]{:S(2)}) async-start(bf16[64,21,512]{2,1,0:T(8,128)(2,1)} %reshape.148), calls=%async_computation.3 | async-start | bytes 3145728 | tf_op jit(solution)/shard_map/all_to_all | solution.py:213
  396.0 10.0 %collective-permute-start.7 = (bf16[128,512]{1,0:T(8,128)(2,1)S(1)}, bf16[128,512]{1,0:T(8,128)(2,1)S(1)}, u32[]{:S(2)}, u32[]{:S(2)}) collective-permute-start(bf16[128,512]{1,0:T(8,128)(2,1)S(1)} %fusion.50), channel_id=1, source_target_pairs={{0,0},{2,128},{4,256},{6,384},{128,2},{130,130},{132,258},{134,386... | collective-permute-start | bytes 393224 | tf_op jit(solution)/shard_map/ppermute | solution.py:30
  406.1 37.1 %all-to-all-done.3 = bf16[64,21,512]{2,1,0:T(8,128)(2,1)S(1)} async-done(((bf16[64,21,512]{2,1,0:T(8,128)(2,1)}), bf16[64,21,512]{2,1,0:T(8,128)(2,1)S(1)}, u32[]{:S(2)}, u32[]{:S(2)}) %all-to-all-start.3) | async-done | bytes 1376288 | tf_op jit(solution)/shard_map/all_to_all | solution.py:213
  446.7 9.1 %collective-permute-done.16 = bf16[128,512]{1,0:T(8,128)(2,1)S(1)} collective-permute-done((bf16[128,512]{1,0:T(8,128)(2,1)S(1)}, bf16[128,512]{1,0:T(8,128)(2,1)S(1)}, u32[]{:S(2)}, u32[]{:S(2)}) %collective-permute-start.16) | collective-permute-done | bytes 131104 | tf_op jit(solution)/shard_map/ppermute | solution.py:30
  (106 shorter events, 46.0 us)
Async XLA Ops:
  7.2 31.5 %copy-start = (bf16[128,512]{1,0:T(8,128)(2,1)S(1)}, bf16[128,512]{1,0:T(8,128)(2,1)}, u32[]{:S(2)}) copy-start(bf16[128,512]{1,0:T(8,128)(2,1)} %param.14) | copy-start | bytes 393220
  7.2 70.4 %all-gather.2.cloned.1.call-start = ((), (), s32[]{:S(2)}) async-start(), calls=%async_computation.4 | async-start | bytes 1179648 | tf_op jit(solution)/shard_map/all_gather | solution.py:119
  8.0 30.5 %collective-permute-start.3 = (bf16[128,256]{1,0:T(8,128)(2,1)S(1)}, bf16[128,256]{1,0:T(8,128)(2,1)S(1)}, u32[]{:S(2)}, u32[]{:S(2)}) collective-permute-start(bf16[128,256]{1,0:T(8,128)(2,1)S(1)} %pad_maximum_fusion.3), channel_id=1, source_target_pairs={{0,8},{8,16},{16,24},{24,32},{32,40},{40,48},{48,56},{56,64},{64,7... | collective-permute-start | bytes 196616 | tf_op jit(solution)/shard_map/ppermute | solution.py:39
  12.3 26.3 %collective-permute-start.2 = (bf16[128,256]{1,0:T(8,128)(2,1)S(1)}, bf16[128,256]{1,0:T(8,128)(2,1)S(1)}, u32[]{:S(2)}, u32[]{:S(2)}) collective-permute-start(bf16[128,256]{1,0:T(8,128)(2,1)S(1)} %pad_maximum_fusion.3), channel_id=1, source_target_pairs={{0,16},{8,24},{16,32},{24,40},{32,48},{40,56},{48,64},{56,72},{64,... | collective-permute-start | bytes 196616 | tf_op jit(solution)/shard_map/ppermute | solution.py:39
  14.9 23.7 %collective-permute-start.1 = (bf16[128,256]{1,0:T(8,128)(2,1)S(1)}, bf16[128,256]{1,0:T(8,128)(2,1)S(1)}, u32[]{:S(2)}, u32[]{:S(2)}) collective-permute-start(bf16[128,256]{1,0:T(8,128)(2,1)S(1)} %pad_maximum_fusion.3), channel_id=1, source_target_pairs={{0,24},{8,32},{16,40},{24,48},{32,56},{40,64},{48,72},{56,80},{64,... | collective-permute-start | bytes 196616 | tf_op jit(solution)/shard_map/ppermute | solution.py:39
  17.0 14.7 %collective-permute-start.4 = (bf16[64,512]{1,0:T(8,128)(2,1)}, bf16[64,512]{1,0:T(8,128)(2,1)S(1)}, u32[]{:S(2)}, u32[]{:S(2)}) collective-permute-start(bf16[64,512]{1,0:T(8,128)(2,1)} %param.17), channel_id=1, source_target_pairs={{0,0},{2,128},{4,256},{6,384},{128,2},{130,130},{132,258},{134,386... | collective-permute-start | bytes 196616 | tf_op jit(solution)/shard_map/ppermute | solution.py:30
  31.7 6.1 %collective-permute-start.5 = (bf16[64,512]{1,0:T(8,128)(2,1)S(1)}, bf16[64,512]{1,0:T(8,128)(2,1)S(1)}, u32[]{:S(2)}, u32[]{:S(2)}) collective-permute-start(bf16[64,512]{1,0:T(8,128)(2,1)S(1)} %collective-permute-done.4), channel_id=1, source_target_pairs={{0,8},{8,0},{1,9},{9,1},{2,10},{10,2},{3,11},{11,3},{4,12},{12,4},... | collective-permute-start | bytes 196616 | tf_op jit(solution)/shard_map/ppermute | solution.py:34
  52.5 26.7 %collective-permute-start.6 = (bf16[512,512]{0,1:T(8,128)(2,1)S(1)}, bf16[512,512]{0,1:T(8,128)(2,1)S(1)}, u32[]{:S(2)}, u32[]{:S(2)}) collective-permute-start(bf16[512,512]{0,1:T(8,128)(2,1)S(1)} %all_gather.9), channel_id=1, source_target_pairs={{0,1},{1,0},{2,3},{3,2},{4,5},{5,4},{6,7},{7,6},{8,9},{9,8},{10,11... | collective-permute-start | bytes 1572872 | tf_op jit(solution)/shard_map/ppermute | solution.py:34
  79.2 18.9 %copy-start.10 = (f32[512]{0:T(512)S(1)}, f32[512]{0:T(512)}, u32[]{:S(2)}) copy-start(f32[512]{0:T(512)} %param.19) | copy-start | bytes 6148
  80.5 23.7 %all-to-all-start = ((bf16[4,128,512]{2,1,0:T(8,128)(2,1)}), bf16[4,128,512]{2,1,0:T(8,128)(2,1)S(1)}, u32[]{:S(2)}, u32[]{:S(2)}) async-start(bf16[4,128,512]{2,1,0:T(8,128)(2,1)} %bitcast.6), calls=%async_computation | async-start | bytes 1048576 | tf_op jit(solution)/shard_map/all_to_all | solution.py:161
  88.0 16.1 %collective-permute-start.8 = (f32[128,16]{0,1:T(8,128)S(1)}, f32[128,16]{0,1:T(8,128)S(1)}, u32[]{:S(2)}, u32[]{:S(2)}) collective-permute-start(f32[128,16]{0,1:T(8,128)S(1)} %pad_maximum_fusion.4), channel_id=1, source_target_pairs={{0,0},{2,128},{4,256},{6,384},{128,2},{130,130},{132,258},{134,386... | collective-permute-start | bytes 24584 | tf_op jit(solution)/shard_map/ppermute | solution.py:30
  94.1 14.0 %collective-permute-start = (bf16[128,512]{1,0:T(8,128)(2,1)S(1)}, bf16[128,512]{1,0:T(8,128)(2,1)S(1)}, u32[]{:S(2)}, u32[]{:S(2)}) collective-permute-start(bf16[128,512]{1,0:T(8,128)(2,1)S(1)} %copy-done.9), channel_id=1, source_target_pairs={{0,0},{2,128},{4,256},{6,384},{128,2},{130,130},{132,258},{134,386... | collective-permute-start | bytes 393224 | tf_op jit(solution)/shard_map/ppermute | solution.py:30
  98.1 9.9 %collective-permute-start.9 = (f32[1,512]{1,0:T(1,128)S(1)}, f32[1,512]{1,0:T(1,128)S(1)}, u32[]{:S(2)}, u32[]{:S(2)}) collective-permute-start(f32[1,512]{1,0:T(1,128)S(1)} %bitcast.112), channel_id=1, source_target_pairs={{0,0},{2,128},{4,256},{6,384},{128,2},{130,130},{132,258},{134,386... | collective-permute-start | bytes 6152 | tf_op jit(solution)/shard_map/ppermute | solution.py:30
  110.3 49.1 %all-to-all-start.1 = ((bf16[64,21,512]{2,1,0:T(8,128)(2,1)}), bf16[64,21,512]{2,1,0:T(8,128)(2,1)S(1)}, u32[]{:S(2)}, u32[]{:S(2)}) async-start(bf16[64,21,512]{2,1,0:T(8,128)(2,1)} %reshape.145), calls=%async_computation.1 | async-start | bytes 3145728 | tf_op jit(solution)/shard_map/all_to_all | solution.py:169
  127.9 34.8 %collective-permute-start.10 = (bf16[512,768]{1,0:T(8,128)(2,1)}, bf16[512,768]{1,0:T(8,128)(2,1)}, u32[]{:S(2)}, u32[]{:S(2)}) collective-permute-start(bf16[512,768]{1,0:T(8,128)(2,1)} %pad_maximum_fusion.1), channel_id=1, source_target_pairs={{0,1},{1,0},{2,3},{3,2},{4,5},{5,4},{6,7},{7,6},{8,9},{9,8},{10,11... | collective-permute-start | bytes 2359304 | tf_op jit(solution)/shard_map/ppermute | solution.py:34
  160.7 11.0 %collective-permute-start.12 = (bf16[1344,512]{1,0:T(8,128)(2,1)}, bf16[1344,512]{1,0:T(8,128)(2,1)S(1)}, u32[]{:S(2)}, u32[]{:S(2)}) collective-permute-start(bf16[1344,512]{1,0:T(8,128)(2,1)} %reshape.146), channel_id=1, source_target_pairs={{0,1},{1,0},{2,3},{3,2},{4,5},{5,4},{6,7},{7,6},{8,9},{9,8},{10,11... | collective-permute-start | bytes 4128776 | tf_op jit(solution)/shard_map/ppermute | solution.py:34
  165.2 105.5 %collective-permute-start.11 = (bf16[1024,768]{1,0:T(8,128)(2,1)}, bf16[1024,768]{1,0:T(8,128)(2,1)}, u32[]{:S(2)}, u32[]{:S(2)}) collective-permute-start(bf16[1024,768]{1,0:T(8,128)(2,1)} %pad_maximum_fusion), channel_id=1, source_target_pairs={{0,0},{2,128},{4,256},{6,384},{128,2},{130,130},{132,258},{134,386... | collective-permute-start | bytes 4718600 | tf_op jit(solution)/shard_map/ppermute | solution.py:30
  168.6 3.1 collective-permute-start.13
  172.3 100.8 %copy-start.1 = (bf16[1344,512]{1,0:T(8,128)(2,1)S(1)}, bf16[1344,512]{1,0:T(8,128)(2,1)}, u32[]{:S(2)}) copy-start(bf16[1344,512]{1,0:T(8,128)(2,1)} %reshape.146) | copy-start | bytes 4128772
  322.3 60.8 %collective-permute-start.15 = (bf16[1344,384]{1,0:T(8,128)(2,1)S(1)}, bf16[1344,384]{1,0:T(8,128)(2,1)S(1)}, u32[]{:S(2)}, u32[]{:S(2)}) collective-permute-start(bf16[1344,384]{1,0:T(8,128)(2,1)S(1)} %all_gather.11), channel_id=1, source_target_pairs={{0,1},{1,0},{2,3},{3,2},{4,5},{5,4},{6,7},{7,6},{8,9},{9,8},{10,11... | collective-permute-start | bytes 3096584 | tf_op jit(solution)/shard_map/ppermute | solution.py:34
  324.2 58.8 %collective-permute-start.14 = (bf16[768,512]{1,0:T(8,128)(2,1)S(1)}, bf16[768,512]{1,0:T(8,128)(2,1)S(1)}, u32[]{:S(2)}, u32[]{:S(2)}) collective-permute-start(bf16[768,512]{1,0:T(8,128)(2,1)S(1)} %bitcast.111), channel_id=1, source_target_pairs={{0,0},{2,128},{4,256},{6,384},{128,2},{130,130},{132,258},{134,386... | collective-permute-start | bytes 2359304 | tf_op jit(solution)/shard_map/ppermute | solution.py:30
  386.2 56.9 %all-to-all-start.3 = ((bf16[64,21,512]{2,1,0:T(8,128)(2,1)}), bf16[64,21,512]{2,1,0:T(8,128)(2,1)S(1)}, u32[]{:S(2)}, u32[]{:S(2)}) async-start(bf16[64,21,512]{2,1,0:T(8,128)(2,1)} %reshape.148), calls=%async_computation.3 | async-start | bytes 3145728 | tf_op jit(solution)/shard_map/all_to_all | solution.py:213
  396.0 50.7 %collective-permute-start.7 = (bf16[128,512]{1,0:T(8,128)(2,1)S(1)}, bf16[128,512]{1,0:T(8,128)(2,1)S(1)}, u32[]{:S(2)}, u32[]{:S(2)}) collective-permute-start(bf16[128,512]{1,0:T(8,128)(2,1)S(1)} %fusion.50), channel_id=1, source_target_pairs={{0,0},{2,128},{4,256},{6,384},{128,2},{130,130},{132,258},{134,386... | collective-permute-start | bytes 393224 | tf_op jit(solution)/shard_map/ppermute | solution.py:30
  444.6 11.2 %collective-permute-start.16 = (bf16[128,512]{1,0:T(8,128)(2,1)S(1)}, bf16[128,512]{1,0:T(8,128)(2,1)S(1)}, u32[]{:S(2)}, u32[]{:S(2)}) collective-permute-start(bf16[128,512]{1,0:T(8,128)(2,1)S(1)} %convolution_convert_fusion.1), channel_id=1, source_target_pairs={{0,0},{2,128},{4,256},{6,384},{128,2},{130,130},{132,258},{134,386... | collective-permute-start | bytes 393224 | tf_op jit(solution)/shard_map/ppermute | solution.py:30
  (8 other events, 73.0 us)
Sparse Core Ops, SparseCore 0:
  38.7 38.8 all-gather.1

commit v2 on v1

v2 whole, which is shorter than its diff:
```python
import jax
import jax.numpy as jnp
import numpy as np
from jax import lax
from jax.sharding import Mesh, PartitionSpec as P

D = 4096
HD = 128
TOPK = 8
QH = 32
KVH = 2
FF = 768
FIX = 32
TOK = 128
SLOTS = 21
NX, NY, NL, NH, NC = 4, 8, 2, 4, 2
N_CTX = NX * NY * NL
GRID = NX * NY
ROWS = GRID * SLOTS
SHARE = ROWS // NH
SLICE = D // (NH * NC)
CTX = ("x", "y", "l")
f32, bf16 = jnp.float32, jnp.bfloat16

epsilon = 1e-06


def turn(block):
    route = [(a * NH + b, b * NX + a) for a in range(NX) for b in range(NH)]
    return lax.ppermute(block, ("x", "h"), route)


def swap(block, axis):
    return lax.ppermute(block, axis, [(0, 1), (1, 0)])


def cycle(block):
    return lax.ppermute(block, ("l", "c"), [(0, 3), (3, 2), (2, 1), (1, 0)])


def cycle_back(block):
    return lax.ppermute(block, ("l", "c"), [(3, 0), (2, 3), (1, 2), (0, 1)])


def across(block):
    return lax.ppermute(block, ("l", "c"), [(1, 3), (3, 1)])


def from_behind(block, distance):
    route = [(i, i + distance) for i in range(N_CTX - distance)]
    return lax.ppermute(block, CTX, route)


def attention(queries, key_rows, value_rows):
    tokens = queries.shape[0]
    block = lax.axis_index(CTX)
    kv_first = lax.axis_index("h") // 2 * HD
    own = jnp.concatenate(
        [
            lax.dynamic_slice_in_dim(key_rows, kv_first, HD, 1),
            lax.dynamic_slice_in_dim(value_rows, kv_first, HD, 1),
        ],
        axis=1,
    )
    pairs = [from_behind(own, 3), from_behind(own, 2), from_behind(own, 1), own]
    keys = jnp.concatenate([pair[:, :HD] for pair in pairs], axis=0)
    values = jnp.concatenate([pair[:, HD:] for pair in pairs], axis=0)
    q_view = queries.reshape(tokens, -1, HD)
    scores = jnp.einsum("tgd,sd->gts", q_view, keys, preferred_element_type=f32) / HD**0.5
    q_pos = block * tokens + jnp.arange(tokens)
    k_pos = (block - 3) * tokens + jnp.arange(4 * tokens)
    allowed = (k_pos[None, :] >= 0) & (k_pos[None, :] <= q_pos[:, None])
    scores = jnp.where(allowed, scores, -1e30)
    highest = jnp.max(scores, axis=2, keepdims=True)
    weights = jnp.where(allowed, jnp.exp(scores - highest), 0.0)
    denominators = jnp.sum(weights, axis=2, keepdims=True)
    mixed = (
        jnp.einsum("gts,sd->gtd", weights.astype(bf16), values, preferred_element_type=f32)
        / denominators
    )
    return jnp.transpose(mixed, (1, 0, 2)).reshape(tokens, -1).astype(bf16)


def slots_of(pred_ids, fix_pair, fix_expert, fix_count):
    tokens = pred_ids.shape[0]
    places = jnp.arange(tokens * TOPK, dtype=jnp.int32).reshape(tokens, TOPK)
    live = jnp.arange(FIX) < fix_count[0]
    hit = (places[:, :, None] == fix_pair[0][None, None, :]) & live[None, None, :]
    fixed = jnp.sum(jnp.where(hit, fix_expert[0][None, None, :], 0), axis=2)
    ids = jnp.where(jnp.any(hit, axis=2), fixed, pred_ids)
    named = ids[:, :, None] == jnp.arange(N_CTX)[None, None, :]
    counts = jnp.sum(named.astype(f32), axis=1)
    earlier = (
        jnp.arange(tokens)[:, None] > jnp.arange(tokens)[None, :]
    ).astype(bf16)
    before = jnp.dot(earlier, counts.astype(bf16), preferred_element_type=f32)
    rank = jnp.sum(jnp.where(named, before[:, None, :], 0.0), axis=2)
    twin = (ids[:, :, None] == ids[:, None, :]) & (
        jnp.arange(TOPK)[None, :, None] > jnp.arange(TOPK)[None, None, :]
    )
    rank = rank + jnp.sum(twin.astype(f32), axis=2)
    return ids.astype(f32), rank


def body(
    queries,
    key_rows,
    value_rows,
    out_weight,
    residual,
    norm_gain,
    w_gate,
    w_up,
    w_down,
    pred_ids,
    route_gates,
    fix_pair,
    fix_expert,
    fix_count,
):
    core, side = lax.axis_index("c"), lax.axis_index("l")
    tokens = queries.shape[0]

    other_strip = swap(out_weight, "l")
    strips = jnp.concatenate(
        [
            jnp.where(side == 0, out_weight, other_strip),
            jnp.where(side == 0, other_strip, out_weight),
        ],
        axis=0,
    )
    quarter = lax.all_gather(strips, "y", axis=0, tiled=True)

    ids, rank = slots_of(pred_ids, fix_pair, fix_expert, fix_count)
    table = jnp.concatenate([ids, rank, route_gates.astype(f32)], axis=1)
    table = jnp.where(core == 0, table, swap(table, "l")).T
    ids, rank, gates = table[:TOPK], table[TOPK : 2 * TOPK], table[2 * TOPK :]
    column = jnp.floor(ids * 0.5)
    slots = jnp.where(ids - 2.0 * column == side.astype(f32), column * SLOTS + rank, -1.0)
    row_ids = jnp.arange(ROWS, dtype=f32)[:, None]
    row_map = jnp.zeros((ROWS, tokens), f32)
    combine = jnp.zeros((ROWS, tokens), f32)
    for k in range(TOPK):
        here = slots[k][None, :] == row_ids
        row_map = row_map + jnp.where(here, 1.0, 0.0)
        combine = combine + jnp.where(here, gates[k][None, :], 0.0)
    row_map, combine = row_map.astype(bf16), combine.astype(bf16)

    gate_up = jnp.concatenate([w_gate[0], w_up[0]], axis=1)
    other_gate_up = swap(gate_up, "c")
    down = jnp.concatenate([w_down[0], swap(w_down[0], "c")], axis=1)
    gain = norm_gain[None, :]
    inverse = 1.0 / (gain * gain)
    other_inverse = swap(inverse, "c")

    attended = turn(attention(queries, key_rows, value_rows))
    heads = lax.all_gather(attended, "h", axis=0, tiled=True)
    other_heads = swap(heads, "c")
    partial = jnp.dot(
        heads,
        lax.dynamic_slice_in_dim(quarter, core * SLICE, SLICE, 0),
        preferred_element_type=f32,
    ) + jnp.dot(
        other_heads,
        lax.dynamic_slice_in_dim(quarter, (1 - core) * SLICE, SLICE, 0),
        preferred_element_type=f32,
    )
    terms = lax.all_to_all(
        partial.astype(bf16).reshape(NX, tokens, SLICE), "x", split_axis=0, concat_axis=0, tiled=True
    )
    stream = residual.astype(f32) + jnp.sum(terms.astype(f32), axis=0)

    scaled = (stream * gain).astype(bf16)
    near, far = cycle(scaled), across(scaled)
    both = jnp.concatenate([jnp.where(core == 0, scaled, far), near], axis=1)
    outgoing = jnp.dot(row_map, both, preferred_element_type=f32).astype(bf16)
    incoming = lax.all_to_all(
        outgoing.reshape(GRID, SLOTS, 2 * SLICE), ("x", "y"), split_axis=0, concat_axis=0, tiled=True
    ).reshape(ROWS, 2 * SLICE)
    own_rows, other_rows = incoming[:, :SLICE], incoming[:, SLICE:]
    part = (
        jnp.dot(own_rows, gate_up, preferred_element_type=f32)
        + jnp.dot(other_rows, other_gate_up, preferred_element_type=f32)
    ).astype(bf16)
    sums = lax.psum_scatter(part, "h", scatter_dimension=0, tiled=True).astype(f32)
    squares = jnp.sum(
        jnp.square(own_rows.astype(f32)) * inverse
        + jnp.square(other_rows.astype(f32)) * other_inverse,
        axis=1,
    )
    totals = lax.psum(squares, "h")
    totals = lax.dynamic_slice_in_dim(totals, lax.axis_index("h") * SHARE, SHARE, 0)
    sums = sums * lax.rsqrt(totals / D + epsilon)[:, None]
    hidden = (jax.nn.silu(sums[:, :FF]) * sums[:, FF:]).astype(bf16)
    all_hidden = lax.all_gather(hidden, "h", axis=0, tiled=True)
    results = jnp.dot(all_hidden, down, preferred_element_type=f32).astype(bf16)
    returned = lax.all_to_all(
        results.reshape(GRID, SLOTS, 2 * SLICE), ("x", "y"), split_axis=0, concat_axis=0, tiled=True
    ).reshape(ROWS, 2 * SLICE)
    mixed = jnp.einsum("rt,rd->td", combine, returned, preferred_element_type=f32)
    own_mixed, other_mixed = mixed[:, :SLICE], mixed[:, SLICE:].astype(bf16)
    from_near, from_far = cycle_back(other_mixed), across(own_mixed.astype(bf16))
    expert_out = from_near.astype(f32) + jnp.where(core == 0, own_mixed, from_far.astype(f32))
    return stream.astype(bf16), expert_out.astype(bf16)


def solution(mesh):
    split = Mesh(np.asarray(mesh.devices).reshape(NX, NY, NL, NH, NC), ("x", "y", "l", "h", "c"))
    ctx, exp = CTX, ("h", "c")
    placed = (
        P(ctx, exp),
        P(ctx, None),
        P(ctx, None),
        P(ctx, exp),
        P(ctx, exp),
        P(exp),
        P(ctx, exp, None),
        P(ctx, exp, None),
        P(ctx, None, exp),
        P(ctx, None),
        P(ctx, None),
        P(ctx, None),
        P(ctx, None),
        P(ctx),
    )
    return jax.shard_map(
        body,
        mesh=split,
        in_specs=placed,
        out_specs=(P(ctx, exp), P(ctx, exp)),
        check_vma=False,
    )
```

time: 466 us -> 295 us (0.63)
  the two profiles are of different devices: /device:TPU:38 before, /device:TPU:8 now
where the time goes in v2:
time: 295 us; the launch traced here: 294 us
  waiting for transfers between devices  121 us (41%)
  blocking collectives  72 us (24%)
  starting transfers between devices  57.2 us (19%)
  between operations  15.3 us (5%)
  matrix products  14.7 us (5%)
  other arithmetic  9.92 us (3%)
  local copies, waits for them, and re-layouts  4.62 us (2%)
    all_gather x1, blocking collectives, body(): heads = lax.all_gather(attended, 'h', axis=0, tiled=True)  40.2 us
    all_to_all x1, waiting for transfers between devices, body(): lax.all_to_all(results.reshape(GRID, SLOTS, 2 * SLICE), ('x', 'y'), split...  37.5 us
    all_to_all x1, waiting for transfers between devices, body(): lax.all_to_all(outgoing.reshape(GRID, SLOTS, 2 * SLICE), ('x', 'y'), spli...  34 us
    reduce_scatter x1, waiting for transfers between devices, body(): lax.psum_scatter(part, 'h', scatter_dimension=0, tiled=True).astype(f32)  32.2 us
    all_gather x1, blocking collectives, body(): all_hidden = lax.all_gather(hidden, 'h', axis=0, tiled=True)  20.5 us
    ppermute x6, starting transfers between devices, swap(): return lax.ppermute(block, axis, [(0, 1), (1, 0)])  15.6 us
    ppermute x3, starting transfers between devices, from_behind(): return lax.ppermute(block, CTX, route)  12.6 us
    all_to_all x1, starting transfers between devices, body(): lax.all_to_all(results.reshape(GRID, SLOTS, 2 * SLICE), ('x', 'y'), split...  12 us
  transfers between devices with their start and end apart: 19, of which 6 were waited for; matrix products, arithmetic and copies ran while one was open for 5% of the time, Pallas kernels for 0%

profile of v2, /device:TPU:8, one launch (start us, length us, event | category | flops | bytes accessed | tf_op | source)
XLA Modules:
  0.0 294.4 jit_solution(7343591451686358169)
XLA Ops:
  8.0 4.3 %collective-permute-start.2 = (bf16[128,256]{1,0:T(8,128)(2,1)S(1)}, bf16[128,256]{1,0:T(8,128)(2,1)S(1)}, u32[]{:S(2)}, u32[]{:S(2)}) collective-permute-start(bf16[128,256]{1,0:T(8,128)(2,1)S(1)} %pad_maximum_fusion.2), channel_id=1, source_target_pairs={{0,8},{8,16},{16,24},{24,32},{32,40},{40,48},{48,56},{56,64},{64,7... | collective-permute-start | bytes 196616 | tf_op jit(solution)/shard_map/ppermute | solution.py:51
  12.3 3.5 %collective-permute-start.1 = (bf16[128,256]{1,0:T(8,128)(2,1)S(1)}, bf16[128,256]{1,0:T(8,128)(2,1)S(1)}, u32[]{:S(2)}, u32[]{:S(2)}) collective-permute-start(bf16[128,256]{1,0:T(8,128)(2,1)S(1)} %pad_maximum_fusion.2), channel_id=1, source_target_pairs={{0,16},{8,24},{16,32},{24,40},{32,48},{40,56},{48,64},{56,72},{64,... | collective-permute-start | bytes 196616 | tf_op jit(solution)/shard_map/ppermute | solution.py:51
  15.8 4.8 %collective-permute-start = (bf16[128,256]{1,0:T(8,128)(2,1)S(1)}, bf16[128,256]{1,0:T(8,128)(2,1)S(1)}, u32[]{:S(2)}, u32[]{:S(2)}) collective-permute-start(bf16[128,256]{1,0:T(8,128)(2,1)S(1)} %pad_maximum_fusion.2), channel_id=1, source_target_pairs={{0,24},{8,32},{16,40},{24,48},{32,56},{40,64},{48,72},{56,80},{64,... | collective-permute-start | bytes 196616 | tf_op jit(solution)/shard_map/ppermute | solution.py:51
  20.6 4.3 %collective-permute-start.4 = (bf16[64,512]{1,0:T(8,128)(2,1)}, bf16[64,512]{1,0:T(8,128)(2,1)S(1)}, u32[]{:S(2)}, u32[]{:S(2)}) collective-permute-start(bf16[64,512]{1,0:T(8,128)(2,1)} %param.17), channel_id=1, source_target_pairs={{0,8},{8,0},{1,9},{9,1},{2,10},{10,2},{3,11},{11,3},{4,12},{12,4},... | collective-permute-start | bytes 196616 | tf_op jit(solution)/shard_map/ppermute | solution.py:34
  31.8 40.2 %all_gather.9 = bf16[512,512]{0,1:T(8,128)(2,1)S(1)} all-gather(bf16[128,512]{0,1:T(8,128)(2,1)S(1)} %collective-permute-done.3), channel_id=1, replica_groups=mesh['x'=4,'y'=8,'l'=2,'h'=4,'c'=2] {'h'}, dimensions={0}, use_global_device_ids=true | all-gather | bytes 655360 | tf_op jit(solution)/shard_map/all_gather | solution.py:157
  79.0 4.5 %all-to-all-start = ((bf16[4,128,512]{2,1,0:T(8,128)(2,1)}), bf16[4,128,512]{2,1,0:T(8,128)(2,1)S(1)}, u32[]{:S(2)}, u32[]{:S(2)}) async-start(bf16[4,128,512]{2,1,0:T(8,128)(2,1)} %bitcast.6), calls=%async_computation | async-start | bytes 1048576 | tf_op jit(solution)/shard_map/all_to_all | solution.py:168
  83.5 10.1 %all-to-all-done = bf16[4,128,512]{2,1,0:T(8,128)(2,1)S(1)} async-done(((bf16[4,128,512]{2,1,0:T(8,128)(2,1)}), bf16[4,128,512]{2,1,0:T(8,128)(2,1)S(1)}, u32[]{:S(2)}, u32[]{:S(2)}) %all-to-all-start) | async-done | bytes 524320 | tf_op jit(solution)/shard_map/all_to_all | solution.py:168
  95.1 3.9 %collective-permute-start.8 = (bf16[128,512]{1,0:T(8,128)(2,1)S(1)}, bf16[128,512]{1,0:T(8,128)(2,1)S(1)}, u32[]{:S(2)}, u32[]{:S(2)}) collective-permute-start(bf16[128,512]{1,0:T(8,128)(2,1)S(1)} %get-tuple-element.6), channel_id=1, source_target_pairs={{0,9},{9,8},{8,1},{1,0},{2,11},{11,10},{10,3},{3,2},{4,13},{13,12}... | collective-permute-start | bytes 393224 | tf_op jit(solution)/shard_map/ppermute | solution.py:38
  99.1 2.5 collective-permute-done.8
  103.6 4.7 %all-to-all-start.1 = ((bf16[32,21,1024]{2,1,0:T(8,128)(2,1)}), bf16[32,21,1024]{2,1,0:T(8,128)(2,1)S(1)}, u32[]{:S(2)}, u32[]{:S(2)}) async-start(bf16[32,21,1024]{2,1,0:T(8,128)(2,1)} %reshape.79), calls=%async_computation.1 | async-start | bytes 3145728 | tf_op jit(solution)/shard_map/all_to_all | solution.py:177
  108.4 2.4 pad_maximum_fusion
  110.8 3.0 %collective-permute-start.9 = (bf16[512,1536]{1,0:T(8,128)(2,1)}, bf16[512,1536]{1,0:T(8,128)(2,1)}, u32[]{:S(2)}, u32[]{:S(2)}) collective-permute-start(bf16[512,1536]{1,0:T(8,128)(2,1)} %pad_maximum_fusion), channel_id=1, source_target_pairs={{0,1},{1,0},{2,3},{3,2},{4,5},{5,4},{6,7},{7,6},{8,9},{9,8},{10,11... | collective-permute-start | bytes 4718600 | tf_op jit(solution)/shard_map/ppermute | solution.py:34
  113.8 34.0 %all-to-all-done.1 = bf16[32,21,1024]{2,1,0:T(8,128)(2,1)S(1)} async-done(((bf16[32,21,1024]{2,1,0:T(8,128)(2,1)}), bf16[32,21,1024]{2,1,0:T(8,128)(2,1)S(1)}, u32[]{:S(2)}, u32[]{:S(2)}) %all-to-all-start.1) | async-done | bytes 1376288 | tf_op jit(solution)/shard_map/all_to_all | solution.py:177
  148.2 2.6 fusion.13
  150.9 4.0 %add_convert_fusion = bf16[672,1536]{1,0:T(8,128)(2,1)} fusion(f32[672,1536]{1,0:T(8,128)S(1)} %fusion.13, bf16[512,1536]{1,0:T(8,128)(2,1)} %collective-permute-done.9, bf16[672,1024]{1,0:T(8,128)(2,1)S(1)} %reshape.80), kind=kOutput, calls=%fused_computation.1 | convolution fusion | flops 1059028992 | bytes 8454144 | tf_op jit(solution)/shard_map/dot_general | solution.py:183
  154.9 2.3 collective-permute-start.10
  157.2 2.2 collective-permute-start.11
  159.8 11.3 %psum.7 = f32[672]{0:T(1024)S(1)} all-reduce(f32[672]{0:T(1024)S(1)} %add_reduce_fusion), channel_id=1, replica_groups=mesh['x'=4,'y'=8,'l'=2,'h'=4,'c'=2] {'h'}, use_global_device_ids=true, to_apply=%region_10.11 | all-reduce | flops 672 | bytes 5376 | tf_op jit(solution)/shard_map/psum | solution.py:191
  171.2 32.2 %reduce-scatter.2.cloned.1.call-done = bf16[168,1536]{1,0:T(8,128)(2,1)} async-done(((bf16[672,1536]{1,0:T(8,128)(2,1)}), bf16[168,1536]{1,0:T(8,128)(2,1)}) %reduce-scatter.2.cloned.1.call-update) | async-done | bytes 516112 | tf_op jit(solution)/shard_map/reduce_scatter | solution.py:185
  204.7 20.5 %all_gather.11 = bf16[672,768]{1,0:T(8,128)(2,1)S(1)} all-gather(bf16[168,768]{1,0:T(8,128)(2,1)S(1)} %fusion.19), channel_id=1, replica_groups=mesh['x'=4,'y'=8,'l'=2,'h'=4,'c'=2] {'h'}, dimensions={0}, use_global_device_ids=true | all-gather | bytes 1290240 | tf_op jit(solution)/shard_map/all_gather | solution.py:195
  225.3 2.4 convolution_convert_fusion
  229.0 12.0 %all-to-all-start.2 = ((bf16[32,21,1024]{2,1,0:T(8,128)(2,1)}), bf16[32,21,1024]{2,1,0:T(8,128)(2,1)S(1)}, u32[]{:S(2)}, u32[]{:S(2)}) async-start(bf16[32,21,1024]{2,1,0:T(8,128)(2,1)} %reshape.81), calls=%async_computation.3 | async-start | bytes 3145728 | tf_op jit(solution)/shard_map/all_to_all | solution.py:197
  241.1 37.5 %all-to-all-done.2 = bf16[32,21,1024]{2,1,0:T(8,128)(2,1)S(1)} async-done(((bf16[32,21,1024]{2,1,0:T(8,128)(2,1)}), bf16[32,21,1024]{2,1,0:T(8,128)(2,1)S(1)}, u32[]{:S(2)}, u32[]{:S(2)}) %all-to-all-start.2) | async-done | bytes 1376288 | tf_op jit(solution)/shard_map/all_to_all | solution.py:197
  282.5 4.3 %collective-permute-done.12 = bf16[128,512]{1,0:T(8,128)(2,1)S(1)} collective-permute-done((bf16[128,512]{1,0:T(8,128)(2,1)S(1)}, bf16[128,512]{1,0:T(8,128)(2,1)S(1)}, u32[]{:S(2)}, u32[]{:S(2)}) %collective-permute-start.12) | collective-permute-done | bytes 131104 | tf_op jit(solution)/shard_map/ppermute | solution.py:42
  (86 shorter events, 25.7 us)
Async XLA Ops:
  7.2 22.5 %copy-start = (bf16[128,512]{1,0:T(8,128)(2,1)S(1)}, bf16[128,512]{1,0:T(8,128)(2,1)}, u32[]{:S(2)}) copy-start(bf16[128,512]{1,0:T(8,128)(2,1)} %param.14) | copy-start | bytes 393220
  7.2 69.0 %all-gather.2.cloned.1.call-start = ((), (), s32[]{:S(2)}) async-start(), calls=%async_computation.4 | async-start | bytes 1179648 | tf_op jit(solution)/shard_map/all_gather | solution.py:132
  8.0 21.6 %collective-permute-start.2 = (bf16[128,256]{1,0:T(8,128)(2,1)S(1)}, bf16[128,256]{1,0:T(8,128)(2,1)S(1)}, u32[]{:S(2)}, u32[]{:S(2)}) collective-permute-start(bf16[128,256]{1,0:T(8,128)(2,1)S(1)} %pad_maximum_fusion.2), channel_id=1, source_target_pairs={{0,8},{8,16},{16,24},{24,32},{32,40},{40,48},{48,56},{56,64},{64,7... | collective-permute-start | bytes 196616 | tf_op jit(solution)/shard_map/ppermute | solution.py:51
  12.3 17.3 %collective-permute-start.1 = (bf16[128,256]{1,0:T(8,128)(2,1)S(1)}, bf16[128,256]{1,0:T(8,128)(2,1)S(1)}, u32[]{:S(2)}, u32[]{:S(2)}) collective-permute-start(bf16[128,256]{1,0:T(8,128)(2,1)S(1)} %pad_maximum_fusion.2), channel_id=1, source_target_pairs={{0,16},{8,24},{16,32},{24,40},{32,48},{40,56},{48,64},{56,72},{64,... | collective-permute-start | bytes 196616 | tf_op jit(solution)/shard_map/ppermute | solution.py:51
  15.8 13.9 %collective-permute-start = (bf16[128,256]{1,0:T(8,128)(2,1)S(1)}, bf16[128,256]{1,0:T(8,128)(2,1)S(1)}, u32[]{:S(2)}, u32[]{:S(2)}) collective-permute-start(bf16[128,256]{1,0:T(8,128)(2,1)S(1)} %pad_maximum_fusion.2), channel_id=1, source_target_pairs={{0,24},{8,32},{16,40},{24,48},{32,56},{40,64},{48,72},{56,80},{64,... | collective-permute-start | bytes 196616 | tf_op jit(solution)/shard_map/ppermute | solution.py:51
  20.6 7.5 %collective-permute-start.4 = (bf16[64,512]{1,0:T(8,128)(2,1)}, bf16[64,512]{1,0:T(8,128)(2,1)S(1)}, u32[]{:S(2)}, u32[]{:S(2)}) collective-permute-start(bf16[64,512]{1,0:T(8,128)(2,1)} %param.17), channel_id=1, source_target_pairs={{0,8},{8,0},{1,9},{9,1},{2,10},{10,2},{3,11},{11,3},{4,12},{12,4},... | collective-permute-start | bytes 196616 | tf_op jit(solution)/shard_map/ppermute | solution.py:34
  31.0 0.8 collective-permute-start.3
  72.0 4.2 %collective-permute-start.5 = (bf16[512,512]{0,1:T(8,128)(2,1)S(1)}, bf16[512,512]{0,1:T(8,128)(2,1)S(1)}, u32[]{:S(2)}, u32[]{:S(2)}) collective-permute-start(bf16[512,512]{0,1:T(8,128)(2,1)S(1)} %all_gather.9), channel_id=1, source_target_pairs={{0,1},{1,0},{2,3},{3,2},{4,5},{5,4},{6,7},{7,6},{8,9},{9,8},{10,11... | collective-permute-start | bytes 1572872 | tf_op jit(solution)/shard_map/ppermute | solution.py:34
  74.2 9.3 %collective-permute-start.6 = (f32[128,24]{0,1:T(8,128)S(1)}, f32[128,24]{0,1:T(8,128)S(1)}, u32[]{:S(2)}, u32[]{:S(2)}) collective-permute-start(f32[128,24]{0,1:T(8,128)S(1)} %pad_maximum_fusion.3), channel_id=1, source_target_pairs={{0,8},{8,0},{1,9},{9,1},{2,10},{10,2},{3,11},{11,3},{4,12},{12,4},... | collective-permute-start | bytes 36872 | tf_op jit(solution)/shard_map/ppermute | solution.py:34
  79.0 14.7 %copy-start.3 = (bf16[128,512]{1,0:T(8,128)(2,1)S(1)}, bf16[128,512]{1,0:T(8,128)(2,1)}, u32[]{:S(2)}) copy-start(bf16[128,512]{1,0:T(8,128)(2,1)} %param.18) | copy-start | bytes 393220
  79.0 14.7 %copy-start.4 = (f32[512]{0:T(512)S(1)}, f32[512]{0:T(512)}, u32[]{:S(2)}) copy-start(f32[512]{0:T(512)} %param.19) | copy-start | bytes 6148
  79.0 14.6 %all-to-all-start = ((bf16[4,128,512]{2,1,0:T(8,128)(2,1)}), bf16[4,128,512]{2,1,0:T(8,128)(2,1)S(1)}, u32[]{:S(2)}, u32[]{:S(2)}) async-start(bf16[4,128,512]{2,1,0:T(8,128)(2,1)} %bitcast.6), calls=%async_computation | async-start | bytes 1048576 | tf_op jit(solution)/shard_map/all_to_all | solution.py:168
  94.5 4.6 %collective-permute-start.7 = (bf16[128,512]{1,0:T(8,128)(2,1)S(1)}, bf16[128,512]{1,0:T(8,128)(2,1)S(1)}, u32[]{:S(2)}, u32[]{:S(2)}) collective-permute-start(bf16[128,512]{1,0:T(8,128)(2,1)S(1)} %get-tuple-element.6), channel_id=1, source_target_pairs={{1,9},{9,1},{3,11},{11,3},{5,13},{13,5},{7,15},{15,7},{17,25},{25,... | collective-permute-start | bytes 393224 | tf_op jit(solution)/shard_map/ppermute | solution.py:46
  95.1 6.4 %collective-permute-start.8 = (bf16[128,512]{1,0:T(8,128)(2,1)S(1)}, bf16[128,512]{1,0:T(8,128)(2,1)S(1)}, u32[]{:S(2)}, u32[]{:S(2)}) collective-permute-start(bf16[128,512]{1,0:T(8,128)(2,1)S(1)} %get-tuple-element.6), channel_id=1, source_target_pairs={{0,9},{9,8},{8,1},{1,0},{2,11},{11,10},{10,3},{3,2},{4,13},{13,12}... | collective-permute-start | bytes 393224 | tf_op jit(solution)/shard_map/ppermute | solution.py:38
  103.6 4.7 %copy-start.1 = (bf16[1,512,768]{2,1,0:T(8,128)(2,1)S(1)}, bf16[1,512,768]{2,1,0:T(8,128)(2,1)}, u32[]{:S(2)}) copy-start(bf16[1,512,768]{2,1,0:T(8,128)(2,1)} %param.21) | copy-start | bytes 2359300
  103.6 44.1 %all-to-all-start.1 = ((bf16[32,21,1024]{2,1,0:T(8,128)(2,1)}), bf16[32,21,1024]{2,1,0:T(8,128)(2,1)S(1)}, u32[]{:S(2)}, u32[]{:S(2)}) async-start(bf16[32,21,1024]{2,1,0:T(8,128)(2,1)} %reshape.79), calls=%async_computation.1 | async-start | bytes 3145728 | tf_op jit(solution)/shard_map/all_to_all | solution.py:177
  108.3 95.1 %reduce-scatter.2.cloned.1.call-start = ((), (), s32[]{:S(2)}) async-start(), calls=%async_computation.5 | async-start | bytes 2580480 | tf_op jit(solution)/shard_map/reduce_scatter | solution.py:185
  110.8 40.1 %collective-permute-start.9 = (bf16[512,1536]{1,0:T(8,128)(2,1)}, bf16[512,1536]{1,0:T(8,128)(2,1)}, u32[]{:S(2)}, u32[]{:S(2)}) collective-permute-start(bf16[512,1536]{1,0:T(8,128)(2,1)} %pad_maximum_fusion), channel_id=1, source_target_pairs={{0,1},{1,0},{2,3},{3,2},{4,5},{5,4},{6,7},{7,6},{8,9},{9,8},{10,11... | collective-permute-start | bytes 4718600 | tf_op jit(solution)/shard_map/ppermute | solution.py:34
  154.9 2.3 copy-start.6
  154.9 4.5 %collective-permute-start.10 = (f32[1,512]{1,0:T(1,128)S(1)}, f32[1,512]{1,0:T(1,128)S(1)}, u32[]{:S(2)}, u32[]{:S(2)}) collective-permute-start(f32[1,512]{1,0:T(1,128)S(1)} %bitcast.96), channel_id=1, source_target_pairs={{0,1},{1,0},{2,3},{3,2},{4,5},{5,4},{6,7},{7,6},{8,9},{9,8},{10,11... | collective-permute-start | bytes 6152 | tf_op jit(solution)/shard_map/ppermute | solution.py:34
  157.2 68.1 %collective-permute-start.11 = (bf16[768,512]{1,0:T(8,128)(2,1)S(1)}, bf16[768,512]{1,0:T(8,128)(2,1)}, u32[]{:S(2)}, u32[]{:S(2)}) collective-permute-start(bf16[768,512]{1,0:T(8,128)(2,1)S(1)} %bitcast.101), channel_id=1, source_target_pairs={{0,1},{1,0},{2,3},{3,2},{4,5},{5,4},{6,7},{7,6},{8,9},{9,8},{10,11... | collective-permute-start | bytes 2359304 | tf_op jit(solution)/shard_map/ppermute | solution.py:34
  229.0 49.6 %all-to-all-start.2 = ((bf16[32,21,1024]{2,1,0:T(8,128)(2,1)}), bf16[32,21,1024]{2,1,0:T(8,128)(2,1)S(1)}, u32[]{:S(2)}, u32[]{:S(2)}) async-start(bf16[32,21,1024]{2,1,0:T(8,128)(2,1)} %reshape.81), calls=%async_computation.3 | async-start | bytes 3145728 | tf_op jit(solution)/shard_map/all_to_all | solution.py:197
  279.9 2.6 collective-permute-start.13
  280.5 6.3 %collective-permute-start.12 = (bf16[128,512]{1,0:T(8,128)(2,1)S(1)}, bf16[128,512]{1,0:T(8,128)(2,1)S(1)}, u32[]{:S(2)}, u32[]{:S(2)}) collective-permute-start(bf16[128,512]{1,0:T(8,128)(2,1)S(1)} %get-tuple-element.4), channel_id=1, source_target_pairs={{9,0},{8,9},{1,8},{0,1},{11,2},{10,11},{3,10},{2,3},{13,4},{12,13}... | collective-permute-start | bytes 393224 | tf_op jit(solution)/shard_map/ppermute | solution.py:42
  (2 other events, 2.7 us)
Sparse Core Ops, SparseCore 0:
  29.7 40.8 all-gather.1
  155.0 48.3 reduce-scatter.1

commit v3 on v2

--- a/solution.py
+++ b/solution.py
@@ -25,25 +25,12 @@
 epsilon = 1e-06
 
 
-def turn(block):
-    route = [(a * NH + b, b * NX + a) for a in range(NX) for b in range(NH)]
-    return lax.ppermute(block, ("x", "h"), route)
-
-
 def swap(block, axis):
     return lax.ppermute(block, axis, [(0, 1), (1, 0)])
 
 
-def cycle(block):
-    return lax.ppermute(block, ("l", "c"), [(0, 3), (3, 2), (2, 1), (1, 0)])
-
-
-def cycle_back(block):
-    return lax.ppermute(block, ("l", "c"), [(3, 0), (2, 3), (1, 2), (0, 1)])
-
-
-def across(block):
-    return lax.ppermute(block, ("l", "c"), [(1, 3), (3, 1)])
+def exchange(blocks, axes):
+    return lax.all_to_all(blocks, axes, split_axis=0, concat_axis=0, tiled=True)
 
 
 def from_behind(block, distance):
@@ -100,6 +87,20 @@
     )
     rank = rank + jnp.sum(twin.astype(f32), axis=2)
     return ids.astype(f32), rank
+
+
+def row_slots(table, side):
+    ids, rank, gates = table[:TOPK], table[TOPK : 2 * TOPK], table[2 * TOPK :]
+    column = jnp.floor(ids * 0.5)
+    return jnp.where(ids - 2.0 * column == side, column * SLOTS + rank, -1.0), gates
+
+
+def spread(slots, values):
+    row_ids = jnp.arange(ROWS, dtype=f32)[:, None]
+    total = jnp.zeros((ROWS, slots.shape[1]), f32)
+    for k in range(TOPK):
+        total = total + jnp.where(slots[k][None, :] == row_ids, values[k][None, :], 0.0)
+    return total.astype(bf16)
 
 
 def body(
@@ -120,6 +121,9 @@
 ):
     core, side = lax.axis_index("c"), lax.axis_index("l")
     tokens = queries.shape[0]
+    half = FF // 2
+
+    attended = attention(queries, key_rows, value_rows)
 
     other_strip = swap(out_weight, "l")
     strips = jnp.concatenate(
@@ -133,28 +137,26 @@
 
     ids, rank = slots_of(pred_ids, fix_pair, fix_expert, fix_count)
     table = jnp.concatenate([ids, rank, route_gates.astype(f32)], axis=1)
-    table = jnp.where(core == 0, table, swap(table, "l")).T
-    ids, rank, gates = table[:TOPK], table[TOPK : 2 * TOPK], table[2 * TOPK :]
-    column = jnp.floor(ids * 0.5)
-    slots = jnp.where(ids - 2.0 * column == side.astype(f32), column * SLOTS + rank, -1.0)
-    row_ids = jnp.arange(ROWS, dtype=f32)[:, None]
-    row_map = jnp.zeros((ROWS, tokens), f32)
-    combine = jnp.zeros((ROWS, tokens), f32)
-    for k in range(TOPK):
-        here = slots[k][None, :] == row_ids
-        row_map = row_map + jnp.where(here, 1.0, 0.0)
-        combine = combine + jnp.where(here, gates[k][None, :], 0.0)
-    row_map, combine = row_map.astype(bf16), combine.astype(bf16)
-
-    gate_up = jnp.concatenate([w_gate[0], w_up[0]], axis=1)
-    other_gate_up = swap(gate_up, "c")
-    down = jnp.concatenate([w_down[0], swap(w_down[0], "c")], axis=1)
+    tables = (table.T, swap(table, "l").T)
+
+    def columns(which):
+        return jnp.concatenate(
+            [
+                lax.dynamic_slice_in_dim(w_gate[0], which * half, half, 1),
+                lax.dynamic_slice_in_dim(w_up[0], which * half, half, 1),
+            ],
+            axis=1,
+        )
+
+    gate_up, other_gate_up = columns(core), swap(columns(1 - core), "c")
+    down = lax.dynamic_slice_in_dim(w_down[0], core * half, half, 0)
+    other_down = lax.dynamic_slice_in_dim(w_down[0], (1 - core) * half, half, 0)
     gain = norm_gain[None, :]
     inverse = 1.0 / (gain * gain)
     other_inverse = swap(inverse, "c")
 
-    attended = turn(attention(queries, key_rows, value_rows))
-    heads = lax.all_gather(attended, "h", axis=0, tiled=True)
+    copies = jnp.broadcast_to(attended[None], (NH, *attended.shape))
+    heads = exchange(exchange(copies, "h"), "x").reshape(NX * tokens, SLICE)
     other_heads = swap(heads, "c")
     partial = jnp.dot(
         heads,
@@ -165,42 +167,50 @@
         lax.dynamic_slice_in_dim(quarter, (1 - core) * SLICE, SLICE, 0),
         preferred_element_type=f32,
     )
-    terms = lax.all_to_all(
-        partial.astype(bf16).reshape(NX, tokens, SLICE), "x", split_axis=0, concat_axis=0, tiled=True
-    )
+    terms = exchange(partial.astype(bf16).reshape(NX, tokens, SLICE), "x")
     stream = residual.astype(f32) + jnp.sum(terms.astype(f32), axis=0)
 
     scaled = (stream * gain).astype(bf16)
-    near, far = cycle(scaled), across(scaled)
-    both = jnp.concatenate([jnp.where(core == 0, scaled, far), near], axis=1)
-    outgoing = jnp.dot(row_map, both, preferred_element_type=f32).astype(bf16)
-    incoming = lax.all_to_all(
-        outgoing.reshape(GRID, SLOTS, 2 * SLICE), ("x", "y"), split_axis=0, concat_axis=0, tiled=True
-    ).reshape(ROWS, 2 * SLICE)
-    own_rows, other_rows = incoming[:, :SLICE], incoming[:, SLICE:]
-    part = (
-        jnp.dot(own_rows, gate_up, preferred_element_type=f32)
-        + jnp.dot(other_rows, other_gate_up, preferred_element_type=f32)
-    ).astype(bf16)
-    sums = lax.psum_scatter(part, "h", scatter_dimension=0, tiled=True).astype(f32)
-    squares = jnp.sum(
-        jnp.square(own_rows.astype(f32)) * inverse
-        + jnp.square(other_rows.astype(f32)) * other_inverse,
-        axis=1,
-    )
-    totals = lax.psum(squares, "h")
-    totals = lax.dynamic_slice_in_dim(totals, lax.axis_index("h") * SHARE, SHARE, 0)
-    sums = sums * lax.rsqrt(totals / D + epsilon)[:, None]
-    hidden = (jax.nn.silu(sums[:, :FF]) * sums[:, FF:]).astype(bf16)
-    all_hidden = lax.all_gather(hidden, "h", axis=0, tiled=True)
-    results = jnp.dot(all_hidden, down, preferred_element_type=f32).astype(bf16)
-    returned = lax.all_to_all(
-        results.reshape(GRID, SLOTS, 2 * SLICE), ("x", "y"), split_axis=0, concat_axis=0, tiled=True
-    ).reshape(ROWS, 2 * SLICE)
-    mixed = jnp.einsum("rt,rd->td", combine, returned, preferred_element_type=f32)
-    own_mixed, other_mixed = mixed[:, :SLICE], mixed[:, SLICE:].astype(bf16)
-    from_near, from_far = cycle_back(other_mixed), across(own_mixed.astype(bf16))
-    expert_out = from_near.astype(f32) + jnp.where(core == 0, own_mixed, from_far.astype(f32))
+    blocks = (scaled, swap(scaled, "l"))
+    mixed = []
+    for table, rows in zip(tables, blocks):
+        slots, gates = row_slots(table, side.astype(f32))
+        outgoing = jnp.dot(
+            spread(slots, jnp.ones_like(gates)), rows, preferred_element_type=f32
+        ).astype(bf16)
+        incoming = exchange(outgoing.reshape(GRID, SLOTS, SLICE), ("x", "y")).reshape(ROWS, SLICE)
+        other_incoming = swap(incoming, "c")
+        part = (
+            jnp.dot(incoming, gate_up, preferred_element_type=f32)
+            + jnp.dot(other_incoming, other_gate_up, preferred_element_type=f32)
+        ).astype(bf16)
+        squares = jnp.sum(
+            jnp.square(incoming.astype(f32)) * inverse
+            + jnp.square(other_incoming.astype(f32)) * other_inverse,
+            axis=1,
+        ).reshape(NH, 1, SHARE)
+        high = squares.astype(bf16)
+        low = (squares - high.astype(f32)).astype(bf16)
+        extra = jnp.pad(jnp.concatenate([high, low], axis=1), ((0, 0), (0, 6), (0, FF - SHARE)))
+        parts = exchange(
+            jnp.concatenate([part.reshape(NH, SHARE, FF), extra], axis=1), "h"
+        ).astype(f32)
+        sums = jnp.sum(parts[:, :SHARE], axis=0)
+        total = jnp.sum(parts[:, SHARE : SHARE + 2, :SHARE], axis=(0, 1))
+        sums = sums * lax.rsqrt(total / D + epsilon)[:, None]
+        hidden = (jax.nn.silu(sums[:, :half]) * sums[:, half:]).astype(bf16)
+        copies = jnp.broadcast_to(hidden[None], (NH, SHARE, half))
+        all_hidden = exchange(copies, "h").reshape(ROWS, half)
+        other_hidden = swap(all_hidden, "c")
+        results = (
+            jnp.dot(all_hidden, down, preferred_element_type=f32)
+            + jnp.dot(other_hidden, other_down, preferred_element_type=f32)
+        ).astype(bf16)
+        returned = exchange(results.reshape(GRID, SLOTS, SLICE), ("x", "y")).reshape(ROWS, SLICE)
+        mixed.append(
+            jnp.einsum("rt,rd->td", spread(slots, gates), returned, preferred_element_type=f32)
+        )
+    expert_out = mixed[0] + swap(mixed[1].astype(bf16), "l").astype(f32)
     return stream.astype(bf16), expert_out.astype(bf16)
 
 

time: 295 us -> 334 us (1.13)
  blocking collectives: 72 us -> 0 us
  waiting for transfers between devices: 121 us -> 181 us
  starting transfers between devices: 57.2 us -> 94 us
  local copies, waits for them, and re-layouts: 4.62 us -> 14.8 us
    all_to_all x3 -> x11, waiting for transfers between devices: 81.6 us -> 170 us  [exchange(): return lax.all_to_all(blocks, axes, split_axis=0, concat_axis=0, tiled=True)]
    all_gather x2 -> x0, blocking collectives: 60.7 us -> none  [the longest x1 40.2 us: body(): heads = lax.all_gather(attended, 'h', axis=0, tiled=True)]
    all_to_all x3 -> x11, starting transfers between devices: 21.2 us -> 55.2 us  [exchange(): return lax.all_to_all(blocks, axes, split_axis=0, concat_axis=0, tiled=True)]
    reduce_scatter x1 -> x0, waiting for transfers between devices: 32.2 us -> none  [body(): lax.psum_scatter(part, 'h', scatter_dimension=0, tiled=True).astype(f32)]
    ppermute x6 -> x11, waiting for transfers between devices: 0.02 us -> 11.3 us  [swap(): return lax.ppermute(block, axis, [(0, 1), (1, 0)])]
    psum x1 -> x0, blocking collectives: 11.3 us -> none  [body(): totals = lax.psum(squares, 'h')]
    ppermute x6 -> x11, starting transfers between devices: 15.6 us -> 26.2 us  [swap(): return lax.ppermute(block, axis, [(0, 1), (1, 0)])]
    ppermute x5 -> x0, starting transfers between devices: 7.82 us -> none  [the longest x1 3.9 us: cycle(): return lax.ppermute(block, ('l', 'c'), [(0, 3), (3, 2), (2, 1), (1, 0)])]
  transfers between devices with their start and end apart: 19 -> 26, of which waited for: 6 -> 16; matrix products, arithmetic and copies ran while one was open for 5% -> 9% of each run, Pallas kernels for 0% -> 0%
where the time goes in v3:
time: 334 us; the launch traced here: 333 us
  waiting for transfers between devices  181 us (54%)
  starting transfers between devices  94 us (28%)
  between operations  16 us (5%)
  matrix products  15.7 us (5%)
  local copies, waits for them, and re-layouts  14.8 us (4%)
  other arithmetic  10.6 us (3%)
    all_to_all x11, waiting for transfers between devices, exchange(): return lax.all_to_all(blocks, axes, split_axis=0, concat_axis=0, tiled=True)  170 us
    all_to_all x11, starting transfers between devices, exchange(): return lax.all_to_all(blocks, axes, split_axis=0, concat_axis=0, tiled=True)  55.2 us
    ppermute x11, starting transfers between devices, swap(): return lax.ppermute(block, axis, [(0, 1), (1, 0)])  26.2 us
    ppermute x3, starting transfers between devices, from_behind(): return lax.ppermute(block, CTX, route)  12.6 us
    ppermute x11, waiting for transfers between devices, swap(): return lax.ppermute(block, axis, [(0, 1), (1, 0)])  11.3 us
  transfers between devices with their start and end apart: 26, of which 16 were waited for; matrix products, arithmetic and copies ran while one was open for 9% of the time, Pallas kernels for 0%

profile of v3, /device:TPU:8, one launch (start us, length us, event | category | flops | bytes accessed | tf_op | source)
XLA Modules:
  0.0 332.6 jit_solution(10325026785997431868)
XLA Ops:
  8.1 5.3 %collective-permute-start = (bf16[128,256]{1,0:T(8,128)(2,1)S(1)}, bf16[128,256]{1,0:T(8,128)(2,1)S(1)}, u32[]{:S(2)}, u32[]{:S(2)}) collective-permute-start(bf16[128,256]{1,0:T(8,128)(2,1)S(1)} %pad_maximum_fusion.7), channel_id=1, source_target_pairs={{0,24},{8,32},{16,40},{24,48},{32,56},{40,64},{48,72},{56,80},{64,... | collective-permute-start | bytes 196616 | tf_op jit(solution)/shard_map/ppermute | solution.py:38
  16.9 3.8 %collective-permute-start.2 = (bf16[128,256]{1,0:T(8,128)(2,1)S(1)}, bf16[128,256]{1,0:T(8,128)(2,1)S(1)}, u32[]{:S(2)}, u32[]{:S(2)}) collective-permute-start(bf16[128,256]{1,0:T(8,128)(2,1)S(1)} %pad_maximum_fusion.7), channel_id=1, source_target_pairs={{0,8},{8,16},{16,24},{24,32},{32,40},{40,48},{48,56},{56,64},{64,7... | collective-permute-start | bytes 196616 | tf_op jit(solution)/shard_map/ppermute | solution.py:38
  20.7 4.3 %collective-permute-start.3 = (bf16[64,512]{1,0:T(8,128)(2,1)}, bf16[64,512]{1,0:T(8,128)(2,1)S(1)}, u32[]{:S(2)}, u32[]{:S(2)}) collective-permute-start(bf16[64,512]{1,0:T(8,128)(2,1)} %param.17), channel_id=1, source_target_pairs={{0,8},{8,0},{1,9},{9,1},{2,10},{10,2},{3,11},{11,3},{4,12},{12,4},... | collective-permute-start | bytes 196616 | tf_op jit(solution)/shard_map/ppermute | solution.py:29
  31.4 9.9 %all-to-all-start = ((bf16[4,128,512]{2,1,0:T(8,128)(2,1)}), bf16[4,128,512]{2,1,0:T(8,128)(2,1)}, u32[]{:S(2)}, u32[]{:S(2)}) async-start(bf16[4,128,512]{2,1,0:T(8,128)(2,1)} %broadcast_in_dim.286), calls=%async_computation | async-start | bytes 1048576 | tf_op jit(solution)/shard_map/all_to_all | solution.py:33
  42.2 13.3 %all-to-all-done = bf16[4,128,512]{2,1,0:T(8,128)(2,1)} async-done(((bf16[4,128,512]{2,1,0:T(8,128)(2,1)}), bf16[4,128,512]{2,1,0:T(8,128)(2,1)}, u32[]{:S(2)}, u32[]{:S(2)}) %all-to-all-start) | async-done | bytes 524320 | tf_op jit(solution)/shard_map/all_to_all | solution.py:33
  55.6 4.3 %all-to-all-start.1 = ((bf16[4,128,512]{2,1,0:T(8,128)(2,1)}), bf16[4,128,512]{2,1,0:T(8,128)(2,1)S(1)}, u32[]{:S(2)}, u32[]{:S(2)}) async-start(bf16[4,128,512]{2,1,0:T(8,128)(2,1)} %all-to-all-done), calls=%async_computation.1 | async-start | bytes 1048576 | tf_op jit(solution)/shard_map/all_to_all | solution.py:33
  60.0 7.9 %all-to-all-done.1 = bf16[4,128,512]{2,1,0:T(8,128)(2,1)S(1)} async-done(((bf16[4,128,512]{2,1,0:T(8,128)(2,1)}), bf16[4,128,512]{2,1,0:T(8,128)(2,1)S(1)}, u32[]{:S(2)}, u32[]{:S(2)}) %all-to-all-start.1) | async-done | bytes 524320 | tf_op jit(solution)/shard_map/all_to_all | solution.py:33
  73.0 4.4 %all-to-all-start.2 = ((bf16[4,128,512]{2,1,0:T(8,128)(2,1)}), bf16[4,128,512]{2,1,0:T(8,128)(2,1)S(1)}, u32[]{:S(2)}, u32[]{:S(2)}) async-start(bf16[4,128,512]{2,1,0:T(8,128)(2,1)} %bitcast.7), calls=%async_computation.2 | async-start | bytes 1048576 | tf_op jit(solution)/shard_map/all_to_all | solution.py:33
  77.5 9.4 %all-to-all-done.2 = bf16[4,128,512]{2,1,0:T(8,128)(2,1)S(1)} async-done(((bf16[4,128,512]{2,1,0:T(8,128)(2,1)}), bf16[4,128,512]{2,1,0:T(8,128)(2,1)S(1)}, u32[]{:S(2)}, u32[]{:S(2)}) %all-to-all-start.2) | async-done | bytes 524320 | tf_op jit(solution)/shard_map/all_to_all | solution.py:33
  89.4 5.8 %all-to-all-start.3 = ((bf16[32,21,512]{2,1,0:T(8,128)(2,1)}), bf16[32,21,512]{2,1,0:T(8,128)(2,1)S(1)}, u32[]{:S(2)}, u32[]{:S(2)}) async-start(bf16[32,21,512]{2,1,0:T(8,128)(2,1)} %reshape.207), calls=%async_computation.3 | async-start | bytes 1572864 | tf_op jit(solution)/shard_map/all_to_all | solution.py:33
  103.3 4.5 %collective-permute-done.10 = bf16[128,512]{1,0:T(8,128)(2,1)S(1)} collective-permute-done((bf16[128,512]{1,0:T(8,128)(2,1)S(1)}, bf16[128,512]{1,0:T(8,128)(2,1)S(1)}, u32[]{:S(2)}, u32[]{:S(2)}) %collective-permute-start.10) | collective-permute-done | bytes 131104 | tf_op jit(solution)/shard_map/ppermute | solution.py:29
  109.4 8.2 %all-to-all-done.3 = bf16[32,21,512]{2,1,0:T(8,128)(2,1)S(1)} async-done(((bf16[32,21,512]{2,1,0:T(8,128)(2,1)}), bf16[32,21,512]{2,1,0:T(8,128)(2,1)S(1)}, u32[]{:S(2)}, u32[]{:S(2)}) %all-to-all-start.3) | async-done | bytes 688160 | tf_op jit(solution)/shard_map/all_to_all | solution.py:33
  117.6 4.9 %all-to-all-start.7 = ((bf16[32,21,512]{2,1,0:T(8,128)(2,1)}), bf16[32,21,512]{2,1,0:T(8,128)(2,1)S(1)}, u32[]{:S(2)}, u32[]{:S(2)}) async-start(bf16[32,21,512]{2,1,0:T(8,128)(2,1)} %reshape.214), calls=%async_computation.7 | async-start | bytes 1572864 | tf_op jit(solution)/shard_map/all_to_all | solution.py:33
  124.7 20.1 %all-to-all-done.7 = bf16[32,21,512]{2,1,0:T(8,128)(2,1)S(1)} async-done(((bf16[32,21,512]{2,1,0:T(8,128)(2,1)}), bf16[32,21,512]{2,1,0:T(8,128)(2,1)S(1)}, u32[]{:S(2)}, u32[]{:S(2)}) %all-to-all-start.7) | async-done | bytes 688160 | tf_op jit(solution)/shard_map/all_to_all | solution.py:33
  165.4 4.1 %all-to-all-start.8 = ((bf16[4,176,768]{2,1,0:T(8,128)(2,1)}), bf16[4,176,768]{2,1,0:T(8,128)(2,1)S(1)}, u32[]{:S(2)}, u32[]{:S(2)}) async-start(bf16[4,176,768]{2,1,0:T(8,128)(2,1)} %pad_maximum_fusion.1), calls=%async_computation.8 | async-start | bytes 2162688 | tf_op jit(solution)/shard_map/all_to_all | solution.py:33
  173.5 25.1 %all-to-all-done.8 = bf16[4,176,768]{2,1,0:T(8,128)(2,1)S(1)} async-done(((bf16[4,176,768]{2,1,0:T(8,128)(2,1)}), bf16[4,176,768]{2,1,0:T(8,128)(2,1)S(1)}, u32[]{:S(2)}, u32[]{:S(2)}) %all-to-all-start.8) | async-done | bytes 1081376 | tf_op jit(solution)/shard_map/all_to_all | solution.py:33
  202.7 25.5 %all-to-all-done.4 = bf16[4,176,768]{2,1,0:T(8,128)(2,1)S(1)} async-done(((bf16[4,176,768]{2,1,0:T(8,128)(2,1)}), bf16[4,176,768]{2,1,0:T(8,128)(2,1)S(1)}, u32[]{:S(2)}, u32[]{:S(2)}) %all-to-all-start.4) | async-done | bytes 1081376 | tf_op jit(solution)/shard_map/all_to_all | solution.py:33
  229.0 4.9 %all-to-all-start.9 = ((bf16[4,168,384]{2,1,0:T(8,128)(2,1)}), bf16[4,168,384]{2,1,0:T(8,128)(2,1)S(1)}, u32[]{:S(2)}, u32[]{:S(2)}) async-start(bf16[4,168,384]{2,1,0:T(8,128)(2,1)} %broadcast_in_dim.328), calls=%async_computation.9 | async-start | bytes 1032192 | tf_op jit(solution)/shard_map/all_to_all | solution.py:33
  234.3 12.2 %all-to-all-done.9 = bf16[4,168,384]{2,1,0:T(8,128)(2,1)S(1)} async-done(((bf16[4,168,384]{2,1,0:T(8,128)(2,1)}), bf16[4,168,384]{2,1,0:T(8,128)(2,1)S(1)}, u32[]{:S(2)}, u32[]{:S(2)}) %all-to-all-start.9) | async-done | bytes 516128 | tf_op jit(solution)/shard_map/all_to_all | solution.py:33
  255.3 13.3 %all-to-all-done.5 = bf16[4,168,384]{2,1,0:T(8,128)(2,1)S(1)} async-done(((bf16[4,168,384]{2,1,0:T(8,128)(2,1)}), bf16[4,168,384]{2,1,0:T(8,128)(2,1)S(1)}, u32[]{:S(2)}, u32[]{:S(2)}) %all-to-all-start.5) | async-done | bytes 516128 | tf_op jit(solution)/shard_map/all_to_all | solution.py:33
  268.6 4.9 %all-to-all-start.10 = ((bf16[32,21,512]{2,1,0:T(8,128)(2,1)}), bf16[32,21,512]{2,1,0:T(8,128)(2,1)S(1)}, u32[]{:S(2)}, u32[]{:S(2)}) async-start(bf16[32,21,512]{2,1,0:T(8,128)(2,1)} %reshape.219), calls=%async_computation.10 | async-start | bytes 1572864 | tf_op jit(solution)/shard_map/all_to_all | solution.py:33
  279.0 17.5 %all-to-all-done.10 = bf16[32,21,512]{2,1,0:T(8,128)(2,1)S(1)} async-done(((bf16[32,21,512]{2,1,0:T(8,128)(2,1)}), bf16[32,21,512]{2,1,0:T(8,128)(2,1)S(1)}, u32[]{:S(2)}, u32[]{:S(2)}) %all-to-all-start.10) | async-done | bytes 688160 | tf_op jit(solution)/shard_map/all_to_all | solution.py:33
  296.5 4.9 %all-to-all-start.6 = ((bf16[32,21,512]{2,1,0:T(8,128)(2,1)}), bf16[32,21,512]{2,1,0:T(8,128)(2,1)S(1)}, u32[]{:S(2)}, u32[]{:S(2)}) async-start(bf16[32,21,512]{2,1,0:T(8,128)(2,1)} %reshape.212), calls=%async_computation.6 | async-start | bytes 1572864 | tf_op jit(solution)/shard_map/all_to_all | solution.py:33
  306.8 17.4 %all-to-all-done.6 = bf16[32,21,512]{2,1,0:T(8,128)(2,1)S(1)} async-done(((bf16[32,21,512]{2,1,0:T(8,128)(2,1)}), bf16[32,21,512]{2,1,0:T(8,128)(2,1)S(1)}, u32[]{:S(2)}, u32[]{:S(2)}) %all-to-all-start.6) | async-done | bytes 688160 | tf_op jit(solution)/shard_map/all_to_all | solution.py:33
  (208 shorter events, 80.6 us)
Async XLA Ops:
  7.2 63.0 %all-gather.2.cloned.1.call-start = ((), (), s32[]{:S(2)}) async-start(), calls=%async_computation.11 | async-start | bytes 1179648 | tf_op jit(solution)/shard_map/all_gather | solution.py:136
  8.1 20.9 %collective-permute-start = (bf16[128,256]{1,0:T(8,128)(2,1)S(1)}, bf16[128,256]{1,0:T(8,128)(2,1)S(1)}, u32[]{:S(2)}, u32[]{:S(2)}) collective-permute-start(bf16[128,256]{1,0:T(8,128)(2,1)S(1)} %pad_maximum_fusion.7), channel_id=1, source_target_pairs={{0,24},{8,32},{16,40},{24,48},{32,56},{40,64},{48,72},{56,80},{64,... | collective-permute-start | bytes 196616 | tf_op jit(solution)/shard_map/ppermute | solution.py:38
  13.4 15.6 %collective-permute-start.1 = (bf16[128,256]{1,0:T(8,128)(2,1)S(1)}, bf16[128,256]{1,0:T(8,128)(2,1)S(1)}, u32[]{:S(2)}, u32[]{:S(2)}) collective-permute-start(bf16[128,256]{1,0:T(8,128)(2,1)S(1)} %pad_maximum_fusion.7), channel_id=1, source_target_pairs={{0,16},{8,24},{16,32},{24,40},{32,48},{40,56},{48,64},{56,72},{64,... | collective-permute-start | bytes 196616 | tf_op jit(solution)/shard_map/ppermute | solution.py:38
  16.9 12.1 %collective-permute-start.2 = (bf16[128,256]{1,0:T(8,128)(2,1)S(1)}, bf16[128,256]{1,0:T(8,128)(2,1)S(1)}, u32[]{:S(2)}, u32[]{:S(2)}) collective-permute-start(bf16[128,256]{1,0:T(8,128)(2,1)S(1)} %pad_maximum_fusion.7), channel_id=1, source_target_pairs={{0,8},{8,16},{16,24},{24,32},{32,40},{40,48},{48,56},{56,64},{64,7... | collective-permute-start | bytes 196616 | tf_op jit(solution)/shard_map/ppermute | solution.py:38
  20.7 6.7 %collective-permute-start.3 = (bf16[64,512]{1,0:T(8,128)(2,1)}, bf16[64,512]{1,0:T(8,128)(2,1)S(1)}, u32[]{:S(2)}, u32[]{:S(2)}) collective-permute-start(bf16[64,512]{1,0:T(8,128)(2,1)} %param.17), channel_id=1, source_target_pairs={{0,8},{8,0},{1,9},{9,1},{2,10},{10,2},{3,11},{11,3},{4,12},{12,4},... | collective-permute-start | bytes 196616 | tf_op jit(solution)/shard_map/ppermute | solution.py:29
  31.4 24.2 %all-to-all-start = ((bf16[4,128,512]{2,1,0:T(8,128)(2,1)}), bf16[4,128,512]{2,1,0:T(8,128)(2,1)}, u32[]{:S(2)}, u32[]{:S(2)}) async-start(bf16[4,128,512]{2,1,0:T(8,128)(2,1)} %broadcast_in_dim.286), calls=%async_computation | async-start | bytes 1048576 | tf_op jit(solution)/shard_map/all_to_all | solution.py:33
  55.6 12.4 %all-to-all-start.1 = ((bf16[4,128,512]{2,1,0:T(8,128)(2,1)}), bf16[4,128,512]{2,1,0:T(8,128)(2,1)S(1)}, u32[]{:S(2)}, u32[]{:S(2)}) async-start(bf16[4,128,512]{2,1,0:T(8,128)(2,1)} %all-to-all-done), calls=%async_computation.1 | async-start | bytes 1048576 | tf_op jit(solution)/shard_map/all_to_all | solution.py:33
  67.9 3.8 %collective-permute-start.4 = (bf16[512,512]{1,0:T(8,128)(2,1)S(1)}, bf16[512,512]{1,0:T(8,128)(2,1)S(1)}, u32[]{:S(2)}, u32[]{:S(2)}) collective-permute-start(bf16[512,512]{1,0:T(8,128)(2,1)S(1)} %bitcast.158), channel_id=1, source_target_pairs={{0,1},{1,0},{2,3},{3,2},{4,5},{5,4},{6,7},{7,6},{8,9},{9,8},{10,11... | collective-permute-start | bytes 1572872 | tf_op jit(solution)/shard_map/ppermute | solution.py:29
  73.0 13.9 %all-to-all-start.2 = ((bf16[4,128,512]{2,1,0:T(8,128)(2,1)}), bf16[4,128,512]{2,1,0:T(8,128)(2,1)S(1)}, u32[]{:S(2)}, u32[]{:S(2)}) async-start(bf16[4,128,512]{2,1,0:T(8,128)(2,1)} %bitcast.7), calls=%async_computation.2 | async-start | bytes 1048576 | tf_op jit(solution)/shard_map/all_to_all | solution.py:33
  89.4 28.2 %all-to-all-start.3 = ((bf16[32,21,512]{2,1,0:T(8,128)(2,1)}), bf16[32,21,512]{2,1,0:T(8,128)(2,1)S(1)}, u32[]{:S(2)}, u32[]{:S(2)}) async-start(bf16[32,21,512]{2,1,0:T(8,128)(2,1)} %reshape.207), calls=%async_computation.3 | async-start | bytes 1572864 | tf_op jit(solution)/shard_map/all_to_all | solution.py:33
  95.3 5.6 %collective-permute-start.9 = (f32[128,24]{0,1:T(8,128)S(1)}, f32[128,24]{0,1:T(8,128)S(1)}, u32[]{:S(2)}, u32[]{:S(2)}) collective-permute-start(f32[128,24]{0,1:T(8,128)S(1)} %get-tuple-element.36), channel_id=1, source_target_pairs={{0,8},{8,0},{1,9},{9,1},{2,10},{10,2},{3,11},{11,3},{4,12},{12,4},... | collective-permute-start | bytes 36872 | tf_op jit(solution)/shard_map/ppermute | solution.py:29
  100.9 6.9 %collective-permute-start.10 = (bf16[128,512]{1,0:T(8,128)(2,1)S(1)}, bf16[128,512]{1,0:T(8,128)(2,1)S(1)}, u32[]{:S(2)}, u32[]{:S(2)}) collective-permute-start(bf16[128,512]{1,0:T(8,128)(2,1)S(1)} %get-tuple-element.10), channel_id=1, source_target_pairs={{0,8},{8,0},{1,9},{9,1},{2,10},{10,2},{3,11},{11,3},{4,12},{12,4},... | collective-permute-start | bytes 393224 | tf_op jit(solution)/shard_map/ppermute | solution.py:29
  117.6 27.2 %all-to-all-start.7 = ((bf16[32,21,512]{2,1,0:T(8,128)(2,1)}), bf16[32,21,512]{2,1,0:T(8,128)(2,1)S(1)}, u32[]{:S(2)}, u32[]{:S(2)}) async-start(bf16[32,21,512]{2,1,0:T(8,128)(2,1)} %reshape.214), calls=%async_computation.7 | async-start | bytes 1572864 | tf_op jit(solution)/shard_map/all_to_all | solution.py:33
  122.8 33.8 %collective-permute-start.5 = (bf16[672,512]{1,0:T(8,128)(2,1)S(1)}, bf16[672,512]{1,0:T(8,128)(2,1)}, u32[]{:S(2)}, u32[]{:S(2)}) collective-permute-start(bf16[672,512]{1,0:T(8,128)(2,1)S(1)} %reshape.208), channel_id=1, source_target_pairs={{0,1},{1,0},{2,3},{3,2},{4,5},{5,4},{6,7},{7,6},{8,9},{9,8},{10,11... | collective-permute-start | bytes 2064392 | tf_op jit(solution)/shard_map/ppermute | solution.py:29
  145.9 10.7 %collective-permute-start.11 = (bf16[672,512]{1,0:T(8,128)(2,1)}, bf16[672,512]{1,0:T(8,128)(2,1)S(1)}, u32[]{:S(2)}, u32[]{:S(2)}) collective-permute-start(bf16[672,512]{1,0:T(8,128)(2,1)} %reshape.215), channel_id=1, source_target_pairs={{0,1},{1,0},{2,3},{3,2},{4,5},{5,4},{6,7},{7,6},{8,9},{9,8},{10,11... | collective-permute-start | bytes 2064392 | tf_op jit(solution)/shard_map/ppermute | solution.py:29
  150.4 11.9 %collective-permute-start.6 = (bf16[512,768]{1,0:T(8,128)(2,1)}, bf16[512,768]{1,0:T(8,128)(2,1)}, u32[]{:S(2)}, u32[]{:S(2)}) collective-permute-start(bf16[512,768]{1,0:T(8,128)(2,1)} %pad_maximum_fusion.3), channel_id=1, source_target_pairs={{0,1},{1,0},{2,3},{3,2},{4,5},{5,4},{6,7},{7,6},{8,9},{9,8},{10,11... | collective-permute-start | bytes 2359304 | tf_op jit(solution)/shard_map/ppermute | solution.py:29
  165.4 33.2 %all-to-all-start.8 = ((bf16[4,176,768]{2,1,0:T(8,128)(2,1)}), bf16[4,176,768]{2,1,0:T(8,128)(2,1)S(1)}, u32[]{:S(2)}, u32[]{:S(2)}) async-start(bf16[4,176,768]{2,1,0:T(8,128)(2,1)} %pad_maximum_fusion.1), calls=%async_computation.8 | async-start | bytes 2162688 | tf_op jit(solution)/shard_map/all_to_all | solution.py:33
  198.6 29.5 %all-to-all-start.4 = ((bf16[4,176,768]{2,1,0:T(8,128)(2,1)}), bf16[4,176,768]{2,1,0:T(8,128)(2,1)S(1)}, u32[]{:S(2)}, u32[]{:S(2)}) async-start(bf16[4,176,768]{2,1,0:T(8,128)(2,1)} %pad_maximum_fusion), calls=%async_computation.4 | async-start | bytes 2162688 | tf_op jit(solution)/shard_map/all_to_all | solution.py:33
  229.0 17.6 %all-to-all-start.9 = ((bf16[4,168,384]{2,1,0:T(8,128)(2,1)}), bf16[4,168,384]{2,1,0:T(8,128)(2,1)S(1)}, u32[]{:S(2)}, u32[]{:S(2)}) async-start(bf16[4,168,384]{2,1,0:T(8,128)(2,1)} %broadcast_in_dim.328), calls=%async_computation.9 | async-start | bytes 1032192 | tf_op jit(solution)/shard_map/all_to_all | solution.py:33
  246.6 7.1 %collective-permute-start.12 = (bf16[672,384]{1,0:T(8,128)(2,1)S(1)}, bf16[672,384]{1,0:T(8,128)(2,1)S(1)}, u32[]{:S(2)}, u32[]{:S(2)}) collective-permute-start(bf16[672,384]{1,0:T(8,128)(2,1)S(1)} %bitcast.160), channel_id=1, source_target_pairs={{0,1},{1,0},{2,3},{3,2},{4,5},{5,4},{6,7},{7,6},{8,9},{9,8},{10,11... | collective-permute-start | bytes 1548296 | tf_op jit(solution)/shard_map/ppermute | solution.py:29
  249.6 18.9 %all-to-all-start.5 = ((bf16[4,168,384]{2,1,0:T(8,128)(2,1)}), bf16[4,168,384]{2,1,0:T(8,128)(2,1)S(1)}, u32[]{:S(2)}, u32[]{:S(2)}) async-start(bf16[4,168,384]{2,1,0:T(8,128)(2,1)} %broadcast_in_dim.311), calls=%async_computation.5 | async-start | bytes 1032192 | tf_op jit(solution)/shard_map/all_to_all | solution.py:33
  268.6 28.0 %all-to-all-start.10 = ((bf16[32,21,512]{2,1,0:T(8,128)(2,1)}), bf16[32,21,512]{2,1,0:T(8,128)(2,1)S(1)}, u32[]{:S(2)}, u32[]{:S(2)}) async-start(bf16[32,21,512]{2,1,0:T(8,128)(2,1)} %reshape.219), calls=%async_computation.10 | async-start | bytes 1572864 | tf_op jit(solution)/shard_map/all_to_all | solution.py:33
  296.5 27.6 %all-to-all-start.6 = ((bf16[32,21,512]{2,1,0:T(8,128)(2,1)}), bf16[32,21,512]{2,1,0:T(8,128)(2,1)S(1)}, u32[]{:S(2)}, u32[]{:S(2)}) async-start(bf16[32,21,512]{2,1,0:T(8,128)(2,1)} %reshape.212), calls=%async_computation.6 | async-start | bytes 1572864 | tf_op jit(solution)/shard_map/all_to_all | solution.py:33
  303.4 20.9 %collective-permute-start.13 = (bf16[128,512]{1,0:T(8,128)(2,1)S(1)}, bf16[128,512]{1,0:T(8,128)(2,1)S(1)}, u32[]{:S(2)}, u32[]{:S(2)}) collective-permute-start(bf16[128,512]{1,0:T(8,128)(2,1)S(1)} %convolution_convert_fusion.2), channel_id=1, source_target_pairs={{0,8},{8,0},{1,9},{9,1},{2,10},{10,2},{3,11},{11,3},{4,12},{12,4},... | collective-permute-start | bytes 393224 | tf_op jit(solution)/shard_map/ppermute | solution.py:29
  (49 other events, 894.7 us)
Sparse Core Ops, SparseCore 0:
  29.1 41.0 all-gather.1

commit v4 on v3

--- a/solution.py
+++ b/solution.py
@@ -2,6 +2,8 @@
 import jax.numpy as jnp
 import numpy as np
 from jax import lax
+from jax.experimental import pallas as pl
+from jax.experimental.pallas import tpu as pltpu
 from jax.sharding import Mesh, PartitionSpec as P
 
 D = 4096
@@ -13,10 +15,11 @@
 FIX = 32
 TOK = 128
 SLOTS = 21
+GROUP = 24
 NX, NY, NL, NH, NC = 4, 8, 2, 4, 2
 N_CTX = NX * NY * NL
 GRID = NX * NY
-ROWS = GRID * SLOTS
+ROWS = GRID * GROUP
 SHARE = ROWS // NH
 SLICE = D // (NH * NC)
 CTX = ("x", "y", "l")
@@ -92,7 +95,7 @@
 def row_slots(table, side):
     ids, rank, gates = table[:TOPK], table[TOPK : 2 * TOPK], table[2 * TOPK :]
     column = jnp.floor(ids * 0.5)
-    return jnp.where(ids - 2.0 * column == side, column * SLOTS + rank, -1.0), gates
+    return jnp.where(ids - 2.0 * column == side, column * GROUP + rank, -1.0), gates
 
 
 def spread(slots, values):
@@ -101,6 +104,50 @@
     for k in range(TOPK):
         total = total + jnp.where(slots[k][None, :] == row_ids, values[k][None, :], 0.0)
     return total.astype(bf16)
+
+
+def products_kernel(own_ref, other_ref, w_own_ref, w_other_ref, inv_own_ref, inv_other_ref, out_ref):
+    own, other = own_ref[...], other_ref[...]
+    w_own, w_other = w_own_ref[...], w_other_ref[...]
+
+    def squares(rows, inverse_ref):
+        weight = jnp.broadcast_to(inverse_ref[...], (8, SLICE))
+        return lax.dot_general(
+            weight,
+            jnp.square(rows.astype(f32)),
+            (((1,), (1,)), ((), ())),
+            precision=lax.Precision.HIGHEST,
+            preferred_element_type=f32,
+        )
+
+    total = (squares(own, inv_own_ref) + squares(other, inv_other_ref))[:1]
+    high = total.astype(bf16).astype(f32)
+    low = total - high
+    row = lax.broadcasted_iota(jnp.int32, (16, FF), 0)
+    for h in range(NH):
+        rows = slice(h * SHARE, (h + 1) * SHARE)
+        part = jnp.dot(own[rows], w_own, preferred_element_type=f32) + jnp.dot(
+            other[rows], w_other, preferred_element_type=f32
+        )
+        out_ref[h] = part.astype(bf16)
+        tile = jnp.where(row == SLOTS - 16, high, part[16:32])
+        tile = jnp.where(row == SLOTS - 15, low, tile)
+        out_ref[h, 16:32] = tile.astype(bf16)
+
+
+def products(own, other, w_own, w_other, inv_own, inv_other):
+    return pl.pallas_call(
+        products_kernel,
+        out_shape=jax.ShapeDtypeStruct((NH, SHARE, FF), bf16),
+        compiler_params=pltpu.CompilerParams(vmem_limit_bytes=48 * 1024 * 1024),
+        cost_estimate=pl.CostEstimate(
+            flops=100_000_000, bytes_accessed=500_000, transcendentals=0
+        ),
+    )(own, other, w_own, w_other, inv_own, inv_other)
+
+
+def to_ahead(block, distance):
+    return lax.ppermute(block, "h", [(i, (i + distance) % NH) for i in range(NH)])
 
 
 def body(
@@ -119,7 +166,7 @@
     fix_expert,
     fix_count,
 ):
-    core, side = lax.axis_index("c"), lax.axis_index("l")
+    core, side, level = lax.axis_index("c"), lax.axis_index("l"), lax.axis_index("h")
     tokens = queries.shape[0]
     half = FF // 2
 
@@ -157,6 +204,9 @@
 
     copies = jnp.broadcast_to(attended[None], (NH, *attended.shape))
     heads = exchange(exchange(copies, "h"), "x").reshape(NX * tokens, SLICE)
+    heads, gate_up, other_gate_up, inverse, other_inverse, tables = lax.optimization_barrier(
+        (heads, gate_up, other_gate_up, inverse, other_inverse, tables)
+    )
     other_heads = swap(heads, "c")
     partial = jnp.dot(
         heads,
@@ -171,46 +221,64 @@
     stream = residual.astype(f32) + jnp.sum(terms.astype(f32), axis=0)
 
     scaled = (stream * gain).astype(bf16)
-    blocks = (scaled, swap(scaled, "l"))
-    mixed = []
-    for table, rows in zip(tables, blocks):
-        slots, gates = row_slots(table, side.astype(f32))
-        outgoing = jnp.dot(
-            spread(slots, jnp.ones_like(gates)), rows, preferred_element_type=f32
+    slot_lists = [row_slots(table, side.astype(f32)) for table in tables]
+    def chosen(slot_list, rows):
+        slots, gates = slot_list
+        picks = spread(slots, jnp.ones_like(gates))
+        return jnp.dot(picks, rows, preferred_element_type=f32).astype(bf16)
+
+    def through(rows):
+        return exchange(rows.reshape(GRID, GROUP, SLICE), ("x", "y")).reshape(ROWS, SLICE)
+
+    def share_products(rows):
+        return products(rows, swap(rows, "c"), gate_up, other_gate_up, inverse, other_inverse)
+
+    def scattered(parts):
+        flat = parts.reshape(ROWS, FF)
+        return lax.psum_scatter(flat, "h", scatter_dimension=0, tiled=True).astype(f32)
+
+    def activated(sums):
+        total = lax.dynamic_slice_in_dim(
+            jnp.sum(sums[SLOTS : SLOTS + 2], axis=0), level * SHARE, SHARE, 0
+        )
+        used = jnp.arange(SHARE) % GROUP < SLOTS
+        sums = jnp.where(
+            used[:, None], sums * lax.rsqrt(total / D + epsilon)[:, None], 0.0
+        )
+        return (jax.nn.silu(sums[:, :half]) * sums[:, half:]).astype(bf16)
+
+    def gathered(hidden):
+        every = jnp.zeros((NH, SHARE, half), bf16)
+        every = lax.dynamic_update_index_in_dim(every, hidden, level, 0)
+        for distance in (2, 1, 3):
+            every = lax.dynamic_update_index_in_dim(
+                every, to_ahead(hidden, distance), (level - distance) % NH, 0
+            )
+        return every.reshape(ROWS, half)
+
+    def finished(hidden):
+        return (
+            jnp.dot(hidden, down, preferred_element_type=f32)
+            + jnp.dot(swap(hidden, "c"), other_down, preferred_element_type=f32)
         ).astype(bf16)
-        incoming = exchange(outgoing.reshape(GRID, SLOTS, SLICE), ("x", "y")).reshape(ROWS, SLICE)
-        other_incoming = swap(incoming, "c")
-        part = (
-            jnp.dot(incoming, gate_up, preferred_element_type=f32)
-            + jnp.dot(other_incoming, other_gate_up, preferred_element_type=f32)
-        ).astype(bf16)
-        squares = jnp.sum(
-            jnp.square(incoming.astype(f32)) * inverse
-            + jnp.square(other_incoming.astype(f32)) * other_inverse,
-            axis=1,
-        ).reshape(NH, 1, SHARE)
-        high = squares.astype(bf16)
-        low = (squares - high.astype(f32)).astype(bf16)
-        extra = jnp.pad(jnp.concatenate([high, low], axis=1), ((0, 0), (0, 6), (0, FF - SHARE)))
-        parts = exchange(
-            jnp.concatenate([part.reshape(NH, SHARE, FF), extra], axis=1), "h"
-        ).astype(f32)
-        sums = jnp.sum(parts[:, :SHARE], axis=0)
-        total = jnp.sum(parts[:, SHARE : SHARE + 2, :SHARE], axis=(0, 1))
-        sums = sums * lax.rsqrt(total / D + epsilon)[:, None]
-        hidden = (jax.nn.silu(sums[:, :half]) * sums[:, half:]).astype(bf16)
-        copies = jnp.broadcast_to(hidden[None], (NH, SHARE, half))
-        all_hidden = exchange(copies, "h").reshape(ROWS, half)
-        other_hidden = swap(all_hidden, "c")
-        results = (
-            jnp.dot(all_hidden, down, preferred_element_type=f32)
-            + jnp.dot(other_hidden, other_down, preferred_element_type=f32)
-        ).astype(bf16)
-        returned = exchange(results.reshape(GRID, SLOTS, SLICE), ("x", "y")).reshape(ROWS, SLICE)
-        mixed.append(
-            jnp.einsum("rt,rd->td", spread(slots, gates), returned, preferred_element_type=f32)
-        )
-    expert_out = mixed[0] + swap(mixed[1].astype(bf16), "l").astype(f32)
+
+    def combined(slot_list, returned):
+        return jnp.einsum("rt,rd->td", spread(*slot_list), returned, preferred_element_type=f32)
+
+    beside = swap(scaled, "l")
+    first = share_products(through(chosen(slot_lists[0], scaled)))
+    first, beside = lax.optimization_barrier((first, beside))
+    second = share_products(through(chosen(slot_lists[1], beside)))
+    parts = exchange(second, "h")
+    first = finished(gathered(activated(scattered(first))))
+    first, parts = lax.optimization_barrier((first, parts))
+    first = through(first)
+    hidden = gathered(activated(jnp.sum(parts.astype(f32), axis=0)))
+    first, hidden = lax.optimization_barrier((first, hidden))
+    second = through(finished(hidden))
+    mixed = combined(slot_lists[0], first)
+    other_mixed = combined(slot_lists[1], second)
+    expert_out = mixed + swap(other_mixed.astype(bf16), "l").astype(f32)
     return stream.astype(bf16), expert_out.astype(bf16)
 
 

time: 334 us -> 315 us (0.943)
  waiting for transfers between devices: 181 us -> 119 us
  blocking collectives: 0 us -> 26.9 us
  starting transfers between devices: 94 us -> 112 us
  Pallas kernels: 0 us -> 10.9 us
  local copies, waits for them, and re-layouts: 14.8 us -> 7.33 us
  other arithmetic: 10.6 us -> 6.99 us
    all_to_all x11 -> x7, waiting for transfers between devices: 170 us -> 73.8 us  [exchange(): return lax.all_to_all(blocks, axes, split_axis=0, concat_axis=0, tiled=True)]
    ppermute x0 -> x6, waiting for transfers between devices: none -> 35.9 us  [to_ahead(): lax.ppermute(block, 'h', [(i, (i + distance) % NH) for i in range(NH)])]
    all_to_all x0 -> x1, blocking collectives: none -> 26.9 us  [exchange(): return lax.all_to_all(blocks, axes, split_axis=0, concat_axis=0, tiled=True)]
    ppermute x0 -> x6, starting transfers between devices: none -> 26.3 us  [to_ahead(): lax.ppermute(block, 'h', [(i, (i + distance) % NH) for i in range(NH)])]
    all_to_all x11 -> x7, starting transfers between devices: 55.2 us -> 42.6 us  [exchange(): return lax.all_to_all(blocks, axes, split_axis=0, concat_axis=0, tiled=True)]
    pallas_call x0 -> x2, Pallas kernels: none -> 10.9 us  [products(): pl.pallas_call(products_kernel, out_shape=jax.ShapeDtypeStruct((NH, SHARE...]
    reshape x10 -> x0, local copies, waits for them, and re-layouts: 7.7 us -> none  [the longest x2 2.26 us: body(): outgoing.reshape(GRID, SLOTS, SLICE)]
    ppermute x11, starting transfers between devices: 26.2 us -> 30.3 us  [swap(): return lax.ppermute(block, axis, [(0, 1), (1, 0)])]
  transfers between devices with their start and end apart: 26 -> 29, of which waited for: 16 -> 15; matrix products, arithmetic and copies ran while one was open for 9% -> 6% of each run, Pallas kernels for 0% -> 3%
where the time goes in v4:
time: 315 us; the launch traced here: 314 us
  waiting for transfers between devices  119 us (38%)
  starting transfers between devices  112 us (36%)
  blocking collectives  26.9 us (9%)
  between operations  15.9 us (5%)
  matrix products  14.9 us (5%)
  Pallas kernels  10.9 us (3%)
  local copies, waits for them, and re-layouts  7.33 us (2%)
  other arithmetic  6.99 us (2%)
    all_to_all x7, waiting for transfers between devices, exchange(): return lax.all_to_all(blocks, axes, split_axis=0, concat_axis=0, tiled=True)  73.8 us
    all_to_all x7, starting transfers between devices, exchange(): return lax.all_to_all(blocks, axes, split_axis=0, concat_axis=0, tiled=True)  42.6 us
    ppermute x6, waiting for transfers between devices, to_ahead(): lax.ppermute(block, 'h', [(i, (i + distance) % NH) for i in range(NH)])  35.9 us
    ppermute x11, starting transfers between devices, swap(): return lax.ppermute(block, axis, [(0, 1), (1, 0)])  30.3 us
    all_to_all x1, blocking collectives, exchange(): return lax.all_to_all(blocks, axes, split_axis=0, concat_axis=0, tiled=True)  26.9 us
    ppermute x6, starting transfers between devices, to_ahead(): lax.ppermute(block, 'h', [(i, (i + distance) % NH) for i in range(NH)])  26.3 us
    ppermute x3, starting transfers between devices, from_behind(): return lax.ppermute(block, CTX, route)  12.6 us
    pallas_call x2, Pallas kernels, products(): pl.pallas_call(products_kernel, out_shape=jax.ShapeDtypeStruct((NH, SHARE...  10.9 us
  transfers between devices with their start and end apart: 29, of which 15 were waited for; matrix products, arithmetic and copies ran while one was open for 6% of the time, Pallas kernels for 3%

profile of v4, /device:TPU:8, one launch (start us, length us, event | category | flops | bytes accessed | tf_op | source)
XLA Modules:
  0.0 313.6 jit_solution(2368486106909908088)
XLA Ops:
  8.1 4.3 %collective-permute-start.2 = (bf16[128,256]{1,0:T(8,128)(2,1)S(1)}, bf16[128,256]{1,0:T(8,128)(2,1)S(1)}, u32[]{:S(2)}, u32[]{:S(2)}) collective-permute-start(bf16[128,256]{1,0:T(8,128)(2,1)S(1)} %pad_maximum_fusion.3), channel_id=1, source_target_pairs={{0,8},{8,16},{16,24},{24,32},{32,40},{40,48},{48,56},{56,64},{64,7... | collective-permute-start | bytes 196616 | tf_op jit(solution)/shard_map/ppermute | solution.py:41
  15.9 4.8 %collective-permute-start = (bf16[128,256]{1,0:T(8,128)(2,1)S(1)}, bf16[128,256]{1,0:T(8,128)(2,1)S(1)}, u32[]{:S(2)}, u32[]{:S(2)}) collective-permute-start(bf16[128,256]{1,0:T(8,128)(2,1)S(1)} %pad_maximum_fusion.3), channel_id=1, source_target_pairs={{0,24},{8,32},{16,40},{24,48},{32,56},{40,64},{48,72},{56,80},{64,... | collective-permute-start | bytes 196616 | tf_op jit(solution)/shard_map/ppermute | solution.py:41
  29.4 4.3 %collective-permute-start.6 = (bf16[64,512]{1,0:T(8,128)(2,1)S(1)}, bf16[64,512]{1,0:T(8,128)(2,1)S(1)}, u32[]{:S(2)}, u32[]{:S(2)}) collective-permute-start(bf16[64,512]{1,0:T(8,128)(2,1)S(1)} %copy-done.5), channel_id=1, source_target_pairs={{0,8},{8,0},{1,9},{9,1},{2,10},{10,2},{3,11},{11,3},{4,12},{12,4},... | collective-permute-start | bytes 196616 | tf_op jit(solution)/shard_map/ppermute | solution.py:32
  39.6 9.9 %all-to-all-start = ((bf16[4,128,512]{2,1,0:T(8,128)(2,1)}), bf16[4,128,512]{2,1,0:T(8,128)(2,1)}, u32[]{:S(2)}, u32[]{:S(2)}) async-start(bf16[4,128,512]{2,1,0:T(8,128)(2,1)} %broadcast_in_dim.319), calls=%async_computation | async-start | bytes 1048576 | tf_op jit(solution)/shard_map/all_to_all | solution.py:36
  49.8 14.5 %all-to-all-done = bf16[4,128,512]{2,1,0:T(8,128)(2,1)} async-done(((bf16[4,128,512]{2,1,0:T(8,128)(2,1)}), bf16[4,128,512]{2,1,0:T(8,128)(2,1)}, u32[]{:S(2)}, u32[]{:S(2)}) %all-to-all-start) | async-done | bytes 524320 | tf_op jit(solution)/shard_map/all_to_all | solution.py:36
  64.3 4.3 %all-to-all-start.1 = ((bf16[4,128,512]{2,1,0:T(8,128)(2,1)}), bf16[4,128,512]{2,1,0:T(8,128)(2,1)S(1)}, u32[]{:S(2)}, u32[]{:S(2)}) async-start(bf16[4,128,512]{2,1,0:T(8,128)(2,1)} %all-to-all-done), calls=%async_computation.1 | async-start | bytes 1048576 | tf_op jit(solution)/shard_map/all_to_all | solution.py:36
  68.8 4.1 %collective-permute-start.5 = (f32[128,24]{0,1:T(8,128)S(1)}, f32[128,24]{0,1:T(8,128)S(1)}, u32[]{:S(2)}, u32[]{:S(2)}) collective-permute-start(f32[128,24]{0,1:T(8,128)S(1)} %get-tuple-element.64), channel_id=1, source_target_pairs={{0,8},{8,0},{1,9},{9,1},{2,10},{10,2},{3,11},{11,3},{4,12},{12,4},... | collective-permute-start | bytes 36872 | tf_op jit(solution)/shard_map/ppermute | solution.py:32
  87.4 9.9 %all-to-all-done.2 = bf16[4,128,512]{2,1,0:T(8,128)(2,1)S(1)} async-done(((bf16[4,128,512]{2,1,0:T(8,128)(2,1)}), bf16[4,128,512]{2,1,0:T(8,128)(2,1)S(1)}, u32[]{:S(2)}, u32[]{:S(2)}) %all-to-all-start.2) | async-done | bytes 524320 | tf_op jit(solution)/shard_map/all_to_all | solution.py:36
  98.6 26.9 %all_to_all.40 = bf16[32,24,512]{2,1,0:T(8,128)(2,1)S(1)} all-to-all(bf16[32,24,512]{2,1,0:T(8,128)(2,1)S(1)} %bitcast.188), channel_id=1, replica_groups=mesh['x'=4,'y'=8,'l'=2,'h'=4,'c'=2] {'x','y'}, dimensions={0} | all-to-all | bytes 1572864 | tf_op jit(solution)/shard_map/all_to_all | solution.py:36
  127.4 4.8 %collective-permute-start.9 = (bf16[128,512]{1,0:T(8,128)(2,1)S(1)}, bf16[128,512]{1,0:T(8,128)(2,1)S(1)}, u32[]{:S(2)}, u32[]{:S(2)}) collective-permute-start(bf16[128,512]{1,0:T(8,128)(2,1)S(1)} %get-tuple-element.38), channel_id=1, source_target_pairs={{0,8},{8,0},{1,9},{9,1},{2,10},{10,2},{3,11},{11,3},{4,12},{12,4},... | collective-permute-start | bytes 393224 | tf_op jit(solution)/shard_map/ppermute | solution.py:32
  132.2 4.9 %shard_map.149 = bf16[4,192,768]{2,1,0:T(8,128)(2,1)} custom-call(bf16[768,512]{1,0:T(8,128)(2,1)S(1)} %bitcast.175, bf16[768,512]{1,0:T(8,128)(2,1)S(1)} %collective-permute-done.8.other_ref, bf16[512,768]{1,0:T(8,128)(2,1)S(1)} %pad_maximum_fusion.w_own_ref, bf16[512,768]{1,0:T(8,128)(2,1)S(1)} %collective-permute-done.3.w_other_ref, ...), custom_call_target="tpu_custom_call" | custom-call | flops 100000000 | bytes 500000 | tf_op jit(solution)/shard_map/pallas_call | solution.py:139
  138.8 4.9 %all-to-all-start.4 = ((bf16[32,24,512]{2,1,0:T(8,128)(2,1)}), bf16[32,24,512]{2,1,0:T(8,128)(2,1)S(1)}, u32[]{:S(2)}, u32[]{:S(2)}) async-start(bf16[32,24,512]{2,1,0:T(8,128)(2,1)} %bitcast.187), calls=%async_computation.5 | async-start | bytes 1572864 | tf_op jit(solution)/shard_map/all_to_all | solution.py:36
  143.8 23.3 %all-to-all-done.4 = bf16[32,24,512]{2,1,0:T(8,128)(2,1)S(1)} async-done(((bf16[32,24,512]{2,1,0:T(8,128)(2,1)}), bf16[32,24,512]{2,1,0:T(8,128)(2,1)S(1)}, u32[]{:S(2)}, u32[]{:S(2)}) %all-to-all-start.4) | async-done | bytes 786464 | tf_op jit(solution)/shard_map/all_to_all | solution.py:36
  172.3 5.1 %collective-permute-start.10 = (bf16[192,384]{1,0:T(8,128)(2,1)S(1)}, bf16[192,384]{1,0:T(8,128)(2,1)S(1)}, u32[]{:S(2)}, u32[]{:S(2)}) collective-permute-start(bf16[192,384]{1,0:T(8,128)(2,1)S(1)} %get-tuple-element.31), channel_id=1, source_target_pairs={{0,4},{2,6},{4,0},{6,2},{1,5},{3,7},{5,1},{7,3},{8,12},{10,14},{12... | collective-permute-start | bytes 442376 | tf_op jit(solution)/shard_map/ppermute | solution.py:150
  177.4 6.0 %shard_map.150 = bf16[4,192,768]{2,1,0:T(8,128)(2,1)} custom-call(bf16[768,512]{1,0:T(8,128)(2,1)S(1)} %bitcast.173, bf16[768,512]{1,0:T(8,128)(2,1)} %collective-permute-done.14.other_ref, bf16[512,768]{1,0:T(8,128)(2,1)S(1)} %pad_maximum_fusion.w_own_ref, bf16[512,768]{1,0:T(8,128)(2,1)S(1)} %collective-permute-done.3.w_other_ref, f32[1,512]{1,0:T(1,128)S(1)} %bitcast.178, ...), custom_call_target="tpu_custom_call" | custom-call | flops 100000000 | bytes 500000 | tf_op jit(solution)/shard_map/pallas_call | solution.py:139
  183.4 4.4 %all-to-all-start.5 = ((bf16[4,192,768]{2,1,0:T(8,128)(2,1)}), bf16[4,192,768]{2,1,0:T(8,128)(2,1)S(1)}, u32[]{:S(2)}, u32[]{:S(2)}) async-start(bf16[4,192,768]{2,1,0:T(8,128)(2,1)} %shard_map.150), calls=%async_computation.6 | async-start | bytes 2359296 | tf_op jit(solution)/shard_map/all_to_all | solution.py:36
  187.8 4.8 %collective-permute-start.11 = (bf16[192,384]{1,0:T(8,128)(2,1)S(1)}, bf16[192,384]{1,0:T(8,128)(2,1)S(1)}, u32[]{:S(2)}, u32[]{:S(2)}) collective-permute-start(bf16[192,384]{1,0:T(8,128)(2,1)S(1)} %get-tuple-element.31), channel_id=1, source_target_pairs={{0,2},{2,4},{4,6},{6,0},{1,3},{3,5},{5,7},{7,1},{8,10},{10,12},{12... | collective-permute-start | bytes 442376 | tf_op jit(solution)/shard_map/ppermute | solution.py:150
  195.8 28.4 %collective-permute-done.11 = bf16[192,384]{1,0:T(8,128)(2,1)S(1)} collective-permute-done((bf16[192,384]{1,0:T(8,128)(2,1)S(1)}, bf16[192,384]{1,0:T(8,128)(2,1)S(1)}, u32[]{:S(2)}, u32[]{:S(2)}) %collective-permute-start.11) | collective-permute-done | bytes 147488 | tf_op jit(solution)/shard_map/ppermute | solution.py:150
  230.3 7.5 %all-to-all-start.6 = ((bf16[32,24,512]{2,1,0:T(8,128)(2,1)}), bf16[32,24,512]{2,1,0:T(8,128)(2,1)S(1)}, u32[]{:S(2)}, u32[]{:S(2)}) async-start(bf16[32,24,512]{2,1,0:T(8,128)(2,1)} %bitcast.54), calls=%async_computation.7 | async-start | bytes 1572864 | tf_op jit(solution)/shard_map/all_to_all | solution.py:36
  238.3 5.3 %collective-permute-start.15 = (bf16[192,384]{1,0:T(8,128)(2,1)S(1)}, bf16[192,384]{1,0:T(8,128)(2,1)S(1)}, u32[]{:S(2)}, u32[]{:S(2)}) collective-permute-start(bf16[192,384]{1,0:T(8,128)(2,1)S(1)} %get-tuple-element.29), channel_id=1, source_target_pairs={{0,4},{2,6},{4,0},{6,2},{1,5},{3,7},{5,1},{7,3},{8,12},{10,14},{12... | collective-permute-start | bytes 442376 | tf_op jit(solution)/shard_map/ppermute | solution.py:150
  243.7 4.0 %collective-permute-start.16 = (bf16[192,384]{1,0:T(8,128)(2,1)S(1)}, bf16[192,384]{1,0:T(8,128)(2,1)S(1)}, u32[]{:S(2)}, u32[]{:S(2)}) collective-permute-start(bf16[192,384]{1,0:T(8,128)(2,1)S(1)} %get-tuple-element.29), channel_id=1, source_target_pairs={{0,2},{2,4},{4,6},{6,0},{1,3},{3,5},{5,7},{7,1},{8,10},{10,12},{12... | collective-permute-start | bytes 442376 | tf_op jit(solution)/shard_map/ppermute | solution.py:150
  251.7 6.3 %collective-permute-done.16 = bf16[192,384]{1,0:T(8,128)(2,1)S(1)} collective-permute-done((bf16[192,384]{1,0:T(8,128)(2,1)S(1)}, bf16[192,384]{1,0:T(8,128)(2,1)S(1)}, u32[]{:S(2)}, u32[]{:S(2)}) %collective-permute-start.16) | collective-permute-done | bytes 147488 | tf_op jit(solution)/shard_map/ppermute | solution.py:150
  266.4 8.0 %all-to-all-start.7 = ((bf16[32,24,512]{2,1,0:T(8,128)(2,1)}), bf16[32,24,512]{2,1,0:T(8,128)(2,1)S(1)}, u32[]{:S(2)}, u32[]{:S(2)}) async-start(bf16[32,24,512]{2,1,0:T(8,128)(2,1)} %bitcast.69), calls=%async_computation.8 | async-start | bytes 1572864 | tf_op jit(solution)/shard_map/all_to_all | solution.py:36
  275.5 22.3 %all-to-all-done.7 = bf16[32,24,512]{2,1,0:T(8,128)(2,1)S(1)} async-done(((bf16[32,24,512]{2,1,0:T(8,128)(2,1)}), bf16[32,24,512]{2,1,0:T(8,128)(2,1)S(1)}, u32[]{:S(2)}, u32[]{:S(2)}) %all-to-all-start.7) | async-done | bytes 786464 | tf_op jit(solution)/shard_map/all_to_all | solution.py:36
  (197 shorter events, 74.6 us)
Async XLA Ops:
  7.2 73.4 %all-gather.2.cloned.1.call-start = ((), (), s32[]{:S(2)}) async-start(), calls=%async_computation.9 | async-start | bytes 1179648 | tf_op jit(solution)/shard_map/all_gather | solution.py:183
  8.1 21.3 %collective-permute-start.2 = (bf16[128,256]{1,0:T(8,128)(2,1)S(1)}, bf16[128,256]{1,0:T(8,128)(2,1)S(1)}, u32[]{:S(2)}, u32[]{:S(2)}) collective-permute-start(bf16[128,256]{1,0:T(8,128)(2,1)S(1)} %pad_maximum_fusion.3), channel_id=1, source_target_pairs={{0,8},{8,16},{16,24},{24,32},{32,40},{40,48},{48,56},{56,64},{64,7... | collective-permute-start | bytes 196616 | tf_op jit(solution)/shard_map/ppermute | solution.py:41
  12.4 21.3 %collective-permute-start.1 = (bf16[128,256]{1,0:T(8,128)(2,1)S(1)}, bf16[128,256]{1,0:T(8,128)(2,1)S(1)}, u32[]{:S(2)}, u32[]{:S(2)}) collective-permute-start(bf16[128,256]{1,0:T(8,128)(2,1)S(1)} %pad_maximum_fusion.3), channel_id=1, source_target_pairs={{0,16},{8,24},{16,32},{24,40},{32,48},{40,56},{48,64},{56,72},{64,... | collective-permute-start | bytes 196616 | tf_op jit(solution)/shard_map/ppermute | solution.py:41
  15.9 17.8 %collective-permute-start = (bf16[128,256]{1,0:T(8,128)(2,1)S(1)}, bf16[128,256]{1,0:T(8,128)(2,1)S(1)}, u32[]{:S(2)}, u32[]{:S(2)}) collective-permute-start(bf16[128,256]{1,0:T(8,128)(2,1)S(1)} %pad_maximum_fusion.3), channel_id=1, source_target_pairs={{0,24},{8,32},{16,40},{24,48},{32,56},{40,64},{48,72},{56,80},{64,... | collective-permute-start | bytes 196616 | tf_op jit(solution)/shard_map/ppermute | solution.py:41
  23.9 50.6 %collective-permute-start.3 = (bf16[512,768]{1,0:T(8,128)(2,1)}, bf16[512,768]{1,0:T(8,128)(2,1)S(1)}, u32[]{:S(2)}, u32[]{:S(2)}) collective-permute-start(bf16[512,768]{1,0:T(8,128)(2,1)} %pad_maximum_fusion.1), channel_id=1, source_target_pairs={{0,1},{1,0},{2,3},{3,2},{4,5},{5,4},{6,7},{7,6},{8,9},{9,8},{10,11... | collective-permute-start | bytes 2359304 | tf_op jit(solution)/shard_map/ppermute | solution.py:32
  25.9 48.1 %collective-permute-start.4 = (f32[1,512]{1,0:T(1,128)S(1)}, f32[1,512]{1,0:T(1,128)S(1)}, u32[]{:S(2)}, u32[]{:S(2)}) collective-permute-start(f32[1,512]{1,0:T(1,128)S(1)} %bitcast.176), channel_id=1, source_target_pairs={{0,1},{1,0},{2,3},{3,2},{4,5},{5,4},{6,7},{7,6},{8,9},{9,8},{10,11... | collective-permute-start | bytes 6152 | tf_op jit(solution)/shard_map/ppermute | solution.py:32
  39.6 24.7 %all-to-all-start = ((bf16[4,128,512]{2,1,0:T(8,128)(2,1)}), bf16[4,128,512]{2,1,0:T(8,128)(2,1)}, u32[]{:S(2)}, u32[]{:S(2)}) async-start(bf16[4,128,512]{2,1,0:T(8,128)(2,1)} %broadcast_in_dim.319), calls=%async_computation | async-start | bytes 1048576 | tf_op jit(solution)/shard_map/all_to_all | solution.py:36
  64.3 12.4 %all-to-all-start.1 = ((bf16[4,128,512]{2,1,0:T(8,128)(2,1)}), bf16[4,128,512]{2,1,0:T(8,128)(2,1)S(1)}, u32[]{:S(2)}, u32[]{:S(2)}) async-start(bf16[4,128,512]{2,1,0:T(8,128)(2,1)} %all-to-all-done), calls=%async_computation.1 | async-start | bytes 1048576 | tf_op jit(solution)/shard_map/all_to_all | solution.py:36
  83.6 13.6 %all-to-all-start.2 = ((bf16[4,128,512]{2,1,0:T(8,128)(2,1)}), bf16[4,128,512]{2,1,0:T(8,128)(2,1)S(1)}, u32[]{:S(2)}, u32[]{:S(2)}) async-start(bf16[4,128,512]{2,1,0:T(8,128)(2,1)} %bitcast.17), calls=%async_computation.2 | async-start | bytes 1048576 | tf_op jit(solution)/shard_map/all_to_all | solution.py:36
  87.2 81.8 %reduce-scatter.2.cloned.1.call-start = ((), (), s32[]{:S(2)}) async-start(), calls=%async_computation.10 | async-start | bytes 1474560 | tf_op jit(solution)/shard_map/reduce_scatter | solution.py:238
  125.5 6.8 %collective-permute-start.8 = (bf16[768,512]{1,0:T(8,128)(2,1)S(1)}, bf16[768,512]{1,0:T(8,128)(2,1)S(1)}, u32[]{:S(2)}, u32[]{:S(2)}) collective-permute-start(bf16[768,512]{1,0:T(8,128)(2,1)S(1)} %bitcast.174), channel_id=1, source_target_pairs={{0,1},{1,0},{2,3},{3,2},{4,5},{5,4},{6,7},{7,6},{8,9},{9,8},{10,11... | collective-permute-start | bytes 2359304 | tf_op jit(solution)/shard_map/ppermute | solution.py:32
  127.4 9.8 %collective-permute-start.9 = (bf16[128,512]{1,0:T(8,128)(2,1)S(1)}, bf16[128,512]{1,0:T(8,128)(2,1)S(1)}, u32[]{:S(2)}, u32[]{:S(2)}) collective-permute-start(bf16[128,512]{1,0:T(8,128)(2,1)S(1)} %get-tuple-element.38), channel_id=1, source_target_pairs={{0,8},{8,0},{1,9},{9,1},{2,10},{10,2},{3,11},{11,3},{4,12},{12,4},... | collective-permute-start | bytes 393224 | tf_op jit(solution)/shard_map/ppermute | solution.py:32
  138.8 28.3 %all-to-all-start.4 = ((bf16[32,24,512]{2,1,0:T(8,128)(2,1)}), bf16[32,24,512]{2,1,0:T(8,128)(2,1)S(1)}, u32[]{:S(2)}, u32[]{:S(2)}) async-start(bf16[32,24,512]{2,1,0:T(8,128)(2,1)} %bitcast.187), calls=%async_computation.5 | async-start | bytes 1572864 | tf_op jit(solution)/shard_map/all_to_all | solution.py:36
  167.1 10.3 %collective-permute-start.14 = (bf16[768,512]{1,0:T(8,128)(2,1)S(1)}, bf16[768,512]{1,0:T(8,128)(2,1)}, u32[]{:S(2)}, u32[]{:S(2)}) collective-permute-start(bf16[768,512]{1,0:T(8,128)(2,1)S(1)} %bitcast.172), channel_id=1, source_target_pairs={{0,1},{1,0},{2,3},{3,2},{4,5},{5,4},{6,7},{7,6},{8,9},{9,8},{10,11... | collective-permute-start | bytes 2359304 | tf_op jit(solution)/shard_map/ppermute | solution.py:32
  172.3 23.5 %collective-permute-start.10 = (bf16[192,384]{1,0:T(8,128)(2,1)S(1)}, bf16[192,384]{1,0:T(8,128)(2,1)S(1)}, u32[]{:S(2)}, u32[]{:S(2)}) collective-permute-start(bf16[192,384]{1,0:T(8,128)(2,1)S(1)} %get-tuple-element.31), channel_id=1, source_target_pairs={{0,4},{2,6},{4,0},{6,2},{1,5},{3,7},{5,1},{7,3},{8,12},{10,14},{12... | collective-permute-start | bytes 442376 | tf_op jit(solution)/shard_map/ppermute | solution.py:150
  183.4 46.8 %all-to-all-start.5 = ((bf16[4,192,768]{2,1,0:T(8,128)(2,1)}), bf16[4,192,768]{2,1,0:T(8,128)(2,1)S(1)}, u32[]{:S(2)}, u32[]{:S(2)}) async-start(bf16[4,192,768]{2,1,0:T(8,128)(2,1)} %shard_map.150), calls=%async_computation.6 | async-start | bytes 2359296 | tf_op jit(solution)/shard_map/all_to_all | solution.py:36
  187.8 36.5 %collective-permute-start.11 = (bf16[192,384]{1,0:T(8,128)(2,1)S(1)}, bf16[192,384]{1,0:T(8,128)(2,1)S(1)}, u32[]{:S(2)}, u32[]{:S(2)}) collective-permute-start(bf16[192,384]{1,0:T(8,128)(2,1)S(1)} %get-tuple-element.31), channel_id=1, source_target_pairs={{0,2},{2,4},{4,6},{6,0},{1,3},{3,5},{5,7},{7,1},{8,10},{10,12},{12... | collective-permute-start | bytes 442376 | tf_op jit(solution)/shard_map/ppermute | solution.py:150
  192.6 31.7 %collective-permute-start.12 = (bf16[192,384]{1,0:T(8,128)(2,1)S(1)}, bf16[192,384]{1,0:T(8,128)(2,1)S(1)}, u32[]{:S(2)}, u32[]{:S(2)}) collective-permute-start(bf16[192,384]{1,0:T(8,128)(2,1)S(1)} %get-tuple-element.31), channel_id=1, source_target_pairs={{0,6},{2,0},{4,2},{6,4},{1,7},{3,1},{5,3},{7,5},{8,14},{10,8},{12,... | collective-permute-start | bytes 442376 | tf_op jit(solution)/shard_map/ppermute | solution.py:150
  230.3 30.8 %all-to-all-start.6 = ((bf16[32,24,512]{2,1,0:T(8,128)(2,1)}), bf16[32,24,512]{2,1,0:T(8,128)(2,1)S(1)}, u32[]{:S(2)}, u32[]{:S(2)}) async-start(bf16[32,24,512]{2,1,0:T(8,128)(2,1)} %bitcast.54), calls=%async_computation.7 | async-start | bytes 1572864 | tf_op jit(solution)/shard_map/all_to_all | solution.py:36
  238.3 13.3 %collective-permute-start.15 = (bf16[192,384]{1,0:T(8,128)(2,1)S(1)}, bf16[192,384]{1,0:T(8,128)(2,1)S(1)}, u32[]{:S(2)}, u32[]{:S(2)}) collective-permute-start(bf16[192,384]{1,0:T(8,128)(2,1)S(1)} %get-tuple-element.29), channel_id=1, source_target_pairs={{0,4},{2,6},{4,0},{6,2},{1,5},{3,7},{5,1},{7,3},{8,12},{10,14},{12... | collective-permute-start | bytes 442376 | tf_op jit(solution)/shard_map/ppermute | solution.py:150
  243.7 14.3 %collective-permute-start.16 = (bf16[192,384]{1,0:T(8,128)(2,1)S(1)}, bf16[192,384]{1,0:T(8,128)(2,1)S(1)}, u32[]{:S(2)}, u32[]{:S(2)}) collective-permute-start(bf16[192,384]{1,0:T(8,128)(2,1)S(1)} %get-tuple-element.29), channel_id=1, source_target_pairs={{0,2},{2,4},{4,6},{6,0},{1,3},{3,5},{5,7},{7,1},{8,10},{10,12},{12... | collective-permute-start | bytes 442376 | tf_op jit(solution)/shard_map/ppermute | solution.py:150
  247.7 11.5 %collective-permute-start.17 = (bf16[192,384]{1,0:T(8,128)(2,1)S(1)}, bf16[192,384]{1,0:T(8,128)(2,1)S(1)}, u32[]{:S(2)}, u32[]{:S(2)}) collective-permute-start(bf16[192,384]{1,0:T(8,128)(2,1)S(1)} %get-tuple-element.29), channel_id=1, source_target_pairs={{0,6},{2,0},{4,2},{6,4},{1,7},{3,1},{5,3},{7,5},{8,14},{10,8},{12,... | collective-permute-start | bytes 442376 | tf_op jit(solution)/shard_map/ppermute | solution.py:150
  266.4 31.3 %all-to-all-start.7 = ((bf16[32,24,512]{2,1,0:T(8,128)(2,1)}), bf16[32,24,512]{2,1,0:T(8,128)(2,1)S(1)}, u32[]{:S(2)}, u32[]{:S(2)}) async-start(bf16[32,24,512]{2,1,0:T(8,128)(2,1)} %bitcast.69), calls=%async_computation.8 | async-start | bytes 1572864 | tf_op jit(solution)/shard_map/all_to_all | solution.py:36
  298.5 6.9 %collective-permute-start.19 = (bf16[128,512]{1,0:T(8,128)(2,1)S(1)}, bf16[128,512]{1,0:T(8,128)(2,1)S(1)}, u32[]{:S(2)}, u32[]{:S(2)}) collective-permute-start(bf16[128,512]{1,0:T(8,128)(2,1)S(1)} %convolution_convert_fusion.2), channel_id=1, source_target_pairs={{0,8},{8,0},{1,9},{9,1},{2,10},{10,2},{3,11},{11,3},{4,12},{12,4},... | collective-permute-start | bytes 393224 | tf_op jit(solution)/shard_map/ppermute | solution.py:32
  (49 other events, 823.4 us)
Sparse Core Ops, SparseCore 0:
  36.8 41.0 all-gather.1
  137.3 31.5 reduce-scatter.1

commit v5 on v3

--- a/solution.py
+++ b/solution.py
@@ -2,6 +2,8 @@
 import jax.numpy as jnp
 import numpy as np
 from jax import lax
+from jax.experimental import pallas as pl
+from jax.experimental.pallas import tpu as pltpu
 from jax.sharding import Mesh, PartitionSpec as P
 
 D = 4096
@@ -13,11 +15,14 @@
 FIX = 32
 TOK = 128
 SLOTS = 21
+GROUP = 24
 NX, NY, NL, NH, NC = 4, 8, 2, 4, 2
 N_CTX = NX * NY * NL
-GRID = NX * NY
-ROWS = GRID * SLOTS
+SENT = N_CTX * GROUP
+ROWS = N_CTX * SLOTS
 SHARE = ROWS // NH
+PACK = 8 * SLOTS
+PACK_SENT = 8 * GROUP
 SLICE = D // (NH * NC)
 CTX = ("x", "y", "l")
 f32, bf16 = jnp.float32, jnp.bfloat16
@@ -89,18 +94,97 @@
     return ids.astype(f32), rank
 
 
-def row_slots(table, side):
-    ids, rank, gates = table[:TOPK], table[TOPK : 2 * TOPK], table[2 * TOPK :]
-    column = jnp.floor(ids * 0.5)
-    return jnp.where(ids - 2.0 * column == side, column * SLOTS + rank, -1.0), gates
-
-
 def spread(slots, values):
-    row_ids = jnp.arange(ROWS, dtype=f32)[:, None]
-    total = jnp.zeros((ROWS, slots.shape[1]), f32)
+    row_ids = jnp.arange(SENT, dtype=f32)[:, None]
+    total = jnp.zeros((SENT, slots.shape[1]), f32)
     for k in range(TOPK):
         total = total + jnp.where(slots[k][None, :] == row_ids, values[k][None, :], 0.0)
     return total.astype(bf16)
+
+
+def packing():
+    place = np.arange(PACK)
+    return (place // SLOTS * GROUP + place % SLOTS)[:, None] == np.arange(PACK_SENT)[None, :]
+
+
+def products_kernel(
+    own_ref, other_ref, w_own_ref, w_other_ref, inv_own_ref, inv_other_ref, pick_ref, gate_ref, up_ref
+):
+    half = FF // 2
+    pick = pick_ref[...]
+    ones = jnp.ones((8, SLICE), bf16)
+
+    def packed(ref, h):
+        first, second = (
+            jnp.dot(
+                pick,
+                ref[(2 * h + i) * PACK_SENT : (2 * h + i + 1) * PACK_SENT],
+                preferred_element_type=f32,
+            )
+            for i in range(2)
+        )
+        return jnp.concatenate([first, second], axis=0)
+
+    def squares(rows, inverse_ref):
+        weighted = jnp.concatenate(
+            [rows * rows * inverse_ref[...], jnp.zeros((half - SHARE, SLICE), f32)], axis=0
+        )
+        high = weighted.astype(bf16)
+        low = (weighted - high.astype(f32)).astype(bf16)
+        across = (((1,), (1,)), ((), ()))
+        return lax.dot_general(ones, high, across, preferred_element_type=f32) + lax.dot_general(
+            ones, low, across, preferred_element_type=f32
+        )
+
+    row = lax.broadcasted_iota(jnp.int32, (16, half), 0)
+    for h in range(NH):
+        own, other = packed(own_ref, h), packed(other_ref, h)
+        part = jnp.dot(own.astype(bf16), w_own_ref[...], preferred_element_type=f32) + jnp.dot(
+            other.astype(bf16), w_other_ref[...], preferred_element_type=f32
+        )
+        gate_ref[h] = part[:, :half].astype(bf16)
+        up_ref[h, :SHARE] = part[:, half:].astype(bf16)
+        total = (squares(own, inv_own_ref) + squares(other, inv_other_ref))[:1]
+        high = total.astype(bf16).astype(f32)
+        tile = jnp.where(row == 0, high, jnp.where(row == 1, total - high, 0.0))
+        up_ref[h, SHARE:] = tile.astype(bf16)
+
+
+def products(own, other, w_own, w_other, inv_own, inv_other):
+    half = FF // 2
+    return pl.pallas_call(
+        products_kernel,
+        out_shape=(
+            jax.ShapeDtypeStruct((NH, SHARE, half), bf16),
+            jax.ShapeDtypeStruct((NH, SHARE + 16, half), bf16),
+        ),
+        compiler_params=pltpu.CompilerParams(vmem_limit_bytes=48 * 1024 * 1024),
+        cost_estimate=pl.CostEstimate(flops=100_000_000, bytes_accessed=500_000, transcendentals=0),
+    )(own, other, w_own, w_other, inv_own, inv_other, jnp.asarray(packing(), bf16))
+
+
+def results_kernel(own_ref, other_ref, down_own_ref, down_other_ref, place_ref, out_ref):
+    place = place_ref[...]
+    for h in range(NH):
+        rows = slice(h * SHARE, (h + 1) * SHARE)
+        part = jnp.dot(own_ref[rows], down_own_ref[...], preferred_element_type=f32) + jnp.dot(
+            other_ref[rows], down_other_ref[...], preferred_element_type=f32
+        )
+        for i in range(2):
+            rows = part[i * PACK : (i + 1) * PACK].astype(bf16)
+            start = (2 * h + i) * PACK_SENT
+            out_ref[start : start + PACK_SENT] = jnp.dot(
+                place, rows, preferred_element_type=f32
+            ).astype(bf16)
+
+
+def expert_results(own, other, down_own, down_other):
+    return pl.pallas_call(
+        results_kernel,
+        out_shape=jax.ShapeDtypeStruct((SENT, SLICE), bf16),
+        compiler_params=pltpu.CompilerParams(vmem_limit_bytes=48 * 1024 * 1024),
+        cost_estimate=pl.CostEstimate(flops=100_000_000, bytes_accessed=500_000, transcendentals=0),
+    )(own, other, down_own, down_other, jnp.asarray(packing().T, bf16))
 
 
 def body(
@@ -123,8 +207,6 @@
     tokens = queries.shape[0]
     half = FF // 2
 
-    attended = attention(queries, key_rows, value_rows)
-
     other_strip = swap(out_weight, "l")
     strips = jnp.concatenate(
         [
@@ -133,11 +215,16 @@
         ],
         axis=0,
     )
+    strips, queries = lax.optimization_barrier((strips, queries))
     quarter = lax.all_gather(strips, "y", axis=0, tiled=True)
 
+    attended = attention(queries, key_rows, value_rows)
+    attended, w_gate, w_up, norm_gain, pred_ids = lax.optimization_barrier(
+        (attended, w_gate, w_up, norm_gain, pred_ids)
+    )
+
     ids, rank = slots_of(pred_ids, fix_pair, fix_expert, fix_count)
-    table = jnp.concatenate([ids, rank, route_gates.astype(f32)], axis=1)
-    tables = (table.T, swap(table, "l").T)
+    slots, gates = (ids * GROUP + rank).T, route_gates.astype(f32).T
 
     def columns(which):
         return jnp.concatenate(
@@ -157,6 +244,9 @@
 
     copies = jnp.broadcast_to(attended[None], (NH, *attended.shape))
     heads = exchange(exchange(copies, "h"), "x").reshape(NX * tokens, SLICE)
+    heads, gate_up, other_gate_up, inverse, other_inverse, slots = lax.optimization_barrier(
+        (heads, gate_up, other_gate_up, inverse, other_inverse, slots)
+    )
     other_heads = swap(heads, "c")
     partial = jnp.dot(
         heads,
@@ -171,46 +261,23 @@
     stream = residual.astype(f32) + jnp.sum(terms.astype(f32), axis=0)
 
     scaled = (stream * gain).astype(bf16)
-    blocks = (scaled, swap(scaled, "l"))
-    mixed = []
-    for table, rows in zip(tables, blocks):
-        slots, gates = row_slots(table, side.astype(f32))
-        outgoing = jnp.dot(
-            spread(slots, jnp.ones_like(gates)), rows, preferred_element_type=f32
-        ).astype(bf16)
-        incoming = exchange(outgoing.reshape(GRID, SLOTS, SLICE), ("x", "y")).reshape(ROWS, SLICE)
-        other_incoming = swap(incoming, "c")
-        part = (
-            jnp.dot(incoming, gate_up, preferred_element_type=f32)
-            + jnp.dot(other_incoming, other_gate_up, preferred_element_type=f32)
-        ).astype(bf16)
-        squares = jnp.sum(
-            jnp.square(incoming.astype(f32)) * inverse
-            + jnp.square(other_incoming.astype(f32)) * other_inverse,
-            axis=1,
-        ).reshape(NH, 1, SHARE)
-        high = squares.astype(bf16)
-        low = (squares - high.astype(f32)).astype(bf16)
-        extra = jnp.pad(jnp.concatenate([high, low], axis=1), ((0, 0), (0, 6), (0, FF - SHARE)))
-        parts = exchange(
-            jnp.concatenate([part.reshape(NH, SHARE, FF), extra], axis=1), "h"
-        ).astype(f32)
-        sums = jnp.sum(parts[:, :SHARE], axis=0)
-        total = jnp.sum(parts[:, SHARE : SHARE + 2, :SHARE], axis=(0, 1))
-        sums = sums * lax.rsqrt(total / D + epsilon)[:, None]
-        hidden = (jax.nn.silu(sums[:, :half]) * sums[:, half:]).astype(bf16)
-        copies = jnp.broadcast_to(hidden[None], (NH, SHARE, half))
-        all_hidden = exchange(copies, "h").reshape(ROWS, half)
-        other_hidden = swap(all_hidden, "c")
-        results = (
-            jnp.dot(all_hidden, down, preferred_element_type=f32)
-            + jnp.dot(other_hidden, other_down, preferred_element_type=f32)
-        ).astype(bf16)
-        returned = exchange(results.reshape(GRID, SLOTS, SLICE), ("x", "y")).reshape(ROWS, SLICE)
-        mixed.append(
-            jnp.einsum("rt,rd->td", spread(slots, gates), returned, preferred_element_type=f32)
-        )
-    expert_out = mixed[0] + swap(mixed[1].astype(bf16), "l").astype(f32)
+    picks = spread(slots, jnp.ones_like(gates))
+    outgoing = jnp.dot(picks, scaled, preferred_element_type=f32).astype(bf16)
+    incoming = exchange(outgoing.reshape(N_CTX, GROUP, SLICE), CTX).reshape(SENT, SLICE)
+    gate_part, up_part = products(
+        incoming, swap(incoming, "c"), gate_up, other_gate_up, inverse, other_inverse
+    )
+    gate_sum = lax.psum_scatter(
+        gate_part.reshape(ROWS, half), "h", scatter_dimension=0, tiled=True
+    ).astype(f32)
+    up_sum = jnp.sum(exchange(up_part, "h").astype(f32), axis=0)
+    total = jnp.sum(up_sum[SHARE:], axis=0)[:SHARE]
+    scale = lax.rsqrt(total / D + epsilon)[:, None]
+    hidden = (jax.nn.silu(gate_sum * scale) * (up_sum[:SHARE] * scale)).astype(bf16)
+    all_hidden = lax.all_gather(hidden, "h", axis=0, tiled=True)
+    results = expert_results(all_hidden, swap(all_hidden, "c"), down, other_down)
+    returned = exchange(results.reshape(N_CTX, GROUP, SLICE), CTX).reshape(SENT, SLICE)
+    expert_out = jnp.einsum("rt,rd->td", spread(slots, gates), returned, preferred_element_type=f32)
     return stream.astype(bf16), expert_out.astype(bf16)
 
 

time: 334 us -> 295 us (0.88)
  the two profiles are of different devices: /device:TPU:8 before, /device:TPU:2 now
where the time goes in v5:
time: 295 us; the launch traced here: 294 us
  waiting for transfers between devices  127 us (43%)
  blocking collectives  63.9 us (22%)
  starting transfers between devices  60.2 us (20%)
  between operations  15.2 us (5%)
  Pallas kernels  10.8 us (4%)
  matrix products  6.89 us (2%)
  other arithmetic  6.65 us (2%)
  local copies, waits for them, and re-layouts  3.35 us (1%)
    all_to_all x5, waiting for transfers between devices, exchange(): return lax.all_to_all(blocks, axes, split_axis=0, concat_axis=0, tiled=True)  91 us
    all_to_all x1, blocking collectives, exchange(): return lax.all_to_all(blocks, axes, split_axis=0, concat_axis=0, tiled=True)  41.8 us
    all_to_all x5, starting transfers between devices, exchange(): return lax.all_to_all(blocks, axes, split_axis=0, concat_axis=0, tiled=True)  34.3 us
    all_gather x1, blocking collectives, body(): all_hidden = lax.all_gather(hidden, 'h', axis=0, tiled=True)  22.1 us
    ppermute x6, starting transfers between devices, swap(): return lax.ppermute(block, axis, [(0, 1), (1, 0)])  14.5 us
    all_gather x1, waiting for transfers between devices, body(): quarter = lax.all_gather(strips, 'y', axis=0, tiled=True)  13.9 us
    reduce_scatter x1, waiting for transfers between devices, body(): lax.psum_scatter(gate_part.reshape(ROWS, half), 'h', scatter_dimension=0,...  12.7 us
    ppermute x3, starting transfers between devices, from_behind(): return lax.ppermute(block, CTX, route)  11.4 us
  transfers between devices with their start and end apart: 16, of which 11 were waited for; matrix products, arithmetic and copies ran while one was open for 2% of the time, Pallas kernels for 0%

profile of v5, /device:TPU:2, one launch (start us, length us, event | category | flops | bytes accessed | tf_op | source)
XLA Modules:
  0.0 294.2 jit_solution(3633154823549209026)
XLA Ops:
  8.0 4.3 %collective-permute-start.2 = (bf16[128,256]{1,0:T(8,128)(2,1)S(1)}, bf16[128,256]{1,0:T(8,128)(2,1)S(1)}, u32[]{:S(2)}, u32[]{:S(2)}) collective-permute-start(bf16[128,256]{1,0:T(8,128)(2,1)S(1)} %pad_maximum_fusion.3), channel_id=1, source_target_pairs={{0,8},{8,16},{16,24},{24,32},{32,40},{40,48},{48,56},{56,64},{64,7... | collective-permute-start | bytes 196616 | tf_op jit(solution)/shard_map/ppermute | solution.py:43
  12.3 3.5 %collective-permute-start.1 = (bf16[128,256]{1,0:T(8,128)(2,1)S(1)}, bf16[128,256]{1,0:T(8,128)(2,1)S(1)}, u32[]{:S(2)}, u32[]{:S(2)}) collective-permute-start(bf16[128,256]{1,0:T(8,128)(2,1)S(1)} %pad_maximum_fusion.3), channel_id=1, source_target_pairs={{0,16},{8,24},{16,32},{24,40},{32,48},{40,56},{48,64},{56,72},{64,... | collective-permute-start | bytes 196616 | tf_op jit(solution)/shard_map/ppermute | solution.py:43
  15.8 3.6 %collective-permute-start = (bf16[128,256]{1,0:T(8,128)(2,1)S(1)}, bf16[128,256]{1,0:T(8,128)(2,1)S(1)}, u32[]{:S(2)}, u32[]{:S(2)}) collective-permute-start(bf16[128,256]{1,0:T(8,128)(2,1)S(1)} %pad_maximum_fusion.3), channel_id=1, source_target_pairs={{0,24},{8,32},{16,40},{24,48},{32,56},{40,64},{48,72},{56,80},{64,... | collective-permute-start | bytes 196616 | tf_op jit(solution)/shard_map/ppermute | solution.py:43
  19.4 4.3 %collective-permute-start.3 = (bf16[64,512]{1,0:T(8,128)(2,1)}, bf16[64,512]{1,0:T(8,128)(2,1)S(1)}, u32[]{:S(2)}, u32[]{:S(2)}) collective-permute-start(bf16[64,512]{1,0:T(8,128)(2,1)} %param.19), channel_id=1, source_target_pairs={{0,8},{8,0},{1,9},{9,1},{2,10},{10,2},{3,11},{11,3},{4,12},{12,4},... | collective-permute-start | bytes 196616 | tf_op jit(solution)/shard_map/ppermute | solution.py:34
  30.6 9.8 %all-to-all-start = ((bf16[4,128,512]{2,1,0:T(8,128)(2,1)}), bf16[4,128,512]{2,1,0:T(8,128)(2,1)}, u32[]{:S(2)}, u32[]{:S(2)}) async-start(bf16[4,128,512]{2,1,0:T(8,128)(2,1)} %broadcast_in_dim.170), calls=%async_computation | async-start | bytes 1048576 | tf_op jit(solution)/shard_map/all_to_all | solution.py:38
  44.4 2.4 collective-permute-start.5
  47.0 7.7 %all-to-all-done = bf16[4,128,512]{2,1,0:T(8,128)(2,1)} async-done(((bf16[4,128,512]{2,1,0:T(8,128)(2,1)}), bf16[4,128,512]{2,1,0:T(8,128)(2,1)}, u32[]{:S(2)}, u32[]{:S(2)}) %all-to-all-start) | async-done | bytes 524320 | tf_op jit(solution)/shard_map/all_to_all | solution.py:38
  54.8 4.8 %all-to-all-start.1 = ((bf16[4,128,512]{2,1,0:T(8,128)(2,1)}), bf16[4,128,512]{2,1,0:T(8,128)(2,1)S(1)}, u32[]{:S(2)}, u32[]{:S(2)}) async-start(bf16[4,128,512]{2,1,0:T(8,128)(2,1)} %all-to-all-done), calls=%async_computation.1 | async-start | bytes 1048576 | tf_op jit(solution)/shard_map/all_to_all | solution.py:38
  59.7 6.4 %all-to-all-done.1 = bf16[4,128,512]{2,1,0:T(8,128)(2,1)S(1)} async-done(((bf16[4,128,512]{2,1,0:T(8,128)(2,1)}), bf16[4,128,512]{2,1,0:T(8,128)(2,1)S(1)}, u32[]{:S(2)}, u32[]{:S(2)}) %all-to-all-start.1) | async-done | bytes 524320 | tf_op jit(solution)/shard_map/all_to_all | solution.py:38
  70.0 13.9 %all-gather.2.cloned.1.call-done = bf16[1024,512]{1,0:T(8,128)(2,1)} async-done(((bf16[128,512]{1,0:T(8,128)(2,1)}), bf16[1024,512]{1,0:T(8,128)(2,1)}) %all-gather.2.cloned.1.call-update) | async-done | bytes 1048592 | tf_op jit(solution)/shard_map/all_gather | solution.py:219
  86.6 4.9 %all-to-all-start.2 = ((bf16[4,128,512]{2,1,0:T(8,128)(2,1)}), bf16[4,128,512]{2,1,0:T(8,128)(2,1)S(1)}, u32[]{:S(2)}, u32[]{:S(2)}) async-start(bf16[4,128,512]{2,1,0:T(8,128)(2,1)} %bitcast.16), calls=%async_computation.2 | async-start | bytes 1048576 | tf_op jit(solution)/shard_map/all_to_all | solution.py:38
  91.6 6.6 %all-to-all-done.2 = bf16[4,128,512]{2,1,0:T(8,128)(2,1)S(1)} async-done(((bf16[4,128,512]{2,1,0:T(8,128)(2,1)}), bf16[4,128,512]{2,1,0:T(8,128)(2,1)S(1)}, u32[]{:S(2)}, u32[]{:S(2)}) %all-to-all-start.2) | async-done | bytes 524320 | tf_op jit(solution)/shard_map/all_to_all | solution.py:38
  99.3 41.8 %all_to_all.30 = bf16[64,24,512]{2,1,0:T(8,128)(2,1)S(1)} all-to-all(bf16[64,24,512]{2,1,0:T(8,128)(2,1)S(1)} %bitcast.113), channel_id=1, replica_groups=mesh['x'=4,'y'=8,'l'=2,'h'=4,'c'=2] {'x','y','l'}, dimensions={0} | all-to-all | bytes 3145728 | tf_op jit(solution)/shard_map/all_to_all | solution.py:38
  143.0 3.4 %collective-permute-done.7.other_ref = bf16[1536,512]{1,0:T(8,128)(2,1)S(1)} collective-permute-done((bf16[1536,512]{1,0:T(8,128)(2,1)S(1)}, bf16[1536,512]{1,0:T(8,128)(2,1)S(1)}, u32[]{:S(2)}, u32[]{:S(2)}) %collective-permute-start.7) | collective-permute-done | bytes 1572896 | tf_op jit(solution)/shard_map/ppermute | solution.py:34
  147.6 7.3 %shard_map.167 = (bf16[4,336,384]{2,1,0:T(8,128)(2,1)}, bf16[4,352,384]{2,1,0:T(8,128)(2,1)}) custom-call(bf16[1536,512]{1,0:T(8,128)(2,1)S(1)} %bitcast.107, bf16[1536,512]{1,0:T(8,128)(2,1)} %copy-done.3, bf16[512,768]{1,0:T(8,128)(2,1)S(1)} %pad_maximum_fusion.w_own_ref, bf16[512,768]{1,0:T(8,128)(2,1)S(1)} %collective-permute-done.4.w_other_ref, ...), custom_call_target="tpu_custom_call" | custom-call | flops 100000000 | bytes 500000 | tf_op jit(solution)/shard_map/pallas_call | solution.py:155
  154.9 6.5 %all-to-all-start.4 = ((bf16[4,352,384]{2,1,0:T(8,128)(2,1)}), bf16[4,352,384]{2,1,0:T(8,128)(2,1)S(1)}, u32[]{:S(2)}, u32[]{:S(2)}) async-start(bf16[4,352,384]{2,1,0:T(8,128)(2,1)} %get-tuple-element.31), calls=%async_computation.5 | async-start | bytes 2162688 | tf_op jit(solution)/shard_map/all_to_all | solution.py:38
  162.1 31.3 %all-to-all-done.4 = bf16[4,352,384]{2,1,0:T(8,128)(2,1)S(1)} async-done(((bf16[4,352,384]{2,1,0:T(8,128)(2,1)}), bf16[4,352,384]{2,1,0:T(8,128)(2,1)S(1)}, u32[]{:S(2)}, u32[]{:S(2)}) %all-to-all-start.4) | async-done | bytes 1081376 | tf_op jit(solution)/shard_map/all_to_all | solution.py:38
  193.6 12.7 %reduce-scatter.2.cloned.1.call-done = bf16[336,384]{1,0:T(8,128)(2,1)} async-done(((bf16[1344,384]{1,0:T(8,128)(2,1)}), bf16[336,384]{1,0:T(8,128)(2,1)}) %reduce-scatter.2.cloned.1.call-update) | async-done | bytes 258064 | tf_op jit(solution)/shard_map/reduce_scatter | solution.py:270
  207.5 22.1 %all_gather.7.own_ref = bf16[1344,384]{1,0:T(8,128)(2,1)S(1)} all-gather(bf16[336,384]{1,0:T(8,128)(2,1)S(1)} %fusion.14), channel_id=1, replica_groups=mesh['x'=4,'y'=8,'l'=2,'h'=4,'c'=2] {'h'}, dimensions={0}, use_global_device_ids=true | all-gather | bytes 1290240 | tf_op jit(solution)/shard_map/all_gather | solution.py:277
  229.6 2.1 collective-permute-start.8
  231.7 2.3 collective-permute-done.8.other_ref
  234.1 3.5 %shard_map.168 = bf16[1536,512]{1,0:T(8,128)(2,1)} custom-call(bf16[1344,384]{1,0:T(8,128)(2,1)S(1)} %all_gather.7.own_ref, bf16[1344,384]{1,0:T(8,128)(2,1)S(1)} %collective-permute-done.8.other_ref, bf16[384,512]{1,0:T(8,128)(2,1)S(1)} %get-tuple-element.33.down_own_ref, bf16[384,512]{1,0:T(8,128)(2,1)S(1)} %get-tuple-element.32.down_other_ref, ...), custom_call_target="tpu_custom_call" | custom-call | flops 100000000 | bytes 500000 | tf_op jit(solution)/shard_map/pallas_call | solution.py:182
  237.6 8.4 %all-to-all-start.5 = ((bf16[64,24,512]{2,1,0:T(8,128)(2,1)}), bf16[64,24,512]{2,1,0:T(8,128)(2,1)S(1)}, u32[]{:S(2)}, u32[]{:S(2)}) async-start(bf16[64,24,512]{2,1,0:T(8,128)(2,1)} %bitcast.39), calls=%async_computation.6 | async-start | bytes 3145728 | tf_op jit(solution)/shard_map/all_to_all | solution.py:38
  246.7 39.0 %all-to-all-done.5 = bf16[64,24,512]{2,1,0:T(8,128)(2,1)S(1)} async-done(((bf16[64,24,512]{2,1,0:T(8,128)(2,1)}), bf16[64,24,512]{2,1,0:T(8,128)(2,1)S(1)}, u32[]{:S(2)}, u32[]{:S(2)}) %all-to-all-start.5) | async-done | bytes 1572896 | tf_op jit(solution)/shard_map/all_to_all | solution.py:38
  (84 shorter events, 26.5 us)
Async XLA Ops:
  7.2 21.2 %copy-start = (bf16[128,512]{1,0:T(8,128)(2,1)S(1)}, bf16[128,512]{1,0:T(8,128)(2,1)}, u32[]{:S(2)}) copy-start(bf16[128,512]{1,0:T(8,128)(2,1)} %param.16) | copy-start | bytes 393220
  8.0 18.2 %collective-permute-start.2 = (bf16[128,256]{1,0:T(8,128)(2,1)S(1)}, bf16[128,256]{1,0:T(8,128)(2,1)S(1)}, u32[]{:S(2)}, u32[]{:S(2)}) collective-permute-start(bf16[128,256]{1,0:T(8,128)(2,1)S(1)} %pad_maximum_fusion.3), channel_id=1, source_target_pairs={{0,8},{8,16},{16,24},{24,32},{32,40},{40,48},{48,56},{56,64},{64,7... | collective-permute-start | bytes 196616 | tf_op jit(solution)/shard_map/ppermute | solution.py:43
  12.3 13.9 %collective-permute-start.1 = (bf16[128,256]{1,0:T(8,128)(2,1)S(1)}, bf16[128,256]{1,0:T(8,128)(2,1)S(1)}, u32[]{:S(2)}, u32[]{:S(2)}) collective-permute-start(bf16[128,256]{1,0:T(8,128)(2,1)S(1)} %pad_maximum_fusion.3), channel_id=1, source_target_pairs={{0,16},{8,24},{16,32},{24,40},{32,48},{40,56},{48,64},{56,72},{64,... | collective-permute-start | bytes 196616 | tf_op jit(solution)/shard_map/ppermute | solution.py:43
  15.8 12.5 %collective-permute-start = (bf16[128,256]{1,0:T(8,128)(2,1)S(1)}, bf16[128,256]{1,0:T(8,128)(2,1)S(1)}, u32[]{:S(2)}, u32[]{:S(2)}) collective-permute-start(bf16[128,256]{1,0:T(8,128)(2,1)S(1)} %pad_maximum_fusion.3), channel_id=1, source_target_pairs={{0,24},{8,32},{16,40},{24,48},{32,56},{40,64},{48,72},{56,80},{64,... | collective-permute-start | bytes 196616 | tf_op jit(solution)/shard_map/ppermute | solution.py:43
  19.4 7.4 %collective-permute-start.3 = (bf16[64,512]{1,0:T(8,128)(2,1)}, bf16[64,512]{1,0:T(8,128)(2,1)S(1)}, u32[]{:S(2)}, u32[]{:S(2)}) collective-permute-start(bf16[64,512]{1,0:T(8,128)(2,1)} %param.19), channel_id=1, source_target_pairs={{0,8},{8,0},{1,9},{9,1},{2,10},{10,2},{3,11},{11,3},{4,12},{12,4},... | collective-permute-start | bytes 196616 | tf_op jit(solution)/shard_map/ppermute | solution.py:34
  29.6 11.5 %copy-start.5 = (bf16[1,512,768]{2,1,0:T(8,128)(2,1)S(1)}, bf16[1,512,768]{2,1,0:T(8,128)(2,1)}, u32[]{:S(2)}) copy-start(bf16[1,512,768]{2,1,0:T(8,128)(2,1)} %param.23) | copy-start | bytes 2359300
  29.8 11.5 %copy-start.6 = (bf16[1,512,768]{2,1,0:T(8,128)(2,1)S(1)}, bf16[1,512,768]{2,1,0:T(8,128)(2,1)}, u32[]{:S(2)}) copy-start(bf16[1,512,768]{2,1,0:T(8,128)(2,1)} %param.22) | copy-start | bytes 2359300
  30.6 24.1 %all-to-all-start = ((bf16[4,128,512]{2,1,0:T(8,128)(2,1)}), bf16[4,128,512]{2,1,0:T(8,128)(2,1)}, u32[]{:S(2)}, u32[]{:S(2)}) async-start(bf16[4,128,512]{2,1,0:T(8,128)(2,1)} %broadcast_in_dim.170), calls=%async_computation | async-start | bytes 1048576 | tf_op jit(solution)/shard_map/all_to_all | solution.py:38
  40.4 43.4 %all-gather.2.cloned.1.call-start = ((), (), s32[]{:S(2)}) async-start(), calls=%async_computation.7 | async-start | bytes 1179648 | tf_op jit(solution)/shard_map/all_gather | solution.py:219
  42.4 17.3 %collective-permute-start.4 = (bf16[512,768]{1,0:T(8,128)(2,1)}, bf16[512,768]{1,0:T(8,128)(2,1)S(1)}, u32[]{:S(2)}, u32[]{:S(2)}) collective-permute-start(bf16[512,768]{1,0:T(8,128)(2,1)} %pad_maximum_fusion.1), channel_id=1, source_target_pairs={{0,1},{1,0},{2,3},{3,2},{4,5},{5,4},{6,7},{7,6},{8,9},{9,8},{10,11... | collective-permute-start | bytes 2359304 | tf_op jit(solution)/shard_map/ppermute | solution.py:34
  44.4 15.4 %collective-permute-start.5 = (f32[1,512]{1,0:T(1,128)S(1)}, f32[1,512]{1,0:T(1,128)S(1)}, u32[]{:S(2)}, u32[]{:S(2)}) collective-permute-start(f32[1,512]{1,0:T(1,128)S(1)} %bitcast.108), channel_id=1, source_target_pairs={{0,1},{1,0},{2,3},{3,2},{4,5},{5,4},{6,7},{7,6},{8,9},{9,8},{10,11... | collective-permute-start | bytes 6152 | tf_op jit(solution)/shard_map/ppermute | solution.py:34
  54.8 11.4 %all-to-all-start.1 = ((bf16[4,128,512]{2,1,0:T(8,128)(2,1)}), bf16[4,128,512]{2,1,0:T(8,128)(2,1)S(1)}, u32[]{:S(2)}, u32[]{:S(2)}) async-start(bf16[4,128,512]{2,1,0:T(8,128)(2,1)} %all-to-all-done), calls=%async_computation.1 | async-start | bytes 1048576 | tf_op jit(solution)/shard_map/all_to_all | solution.py:38
  66.2 3.8 %collective-permute-start.6 = (bf16[512,512]{1,0:T(8,128)(2,1)S(1)}, bf16[512,512]{1,0:T(8,128)(2,1)S(1)}, u32[]{:S(2)}, u32[]{:S(2)}) collective-permute-start(bf16[512,512]{1,0:T(8,128)(2,1)S(1)} %bitcast.110), channel_id=1, source_target_pairs={{0,1},{1,0},{2,3},{3,2},{4,5},{5,4},{6,7},{7,6},{8,9},{9,8},{10,11... | collective-permute-start | bytes 1572872 | tf_op jit(solution)/shard_map/ppermute | solution.py:34
  86.6 11.6 %copy-start.8 = (bf16[128,512]{1,0:T(8,128)(2,1)S(1)}, bf16[128,512]{1,0:T(8,128)(2,1)}, u32[]{:S(2)}) copy-start(bf16[128,512]{1,0:T(8,128)(2,1)} %param.20) | copy-start | bytes 393220
  86.6 11.6 %all-to-all-start.2 = ((bf16[4,128,512]{2,1,0:T(8,128)(2,1)}), bf16[4,128,512]{2,1,0:T(8,128)(2,1)S(1)}, u32[]{:S(2)}, u32[]{:S(2)}) async-start(bf16[4,128,512]{2,1,0:T(8,128)(2,1)} %bitcast.16), calls=%async_computation.2 | async-start | bytes 1048576 | tf_op jit(solution)/shard_map/all_to_all | solution.py:38
  99.3 48.3 %copy-start.2 = (bf16[168,192]{1,0:T(8,128)(2,1)S(1)}, bf16[168,192]{1,0:T(8,128)(2,1)}, u32[]{:S(2)}) copy-start(bf16[168,192]{1,0:T(8,128)(2,1)} %constant.89.clone.pick_ref) | copy-start | bytes 193540
  141.1 5.3 %collective-permute-start.7 = (bf16[1536,512]{1,0:T(8,128)(2,1)S(1)}, bf16[1536,512]{1,0:T(8,128)(2,1)S(1)}, u32[]{:S(2)}, u32[]{:S(2)}) collective-permute-start(bf16[1536,512]{1,0:T(8,128)(2,1)S(1)} %bitcast.106), channel_id=1, source_target_pairs={{0,1},{1,0},{2,3},{3,2},{4,5},{5,4},{6,7},{7,6},{8,9},{9,8},{10,11... | collective-permute-start | bytes 4718600 | tf_op jit(solution)/shard_map/ppermute | solution.py:34
  154.9 38.5 %all-to-all-start.4 = ((bf16[4,352,384]{2,1,0:T(8,128)(2,1)}), bf16[4,352,384]{2,1,0:T(8,128)(2,1)S(1)}, u32[]{:S(2)}, u32[]{:S(2)}) async-start(bf16[4,352,384]{2,1,0:T(8,128)(2,1)} %get-tuple-element.31), calls=%async_computation.5 | async-start | bytes 2162688 | tf_op jit(solution)/shard_map/all_to_all | solution.py:38
  161.4 44.9 %reduce-scatter.2.cloned.1.call-start = ((), (), s32[]{:S(2)}) async-start(), calls=%async_computation.8 | async-start | bytes 1290240 | tf_op jit(solution)/shard_map/reduce_scatter | solution.py:270
  193.5 38.1 %copy-start.7 = (bf16[1,768,512]{2,1,0:T(8,128)(2,1)S(1)}, bf16[1,768,512]{2,1,0:T(8,128)(2,1)}, u32[]{:S(2)}) copy-start(bf16[1,768,512]{2,1,0:T(8,128)(2,1)} %param.24) | copy-start | bytes 2359300
  207.4 26.6 %copy-start.1 = (bf16[192,168]{1,0:T(8,128)(2,1)S(1)}, bf16[192,168]{1,0:T(8,128)(2,1)}, u32[]{:S(2)}) copy-start(bf16[192,168]{1,0:T(8,128)(2,1)} %constant.90.clone.place_ref) | copy-start | bytes 193540
  229.6 4.5 %collective-permute-start.8 = (bf16[1344,384]{1,0:T(8,128)(2,1)S(1)}, bf16[1344,384]{1,0:T(8,128)(2,1)S(1)}, u32[]{:S(2)}, u32[]{:S(2)}) collective-permute-start(bf16[1344,384]{1,0:T(8,128)(2,1)S(1)} %all_gather.7.own_ref), channel_id=1, source_target_pairs={{0,1},{1,0},{2,3},{3,2},{4,5},{5,4},{6,7},{7,6},{8,9},{9,8},{10,11... | collective-permute-start | bytes 3096584 | tf_op jit(solution)/shard_map/ppermute | solution.py:34
  237.6 8.4 %copy-start.10 = (bf16[128,8]{0,1:T(8,128)(2,1)S(1)}, bf16[128,8]{0,1:T(8,128)(2,1)}, u32[]{:S(2)}) copy-start(bf16[128,8]{0,1:T(8,128)(2,1)} %param.26) | copy-start | bytes 6148
  237.6 48.0 %all-to-all-start.5 = ((bf16[64,24,512]{2,1,0:T(8,128)(2,1)}), bf16[64,24,512]{2,1,0:T(8,128)(2,1)S(1)}, u32[]{:S(2)}, u32[]{:S(2)}) async-start(bf16[64,24,512]{2,1,0:T(8,128)(2,1)} %bitcast.39), calls=%async_computation.6 | async-start | bytes 3145728 | tf_op jit(solution)/shard_map/all_to_all | solution.py:38
  (4 other events, 11.3 us)
Sparse Core Ops, SparseCore 0:
  43.9 39.8 all-gather.1
  165.0 41.1 reduce-scatter.1

commit v6 on v5

--- a/solution.py
+++ b/solution.py
@@ -21,6 +21,7 @@
 SENT = N_CTX * GROUP
 ROWS = N_CTX * SLOTS
 SHARE = ROWS // NH
+LANES = 384
 PACK = 8 * SLOTS
 PACK_SENT = 8 * GROUP
 SLICE = D // (NH * NC)
@@ -108,11 +109,11 @@
 
 
 def products_kernel(
-    own_ref, other_ref, w_own_ref, w_other_ref, inv_own_ref, inv_other_ref, pick_ref, gate_ref, up_ref
+    own_ref, other_ref, w_own_ref, w_other_ref, inv_own_ref, inv_other_ref, pick_ref, part_ref, total_ref
 ):
-    half = FF // 2
     pick = pick_ref[...]
     ones = jnp.ones((8, SLICE), bf16)
+    blank = jnp.zeros((LANES - SHARE, SLICE), bf16)
 
     def packed(ref, h):
         first, second = (
@@ -126,37 +127,29 @@
         return jnp.concatenate([first, second], axis=0)
 
     def squares(rows, inverse_ref):
-        weighted = jnp.concatenate(
-            [rows * rows * inverse_ref[...], jnp.zeros((half - SHARE, SLICE), f32)], axis=0
-        )
-        high = weighted.astype(bf16)
-        low = (weighted - high.astype(f32)).astype(bf16)
-        across = (((1,), (1,)), ((), ()))
-        return lax.dot_general(ones, high, across, preferred_element_type=f32) + lax.dot_general(
-            ones, low, across, preferred_element_type=f32
-        )
-
-    row = lax.broadcasted_iota(jnp.int32, (16, half), 0)
+        weighted = (rows * rows * inverse_ref[...]).astype(bf16)
+        return lax.dot_general(
+            ones,
+            jnp.concatenate([weighted, blank], axis=0),
+            (((1,), (1,)), ((), ())),
+            preferred_element_type=f32,
+        )
+
     for h in range(NH):
         own, other = packed(own_ref, h), packed(other_ref, h)
         part = jnp.dot(own.astype(bf16), w_own_ref[...], preferred_element_type=f32) + jnp.dot(
             other.astype(bf16), w_other_ref[...], preferred_element_type=f32
         )
-        gate_ref[h] = part[:, :half].astype(bf16)
-        up_ref[h, :SHARE] = part[:, half:].astype(bf16)
-        total = (squares(own, inv_own_ref) + squares(other, inv_other_ref))[:1]
-        high = total.astype(bf16).astype(f32)
-        tile = jnp.where(row == 0, high, jnp.where(row == 1, total - high, 0.0))
-        up_ref[h, SHARE:] = tile.astype(bf16)
+        part_ref[h] = part.astype(bf16)
+        total_ref[h] = squares(own, inv_own_ref) + squares(other, inv_other_ref)
 
 
 def products(own, other, w_own, w_other, inv_own, inv_other):
-    half = FF // 2
     return pl.pallas_call(
         products_kernel,
         out_shape=(
-            jax.ShapeDtypeStruct((NH, SHARE, half), bf16),
-            jax.ShapeDtypeStruct((NH, SHARE + 16, half), bf16),
+            jax.ShapeDtypeStruct((NH, SHARE, FF), bf16),
+            jax.ShapeDtypeStruct((NH, 8, LANES), f32),
         ),
         compiler_params=pltpu.CompilerParams(vmem_limit_bytes=48 * 1024 * 1024),
         cost_estimate=pl.CostEstimate(flops=100_000_000, bytes_accessed=500_000, transcendentals=0),
@@ -219,12 +212,13 @@
     quarter = lax.all_gather(strips, "y", axis=0, tiled=True)
 
     attended = attention(queries, key_rows, value_rows)
-    attended, w_gate, w_up, norm_gain, pred_ids = lax.optimization_barrier(
-        (attended, w_gate, w_up, norm_gain, pred_ids)
+    heads = lax.all_gather(attended, "h", axis=0, tiled=True).reshape(NH, tokens, SLICE)
+    heads, w_gate, w_up, norm_gain, pred_ids, fix_pair = lax.optimization_barrier(
+        (heads, w_gate, w_up, norm_gain, pred_ids, fix_pair)
     )
 
     ids, rank = slots_of(pred_ids, fix_pair, fix_expert, fix_count)
-    slots, gates = (ids * GROUP + rank).T, route_gates.astype(f32).T
+    slots = (ids * GROUP + rank).T
 
     def columns(which):
         return jnp.concatenate(
@@ -236,16 +230,14 @@
         )
 
     gate_up, other_gate_up = columns(core), swap(columns(1 - core), "c")
-    down = lax.dynamic_slice_in_dim(w_down[0], core * half, half, 0)
-    other_down = lax.dynamic_slice_in_dim(w_down[0], (1 - core) * half, half, 0)
     gain = norm_gain[None, :]
     inverse = 1.0 / (gain * gain)
     other_inverse = swap(inverse, "c")
 
-    copies = jnp.broadcast_to(attended[None], (NH, *attended.shape))
-    heads = exchange(exchange(copies, "h"), "x").reshape(NX * tokens, SLICE)
-    heads, gate_up, other_gate_up, inverse, other_inverse, slots = lax.optimization_barrier(
-        (heads, gate_up, other_gate_up, inverse, other_inverse, slots)
+    heads = exchange(heads, "x").reshape(NX * tokens, SLICE)
+    picks = spread(slots, jnp.ones_like(slots))
+    heads, gate_up, other_gate_up, inverse, other_inverse, picks = lax.optimization_barrier(
+        (heads, gate_up, other_gate_up, inverse, other_inverse, picks)
     )
     other_heads = swap(heads, "c")
     partial = jnp.dot(
@@ -261,24 +253,32 @@
     stream = residual.astype(f32) + jnp.sum(terms.astype(f32), axis=0)
 
     scaled = (stream * gain).astype(bf16)
-    picks = spread(slots, jnp.ones_like(gates))
     outgoing = jnp.dot(picks, scaled, preferred_element_type=f32).astype(bf16)
     incoming = exchange(outgoing.reshape(N_CTX, GROUP, SLICE), CTX).reshape(SENT, SLICE)
-    gate_part, up_part = products(
+    part, squares = products(
         incoming, swap(incoming, "c"), gate_up, other_gate_up, inverse, other_inverse
     )
-    gate_sum = lax.psum_scatter(
-        gate_part.reshape(ROWS, half), "h", scatter_dimension=0, tiled=True
-    ).astype(f32)
-    up_sum = jnp.sum(exchange(up_part, "h").astype(f32), axis=0)
-    total = jnp.sum(up_sum[SHARE:], axis=0)[:SHARE]
+    squares, slots, route_gates, w_down, stream = lax.optimization_barrier(
+        (squares, slots, route_gates, w_down, stream)
+    )
+    stream_out = stream.astype(bf16)
+    combine = spread(slots, route_gates.astype(f32).T)
+    down = lax.dynamic_slice_in_dim(w_down[0], core * half, half, 0)
+    other_down = lax.dynamic_slice_in_dim(w_down[0], (1 - core) * half, half, 0)
+    totals = lax.psum(squares[:, 0], "h")
+    total = lax.dynamic_index_in_dim(totals, lax.axis_index("h"), 0, keepdims=False)[:SHARE]
     scale = lax.rsqrt(total / D + epsilon)[:, None]
-    hidden = (jax.nn.silu(gate_sum * scale) * (up_sum[:SHARE] * scale)).astype(bf16)
+    sums = lax.psum_scatter(part.reshape(ROWS, FF), "h", scatter_dimension=0, tiled=True)
+    sums, scale, combine, down, other_down, stream_out = lax.optimization_barrier(
+        (sums, scale, combine, down, other_down, stream_out)
+    )
+    sums = sums.astype(f32) * scale
+    hidden = (jax.nn.silu(sums[:, :half]) * sums[:, half:]).astype(bf16)
     all_hidden = lax.all_gather(hidden, "h", axis=0, tiled=True)
     results = expert_results(all_hidden, swap(all_hidden, "c"), down, other_down)
     returned = exchange(results.reshape(N_CTX, GROUP, SLICE), CTX).reshape(SENT, SLICE)
-    expert_out = jnp.einsum("rt,rd->td", spread(slots, gates), returned, preferred_element_type=f32)
-    return stream.astype(bf16), expert_out.astype(bf16)
+    expert_out = jnp.einsum("rt,rd->td", combine, returned, preferred_element_type=f32)
+    return stream_out, expert_out.astype(bf16)
 
 
 def solution(mesh):

time: 295 us -> 278 us (0.942)
  blocking collectives: 63.9 us -> 162 us
  waiting for transfers between devices: 127 us -> 46.5 us
  starting transfers between devices: 60.2 us -> 31 us
  Pallas kernels: 10.8 us -> 7.55 us
    all_to_all x5 -> x1, waiting for transfers between devices: 91 us -> 0.01 us  [exchange(): return lax.all_to_all(blocks, axes, split_axis=0, concat_axis=0, tiled=True)]
    all_to_all x1 -> x3, blocking collectives: 41.8 us -> 106 us  [exchange(): return lax.all_to_all(blocks, axes, split_axis=0, concat_axis=0, tiled=True)]
    all_to_all x5 -> x1, starting transfers between devices: 34.3 us -> 4.78 us  [exchange(): return lax.all_to_all(blocks, axes, split_axis=0, concat_axis=0, tiled=True)]
    all_gather x0 -> x1, blocking collectives: none -> 22.1 us  [body(): lax.all_gather(attended, 'h', axis=0, tiled=True).reshape(NH, tokens, SLICE)]
    reduce_scatter x1, waiting for transfers between devices: 12.7 us -> 33.9 us  [body(): lax.psum_scatter(part.reshape(ROWS, FF), 'h', scatter_dimension=0, tiled=...]
    all_gather x1, waiting for transfers between devices: 13.9 us -> 2.32 us  [body(): quarter = lax.all_gather(strips, 'y', axis=0, tiled=True)]
    psum x0 -> x1, blocking collectives: none -> 10.9 us  [body(): totals = lax.psum(squares[:, 0], 'h')]
  transfers between devices with their start and end apart: 16 -> 12, of which waited for: 11 -> 7; matrix products, arithmetic and copies ran while one was open for 2% -> 3% of each run, Pallas kernels for 0% -> 0%
where the time goes in v6:
time: 278 us; the launch traced here: 277 us
  blocking collectives  162 us (58%)
  waiting for transfers between devices  46.5 us (17%)
  starting transfers between devices  31 us (11%)
  between operations  15.3 us (6%)
  Pallas kernels  7.55 us (3%)
  other arithmetic  6.93 us (2%)
  matrix products  5.05 us (2%)
    all_to_all x3, blocking collectives, exchange(): return lax.all_to_all(blocks, axes, split_axis=0, concat_axis=0, tiled=True)  106 us
    reduce_scatter x1, waiting for transfers between devices, body(): lax.psum_scatter(part.reshape(ROWS, FF), 'h', scatter_dimension=0, tiled=...  33.9 us
    all_gather x1, blocking collectives, body(): all_hidden = lax.all_gather(hidden, 'h', axis=0, tiled=True)  22.8 us
    all_gather x1, blocking collectives, body(): lax.all_gather(attended, 'h', axis=0, tiled=True).reshape(NH, tokens, SLICE)  22.1 us
    ppermute x6, starting transfers between devices, swap(): return lax.ppermute(block, axis, [(0, 1), (1, 0)])  14.8 us
    ppermute x3, starting transfers between devices, from_behind(): return lax.ppermute(block, CTX, route)  11.4 us
    psum x1, blocking collectives, body(): totals = lax.psum(squares[:, 0], 'h')  10.9 us
    ppermute x6, waiting for transfers between devices, swap(): return lax.ppermute(block, axis, [(0, 1), (1, 0)])  10.2 us
  transfers between devices with their start and end apart: 12, of which 7 were waited for; matrix products, arithmetic and copies ran while one was open for 3% of the time, Pallas kernels for 0%

profile of v6, /device:TPU:2, one launch (start us, length us, event | category | flops | bytes accessed | tf_op | source)
XLA Modules:
  0.0 276.8 jit_solution(6582572477495619820)
XLA Ops:
  8.0 4.3 %collective-permute-start.2 = (bf16[128,256]{1,0:T(8,128)(2,1)S(1)}, bf16[128,256]{1,0:T(8,128)(2,1)S(1)}, u32[]{:S(2)}, u32[]{:S(2)}) collective-permute-start(bf16[128,256]{1,0:T(8,128)(2,1)S(1)} %pad_maximum_fusion.3), channel_id=1, source_target_pairs={{0,8},{8,16},{16,24},{24,32},{32,40},{40,48},{48,56},{56,64},{64,7... | collective-permute-start | bytes 196616 | tf_op jit(solution)/shard_map/ppermute | solution.py:44
  12.3 3.5 %collective-permute-start.1 = (bf16[128,256]{1,0:T(8,128)(2,1)S(1)}, bf16[128,256]{1,0:T(8,128)(2,1)S(1)}, u32[]{:S(2)}, u32[]{:S(2)}) collective-permute-start(bf16[128,256]{1,0:T(8,128)(2,1)S(1)} %pad_maximum_fusion.3), channel_id=1, source_target_pairs={{0,16},{8,24},{16,32},{24,40},{32,48},{40,56},{48,64},{56,72},{64,... | collective-permute-start | bytes 196616 | tf_op jit(solution)/shard_map/ppermute | solution.py:44
  15.8 3.6 %collective-permute-start = (bf16[128,256]{1,0:T(8,128)(2,1)S(1)}, bf16[128,256]{1,0:T(8,128)(2,1)S(1)}, u32[]{:S(2)}, u32[]{:S(2)}) collective-permute-start(bf16[128,256]{1,0:T(8,128)(2,1)S(1)} %pad_maximum_fusion.3), channel_id=1, source_target_pairs={{0,24},{8,32},{16,40},{24,48},{32,56},{40,64},{48,72},{56,80},{64,... | collective-permute-start | bytes 196616 | tf_op jit(solution)/shard_map/ppermute | solution.py:44
  19.4 4.3 %collective-permute-start.3 = (bf16[64,512]{1,0:T(8,128)(2,1)}, bf16[64,512]{1,0:T(8,128)(2,1)S(1)}, u32[]{:S(2)}, u32[]{:S(2)}) collective-permute-start(bf16[64,512]{1,0:T(8,128)(2,1)} %param.19), channel_id=1, source_target_pairs={{0,8},{8,0},{1,9},{9,1},{2,10},{10,2},{3,11},{11,3},{4,12},{12,4},... | collective-permute-start | bytes 196616 | tf_op jit(solution)/shard_map/ppermute | solution.py:35
  24.7 2.1 collective-permute-done.3
  29.9 22.1 %all_gather.9 = bf16[512,512]{1,0:T(8,128)(2,1)S(1)} all-gather(bf16[128,512]{1,0:T(8,128)(2,1)S(1)} %copy.52), channel_id=1, replica_groups=mesh['x'=4,'y'=8,'l'=2,'h'=4,'c'=2] {'h'}, dimensions={0}, use_global_device_ids=true | all-gather | bytes 655360 | tf_op jit(solution)/shard_map/all_gather | solution.py:215
  53.2 4.8 %all-to-all-start = ((bf16[4,128,512]{1,2,0:T(8,128)(2,1)}), bf16[4,128,512]{1,2,0:T(8,128)(2,1)S(1)}, u32[]{:S(2)}, u32[]{:S(2)}) async-start(bf16[4,128,512]{1,2,0:T(8,128)(2,1)} %copy.53), calls=%async_computation | async-start | bytes 1048576 | tf_op jit(solution)/shard_map/all_to_all | solution.py:39
  58.0 1.9 collective-permute-start.5
  61.4 2.3 collective-permute-start.4
  65.8 2.3 collective-permute-start.6
  69.6 2.3 all-gather.2.cloned.1.call-done
  71.9 1.6 fusion.9
  74.0 11.4 %all_to_all.20 = bf16[4,128,512]{2,1,0:T(8,128)(2,1)S(1)} all-to-all(bf16[4,128,512]{2,1,0:T(8,128)(2,1)S(1)} %bitcast.140), channel_id=1, replica_groups=mesh['x'=4,'y'=8,'l'=2,'h'=4,'c'=2] {'x'}, dimensions={0} | all-to-all | bytes 1048576 | tf_op jit(solution)/shard_map/all_to_all | solution.py:39
  86.0 44.3 %all_to_all.21 = bf16[64,24,512]{2,1,0:T(8,128)(2,1)S(1)} all-to-all(bf16[64,24,512]{2,1,0:T(8,128)(2,1)S(1)} %bitcast.136), channel_id=1, replica_groups=mesh['x'=4,'y'=8,'l'=2,'h'=4,'c'=2] {'x','y','l'}, dimensions={0} | all-to-all | bytes 3145728 | tf_op jit(solution)/shard_map/all_to_all | solution.py:39
  130.3 1.9 collective-permute-start.7
  132.3 3.4 %collective-permute-done.7.other_ref = bf16[1536,512]{1,0:T(8,128)(2,1)S(1)} collective-permute-done((bf16[1536,512]{1,0:T(8,128)(2,1)S(1)}, bf16[1536,512]{1,0:T(8,128)(2,1)S(1)}, u32[]{:S(2)}, u32[]{:S(2)}) %collective-permute-start.7) | collective-permute-done | bytes 1572896 | tf_op jit(solution)/shard_map/ppermute | solution.py:35
  135.6 5.2 %shard_map.167 = (bf16[4,336,768]{2,1,0:T(8,128)(2,1)}, f32[4,8,384]{2,1,0:T(8,128)S(1)}) custom-call(bf16[1536,512]{1,0:T(8,128)(2,1)S(1)} %bitcast.132, bf16[1536,512]{1,0:T(8,128)(2,1)S(1)} %collective-permute-done.7.other_ref, bf16[512,768]{1,0:T(8,128)(2,1)S(1)} %pad_maximum_fusion.w_own_ref, bf16[512,768]{1,0:T(8,128)(2,1)S(1)} %collective-permute-done.4.w_other_ref, ...), custom_call_target="tpu_custom_call" | custom-call | flops 100000000 | bytes 500000 | tf_op jit(solution)/shard_map/pallas_call | solution.py:148
  141.6 10.9 %psum.7 = f32[4,384]{1,0:T(4,128)S(1)} all-reduce(f32[4,384]{1,0:T(4,128)S(1)} %bitcast.143), channel_id=1, replica_groups=mesh['x'=4,'y'=8,'l'=2,'h'=4,'c'=2] {'h'}, use_global_device_ids=true, to_apply=%region_9.10 | all-reduce | flops 1536 | bytes 12288 | tf_op jit(solution)/shard_map/psum | solution.py:268
  153.4 33.9 %reduce-scatter.2.cloned.1.call-done = bf16[336,768]{1,0:T(8,128)(2,1)} async-done(((bf16[1344,768]{1,0:T(8,128)(2,1)}), bf16[336,768]{1,0:T(8,128)(2,1)}) %reduce-scatter.2.cloned.1.call-update) | async-done | bytes 516112 | tf_op jit(solution)/shard_map/reduce_scatter | solution.py:271
  188.7 22.8 %all_gather.11.own_ref = bf16[1344,384]{1,0:T(8,128)(2,1)S(1)} all-gather(bf16[336,384]{1,0:T(8,128)(2,1)S(1)} %fusion.13), channel_id=1, replica_groups=mesh['x'=4,'y'=8,'l'=2,'h'=4,'c'=2] {'h'}, dimensions={0}, use_global_device_ids=true | all-gather | bytes 1290240 | tf_op jit(solution)/shard_map/all_gather | solution.py:277
  211.5 2.1 collective-permute-start.8
  213.6 2.4 collective-permute-done.8.other_ref
  216.0 2.4 shard_map.168
  218.4 50.5 %all_to_all.22 = bf16[64,24,512]{2,1,0:T(8,128)(2,1)S(1)} all-to-all(bf16[64,24,512]{2,1,0:T(8,128)(2,1)S(1)} %bitcast.130), channel_id=1, replica_groups=mesh['x'=4,'y'=8,'l'=2,'h'=4,'c'=2] {'x','y','l'}, dimensions={0} | all-to-all | bytes 3145728 | tf_op jit(solution)/shard_map/all_to_all | solution.py:39
  (89 shorter events, 15.4 us)
Async XLA Ops:
  7.2 21.2 %copy-start = (bf16[128,512]{1,0:T(8,128)(2,1)S(1)}, bf16[128,512]{1,0:T(8,128)(2,1)}, u32[]{:S(2)}) copy-start(bf16[128,512]{1,0:T(8,128)(2,1)} %param.16) | copy-start | bytes 393220
  7.2 64.7 %all-gather.2.cloned.1.call-start = ((), (), s32[]{:S(2)}) async-start(), calls=%async_computation.5 | async-start | bytes 1179648 | tf_op jit(solution)/shard_map/all_gather | solution.py:212
  8.0 16.6 %collective-permute-start.2 = (bf16[128,256]{1,0:T(8,128)(2,1)S(1)}, bf16[128,256]{1,0:T(8,128)(2,1)S(1)}, u32[]{:S(2)}, u32[]{:S(2)}) collective-permute-start(bf16[128,256]{1,0:T(8,128)(2,1)S(1)} %pad_maximum_fusion.3), channel_id=1, source_target_pairs={{0,8},{8,16},{16,24},{24,32},{32,40},{40,48},{48,56},{56,64},{64,7... | collective-permute-start | bytes 196616 | tf_op jit(solution)/shard_map/ppermute | solution.py:44
  12.3 12.4 %collective-permute-start.1 = (bf16[128,256]{1,0:T(8,128)(2,1)S(1)}, bf16[128,256]{1,0:T(8,128)(2,1)S(1)}, u32[]{:S(2)}, u32[]{:S(2)}) collective-permute-start(bf16[128,256]{1,0:T(8,128)(2,1)S(1)} %pad_maximum_fusion.3), channel_id=1, source_target_pairs={{0,16},{8,24},{16,32},{24,40},{32,48},{40,56},{48,64},{56,72},{64,... | collective-permute-start | bytes 196616 | tf_op jit(solution)/shard_map/ppermute | solution.py:44
  15.8 12.5 %collective-permute-start = (bf16[128,256]{1,0:T(8,128)(2,1)S(1)}, bf16[128,256]{1,0:T(8,128)(2,1)S(1)}, u32[]{:S(2)}, u32[]{:S(2)}) collective-permute-start(bf16[128,256]{1,0:T(8,128)(2,1)S(1)} %pad_maximum_fusion.3), channel_id=1, source_target_pairs={{0,24},{8,32},{16,40},{24,48},{32,56},{40,64},{48,72},{56,80},{64,... | collective-permute-start | bytes 196616 | tf_op jit(solution)/shard_map/ppermute | solution.py:44
  19.4 7.4 %collective-permute-start.3 = (bf16[64,512]{1,0:T(8,128)(2,1)}, bf16[64,512]{1,0:T(8,128)(2,1)S(1)}, u32[]{:S(2)}, u32[]{:S(2)}) collective-permute-start(bf16[64,512]{1,0:T(8,128)(2,1)} %param.19), channel_id=1, source_target_pairs={{0,8},{8,0},{1,9},{9,1},{2,10},{10,2},{3,11},{11,3},{4,12},{12,4},... | collective-permute-start | bytes 196616 | tf_op jit(solution)/shard_map/ppermute | solution.py:35
  29.7 23.3 %copy-start.11 = (s32[1,32]{1,0:T(1,128)S(1)}, s32[1,32]{1,0:T(1,128)}, u32[]{:S(2)}) copy-start(s32[1,32]{1,0:T(1,128)} %param.27) | copy-start | bytes 388
  29.7 23.4 %copy-start.12 = (s32[1,32]{1,0:T(1,128)S(1)}, s32[1,32]{1,0:T(1,128)}, u32[]{:S(2)}) copy-start(s32[1,32]{1,0:T(1,128)} %param.28) | copy-start | bytes 388
  29.7 23.5 %copy-start.8 = (f32[512]{0:T(512)S(1)}, f32[512]{0:T(512)}, u32[]{:S(2)}) copy-start(f32[512]{0:T(512)} %param.21) | copy-start | bytes 6148
  29.7 30.2 %copy-start.9 = (s32[128,8]{0,1:T(8,128)S(1)}, s32[128,8]{0,1:T(8,128)}, u32[]{:S(2)}) copy-start(s32[128,8]{0,1:T(8,128)} %param.25) | copy-start | bytes 12292
  29.7 30.4 %copy-start.4 = (bf16[1,512,768]{2,1,0:T(8,128)(2,1)S(1)}, bf16[1,512,768]{2,1,0:T(8,128)(2,1)}, u32[]{:S(2)}) copy-start(bf16[1,512,768]{2,1,0:T(8,128)(2,1)} %param.22) | copy-start | bytes 2359300
  53.0 7.3 %copy-start.5 = (bf16[1,512,768]{2,1,0:T(8,128)(2,1)S(1)}, bf16[1,512,768]{2,1,0:T(8,128)(2,1)}, u32[]{:S(2)}) copy-start(bf16[1,512,768]{2,1,0:T(8,128)(2,1)} %param.23) | copy-start | bytes 2359300
  53.2 11.5 %all-to-all-start = ((bf16[4,128,512]{1,2,0:T(8,128)(2,1)}), bf16[4,128,512]{1,2,0:T(8,128)(2,1)S(1)}, u32[]{:S(2)}, u32[]{:S(2)}) async-start(bf16[4,128,512]{1,2,0:T(8,128)(2,1)} %copy.53), calls=%async_computation | async-start | bytes 1048576 | tf_op jit(solution)/shard_map/all_to_all | solution.py:39
  58.0 129.3 %reduce-scatter.2.cloned.1.call-start = ((), (), s32[]{:S(2)}) async-start(), calls=%async_computation.6 | async-start | bytes 2580480 | tf_op jit(solution)/shard_map/reduce_scatter | solution.py:271
  58.0 7.0 %collective-permute-start.5 = (f32[1,512]{1,0:T(1,128)S(1)}, f32[1,512]{1,0:T(1,128)S(1)}, u32[]{:S(2)}, u32[]{:S(2)}) collective-permute-start(f32[1,512]{1,0:T(1,128)S(1)} %bitcast.133), channel_id=1, source_target_pairs={{0,1},{1,0},{2,3},{3,2},{4,5},{5,4},{6,7},{7,6},{8,9},{9,8},{10,11... | collective-permute-start | bytes 6152 | tf_op jit(solution)/shard_map/ppermute | solution.py:35
  61.4 4.4 %collective-permute-start.4 = (bf16[512,768]{1,0:T(8,128)(2,1)}, bf16[512,768]{1,0:T(8,128)(2,1)S(1)}, u32[]{:S(2)}, u32[]{:S(2)}) collective-permute-start(bf16[512,768]{1,0:T(8,128)(2,1)} %pad_maximum_fusion.1), channel_id=1, source_target_pairs={{0,1},{1,0},{2,3},{3,2},{4,5},{5,4},{6,7},{7,6},{8,9},{9,8},{10,11... | collective-permute-start | bytes 2359304 | tf_op jit(solution)/shard_map/ppermute | solution.py:35
  65.8 3.8 %collective-permute-start.6 = (bf16[512,512]{1,0:T(8,128)(2,1)S(1)}, bf16[512,512]{1,0:T(8,128)(2,1)S(1)}, u32[]{:S(2)}, u32[]{:S(2)}) collective-permute-start(bf16[512,512]{1,0:T(8,128)(2,1)S(1)} %bitcast.138), channel_id=1, source_target_pairs={{0,1},{1,0},{2,3},{3,2},{4,5},{5,4},{6,7},{7,6},{8,9},{9,8},{10,11... | collective-permute-start | bytes 1572872 | tf_op jit(solution)/shard_map/ppermute | solution.py:35
  74.0 11.4 %copy-start.7 = (bf16[128,512]{1,0:T(8,128)(2,1)S(1)}, bf16[128,512]{1,0:T(8,128)(2,1)}, u32[]{:S(2)}) copy-start(bf16[128,512]{1,0:T(8,128)(2,1)} %param.20) | copy-start | bytes 393220
  86.0 49.6 %copy-start.2 = (bf16[168,192]{1,0:T(8,128)(2,1)S(1)}, bf16[168,192]{1,0:T(8,128)(2,1)}, u32[]{:S(2)}) copy-start(bf16[168,192]{1,0:T(8,128)(2,1)} %constant.94.clone.pick_ref) | copy-start | bytes 193540
  130.3 5.3 %collective-permute-start.7 = (bf16[1536,512]{1,0:T(8,128)(2,1)S(1)}, bf16[1536,512]{1,0:T(8,128)(2,1)S(1)}, u32[]{:S(2)}, u32[]{:S(2)}) collective-permute-start(bf16[1536,512]{1,0:T(8,128)(2,1)S(1)} %bitcast.131), channel_id=1, source_target_pairs={{0,1},{1,0},{2,3},{3,2},{4,5},{5,4},{6,7},{7,6},{8,9},{9,8},{10,11... | collective-permute-start | bytes 4718600 | tf_op jit(solution)/shard_map/ppermute | solution.py:35
  140.8 11.6 %copy-start.6 = (bf16[1,768,512]{2,1,0:T(8,128)(2,1)S(1)}, bf16[1,768,512]{2,1,0:T(8,128)(2,1)}, u32[]{:S(2)}) copy-start(bf16[1,768,512]{2,1,0:T(8,128)(2,1)} %param.24) | copy-start | bytes 2359300
  140.8 11.7 %copy-start.10 = (bf16[128,8]{0,1:T(8,128)(2,1)S(1)}, bf16[128,8]{0,1:T(8,128)(2,1)}, u32[]{:S(2)}) copy-start(bf16[128,8]{0,1:T(8,128)(2,1)} %param.26) | copy-start | bytes 6148
  188.6 27.5 %copy-start.1 = (bf16[192,168]{1,0:T(8,128)(2,1)S(1)}, bf16[192,168]{1,0:T(8,128)(2,1)}, u32[]{:S(2)}) copy-start(bf16[192,168]{1,0:T(8,128)(2,1)} %constant.95.clone.place_ref) | copy-start | bytes 193540
  211.5 4.5 %collective-permute-start.8 = (bf16[1344,384]{1,0:T(8,128)(2,1)S(1)}, bf16[1344,384]{1,0:T(8,128)(2,1)S(1)}, u32[]{:S(2)}, u32[]{:S(2)}) collective-permute-start(bf16[1344,384]{1,0:T(8,128)(2,1)S(1)} %all_gather.11.own_ref), channel_id=1, source_target_pairs={{0,1},{1,0},{2,3},{3,2},{4,5},{5,4},{6,7},{7,6},{8,9},{9,8},{10,11... | collective-permute-start | bytes 3096584 | tf_op jit(solution)/shard_map/ppermute | solution.py:35
  (1 other events, 1.6 us)
Sparse Core Ops, SparseCore 0:
  29.4 42.4 all-gather.1
  141.0 46.3 reduce-scatter.1

commit v7 on v6

--- a/solution.py
+++ b/solution.py
@@ -18,10 +18,12 @@
 GROUP = 24
 NX, NY, NL, NH, NC = 4, 8, 2, 4, 2
 N_CTX = NX * NY * NL
-SENT = N_CTX * GROUP
-ROWS = N_CTX * SLOTS
+GRID = NX * NY
+SENT = GRID * GROUP
+ROWS = GRID * SLOTS
 SHARE = ROWS // NH
-LANES = 384
+LANES = 256
+EXTRA = 8
 PACK = 8 * SLOTS
 PACK_SENT = 8 * GROUP
 SLICE = D // (NH * NC)
@@ -95,6 +97,12 @@
     return ids.astype(f32), rank
 
 
+def row_slots(table, side):
+    ids, rank, gates = table[:TOPK], table[TOPK : 2 * TOPK], table[2 * TOPK :]
+    column = jnp.floor(ids * 0.5)
+    return jnp.where(ids - 2.0 * column == side, column * GROUP + rank, -1.0), gates
+
+
 def spread(slots, values):
     row_ids = jnp.arange(SENT, dtype=f32)[:, None]
     total = jnp.zeros((SENT, slots.shape[1]), f32)
@@ -109,22 +117,12 @@
 
 
 def products_kernel(
-    own_ref, other_ref, w_own_ref, w_other_ref, inv_own_ref, inv_other_ref, pick_ref, part_ref, total_ref
+    own_ref, other_ref, w_own_ref, w_other_ref, inv_own_ref, inv_other_ref, pick_ref, part_ref
 ):
     pick = pick_ref[...]
     ones = jnp.ones((8, SLICE), bf16)
     blank = jnp.zeros((LANES - SHARE, SLICE), bf16)
-
-    def packed(ref, h):
-        first, second = (
-            jnp.dot(
-                pick,
-                ref[(2 * h + i) * PACK_SENT : (2 * h + i + 1) * PACK_SENT],
-                preferred_element_type=f32,
-            )
-            for i in range(2)
-        )
-        return jnp.concatenate([first, second], axis=0)
+    row = lax.broadcasted_iota(jnp.int32, (EXTRA, FF), 0)
 
     def squares(rows, inverse_ref):
         weighted = (rows * rows * inverse_ref[...]).astype(bf16)
@@ -136,21 +134,23 @@
         )
 
     for h in range(NH):
-        own, other = packed(own_ref, h), packed(other_ref, h)
+        taken = slice(h * PACK_SENT, (h + 1) * PACK_SENT)
+        own = jnp.dot(pick, own_ref[taken], preferred_element_type=f32)
+        other = jnp.dot(pick, other_ref[taken], preferred_element_type=f32)
         part = jnp.dot(own.astype(bf16), w_own_ref[...], preferred_element_type=f32) + jnp.dot(
             other.astype(bf16), w_other_ref[...], preferred_element_type=f32
         )
-        part_ref[h] = part.astype(bf16)
-        total_ref[h] = squares(own, inv_own_ref) + squares(other, inv_other_ref)
+        total = squares(own, inv_own_ref) + squares(other, inv_other_ref)
+        total = jnp.concatenate([total, jnp.zeros((8, FF - LANES), f32)], axis=1)
+        high = total.astype(bf16).astype(f32)
+        tail = jnp.where(row == 0, high, jnp.where(row == 1, total - high, 0.0))
+        part_ref[h] = jnp.concatenate([part, tail], axis=0).astype(bf16)
 
 
 def products(own, other, w_own, w_other, inv_own, inv_other):
     return pl.pallas_call(
         products_kernel,
-        out_shape=(
-            jax.ShapeDtypeStruct((NH, SHARE, FF), bf16),
-            jax.ShapeDtypeStruct((NH, 8, LANES), f32),
-        ),
+        out_shape=jax.ShapeDtypeStruct((NH, SHARE + EXTRA, FF), bf16),
         compiler_params=pltpu.CompilerParams(vmem_limit_bytes=48 * 1024 * 1024),
         cost_estimate=pl.CostEstimate(flops=100_000_000, bytes_accessed=500_000, transcendentals=0),
     )(own, other, w_own, w_other, inv_own, inv_other, jnp.asarray(packing(), bf16))
@@ -158,14 +158,14 @@
 
 def results_kernel(own_ref, other_ref, down_own_ref, down_other_ref, place_ref, out_ref):
     place = place_ref[...]
-    for h in range(NH):
-        rows = slice(h * SHARE, (h + 1) * SHARE)
+    for i in range(NH // 2):
+        rows = slice(2 * i * SHARE, 2 * (i + 1) * SHARE)
         part = jnp.dot(own_ref[rows], down_own_ref[...], preferred_element_type=f32) + jnp.dot(
             other_ref[rows], down_other_ref[...], preferred_element_type=f32
         )
-        for i in range(2):
-            rows = part[i * PACK : (i + 1) * PACK].astype(bf16)
-            start = (2 * h + i) * PACK_SENT
+        for j in range(2):
+            rows = part[j * PACK : (j + 1) * PACK].astype(bf16)
+            start = (2 * i + j) * PACK_SENT
             out_ref[start : start + PACK_SENT] = jnp.dot(
                 place, rows, preferred_element_type=f32
             ).astype(bf16)
@@ -213,32 +213,7 @@
 
     attended = attention(queries, key_rows, value_rows)
     heads = lax.all_gather(attended, "h", axis=0, tiled=True).reshape(NH, tokens, SLICE)
-    heads, w_gate, w_up, norm_gain, pred_ids, fix_pair = lax.optimization_barrier(
-        (heads, w_gate, w_up, norm_gain, pred_ids, fix_pair)
-    )
-
-    ids, rank = slots_of(pred_ids, fix_pair, fix_expert, fix_count)
-    slots = (ids * GROUP + rank).T
-
-    def columns(which):
-        return jnp.concatenate(
-            [
-                lax.dynamic_slice_in_dim(w_gate[0], which * half, half, 1),
-                lax.dynamic_slice_in_dim(w_up[0], which * half, half, 1),
-            ],
-            axis=1,
-        )
-
-    gate_up, other_gate_up = columns(core), swap(columns(1 - core), "c")
-    gain = norm_gain[None, :]
-    inverse = 1.0 / (gain * gain)
-    other_inverse = swap(inverse, "c")
-
     heads = exchange(heads, "x").reshape(NX * tokens, SLICE)
-    picks = spread(slots, jnp.ones_like(slots))
-    heads, gate_up, other_gate_up, inverse, other_inverse, picks = lax.optimization_barrier(
-        (heads, gate_up, other_gate_up, inverse, other_inverse, picks)
-    )
     other_heads = swap(heads, "c")
     partial = jnp.dot(
         heads,
@@ -249,36 +224,82 @@
         lax.dynamic_slice_in_dim(quarter, (1 - core) * SLICE, SLICE, 0),
         preferred_element_type=f32,
     )
-    terms = exchange(partial.astype(bf16).reshape(NX, tokens, SLICE), "x")
-    stream = residual.astype(f32) + jnp.sum(terms.astype(f32), axis=0)
-
-    scaled = (stream * gain).astype(bf16)
-    outgoing = jnp.dot(picks, scaled, preferred_element_type=f32).astype(bf16)
-    incoming = exchange(outgoing.reshape(N_CTX, GROUP, SLICE), CTX).reshape(SENT, SLICE)
-    part, squares = products(
-        incoming, swap(incoming, "c"), gate_up, other_gate_up, inverse, other_inverse
-    )
-    squares, slots, route_gates, w_down, stream = lax.optimization_barrier(
-        (squares, slots, route_gates, w_down, stream)
-    )
-    stream_out = stream.astype(bf16)
-    combine = spread(slots, route_gates.astype(f32).T)
+    partial, pred_ids, fix_pair, w_gate, w_up, norm_gain = lax.optimization_barrier(
+        (partial.astype(bf16), pred_ids, fix_pair, w_gate, w_up, norm_gain)
+    )
+
+    ids, rank = slots_of(pred_ids, fix_pair, fix_expert, fix_count)
+    table = jnp.concatenate([ids, rank, route_gates.astype(f32)], axis=1)
+    slots, gates = row_slots(table.T, side.astype(f32))
+    pick = spread(slots, jnp.ones_like(slots))
+
+    def columns(which):
+        return jnp.concatenate(
+            [
+                lax.dynamic_slice_in_dim(w_gate[0], which * half, half, 1),
+                lax.dynamic_slice_in_dim(w_up[0], which * half, half, 1),
+            ],
+            axis=1,
+        )
+
+    gate_up, other_gate_up = columns(core), swap(columns(1 - core), "c")
     down = lax.dynamic_slice_in_dim(w_down[0], core * half, half, 0)
     other_down = lax.dynamic_slice_in_dim(w_down[0], (1 - core) * half, half, 0)
-    totals = lax.psum(squares[:, 0], "h")
-    total = lax.dynamic_index_in_dim(totals, lax.axis_index("h"), 0, keepdims=False)[:SHARE]
-    scale = lax.rsqrt(total / D + epsilon)[:, None]
-    sums = lax.psum_scatter(part.reshape(ROWS, FF), "h", scatter_dimension=0, tiled=True)
-    sums, scale, combine, down, other_down, stream_out = lax.optimization_barrier(
-        (sums, scale, combine, down, other_down, stream_out)
-    )
-    sums = sums.astype(f32) * scale
-    hidden = (jax.nn.silu(sums[:, :half]) * sums[:, half:]).astype(bf16)
-    all_hidden = lax.all_gather(hidden, "h", axis=0, tiled=True)
-    results = expert_results(all_hidden, swap(all_hidden, "c"), down, other_down)
-    returned = exchange(results.reshape(N_CTX, GROUP, SLICE), CTX).reshape(SENT, SLICE)
-    expert_out = jnp.einsum("rt,rd->td", combine, returned, preferred_element_type=f32)
-    return stream_out, expert_out.astype(bf16)
+    gain = norm_gain[None, :]
+    inverse = 1.0 / (gain * gain)
+    other_inverse = swap(inverse, "c")
+
+    terms = exchange(partial.reshape(NX, tokens, SLICE), "x")
+    other_slots, other_gates = row_slots(swap(table, "l").T, side.astype(f32))
+    other_pick = spread(other_slots, jnp.ones_like(other_slots))
+    terms, pick = lax.optimization_barrier((terms, pick))
+    stream = residual.astype(f32) + jnp.sum(terms.astype(f32), axis=0)
+
+    scaled = (stream * gain).astype(bf16)
+    beside = swap(scaled, "l")
+
+    def through(rows):
+        return exchange(rows.reshape(GRID, GROUP, SLICE), ("x", "y")).reshape(SENT, SLICE)
+
+    def sent(pick, rows):
+        return through(jnp.dot(pick, rows, preferred_element_type=f32).astype(bf16))
+
+    def share_products(rows):
+        return products(rows, swap(rows, "c"), gate_up, other_gate_up, inverse, other_inverse)
+
+    def reduced(part):
+        flat = part.reshape(NH * (SHARE + EXTRA), FF)
+        return lax.psum_scatter(flat, "h", scatter_dimension=0, tiled=True)
+
+    def gathered(sums):
+        sums = sums.astype(f32)
+        total = (sums[SHARE] + sums[SHARE + 1])[:SHARE]
+        sums = sums[:SHARE] * lax.rsqrt(total / D + epsilon)[:, None]
+        hidden = (jax.nn.silu(sums[:, :half]) * sums[:, half:]).astype(bf16)
+        return lax.all_gather(hidden, "h", axis=0, tiled=True)
+
+    def finished(hidden):
+        return expert_results(hidden, swap(hidden, "c"), down, other_down)
+
+    first = sent(pick, scaled)
+    first, beside, other_pick, gate_up, other_gate_up, inverse, other_inverse = (
+        lax.optimization_barrier(
+            (first, beside, other_pick, gate_up, other_gate_up, inverse, other_inverse)
+        )
+    )
+    first = share_products(first)
+    first, beside = lax.optimization_barrier((first, beside))
+    second = share_products(sent(other_pick, beside))
+    first, second = reduced(first), reduced(second)
+    first = through(finished(gathered(first)))
+    hidden = gathered(second)
+    combine = spread(other_slots, other_gates)
+    first, hidden, combine = lax.optimization_barrier((first, hidden, combine))
+    second = through(finished(hidden))
+    mixed = jnp.einsum("rt,rd->td", spread(slots, gates), first, preferred_element_type=f32)
+    other_mixed = jnp.einsum("rt,rd->td", combine, second, preferred_element_type=f32)
+    expert_out = mixed + swap(other_mixed.astype(bf16), "l").astype(f32)
+    return stream.astype(bf16), expert_out.astype(bf16)
 
 
 def solution(mesh):

time: 278 us -> 281 us (1.011)
  the two profiles are of different devices: /device:TPU:2 before, /device:TPU:8 now
where the time goes in v7:
time: 281 us; the launch traced here: 280 us
  blocking collectives  84.4 us (30%)
  starting transfers between devices  75.6 us (27%)
  waiting for transfers between devices  75.4 us (27%)
  between operations  15.1 us (5%)
  Pallas kernels  10.2 us (4%)
  matrix products  8.3 us (3%)
  other arithmetic  6.45 us (2%)
  local copies, waits for them, and re-layouts  4.14 us (1%)
    all_to_all x5, waiting for transfers between devices, exchange(): return lax.all_to_all(blocks, axes, split_axis=0, concat_axis=0, tiled=True)  40.3 us
    all_to_all x5, starting transfers between devices, exchange(): return lax.all_to_all(blocks, axes, split_axis=0, concat_axis=0, tiled=True)  34.3 us
    all_to_all x1, blocking collectives, exchange(): return lax.all_to_all(blocks, axes, split_axis=0, concat_axis=0, tiled=True)  31.6 us
    all_gather x2, blocking collectives, gathered(): return lax.all_gather(hidden, 'h', axis=0, tiled=True)  31.4 us
    ppermute x11, starting transfers between devices, swap(): return lax.ppermute(block, axis, [(0, 1), (1, 0)])  28.6 us
    all_gather x1, blocking collectives, body(): lax.all_gather(attended, 'h', axis=0, tiled=True).reshape(NH, tokens, SLICE)  21.5 us
    ppermute x11, waiting for transfers between devices, swap(): return lax.ppermute(block, axis, [(0, 1), (1, 0)])  17.1 us
    reduce_scatter x2, waiting for transfers between devices, reduced(): return lax.psum_scatter(flat, 'h', scatter_dimension=0, tiled=True)  14.7 us
  transfers between devices with their start and end apart: 22, of which 15 were waited for; matrix products, arithmetic and copies ran while one was open for 4% of the time, Pallas kernels for 2%

profile of v7, /device:TPU:8, one launch (start us, length us, event | category | flops | bytes accessed | tf_op | source)
XLA Modules:
  0.0 279.6 jit_solution(16768008394840532592)
XLA Ops:
  8.0 5.3 %collective-permute-start = (bf16[128,256]{1,0:T(8,128)(2,1)S(1)}, bf16[128,256]{1,0:T(8,128)(2,1)S(1)}, u32[]{:S(2)}, u32[]{:S(2)}) collective-permute-start(bf16[128,256]{1,0:T(8,128)(2,1)S(1)} %pad_maximum_fusion.3), channel_id=1, source_target_pairs={{0,24},{8,32},{16,40},{24,48},{32,56},{40,64},{48,72},{56,80},{64,... | collective-permute-start | bytes 196616 | tf_op jit(solution)/shard_map/ppermute | solution.py:46
  13.3 3.5 %collective-permute-start.1 = (bf16[128,256]{1,0:T(8,128)(2,1)S(1)}, bf16[128,256]{1,0:T(8,128)(2,1)S(1)}, u32[]{:S(2)}, u32[]{:S(2)}) collective-permute-start(bf16[128,256]{1,0:T(8,128)(2,1)S(1)} %pad_maximum_fusion.3), channel_id=1, source_target_pairs={{0,16},{8,24},{16,32},{24,40},{32,48},{40,56},{48,64},{56,72},{64,... | collective-permute-start | bytes 196616 | tf_op jit(solution)/shard_map/ppermute | solution.py:46
  16.8 3.8 %collective-permute-start.2 = (bf16[128,256]{1,0:T(8,128)(2,1)S(1)}, bf16[128,256]{1,0:T(8,128)(2,1)S(1)}, u32[]{:S(2)}, u32[]{:S(2)}) collective-permute-start(bf16[128,256]{1,0:T(8,128)(2,1)S(1)} %pad_maximum_fusion.3), channel_id=1, source_target_pairs={{0,8},{8,16},{16,24},{24,32},{32,40},{40,48},{48,56},{56,64},{64,7... | collective-permute-start | bytes 196616 | tf_op jit(solution)/shard_map/ppermute | solution.py:46
  20.6 4.3 %collective-permute-start.3 = (bf16[64,512]{1,0:T(8,128)(2,1)}, bf16[64,512]{1,0:T(8,128)(2,1)S(1)}, u32[]{:S(2)}, u32[]{:S(2)}) collective-permute-start(bf16[64,512]{1,0:T(8,128)(2,1)} %param.21), channel_id=1, source_target_pairs={{0,8},{8,0},{1,9},{9,1},{2,10},{10,2},{3,11},{11,3},{4,12},{12,4},... | collective-permute-start | bytes 196616 | tf_op jit(solution)/shard_map/ppermute | solution.py:37
  30.4 21.5 %all_gather.12 = bf16[512,512]{1,0:T(8,128)(2,1)S(1)} all-gather(bf16[128,512]{1,0:T(8,128)(2,1)S(1)} %copy.47), channel_id=1, replica_groups=mesh['x'=4,'y'=8,'l'=2,'h'=4,'c'=2] {'h'}, dimensions={0}, use_global_device_ids=true | all-gather | bytes 655360 | tf_op jit(solution)/shard_map/all_gather | solution.py:215
  52.9 4.4 %all-to-all-start = ((bf16[4,128,512]{1,2,0:T(8,128)(2,1)}), bf16[4,128,512]{1,2,0:T(8,128)(2,1)S(1)}, u32[]{:S(2)}, u32[]{:S(2)}) async-start(bf16[4,128,512]{1,2,0:T(8,128)(2,1)} %copy.48), calls=%async_computation | async-start | bytes 1048576 | tf_op jit(solution)/shard_map/all_to_all | solution.py:41
  58.0 7.4 %all-to-all-done = bf16[4,128,512]{1,2,0:T(8,128)(2,1)S(1)} async-done(((bf16[4,128,512]{1,2,0:T(8,128)(2,1)}), bf16[4,128,512]{1,2,0:T(8,128)(2,1)S(1)}, u32[]{:S(2)}, u32[]{:S(2)}) %all-to-all-start) | async-done | bytes 524320 | tf_op jit(solution)/shard_map/all_to_all | solution.py:41
  73.6 4.3 %all-to-all-start.1 = ((bf16[4,128,512]{2,1,0:T(8,128)(2,1)}), bf16[4,128,512]{2,1,0:T(8,128)(2,1)S(1)}, u32[]{:S(2)}, u32[]{:S(2)}) async-start(bf16[4,128,512]{2,1,0:T(8,128)(2,1)} %bitcast.8), calls=%async_computation.1 | async-start | bytes 1048576 | tf_op jit(solution)/shard_map/all_to_all | solution.py:41
  78.4 7.5 %all-to-all-done.1 = bf16[4,128,512]{2,1,0:T(8,128)(2,1)S(1)} async-done(((bf16[4,128,512]{2,1,0:T(8,128)(2,1)}), bf16[4,128,512]{2,1,0:T(8,128)(2,1)S(1)}, u32[]{:S(2)}, u32[]{:S(2)}) %all-to-all-start.1) | async-done | bytes 524320 | tf_op jit(solution)/shard_map/all_to_all | solution.py:41
  88.0 5.9 %all-to-all-start.2 = ((bf16[32,24,512]{2,1,0:T(8,128)(2,1)}), bf16[32,24,512]{2,1,0:T(8,128)(2,1)S(1)}, u32[]{:S(2)}, u32[]{:S(2)}) async-start(bf16[32,24,512]{2,1,0:T(8,128)(2,1)} %bitcast.29), calls=%async_computation.2 | async-start | bytes 1572864 | tf_op jit(solution)/shard_map/all_to_all | solution.py:41
  96.1 3.6 %collective-permute-start.6 = (f32[128,24]{0,1:T(8,128)S(1)}, f32[128,24]{0,1:T(8,128)S(1)}, u32[]{:S(2)}, u32[]{:S(2)}) collective-permute-start(f32[128,24]{0,1:T(8,128)S(1)} %get-tuple-element.84), channel_id=1, source_target_pairs={{0,8},{8,0},{1,9},{9,1},{2,10},{10,2},{3,11},{11,3},{4,12},{12,4},... | collective-permute-start | bytes 36872 | tf_op jit(solution)/shard_map/ppermute | solution.py:37
  106.0 3.6 %collective-permute-done.5 = bf16[128,512]{1,0:T(8,128)(2,1)S(1)} collective-permute-done((bf16[128,512]{1,0:T(8,128)(2,1)S(1)}, bf16[128,512]{1,0:T(8,128)(2,1)S(1)}, u32[]{:S(2)}, u32[]{:S(2)}) %collective-permute-start.5) | collective-permute-done | bytes 131104 | tf_op jit(solution)/shard_map/ppermute | solution.py:37
  116.0 3.4 %shard_map.185 = bf16[4,176,768]{2,1,0:T(8,128)(2,1)} custom-call(bf16[768,512]{1,0:T(8,128)(2,1)S(1)} %bitcast.153, bf16[768,512]{1,0:T(8,128)(2,1)S(1)} %collective-permute-done.9.other_ref, bf16[512,768]{1,0:T(8,128)(2,1)S(1)} %pad_maximum_fusion.w_own_ref, bf16[512,768]{1,0:T(8,128)(2,1)S(1)} %collective-permute-done.7.w_other_ref, ...), custom_call_target="tpu_custom_call" | custom-call | flops 100000000 | bytes 500000 | tf_op jit(solution)/shard_map/pallas_call | solution.py:151
  120.6 7.6 %all-to-all-start.4 = ((bf16[32,24,512]{2,1,0:T(8,128)(2,1)}), bf16[32,24,512]{2,1,0:T(8,128)(2,1)S(1)}, u32[]{:S(2)}, u32[]{:S(2)}) async-start(bf16[32,24,512]{2,1,0:T(8,128)(2,1)} %bitcast.51), calls=%async_computation.5 | async-start | bytes 1572864 | tf_op jit(solution)/shard_map/all_to_all | solution.py:41
  129.0 22.5 %all-to-all-done.4 = bf16[32,24,512]{2,1,0:T(8,128)(2,1)S(1)} async-done(((bf16[32,24,512]{2,1,0:T(8,128)(2,1)}), bf16[32,24,512]{2,1,0:T(8,128)(2,1)S(1)}, u32[]{:S(2)}, u32[]{:S(2)}) %all-to-all-start.4) | async-done | bytes 786464 | tf_op jit(solution)/shard_map/all_to_all | solution.py:41
  155.7 3.4 %shard_map.187 = bf16[4,176,768]{2,1,0:T(8,128)(2,1)} custom-call(bf16[768,512]{1,0:T(8,128)(2,1)S(1)} %bitcast.155, bf16[768,512]{1,0:T(8,128)(2,1)S(1)} %collective-permute-done.11.other_ref, bf16[512,768]{1,0:T(8,128)(2,1)S(1)} %pad_maximum_fusion.w_own_ref, bf16[512,768]{1,0:T(8,128)(2,1)S(1)} %collective-permute-done.7.w_other_ref, ...), custom_call_target="tpu_custom_call" | custom-call | flops 100000000 | bytes 500000 | tf_op jit(solution)/shard_map/pallas_call | solution.py:151
  159.1 10.4 %reduce-scatter.3.cloned.1.call-done = bf16[176,768]{1,0:T(8,128)(2,1)} async-done(((bf16[704,768]{1,0:T(8,128)(2,1)}), bf16[176,768]{1,0:T(8,128)(2,1)}) %reduce-scatter.3.cloned.1.call-update) | async-done | bytes 270352 | tf_op jit(solution)/shard_map/reduce_scatter | solution.py:272
  171.5 15.1 %all_gather.14.own_ref = bf16[672,384]{1,0:T(8,128)(2,1)S(1)} all-gather(bf16[168,384]{1,0:T(8,128)(2,1)S(1)} %fusion.14), channel_id=1, replica_groups=mesh['x'=4,'y'=8,'l'=2,'h'=4,'c'=2] {'h'}, dimensions={0}, use_global_device_ids=true | all-gather | bytes 645120 | tf_op jit(solution)/shard_map/all_gather | solution.py:279
  192.6 12.1 %all-to-all-start.3 = ((bf16[32,24,512]{2,1,0:T(8,128)(2,1)}), bf16[32,24,512]{2,1,0:T(8,128)(2,1)S(1)}, u32[]{:S(2)}, u32[]{:S(2)}) async-start(bf16[32,24,512]{2,1,0:T(8,128)(2,1)} %bitcast.49), calls=%async_computation.4 | async-start | bytes 1572864 | tf_op jit(solution)/shard_map/all_to_all | solution.py:41
  204.7 4.3 %reduce-scatter.5.cloned.1.call-done = bf16[176,768]{1,0:T(8,128)(2,1)} async-done(((bf16[704,768]{1,0:T(8,128)(2,1)}), bf16[176,768]{1,0:T(8,128)(2,1)}) %reduce-scatter.5.cloned.1.call-update) | async-done | bytes 270352 | tf_op jit(solution)/shard_map/reduce_scatter | solution.py:272
  211.0 16.3 %all_gather.15.own_ref = bf16[672,384]{1,0:T(8,128)(2,1)S(1)} all-gather(bf16[168,384]{1,0:T(8,128)(2,1)S(1)} %fusion.13), channel_id=1, replica_groups=mesh['x'=4,'y'=8,'l'=2,'h'=4,'c'=2] {'h'}, dimensions={0}, use_global_device_ids=true | all-gather | bytes 645120 | tf_op jit(solution)/shard_map/all_gather | solution.py:279
  233.1 31.6 %all_to_all.30 = bf16[32,24,512]{2,1,0:T(8,128)(2,1)S(1)} all-to-all(bf16[32,24,512]{2,1,0:T(8,128)(2,1)S(1)} %bitcast.151), channel_id=1, replica_groups=mesh['x'=4,'y'=8,'l'=2,'h'=4,'c'=2] {'x','y'}, dimensions={0} | all-to-all | bytes 1572864 | tf_op jit(solution)/shard_map/all_to_all | solution.py:41
  264.9 3.5 %collective-permute-start.13 = (bf16[128,512]{1,0:T(8,128)(2,1)S(1)}, bf16[128,512]{1,0:T(8,128)(2,1)S(1)}, u32[]{:S(2)}, u32[]{:S(2)}) collective-permute-start(bf16[128,512]{1,0:T(8,128)(2,1)S(1)} %convolution_convert_fusion.2), channel_id=1, source_target_pairs={{0,8},{8,0},{1,9},{9,1},{2,10},{10,2},{3,11},{11,3},{4,12},{12,4},... | collective-permute-start | bytes 393224 | tf_op jit(solution)/shard_map/ppermute | solution.py:37
  268.5 3.3 %collective-permute-done.13 = bf16[128,512]{1,0:T(8,128)(2,1)S(1)} collective-permute-done((bf16[128,512]{1,0:T(8,128)(2,1)S(1)}, bf16[128,512]{1,0:T(8,128)(2,1)S(1)}, u32[]{:S(2)}, u32[]{:S(2)}) %collective-permute-start.13) | collective-permute-done | bytes 131104 | tf_op jit(solution)/shard_map/ppermute | solution.py:37
  (119 shorter events, 56.0 us)
Async XLA Ops:
  7.2 21.8 %copy-start = (bf16[128,512]{1,0:T(8,128)(2,1)S(1)}, bf16[128,512]{1,0:T(8,128)(2,1)}, u32[]{:S(2)}) copy-start(bf16[128,512]{1,0:T(8,128)(2,1)} %param.18) | copy-start | bytes 393220
  7.2 62.9 %all-gather.2.cloned.1.call-start = ((), (), s32[]{:S(2)}) async-start(), calls=%async_computation.8 | async-start | bytes 1179648 | tf_op jit(solution)/shard_map/all_gather | solution.py:212
  8.0 20.9 %collective-permute-start = (bf16[128,256]{1,0:T(8,128)(2,1)S(1)}, bf16[128,256]{1,0:T(8,128)(2,1)S(1)}, u32[]{:S(2)}, u32[]{:S(2)}) collective-permute-start(bf16[128,256]{1,0:T(8,128)(2,1)S(1)} %pad_maximum_fusion.3), channel_id=1, source_target_pairs={{0,24},{8,32},{16,40},{24,48},{32,56},{40,64},{48,72},{56,80},{64,... | collective-permute-start | bytes 196616 | tf_op jit(solution)/shard_map/ppermute | solution.py:46
  13.3 15.6 %collective-permute-start.1 = (bf16[128,256]{1,0:T(8,128)(2,1)S(1)}, bf16[128,256]{1,0:T(8,128)(2,1)S(1)}, u32[]{:S(2)}, u32[]{:S(2)}) collective-permute-start(bf16[128,256]{1,0:T(8,128)(2,1)S(1)} %pad_maximum_fusion.3), channel_id=1, source_target_pairs={{0,16},{8,24},{16,32},{24,40},{32,48},{40,56},{48,64},{56,72},{64,... | collective-permute-start | bytes 196616 | tf_op jit(solution)/shard_map/ppermute | solution.py:46
  16.8 12.1 %collective-permute-start.2 = (bf16[128,256]{1,0:T(8,128)(2,1)S(1)}, bf16[128,256]{1,0:T(8,128)(2,1)S(1)}, u32[]{:S(2)}, u32[]{:S(2)}) collective-permute-start(bf16[128,256]{1,0:T(8,128)(2,1)S(1)} %pad_maximum_fusion.3), channel_id=1, source_target_pairs={{0,8},{8,16},{16,24},{24,32},{32,40},{40,48},{48,56},{56,64},{64,7... | collective-permute-start | bytes 196616 | tf_op jit(solution)/shard_map/ppermute | solution.py:46
  20.6 6.7 %collective-permute-start.3 = (bf16[64,512]{1,0:T(8,128)(2,1)}, bf16[64,512]{1,0:T(8,128)(2,1)S(1)}, u32[]{:S(2)}, u32[]{:S(2)}) collective-permute-start(bf16[64,512]{1,0:T(8,128)(2,1)} %param.21), channel_id=1, source_target_pairs={{0,8},{8,0},{1,9},{9,1},{2,10},{10,2},{3,11},{11,3},{4,12},{12,4},... | collective-permute-start | bytes 196616 | tf_op jit(solution)/shard_map/ppermute | solution.py:37
  52.9 12.5 %all-to-all-start = ((bf16[4,128,512]{1,2,0:T(8,128)(2,1)}), bf16[4,128,512]{1,2,0:T(8,128)(2,1)S(1)}, u32[]{:S(2)}, u32[]{:S(2)}) async-start(bf16[4,128,512]{1,2,0:T(8,128)(2,1)} %copy.48), calls=%async_computation | async-start | bytes 1048576 | tf_op jit(solution)/shard_map/all_to_all | solution.py:41
  65.6 6.1 %collective-permute-start.4 = (bf16[512,512]{1,0:T(8,128)(2,1)S(1)}, bf16[512,512]{1,0:T(8,128)(2,1)S(1)}, u32[]{:S(2)}, u32[]{:S(2)}) collective-permute-start(bf16[512,512]{1,0:T(8,128)(2,1)S(1)} %bitcast.160), channel_id=1, source_target_pairs={{0,1},{1,0},{2,3},{3,2},{4,5},{5,4},{6,7},{7,6},{8,9},{9,8},{10,11... | collective-permute-start | bytes 1572872 | tf_op jit(solution)/shard_map/ppermute | solution.py:37
  73.6 12.3 %all-to-all-start.1 = ((bf16[4,128,512]{2,1,0:T(8,128)(2,1)}), bf16[4,128,512]{2,1,0:T(8,128)(2,1)S(1)}, u32[]{:S(2)}, u32[]{:S(2)}) async-start(bf16[4,128,512]{2,1,0:T(8,128)(2,1)} %bitcast.8), calls=%async_computation.1 | async-start | bytes 1048576 | tf_op jit(solution)/shard_map/all_to_all | solution.py:41
  88.0 23.9 %all-to-all-start.2 = ((bf16[32,24,512]{2,1,0:T(8,128)(2,1)}), bf16[32,24,512]{2,1,0:T(8,128)(2,1)S(1)}, u32[]{:S(2)}, u32[]{:S(2)}) async-start(bf16[32,24,512]{2,1,0:T(8,128)(2,1)} %bitcast.29), calls=%async_computation.2 | async-start | bytes 1572864 | tf_op jit(solution)/shard_map/all_to_all | solution.py:41
  94.1 21.9 %copy-start.2 = (bf16[168,192]{1,0:T(8,128)(2,1)S(1)}, bf16[168,192]{1,0:T(8,128)(2,1)}, u32[]{:S(2)}) copy-start(bf16[168,192]{1,0:T(8,128)(2,1)} %constant.97.clone.pick_ref) | copy-start | bytes 193540
  94.1 15.5 %collective-permute-start.7 = (bf16[512,768]{1,0:T(8,128)(2,1)S(1)}, bf16[512,768]{1,0:T(8,128)(2,1)S(1)}, u32[]{:S(2)}, u32[]{:S(2)}) collective-permute-start(bf16[512,768]{1,0:T(8,128)(2,1)S(1)} %pad_maximum_fusion.1), channel_id=1, source_target_pairs={{0,1},{1,0},{2,3},{3,2},{4,5},{5,4},{6,7},{7,6},{8,9},{9,8},{10,11... | collective-permute-start | bytes 2359304 | tf_op jit(solution)/shard_map/ppermute | solution.py:37
  96.1 5.8 %collective-permute-start.6 = (f32[128,24]{0,1:T(8,128)S(1)}, f32[128,24]{0,1:T(8,128)S(1)}, u32[]{:S(2)}, u32[]{:S(2)}) collective-permute-start(f32[128,24]{0,1:T(8,128)S(1)} %get-tuple-element.84), channel_id=1, source_target_pairs={{0,8},{8,0},{1,9},{9,1},{2,10},{10,2},{3,11},{11,3},{4,12},{12,4},... | collective-permute-start | bytes 36872 | tf_op jit(solution)/shard_map/ppermute | solution.py:37
  99.8 6.2 %collective-permute-start.8 = (f32[1,512]{1,0:T(1,128)S(1)}, f32[1,512]{1,0:T(1,128)S(1)}, u32[]{:S(2)}, u32[]{:S(2)}) collective-permute-start(f32[1,512]{1,0:T(1,128)S(1)} %bitcast.156), channel_id=1, source_target_pairs={{0,1},{1,0},{2,3},{3,2},{4,5},{5,4},{6,7},{7,6},{8,9},{9,8},{10,11... | collective-permute-start | bytes 6152 | tf_op jit(solution)/shard_map/ppermute | solution.py:37
  102.0 7.6 %collective-permute-start.5 = (bf16[128,512]{1,0:T(8,128)(2,1)S(1)}, bf16[128,512]{1,0:T(8,128)(2,1)S(1)}, u32[]{:S(2)}, u32[]{:S(2)}) collective-permute-start(bf16[128,512]{1,0:T(8,128)(2,1)S(1)} %get-tuple-element.54), channel_id=1, source_target_pairs={{0,8},{8,0},{1,9},{9,1},{2,10},{10,2},{3,11},{11,3},{4,12},{12,4},... | collective-permute-start | bytes 393224 | tf_op jit(solution)/shard_map/ppermute | solution.py:37
  111.8 4.2 %collective-permute-start.9 = (bf16[768,512]{1,0:T(8,128)(2,1)S(1)}, bf16[768,512]{1,0:T(8,128)(2,1)S(1)}, u32[]{:S(2)}, u32[]{:S(2)}) collective-permute-start(bf16[768,512]{1,0:T(8,128)(2,1)S(1)} %bitcast.152), channel_id=1, source_target_pairs={{0,1},{1,0},{2,3},{3,2},{4,5},{5,4},{6,7},{7,6},{8,9},{9,8},{10,11... | collective-permute-start | bytes 2359304 | tf_op jit(solution)/shard_map/ppermute | solution.py:37
  120.6 30.9 %all-to-all-start.4 = ((bf16[32,24,512]{2,1,0:T(8,128)(2,1)}), bf16[32,24,512]{2,1,0:T(8,128)(2,1)S(1)}, u32[]{:S(2)}, u32[]{:S(2)}) async-start(bf16[32,24,512]{2,1,0:T(8,128)(2,1)} %bitcast.51), calls=%async_computation.5 | async-start | bytes 1572864 | tf_op jit(solution)/shard_map/all_to_all | solution.py:41
  128.2 41.3 %reduce-scatter.3.cloned.1.call-start = ((), (), s32[]{:S(2)}) async-start(), calls=%async_computation.9 | async-start | bytes 1351680 | tf_op jit(solution)/shard_map/reduce_scatter | solution.py:272
  129.0 80.0 %reduce-scatter.5.cloned.1.call-start = ((), (), s32[]{:S(2)}) async-start(), calls=%async_computation.10 | async-start | bytes 1351680 | tf_op jit(solution)/shard_map/reduce_scatter | solution.py:272
  151.5 4.2 %collective-permute-start.11 = (bf16[768,512]{1,0:T(8,128)(2,1)S(1)}, bf16[768,512]{1,0:T(8,128)(2,1)S(1)}, u32[]{:S(2)}, u32[]{:S(2)}) collective-permute-start(bf16[768,512]{1,0:T(8,128)(2,1)S(1)} %bitcast.154), channel_id=1, source_target_pairs={{0,1},{1,0},{2,3},{3,2},{4,5},{5,4},{6,7},{7,6},{8,9},{9,8},{10,11... | collective-permute-start | bytes 2359304 | tf_op jit(solution)/shard_map/ppermute | solution.py:37
  186.6 3.8 %collective-permute-start.10 = (bf16[672,384]{1,0:T(8,128)(2,1)S(1)}, bf16[672,384]{1,0:T(8,128)(2,1)S(1)}, u32[]{:S(2)}, u32[]{:S(2)}) collective-permute-start(bf16[672,384]{1,0:T(8,128)(2,1)S(1)} %all_gather.14.own_ref), channel_id=1, source_target_pairs={{0,1},{1,0},{2,3},{3,2},{4,5},{5,4},{6,7},{7,6},{8,9},{9,8},{10,11... | collective-permute-start | bytes 1548296 | tf_op jit(solution)/shard_map/ppermute | solution.py:37
  192.6 35.4 %all-to-all-start.3 = ((bf16[32,24,512]{2,1,0:T(8,128)(2,1)}), bf16[32,24,512]{2,1,0:T(8,128)(2,1)S(1)}, u32[]{:S(2)}, u32[]{:S(2)}) async-start(bf16[32,24,512]{2,1,0:T(8,128)(2,1)} %bitcast.49), calls=%async_computation.4 | async-start | bytes 1572864 | tf_op jit(solution)/shard_map/all_to_all | solution.py:41
  228.0 3.8 %collective-permute-start.12 = (bf16[672,384]{1,0:T(8,128)(2,1)S(1)}, bf16[672,384]{1,0:T(8,128)(2,1)S(1)}, u32[]{:S(2)}, u32[]{:S(2)}) collective-permute-start(bf16[672,384]{1,0:T(8,128)(2,1)S(1)} %all_gather.15.own_ref), channel_id=1, source_target_pairs={{0,1},{1,0},{2,3},{3,2},{4,5},{5,4},{6,7},{7,6},{8,9},{9,8},{10,11... | collective-permute-start | bytes 1548296 | tf_op jit(solution)/shard_map/ppermute | solution.py:37
  264.9 6.9 %collective-permute-start.13 = (bf16[128,512]{1,0:T(8,128)(2,1)S(1)}, bf16[128,512]{1,0:T(8,128)(2,1)S(1)}, u32[]{:S(2)}, u32[]{:S(2)}) collective-permute-start(bf16[128,512]{1,0:T(8,128)(2,1)S(1)} %convolution_convert_fusion.2), channel_id=1, source_target_pairs={{0,8},{8,0},{1,9},{9,1},{2,10},{10,2},{3,11},{11,3},{4,12},{12,4},... | collective-permute-start | bytes 393224 | tf_op jit(solution)/shard_map/ppermute | solution.py:37
  (11 other events, 85.1 us)
Sparse Core Ops, SparseCore 0:
  29.0 41.0 all-gather.1
  131.9 37.5 reduce-scatter.2
  172.4 36.5 reduce-scatter.4

commit v8 on v7

--- a/solution.py
+++ b/solution.py
@@ -269,10 +269,9 @@
 
     def reduced(part):
         flat = part.reshape(NH * (SHARE + EXTRA), FF)
-        return lax.psum_scatter(flat, "h", scatter_dimension=0, tiled=True)
+        return lax.psum_scatter(flat, "h", scatter_dimension=0, tiled=True).astype(f32)
 
     def gathered(sums):
-        sums = sums.astype(f32)
         total = (sums[SHARE] + sums[SHARE + 1])[:SHARE]
         sums = sums[:SHARE] * lax.rsqrt(total / D + epsilon)[:, None]
         hidden = (jax.nn.silu(sums[:, :half]) * sums[:, half:]).astype(bf16)
@@ -288,11 +287,10 @@
         )
     )
     first = share_products(first)
-    first, beside = lax.optimization_barrier((first, beside))
     second = share_products(sent(other_pick, beside))
-    first, second = reduced(first), reduced(second)
+    first, parts = reduced(first), exchange(second, "h")
     first = through(finished(gathered(first)))
-    hidden = gathered(second)
+    hidden = gathered(jnp.sum(parts.astype(f32), axis=0))
     combine = spread(other_slots, other_gates)
     first, hidden, combine = lax.optimization_barrier((first, hidden, combine))
     second = through(finished(hidden))

time: 281 us -> 289 us (1.028)
  blocking collectives: 84.4 us -> 97.7 us
  waiting for transfers between devices: 75.4 us -> 66.5 us
  starting transfers between devices: 75.6 us -> 78.5 us
    all_gather x2, blocking collectives: 31.4 us -> 47.9 us  [gathered(): return lax.all_gather(hidden, 'h', axis=0, tiled=True)]
    reduce_scatter x2 -> x1, waiting for transfers between devices: 14.7 us -> 5.94 us  [reduced(): lax.psum_scatter(flat, 'h', scatter_dimension=0, tiled=True).astype(f32)]
    all_to_all x5 -> x6, starting transfers between devices: 34.3 us -> 38.8 us  [exchange(): return lax.all_to_all(blocks, axes, split_axis=0, concat_axis=0, tiled=True)]
    all_to_all x1, blocking collectives: 31.6 us -> 28.3 us  [exchange(): return lax.all_to_all(blocks, axes, split_axis=0, concat_axis=0, tiled=True)]
    all_to_all x5 -> x6, waiting for transfers between devices: 40.3 us -> 42.2 us  [exchange(): return lax.all_to_all(blocks, axes, split_axis=0, concat_axis=0, tiled=True)]
  transfers between devices with their start and end apart: 22 -> 22, of which waited for: 15 -> 13; matrix products, arithmetic and copies ran while one was open for 4% -> 4% of each run, Pallas kernels for 2% -> 4%
where the time goes in v8:
time: 289 us; the launch traced here: 287 us
  blocking collectives  97.7 us (34%)
  starting transfers between devices  78.5 us (27%)
  waiting for transfers between devices  66.5 us (23%)
  between operations  15.4 us (5%)
  Pallas kernels  11.3 us (4%)
  matrix products  8.3 us (3%)
  other arithmetic  6.29 us (2%)
  local copies, waits for them, and re-layouts  3.36 us (1%)
    all_gather x2, blocking collectives, gathered(): return lax.all_gather(hidden, 'h', axis=0, tiled=True)  47.9 us
    all_to_all x6, waiting for transfers between devices, exchange(): return lax.all_to_all(blocks, axes, split_axis=0, concat_axis=0, tiled=True)  42.2 us
    all_to_all x6, starting transfers between devices, exchange(): return lax.all_to_all(blocks, axes, split_axis=0, concat_axis=0, tiled=True)  38.8 us
    all_to_all x1, blocking collectives, exchange(): return lax.all_to_all(blocks, axes, split_axis=0, concat_axis=0, tiled=True)  28.3 us
    ppermute x11, starting transfers between devices, swap(): return lax.ppermute(block, axis, [(0, 1), (1, 0)])  27 us
    all_gather x1, blocking collectives, body(): lax.all_gather(attended, 'h', axis=0, tiled=True).reshape(NH, tokens, SLICE)  21.5 us
    ppermute x11, waiting for transfers between devices, swap(): return lax.ppermute(block, axis, [(0, 1), (1, 0)])  15.8 us
    ppermute x3, starting transfers between devices, from_behind(): return lax.ppermute(block, CTX, route)  12.6 us
  transfers between devices with their start and end apart: 22, of which 13 were waited for; matrix products, arithmetic and copies ran while one was open for 4% of the time, Pallas kernels for 4%

profile of v8, /device:TPU:8, one launch (start us, length us, event | category | flops | bytes accessed | tf_op | source)
XLA Modules:
  0.0 287.4 jit_solution(269048994988528955)
XLA Ops:
  8.0 5.3 %collective-permute-start = (bf16[128,256]{1,0:T(8,128)(2,1)S(1)}, bf16[128,256]{1,0:T(8,128)(2,1)S(1)}, u32[]{:S(2)}, u32[]{:S(2)}) collective-permute-start(bf16[128,256]{1,0:T(8,128)(2,1)S(1)} %pad_maximum_fusion.3), channel_id=1, source_target_pairs={{0,24},{8,32},{16,40},{24,48},{32,56},{40,64},{48,72},{56,80},{64,... | collective-permute-start | bytes 196616 | tf_op jit(solution)/shard_map/ppermute | solution.py:46
  13.3 3.5 %collective-permute-start.1 = (bf16[128,256]{1,0:T(8,128)(2,1)S(1)}, bf16[128,256]{1,0:T(8,128)(2,1)S(1)}, u32[]{:S(2)}, u32[]{:S(2)}) collective-permute-start(bf16[128,256]{1,0:T(8,128)(2,1)S(1)} %pad_maximum_fusion.3), channel_id=1, source_target_pairs={{0,16},{8,24},{16,32},{24,40},{32,48},{40,56},{48,64},{56,72},{64,... | collective-permute-start | bytes 196616 | tf_op jit(solution)/shard_map/ppermute | solution.py:46
  16.8 3.8 %collective-permute-start.2 = (bf16[128,256]{1,0:T(8,128)(2,1)S(1)}, bf16[128,256]{1,0:T(8,128)(2,1)S(1)}, u32[]{:S(2)}, u32[]{:S(2)}) collective-permute-start(bf16[128,256]{1,0:T(8,128)(2,1)S(1)} %pad_maximum_fusion.3), channel_id=1, source_target_pairs={{0,8},{8,16},{16,24},{24,32},{32,40},{40,48},{48,56},{56,64},{64,7... | collective-permute-start | bytes 196616 | tf_op jit(solution)/shard_map/ppermute | solution.py:46
  20.6 4.3 %collective-permute-start.3 = (bf16[64,512]{1,0:T(8,128)(2,1)}, bf16[64,512]{1,0:T(8,128)(2,1)S(1)}, u32[]{:S(2)}, u32[]{:S(2)}) collective-permute-start(bf16[64,512]{1,0:T(8,128)(2,1)} %param.21), channel_id=1, source_target_pairs={{0,8},{8,0},{1,9},{9,1},{2,10},{10,2},{3,11},{11,3},{4,12},{12,4},... | collective-permute-start | bytes 196616 | tf_op jit(solution)/shard_map/ppermute | solution.py:37
  30.4 21.5 %all_gather.12 = bf16[512,512]{1,0:T(8,128)(2,1)S(1)} all-gather(bf16[128,512]{1,0:T(8,128)(2,1)S(1)} %copy.47), channel_id=1, replica_groups=mesh['x'=4,'y'=8,'l'=2,'h'=4,'c'=2] {'h'}, dimensions={0}, use_global_device_ids=true | all-gather | bytes 655360 | tf_op jit(solution)/shard_map/all_gather | solution.py:215
  52.9 4.4 %all-to-all-start = ((bf16[4,128,512]{1,2,0:T(8,128)(2,1)}), bf16[4,128,512]{1,2,0:T(8,128)(2,1)S(1)}, u32[]{:S(2)}, u32[]{:S(2)}) async-start(bf16[4,128,512]{1,2,0:T(8,128)(2,1)} %copy.48), calls=%async_computation | async-start | bytes 1048576 | tf_op jit(solution)/shard_map/all_to_all | solution.py:41
  58.0 7.4 %all-to-all-done = bf16[4,128,512]{1,2,0:T(8,128)(2,1)S(1)} async-done(((bf16[4,128,512]{1,2,0:T(8,128)(2,1)}), bf16[4,128,512]{1,2,0:T(8,128)(2,1)S(1)}, u32[]{:S(2)}, u32[]{:S(2)}) %all-to-all-start) | async-done | bytes 524320 | tf_op jit(solution)/shard_map/all_to_all | solution.py:41
  73.6 4.3 %all-to-all-start.1 = ((bf16[4,128,512]{2,1,0:T(8,128)(2,1)}), bf16[4,128,512]{2,1,0:T(8,128)(2,1)S(1)}, u32[]{:S(2)}, u32[]{:S(2)}) async-start(bf16[4,128,512]{2,1,0:T(8,128)(2,1)} %bitcast.8), calls=%async_computation.1 | async-start | bytes 1048576 | tf_op jit(solution)/shard_map/all_to_all | solution.py:41
  78.4 7.5 %all-to-all-done.1 = bf16[4,128,512]{2,1,0:T(8,128)(2,1)S(1)} async-done(((bf16[4,128,512]{2,1,0:T(8,128)(2,1)}), bf16[4,128,512]{2,1,0:T(8,128)(2,1)S(1)}, u32[]{:S(2)}, u32[]{:S(2)}) %all-to-all-start.1) | async-done | bytes 524320 | tf_op jit(solution)/shard_map/all_to_all | solution.py:41
  88.0 5.9 %all-to-all-start.2 = ((bf16[32,24,512]{2,1,0:T(8,128)(2,1)}), bf16[32,24,512]{2,1,0:T(8,128)(2,1)S(1)}, u32[]{:S(2)}, u32[]{:S(2)}) async-start(bf16[32,24,512]{2,1,0:T(8,128)(2,1)} %bitcast.29), calls=%async_computation.2 | async-start | bytes 1572864 | tf_op jit(solution)/shard_map/all_to_all | solution.py:41
  96.0 3.6 %collective-permute-start.6 = (f32[128,24]{0,1:T(8,128)S(1)}, f32[128,24]{0,1:T(8,128)S(1)}, u32[]{:S(2)}, u32[]{:S(2)}) collective-permute-start(f32[128,24]{0,1:T(8,128)S(1)} %get-tuple-element.80), channel_id=1, source_target_pairs={{0,8},{8,0},{1,9},{9,1},{2,10},{10,2},{3,11},{11,3},{4,12},{12,4},... | collective-permute-start | bytes 36872 | tf_op jit(solution)/shard_map/ppermute | solution.py:37
  101.9 3.3 %collective-permute-start.5 = (bf16[128,512]{1,0:T(8,128)(2,1)S(1)}, bf16[128,512]{1,0:T(8,128)(2,1)S(1)}, u32[]{:S(2)}, u32[]{:S(2)}) collective-permute-start(bf16[128,512]{1,0:T(8,128)(2,1)S(1)} %get-tuple-element.52), channel_id=1, source_target_pairs={{0,8},{8,0},{1,9},{9,1},{2,10},{10,2},{3,11},{11,3},{4,12},{12,4},... | collective-permute-start | bytes 393224 | tf_op jit(solution)/shard_map/ppermute | solution.py:37
  115.1 7.5 %all-to-all-start.4 = ((bf16[32,24,512]{2,1,0:T(8,128)(2,1)}), bf16[32,24,512]{2,1,0:T(8,128)(2,1)S(1)}, u32[]{:S(2)}, u32[]{:S(2)}) async-start(bf16[32,24,512]{2,1,0:T(8,128)(2,1)} %bitcast.158), calls=%async_computation.5 | async-start | bytes 1572864 | tf_op jit(solution)/shard_map/all_to_all | solution.py:41
  122.7 4.5 %shard_map.185 = bf16[4,176,768]{2,1,0:T(8,128)(2,1)} custom-call(bf16[768,512]{1,0:T(8,128)(2,1)S(1)} %bitcast.152, bf16[768,512]{1,0:T(8,128)(2,1)} %collective-permute-done.9.other_ref, bf16[512,768]{1,0:T(8,128)(2,1)S(1)} %pad_maximum_fusion.w_own_ref, bf16[512,768]{1,0:T(8,128)(2,1)S(1)} %collective-permute-done.7.w_other_ref, f32[1,512]{1,0:T(1,128)S(1)} %bitcast.156, ...), custom_call_target="tpu_custom_call" | custom-call | flops 100000000 | bytes 500000 | tf_op jit(solution)/shard_map/pallas_call | solution.py:151
  127.2 18.7 %all-to-all-done.4 = bf16[32,24,512]{2,1,0:T(8,128)(2,1)S(1)} async-done(((bf16[32,24,512]{2,1,0:T(8,128)(2,1)}), bf16[32,24,512]{2,1,0:T(8,128)(2,1)S(1)}, u32[]{:S(2)}, u32[]{:S(2)}) %all-to-all-start.4) | async-done | bytes 786464 | tf_op jit(solution)/shard_map/all_to_all | solution.py:41
  150.1 3.4 %shard_map.187 = bf16[4,176,768]{2,1,0:T(8,128)(2,1)} custom-call(bf16[768,512]{1,0:T(8,128)(2,1)S(1)} %bitcast.154, bf16[768,512]{1,0:T(8,128)(2,1)S(1)} %collective-permute-done.11.other_ref, bf16[512,768]{1,0:T(8,128)(2,1)S(1)} %pad_maximum_fusion.w_own_ref, bf16[512,768]{1,0:T(8,128)(2,1)S(1)} %collective-permute-done.7.w_other_ref, ...), custom_call_target="tpu_custom_call" | custom-call | flops 100000000 | bytes 500000 | tf_op jit(solution)/shard_map/pallas_call | solution.py:151
  153.5 6.4 %all-to-all-start.5 = ((bf16[4,176,768]{2,1,0:T(8,128)(2,1)}), bf16[4,176,768]{2,1,0:T(8,128)(2,1)S(1)}, u32[]{:S(2)}, u32[]{:S(2)}) async-start(bf16[4,176,768]{2,1,0:T(8,128)(2,1)} %shard_map.187), calls=%async_computation.6 | async-start | bytes 2162688 | tf_op jit(solution)/shard_map/all_to_all | solution.py:41
  160.0 5.9 %reduce-scatter.2.cloned.1.call-done = bf16[176,768]{1,0:T(8,128)(2,1)} async-done(((bf16[704,768]{1,0:T(8,128)(2,1)}), bf16[176,768]{1,0:T(8,128)(2,1)}) %reduce-scatter.2.cloned.1.call-update) | async-done | bytes 270352 | tf_op jit(solution)/shard_map/reduce_scatter | solution.py:272
  167.9 31.2 %all_gather.14.own_ref = bf16[672,384]{1,0:T(8,128)(2,1)S(1)} all-gather(bf16[168,384]{1,0:T(8,128)(2,1)S(1)} %fusion.14), channel_id=1, replica_groups=mesh['x'=4,'y'=8,'l'=2,'h'=4,'c'=2] {'h'}, dimensions={0}, use_global_device_ids=true | all-gather | bytes 645120 | tf_op jit(solution)/shard_map/all_gather | solution.py:278
  205.1 10.3 %all-to-all-start.3 = ((bf16[32,24,512]{2,1,0:T(8,128)(2,1)}), bf16[32,24,512]{2,1,0:T(8,128)(2,1)S(1)}, u32[]{:S(2)}, u32[]{:S(2)}) async-start(bf16[32,24,512]{2,1,0:T(8,128)(2,1)} %bitcast.49), calls=%async_computation.4 | async-start | bytes 1572864 | tf_op jit(solution)/shard_map/all_to_all | solution.py:41
  215.8 16.7 %all_gather.15.own_ref = bf16[672,384]{1,0:T(8,128)(2,1)S(1)} all-gather(bf16[168,384]{1,0:T(8,128)(2,1)S(1)} %fusion.13), channel_id=1, replica_groups=mesh['x'=4,'y'=8,'l'=2,'h'=4,'c'=2] {'h'}, dimensions={0}, use_global_device_ids=true | all-gather | bytes 645120 | tf_op jit(solution)/shard_map/all_gather | solution.py:278
  232.5 6.2 %all-to-all-done.3 = bf16[32,24,512]{2,1,0:T(8,128)(2,1)S(1)} async-done(((bf16[32,24,512]{2,1,0:T(8,128)(2,1)}), bf16[32,24,512]{2,1,0:T(8,128)(2,1)S(1)}, u32[]{:S(2)}, u32[]{:S(2)}) %all-to-all-start.3) | async-done | bytes 786464 | tf_op jit(solution)/shard_map/all_to_all | solution.py:41
  243.8 28.3 %all_to_all.35 = bf16[32,24,512]{2,1,0:T(8,128)(2,1)S(1)} all-to-all(bf16[32,24,512]{2,1,0:T(8,128)(2,1)S(1)} %bitcast.150), channel_id=1, replica_groups=mesh['x'=4,'y'=8,'l'=2,'h'=4,'c'=2] {'x','y'}, dimensions={0} | all-to-all | bytes 1572864 | tf_op jit(solution)/shard_map/all_to_all | solution.py:41
  274.4 4.9 %collective-permute-done.13 = bf16[128,512]{1,0:T(8,128)(2,1)S(1)} collective-permute-done((bf16[128,512]{1,0:T(8,128)(2,1)S(1)}, bf16[128,512]{1,0:T(8,128)(2,1)S(1)}, u32[]{:S(2)}, u32[]{:S(2)}) %collective-permute-start.13) | collective-permute-done | bytes 131104 | tf_op jit(solution)/shard_map/ppermute | solution.py:37
  (120 shorter events, 53.1 us)
Async XLA Ops:
  7.2 62.9 %all-gather.2.cloned.1.call-start = ((), (), s32[]{:S(2)}) async-start(), calls=%async_computation.8 | async-start | bytes 1179648 | tf_op jit(solution)/shard_map/all_gather | solution.py:212
  8.0 20.9 %collective-permute-start = (bf16[128,256]{1,0:T(8,128)(2,1)S(1)}, bf16[128,256]{1,0:T(8,128)(2,1)S(1)}, u32[]{:S(2)}, u32[]{:S(2)}) collective-permute-start(bf16[128,256]{1,0:T(8,128)(2,1)S(1)} %pad_maximum_fusion.3), channel_id=1, source_target_pairs={{0,24},{8,32},{16,40},{24,48},{32,56},{40,64},{48,72},{56,80},{64,... | collective-permute-start | bytes 196616 | tf_op jit(solution)/shard_map/ppermute | solution.py:46
  13.3 15.6 %collective-permute-start.1 = (bf16[128,256]{1,0:T(8,128)(2,1)S(1)}, bf16[128,256]{1,0:T(8,128)(2,1)S(1)}, u32[]{:S(2)}, u32[]{:S(2)}) collective-permute-start(bf16[128,256]{1,0:T(8,128)(2,1)S(1)} %pad_maximum_fusion.3), channel_id=1, source_target_pairs={{0,16},{8,24},{16,32},{24,40},{32,48},{40,56},{48,64},{56,72},{64,... | collective-permute-start | bytes 196616 | tf_op jit(solution)/shard_map/ppermute | solution.py:46
  16.8 12.1 %collective-permute-start.2 = (bf16[128,256]{1,0:T(8,128)(2,1)S(1)}, bf16[128,256]{1,0:T(8,128)(2,1)S(1)}, u32[]{:S(2)}, u32[]{:S(2)}) collective-permute-start(bf16[128,256]{1,0:T(8,128)(2,1)S(1)} %pad_maximum_fusion.3), channel_id=1, source_target_pairs={{0,8},{8,16},{16,24},{24,32},{32,40},{40,48},{48,56},{56,64},{64,7... | collective-permute-start | bytes 196616 | tf_op jit(solution)/shard_map/ppermute | solution.py:46
  20.6 6.7 %collective-permute-start.3 = (bf16[64,512]{1,0:T(8,128)(2,1)}, bf16[64,512]{1,0:T(8,128)(2,1)S(1)}, u32[]{:S(2)}, u32[]{:S(2)}) collective-permute-start(bf16[64,512]{1,0:T(8,128)(2,1)} %param.21), channel_id=1, source_target_pairs={{0,8},{8,0},{1,9},{9,1},{2,10},{10,2},{3,11},{11,3},{4,12},{12,4},... | collective-permute-start | bytes 196616 | tf_op jit(solution)/shard_map/ppermute | solution.py:37
  52.9 12.5 %all-to-all-start = ((bf16[4,128,512]{1,2,0:T(8,128)(2,1)}), bf16[4,128,512]{1,2,0:T(8,128)(2,1)S(1)}, u32[]{:S(2)}, u32[]{:S(2)}) async-start(bf16[4,128,512]{1,2,0:T(8,128)(2,1)} %copy.48), calls=%async_computation | async-start | bytes 1048576 | tf_op jit(solution)/shard_map/all_to_all | solution.py:41
  65.6 6.1 %collective-permute-start.4 = (bf16[512,512]{1,0:T(8,128)(2,1)S(1)}, bf16[512,512]{1,0:T(8,128)(2,1)S(1)}, u32[]{:S(2)}, u32[]{:S(2)}) collective-permute-start(bf16[512,512]{1,0:T(8,128)(2,1)S(1)} %bitcast.160), channel_id=1, source_target_pairs={{0,1},{1,0},{2,3},{3,2},{4,5},{5,4},{6,7},{7,6},{8,9},{9,8},{10,11... | collective-permute-start | bytes 1572872 | tf_op jit(solution)/shard_map/ppermute | solution.py:37
  73.6 12.3 %all-to-all-start.1 = ((bf16[4,128,512]{2,1,0:T(8,128)(2,1)}), bf16[4,128,512]{2,1,0:T(8,128)(2,1)S(1)}, u32[]{:S(2)}, u32[]{:S(2)}) async-start(bf16[4,128,512]{2,1,0:T(8,128)(2,1)} %bitcast.8), calls=%async_computation.1 | async-start | bytes 1048576 | tf_op jit(solution)/shard_map/all_to_all | solution.py:41
  88.0 23.9 %all-to-all-start.2 = ((bf16[32,24,512]{2,1,0:T(8,128)(2,1)}), bf16[32,24,512]{2,1,0:T(8,128)(2,1)S(1)}, u32[]{:S(2)}, u32[]{:S(2)}) async-start(bf16[32,24,512]{2,1,0:T(8,128)(2,1)} %bitcast.29), calls=%async_computation.2 | async-start | bytes 1572864 | tf_op jit(solution)/shard_map/all_to_all | solution.py:41
  94.1 15.4 %collective-permute-start.7 = (bf16[512,768]{1,0:T(8,128)(2,1)S(1)}, bf16[512,768]{1,0:T(8,128)(2,1)S(1)}, u32[]{:S(2)}, u32[]{:S(2)}) collective-permute-start(bf16[512,768]{1,0:T(8,128)(2,1)S(1)} %pad_maximum_fusion.1), channel_id=1, source_target_pairs={{0,1},{1,0},{2,3},{3,2},{4,5},{5,4},{6,7},{7,6},{8,9},{9,8},{10,11... | collective-permute-start | bytes 2359304 | tf_op jit(solution)/shard_map/ppermute | solution.py:37
  96.0 5.8 %collective-permute-start.6 = (f32[128,24]{0,1:T(8,128)S(1)}, f32[128,24]{0,1:T(8,128)S(1)}, u32[]{:S(2)}, u32[]{:S(2)}) collective-permute-start(f32[128,24]{0,1:T(8,128)S(1)} %get-tuple-element.80), channel_id=1, source_target_pairs={{0,8},{8,0},{1,9},{9,1},{2,10},{10,2},{3,11},{11,3},{4,12},{12,4},... | collective-permute-start | bytes 36872 | tf_op jit(solution)/shard_map/ppermute | solution.py:37
  99.6 6.9 %collective-permute-start.8 = (f32[1,512]{1,0:T(1,128)S(1)}, f32[1,512]{1,0:T(1,128)S(1)}, u32[]{:S(2)}, u32[]{:S(2)}) collective-permute-start(f32[1,512]{1,0:T(1,128)S(1)} %bitcast.155), channel_id=1, source_target_pairs={{0,1},{1,0},{2,3},{3,2},{4,5},{5,4},{6,7},{7,6},{8,9},{9,8},{10,11... | collective-permute-start | bytes 6152 | tf_op jit(solution)/shard_map/ppermute | solution.py:37
  101.9 7.6 %collective-permute-start.5 = (bf16[128,512]{1,0:T(8,128)(2,1)S(1)}, bf16[128,512]{1,0:T(8,128)(2,1)S(1)}, u32[]{:S(2)}, u32[]{:S(2)}) collective-permute-start(bf16[128,512]{1,0:T(8,128)(2,1)S(1)} %get-tuple-element.52), channel_id=1, source_target_pairs={{0,8},{8,0},{1,9},{9,1},{2,10},{10,2},{3,11},{11,3},{4,12},{12,4},... | collective-permute-start | bytes 393224 | tf_op jit(solution)/shard_map/ppermute | solution.py:37
  111.8 10.8 %collective-permute-start.9 = (bf16[768,512]{1,0:T(8,128)(2,1)S(1)}, bf16[768,512]{1,0:T(8,128)(2,1)}, u32[]{:S(2)}, u32[]{:S(2)}) collective-permute-start(bf16[768,512]{1,0:T(8,128)(2,1)S(1)} %bitcast.151), channel_id=1, source_target_pairs={{0,1},{1,0},{2,3},{3,2},{4,5},{5,4},{6,7},{7,6},{8,9},{9,8},{10,11... | collective-permute-start | bytes 2359304 | tf_op jit(solution)/shard_map/ppermute | solution.py:37
  115.1 30.8 %all-to-all-start.4 = ((bf16[32,24,512]{2,1,0:T(8,128)(2,1)}), bf16[32,24,512]{2,1,0:T(8,128)(2,1)S(1)}, u32[]{:S(2)}, u32[]{:S(2)}) async-start(bf16[32,24,512]{2,1,0:T(8,128)(2,1)} %bitcast.158), calls=%async_computation.5 | async-start | bytes 1572864 | tf_op jit(solution)/shard_map/all_to_all | solution.py:41
  122.6 43.3 %reduce-scatter.2.cloned.1.call-start = ((), (), s32[]{:S(2)}) async-start(), calls=%async_computation.9 | async-start | bytes 1351680 | tf_op jit(solution)/shard_map/reduce_scatter | solution.py:272
  146.0 4.2 %collective-permute-start.11 = (bf16[768,512]{1,0:T(8,128)(2,1)S(1)}, bf16[768,512]{1,0:T(8,128)(2,1)S(1)}, u32[]{:S(2)}, u32[]{:S(2)}) collective-permute-start(bf16[768,512]{1,0:T(8,128)(2,1)S(1)} %bitcast.153), channel_id=1, source_target_pairs={{0,1},{1,0},{2,3},{3,2},{4,5},{5,4},{6,7},{7,6},{8,9},{9,8},{10,11... | collective-permute-start | bytes 2359304 | tf_op jit(solution)/shard_map/ppermute | solution.py:37
  153.5 51.6 %all-to-all-start.5 = ((bf16[4,176,768]{2,1,0:T(8,128)(2,1)}), bf16[4,176,768]{2,1,0:T(8,128)(2,1)S(1)}, u32[]{:S(2)}, u32[]{:S(2)}) async-start(bf16[4,176,768]{2,1,0:T(8,128)(2,1)} %shard_map.187), calls=%async_computation.6 | async-start | bytes 2162688 | tf_op jit(solution)/shard_map/all_to_all | solution.py:41
  167.7 33.6 %copy-start.6 = (bf16[1,768,512]{2,1,0:T(8,128)(2,1)S(1)}, bf16[1,768,512]{2,1,0:T(8,128)(2,1)}, u32[]{:S(2)}) copy-start(bf16[1,768,512]{2,1,0:T(8,128)(2,1)} %param.26) | copy-start | bytes 2359300
  167.9 35.0 %copy-start.1 = (bf16[192,168]{1,0:T(8,128)(2,1)S(1)}, bf16[192,168]{1,0:T(8,128)(2,1)}, u32[]{:S(2)}) copy-start(bf16[192,168]{1,0:T(8,128)(2,1)} %constant.98.clone.place_ref) | copy-start | bytes 193540
  199.1 3.8 %collective-permute-start.10 = (bf16[672,384]{1,0:T(8,128)(2,1)S(1)}, bf16[672,384]{1,0:T(8,128)(2,1)S(1)}, u32[]{:S(2)}, u32[]{:S(2)}) collective-permute-start(bf16[672,384]{1,0:T(8,128)(2,1)S(1)} %all_gather.14.own_ref), channel_id=1, source_target_pairs={{0,1},{1,0},{2,3},{3,2},{4,5},{5,4},{6,7},{7,6},{8,9},{9,8},{10,11... | collective-permute-start | bytes 1548296 | tf_op jit(solution)/shard_map/ppermute | solution.py:37
  205.1 33.6 %all-to-all-start.3 = ((bf16[32,24,512]{2,1,0:T(8,128)(2,1)}), bf16[32,24,512]{2,1,0:T(8,128)(2,1)S(1)}, u32[]{:S(2)}, u32[]{:S(2)}) async-start(bf16[32,24,512]{2,1,0:T(8,128)(2,1)} %bitcast.49), calls=%async_computation.4 | async-start | bytes 1572864 | tf_op jit(solution)/shard_map/all_to_all | solution.py:41
  238.7 3.8 %collective-permute-start.12 = (bf16[672,384]{1,0:T(8,128)(2,1)S(1)}, bf16[672,384]{1,0:T(8,128)(2,1)S(1)}, u32[]{:S(2)}, u32[]{:S(2)}) collective-permute-start(bf16[672,384]{1,0:T(8,128)(2,1)S(1)} %all_gather.15.own_ref), channel_id=1, source_target_pairs={{0,1},{1,0},{2,3},{3,2},{4,5},{5,4},{6,7},{7,6},{8,9},{9,8},{10,11... | collective-permute-start | bytes 1548296 | tf_op jit(solution)/shard_map/ppermute | solution.py:37
  272.4 6.9 %collective-permute-start.13 = (bf16[128,512]{1,0:T(8,128)(2,1)S(1)}, bf16[128,512]{1,0:T(8,128)(2,1)S(1)}, u32[]{:S(2)}, u32[]{:S(2)}) collective-permute-start(bf16[128,512]{1,0:T(8,128)(2,1)S(1)} %convolution_convert_fusion.2), channel_id=1, source_target_pairs={{0,8},{8,0},{1,9},{9,1},{2,10},{10,2},{3,11},{11,3},{4,12},{12,4},... | collective-permute-start | bytes 393224 | tf_op jit(solution)/shard_map/ppermute | solution.py:37
  (12 other events, 109.8 us)
Sparse Core Ops, SparseCore 0:
  29.0 41.0 all-gather.1
  127.3 38.5 reduce-scatter.1

commit v9 on v7

--- a/solution.py
+++ b/solution.py
@@ -201,18 +201,16 @@
     half = FF // 2
 
     other_strip = swap(out_weight, "l")
-    strips = jnp.concatenate(
-        [
-            jnp.where(side == 0, out_weight, other_strip),
-            jnp.where(side == 0, other_strip, out_weight),
-        ],
-        axis=0,
+    strips = jnp.where(
+        side == 0,
+        jnp.concatenate([out_weight, other_strip], axis=0),
+        jnp.concatenate([other_strip, out_weight], axis=0),
     )
     strips, queries = lax.optimization_barrier((strips, queries))
     quarter = lax.all_gather(strips, "y", axis=0, tiled=True)
 
     attended = attention(queries, key_rows, value_rows)
-    heads = lax.all_gather(attended, "h", axis=0, tiled=True).reshape(NH, tokens, SLICE)
+    heads = exchange(jnp.broadcast_to(attended[None], (NH, *attended.shape)), "h")
     heads = exchange(heads, "x").reshape(NX * tokens, SLICE)
     other_heads = swap(heads, "c")
     partial = jnp.dot(
@@ -287,10 +285,10 @@
             (first, beside, other_pick, gate_up, other_gate_up, inverse, other_inverse)
         )
     )
-    first = share_products(first)
-    first, beside = lax.optimization_barrier((first, beside))
-    second = share_products(sent(other_pick, beside))
-    first, second = reduced(first), reduced(second)
+    first = reduced(share_products(first))
+    second = sent(other_pick, beside)
+    first, second = lax.optimization_barrier((first, second))
+    second = reduced(share_products(second))
     first = through(finished(gathered(first)))
     hidden = gathered(second)
     combine = spread(other_slots, other_gates)

time: 281 us -> 272 us (0.968)
  blocking collectives: 84.4 us -> 115 us
  waiting for transfers between devices: 75.4 us -> 49 us
  starting transfers between devices: 75.6 us -> 65.4 us
    all_to_all x1 -> x3, blocking collectives: 31.6 us -> 82.4 us  [exchange(): return lax.all_to_all(blocks, axes, split_axis=0, concat_axis=0, tiled=True)]
    all_gather x1 -> x0, blocking collectives: 21.5 us -> none  [body(): lax.all_gather(attended, 'h', axis=0, tiled=True).reshape(NH, tokens, SLICE)]
    all_to_all x5 -> x4, waiting for transfers between devices: 40.3 us -> 26.1 us  [exchange(): return lax.all_to_all(blocks, axes, split_axis=0, concat_axis=0, tiled=True)]
    reduce_scatter x2, waiting for transfers between devices: 14.7 us -> 4.94 us  [reduced(): return lax.psum_scatter(flat, 'h', scatter_dimension=0, tiled=True)]
    all_to_all x5 -> x4, starting transfers between devices: 34.3 us -> 24.8 us  [exchange(): return lax.all_to_all(blocks, axes, split_axis=0, concat_axis=0, tiled=True)]
  transfers between devices with their start and end apart: 22 -> 21, of which waited for: 15 -> 14; matrix products, arithmetic and copies ran while one was open for 4% -> 3% of each run, Pallas kernels for 2% -> 1%
where the time goes in v9:
time: 272 us; the launch traced here: 271 us
  blocking collectives  115 us (42%)
  starting transfers between devices  65.4 us (24%)
  waiting for transfers between devices  49 us (18%)
  between operations  15.1 us (6%)
  Pallas kernels  10.2 us (4%)
  matrix products  7.37 us (3%)
  other arithmetic  5.58 us (2%)
  local copies, waits for them, and re-layouts  3.1 us (1%)
    all_to_all x3, blocking collectives, exchange(): return lax.all_to_all(blocks, axes, split_axis=0, concat_axis=0, tiled=True)  82.4 us
    all_gather x2, blocking collectives, gathered(): return lax.all_gather(hidden, 'h', axis=0, tiled=True)  32.6 us
    ppermute x11, starting transfers between devices, swap(): return lax.ppermute(block, axis, [(0, 1), (1, 0)])  27.9 us
    all_to_all x4, waiting for transfers between devices, exchange(): return lax.all_to_all(blocks, axes, split_axis=0, concat_axis=0, tiled=True)  26.1 us
    all_to_all x4, starting transfers between devices, exchange(): return lax.all_to_all(blocks, axes, split_axis=0, concat_axis=0, tiled=True)  24.8 us
    ppermute x11, waiting for transfers between devices, swap(): return lax.ppermute(block, axis, [(0, 1), (1, 0)])  17.7 us
    ppermute x3, starting transfers between devices, from_behind(): return lax.ppermute(block, CTX, route)  12.6 us
    pallas_call x2, Pallas kernels, products(): pl.pallas_call(products_kernel, out_shape=jax.ShapeDtypeStruct((NH, SHARE...  6.79 us
  transfers between devices with their start and end apart: 21, of which 14 were waited for; matrix products, arithmetic and copies ran while one was open for 3% of the time, Pallas kernels for 1%

profile of v9, /device:TPU:8, one launch (start us, length us, event | category | flops | bytes accessed | tf_op | source)
XLA Modules:
  0.0 270.7 jit_solution(14782913292579272467)
XLA Ops:
  8.0 5.3 %collective-permute-start = (bf16[128,256]{1,0:T(8,128)(2,1)S(1)}, bf16[128,256]{1,0:T(8,128)(2,1)S(1)}, u32[]{:S(2)}, u32[]{:S(2)}) collective-permute-start(bf16[128,256]{1,0:T(8,128)(2,1)S(1)} %pad_maximum_fusion.2), channel_id=1, source_target_pairs={{0,24},{8,32},{16,40},{24,48},{32,56},{40,64},{48,72},{56,80},{64,... | collective-permute-start | bytes 196616 | tf_op jit(solution)/shard_map/ppermute | solution.py:46
  13.3 3.5 %collective-permute-start.1 = (bf16[128,256]{1,0:T(8,128)(2,1)S(1)}, bf16[128,256]{1,0:T(8,128)(2,1)S(1)}, u32[]{:S(2)}, u32[]{:S(2)}) collective-permute-start(bf16[128,256]{1,0:T(8,128)(2,1)S(1)} %pad_maximum_fusion.2), channel_id=1, source_target_pairs={{0,16},{8,24},{16,32},{24,40},{32,48},{40,56},{48,64},{56,72},{64,... | collective-permute-start | bytes 196616 | tf_op jit(solution)/shard_map/ppermute | solution.py:46
  16.8 3.8 %collective-permute-start.2 = (bf16[128,256]{1,0:T(8,128)(2,1)S(1)}, bf16[128,256]{1,0:T(8,128)(2,1)S(1)}, u32[]{:S(2)}, u32[]{:S(2)}) collective-permute-start(bf16[128,256]{1,0:T(8,128)(2,1)S(1)} %pad_maximum_fusion.2), channel_id=1, source_target_pairs={{0,8},{8,16},{16,24},{24,32},{32,40},{40,48},{48,56},{56,64},{64,7... | collective-permute-start | bytes 196616 | tf_op jit(solution)/shard_map/ppermute | solution.py:46
  20.6 4.3 %collective-permute-start.3 = (bf16[64,512]{1,0:T(8,128)(2,1)}, bf16[64,512]{1,0:T(8,128)(2,1)S(1)}, u32[]{:S(2)}, u32[]{:S(2)}) collective-permute-start(bf16[64,512]{1,0:T(8,128)(2,1)} %param.21), channel_id=1, source_target_pairs={{0,8},{8,0},{1,9},{9,1},{2,10},{10,2},{3,11},{11,3},{4,12},{12,4},... | collective-permute-start | bytes 196616 | tf_op jit(solution)/shard_map/ppermute | solution.py:37
  30.5 25.0 %all_to_all.35 = bf16[4,128,512]{2,1,0:T(8,128)(2,1)} all-to-all(bf16[4,128,512]{2,1,0:T(8,128)(2,1)S(1)} %broadcast_in_dim.274), channel_id=1, replica_groups=mesh['x'=4,'y'=8,'l'=2,'h'=4,'c'=2] {'h'}, dimensions={0} | all-to-all | bytes 1048576 | tf_op jit(solution)/shard_map/all_to_all | solution.py:41
  55.5 4.3 %all-to-all-start.1 = ((bf16[4,128,512]{2,1,0:T(8,128)(2,1)}), bf16[4,128,512]{2,1,0:T(8,128)(2,1)S(1)}, u32[]{:S(2)}, u32[]{:S(2)}) async-start(bf16[4,128,512]{2,1,0:T(8,128)(2,1)} %all_to_all.35), calls=%async_computation.1 | async-start | bytes 1048576 | tf_op jit(solution)/shard_map/all_to_all | solution.py:41
  60.5 7.4 %all-to-all-done.1 = bf16[4,128,512]{2,1,0:T(8,128)(2,1)S(1)} async-done(((bf16[4,128,512]{2,1,0:T(8,128)(2,1)}), bf16[4,128,512]{2,1,0:T(8,128)(2,1)S(1)}, u32[]{:S(2)}, u32[]{:S(2)}) %all-to-all-start.1) | async-done | bytes 524320 | tf_op jit(solution)/shard_map/all_to_all | solution.py:41
  73.7 4.3 %all-to-all-start.2 = ((bf16[4,128,512]{2,1,0:T(8,128)(2,1)}), bf16[4,128,512]{2,1,0:T(8,128)(2,1)S(1)}, u32[]{:S(2)}, u32[]{:S(2)}) async-start(bf16[4,128,512]{2,1,0:T(8,128)(2,1)} %bitcast.7), calls=%async_computation.2 | async-start | bytes 1048576 | tf_op jit(solution)/shard_map/all_to_all | solution.py:41
  78.5 8.7 %all-to-all-done.2 = bf16[4,128,512]{2,1,0:T(8,128)(2,1)S(1)} async-done(((bf16[4,128,512]{2,1,0:T(8,128)(2,1)}), bf16[4,128,512]{2,1,0:T(8,128)(2,1)S(1)}, u32[]{:S(2)}, u32[]{:S(2)}) %all-to-all-start.2) | async-done | bytes 524320 | tf_op jit(solution)/shard_map/all_to_all | solution.py:41
  89.3 4.8 %all-to-all-start.3 = ((bf16[32,24,512]{2,1,0:T(8,128)(2,1)}), bf16[32,24,512]{2,1,0:T(8,128)(2,1)S(1)}, u32[]{:S(2)}, u32[]{:S(2)}) async-start(bf16[32,24,512]{2,1,0:T(8,128)(2,1)} %bitcast.28), calls=%async_computation.3 | async-start | bytes 1572864 | tf_op jit(solution)/shard_map/all_to_all | solution.py:41
  96.5 3.5 %collective-permute-start.6 = (f32[128,24]{0,1:T(8,128)S(1)}, f32[128,24]{0,1:T(8,128)S(1)}, u32[]{:S(2)}, u32[]{:S(2)}) collective-permute-start(f32[128,24]{0,1:T(8,128)S(1)} %get-tuple-element.82), channel_id=1, source_target_pairs={{0,8},{8,0},{1,9},{9,1},{2,10},{10,2},{3,11},{11,3},{4,12},{12,4},... | collective-permute-start | bytes 36872 | tf_op jit(solution)/shard_map/ppermute | solution.py:37
  102.2 3.3 %collective-permute-start.5 = (bf16[128,512]{1,0:T(8,128)(2,1)S(1)}, bf16[128,512]{1,0:T(8,128)(2,1)S(1)}, u32[]{:S(2)}, u32[]{:S(2)}) collective-permute-start(bf16[128,512]{1,0:T(8,128)(2,1)S(1)} %get-tuple-element.54), channel_id=1, source_target_pairs={{0,8},{8,0},{1,9},{9,1},{2,10},{10,2},{3,11},{11,3},{4,12},{12,4},... | collective-permute-start | bytes 393224 | tf_op jit(solution)/shard_map/ppermute | solution.py:37
  106.2 3.6 %collective-permute-done.5 = bf16[128,512]{1,0:T(8,128)(2,1)S(1)} collective-permute-done((bf16[128,512]{1,0:T(8,128)(2,1)S(1)}, bf16[128,512]{1,0:T(8,128)(2,1)S(1)}, u32[]{:S(2)}, u32[]{:S(2)}) %collective-permute-start.5) | collective-permute-done | bytes 131104 | tf_op jit(solution)/shard_map/ppermute | solution.py:37
  109.8 5.7 %all-to-all-done.3 = bf16[32,24,512]{2,1,0:T(8,128)(2,1)S(1)} async-done(((bf16[32,24,512]{2,1,0:T(8,128)(2,1)}), bf16[32,24,512]{2,1,0:T(8,128)(2,1)S(1)}, u32[]{:S(2)}, u32[]{:S(2)}) %all-to-all-start.3) | async-done | bytes 786464 | tf_op jit(solution)/shard_map/all_to_all | solution.py:41
  119.7 3.4 %shard_map.185 = bf16[4,176,768]{2,1,0:T(8,128)(2,1)} custom-call(bf16[768,512]{1,0:T(8,128)(2,1)S(1)} %bitcast.152, bf16[768,512]{1,0:T(8,128)(2,1)S(1)} %collective-permute-done.9.other_ref, bf16[512,768]{1,0:T(8,128)(2,1)S(1)} %pad_maximum_fusion.w_own_ref, bf16[512,768]{1,0:T(8,128)(2,1)S(1)} %collective-permute-done.7.w_other_ref, ...), custom_call_target="tpu_custom_call" | custom-call | flops 100000000 | bytes 500000 | tf_op jit(solution)/shard_map/pallas_call | solution.py:151
  123.5 28.0 %all_to_all.36 = bf16[32,24,512]{2,1,0:T(8,128)(2,1)S(1)} all-to-all(bf16[32,24,512]{2,1,0:T(8,128)(2,1)S(1)} %bitcast.158), channel_id=1, replica_groups=mesh['x'=4,'y'=8,'l'=2,'h'=4,'c'=2] {'x','y'}, dimensions={0} | all-to-all | bytes 1572864 | tf_op jit(solution)/shard_map/all_to_all | solution.py:41
  151.5 3.6 %reduce-scatter.3.cloned.1.call-done = bf16[176,768]{1,0:T(8,128)(2,1)} async-done(((bf16[704,768]{1,0:T(8,128)(2,1)}), bf16[176,768]{1,0:T(8,128)(2,1)}) %reduce-scatter.3.cloned.1.call-update) | async-done | bytes 270352 | tf_op jit(solution)/shard_map/reduce_scatter | solution.py:270
  159.3 3.4 %shard_map.187 = bf16[4,176,768]{2,1,0:T(8,128)(2,1)} custom-call(bf16[768,512]{1,0:T(8,128)(2,1)S(1)} %bitcast.154, bf16[768,512]{1,0:T(8,128)(2,1)S(1)} %collective-permute-done.11.other_ref, bf16[512,768]{1,0:T(8,128)(2,1)S(1)} %pad_maximum_fusion.w_own_ref, bf16[512,768]{1,0:T(8,128)(2,1)S(1)} %collective-permute-done.7.w_other_ref, ...), custom_call_target="tpu_custom_call" | custom-call | flops 100000000 | bytes 500000 | tf_op jit(solution)/shard_map/pallas_call | solution.py:151
  164.0 16.8 %all_gather.10.own_ref = bf16[672,384]{1,0:T(8,128)(2,1)S(1)} all-gather(bf16[168,384]{1,0:T(8,128)(2,1)S(1)} %fusion.14), channel_id=1, replica_groups=mesh['x'=4,'y'=8,'l'=2,'h'=4,'c'=2] {'h'}, dimensions={0}, use_global_device_ids=true | all-gather | bytes 645120 | tf_op jit(solution)/shard_map/all_gather | solution.py:277
  186.7 11.4 %all-to-all-start.5 = ((bf16[32,24,512]{2,1,0:T(8,128)(2,1)}), bf16[32,24,512]{2,1,0:T(8,128)(2,1)S(1)}, u32[]{:S(2)}, u32[]{:S(2)}) async-start(bf16[32,24,512]{2,1,0:T(8,128)(2,1)} %bitcast.50), calls=%async_computation.6 | async-start | bytes 1572864 | tf_op jit(solution)/shard_map/all_to_all | solution.py:41
  201.4 15.8 %all_gather.11.own_ref = bf16[672,384]{1,0:T(8,128)(2,1)S(1)} all-gather(bf16[168,384]{1,0:T(8,128)(2,1)S(1)} %fusion.13), channel_id=1, replica_groups=mesh['x'=4,'y'=8,'l'=2,'h'=4,'c'=2] {'h'}, dimensions={0}, use_global_device_ids=true | all-gather | bytes 645120 | tf_op jit(solution)/shard_map/all_gather | solution.py:277
  217.2 4.2 %all-to-all-done.5 = bf16[32,24,512]{2,1,0:T(8,128)(2,1)S(1)} async-done(((bf16[32,24,512]{2,1,0:T(8,128)(2,1)}), bf16[32,24,512]{2,1,0:T(8,128)(2,1)S(1)}, u32[]{:S(2)}, u32[]{:S(2)}) %all-to-all-start.5) | async-done | bytes 786464 | tf_op jit(solution)/shard_map/all_to_all | solution.py:41
  226.4 29.3 %all_to_all.37 = bf16[32,24,512]{2,1,0:T(8,128)(2,1)S(1)} all-to-all(bf16[32,24,512]{2,1,0:T(8,128)(2,1)S(1)} %bitcast.150), channel_id=1, replica_groups=mesh['x'=4,'y'=8,'l'=2,'h'=4,'c'=2] {'x','y'}, dimensions={0} | all-to-all | bytes 1572864 | tf_op jit(solution)/shard_map/all_to_all | solution.py:41
  259.0 3.9 %collective-permute-done.13 = bf16[128,512]{1,0:T(8,128)(2,1)S(1)} collective-permute-done((bf16[128,512]{1,0:T(8,128)(2,1)S(1)}, bf16[128,512]{1,0:T(8,128)(2,1)S(1)}, u32[]{:S(2)}, u32[]{:S(2)}) %collective-permute-start.13) | collective-permute-done | bytes 131104 | tf_op jit(solution)/shard_map/ppermute | solution.py:37
  (118 shorter events, 48.3 us)
Async XLA Ops:
  7.2 21.9 %copy-start = (bf16[128,512]{1,0:T(8,128)(2,1)S(1)}, bf16[128,512]{1,0:T(8,128)(2,1)}, u32[]{:S(2)}) copy-start(bf16[128,512]{1,0:T(8,128)(2,1)} %param.18) | copy-start | bytes 393220
  7.2 63.0 %all-gather.2.cloned.1.call-start = ((), (), s32[]{:S(2)}) async-start(), calls=%async_computation.9 | async-start | bytes 1179648 | tf_op jit(solution)/shard_map/all_gather | solution.py:210
  8.0 20.9 %collective-permute-start = (bf16[128,256]{1,0:T(8,128)(2,1)S(1)}, bf16[128,256]{1,0:T(8,128)(2,1)S(1)}, u32[]{:S(2)}, u32[]{:S(2)}) collective-permute-start(bf16[128,256]{1,0:T(8,128)(2,1)S(1)} %pad_maximum_fusion.2), channel_id=1, source_target_pairs={{0,24},{8,32},{16,40},{24,48},{32,56},{40,64},{48,72},{56,80},{64,... | collective-permute-start | bytes 196616 | tf_op jit(solution)/shard_map/ppermute | solution.py:46
  13.3 15.7 %collective-permute-start.1 = (bf16[128,256]{1,0:T(8,128)(2,1)S(1)}, bf16[128,256]{1,0:T(8,128)(2,1)S(1)}, u32[]{:S(2)}, u32[]{:S(2)}) collective-permute-start(bf16[128,256]{1,0:T(8,128)(2,1)S(1)} %pad_maximum_fusion.2), channel_id=1, source_target_pairs={{0,16},{8,24},{16,32},{24,40},{32,48},{40,56},{48,64},{56,72},{64,... | collective-permute-start | bytes 196616 | tf_op jit(solution)/shard_map/ppermute | solution.py:46
  16.8 12.2 %collective-permute-start.2 = (bf16[128,256]{1,0:T(8,128)(2,1)S(1)}, bf16[128,256]{1,0:T(8,128)(2,1)S(1)}, u32[]{:S(2)}, u32[]{:S(2)}) collective-permute-start(bf16[128,256]{1,0:T(8,128)(2,1)S(1)} %pad_maximum_fusion.2), channel_id=1, source_target_pairs={{0,8},{8,16},{16,24},{24,32},{32,40},{40,48},{48,56},{56,64},{64,7... | collective-permute-start | bytes 196616 | tf_op jit(solution)/shard_map/ppermute | solution.py:46
  20.6 6.7 %collective-permute-start.3 = (bf16[64,512]{1,0:T(8,128)(2,1)}, bf16[64,512]{1,0:T(8,128)(2,1)S(1)}, u32[]{:S(2)}, u32[]{:S(2)}) collective-permute-start(bf16[64,512]{1,0:T(8,128)(2,1)} %param.21), channel_id=1, source_target_pairs={{0,8},{8,0},{1,9},{9,1},{2,10},{10,2},{3,11},{11,3},{4,12},{12,4},... | collective-permute-start | bytes 196616 | tf_op jit(solution)/shard_map/ppermute | solution.py:37
  30.5 39.3 %copy-start.11 = (bf16[128,8]{0,1:T(8,128)(2,1)S(1)}, bf16[128,8]{0,1:T(8,128)(2,1)}, u32[]{:S(2)}) copy-start(bf16[128,8]{0,1:T(8,128)(2,1)} %param.28) | copy-start | bytes 6148
  55.5 12.4 %all-to-all-start.1 = ((bf16[4,128,512]{2,1,0:T(8,128)(2,1)}), bf16[4,128,512]{2,1,0:T(8,128)(2,1)S(1)}, u32[]{:S(2)}, u32[]{:S(2)}) async-start(bf16[4,128,512]{2,1,0:T(8,128)(2,1)} %all_to_all.35), calls=%async_computation.1 | async-start | bytes 1048576 | tf_op jit(solution)/shard_map/all_to_all | solution.py:41
  67.9 3.9 %collective-permute-start.4 = (bf16[512,512]{1,0:T(8,128)(2,1)S(1)}, bf16[512,512]{1,0:T(8,128)(2,1)S(1)}, u32[]{:S(2)}, u32[]{:S(2)}) collective-permute-start(bf16[512,512]{1,0:T(8,128)(2,1)S(1)} %bitcast.160), channel_id=1, source_target_pairs={{0,1},{1,0},{2,3},{3,2},{4,5},{5,4},{6,7},{7,6},{8,9},{9,8},{10,11... | collective-permute-start | bytes 1572872 | tf_op jit(solution)/shard_map/ppermute | solution.py:37
  73.7 13.6 %all-to-all-start.2 = ((bf16[4,128,512]{2,1,0:T(8,128)(2,1)}), bf16[4,128,512]{2,1,0:T(8,128)(2,1)S(1)}, u32[]{:S(2)}, u32[]{:S(2)}) async-start(bf16[4,128,512]{2,1,0:T(8,128)(2,1)} %bitcast.7), calls=%async_computation.2 | async-start | bytes 1048576 | tf_op jit(solution)/shard_map/all_to_all | solution.py:41
  89.3 26.2 %all-to-all-start.3 = ((bf16[32,24,512]{2,1,0:T(8,128)(2,1)}), bf16[32,24,512]{2,1,0:T(8,128)(2,1)S(1)}, u32[]{:S(2)}, u32[]{:S(2)}) async-start(bf16[32,24,512]{2,1,0:T(8,128)(2,1)} %bitcast.28), calls=%async_computation.3 | async-start | bytes 1572864 | tf_op jit(solution)/shard_map/all_to_all | solution.py:41
  94.1 61.0 %reduce-scatter.3.cloned.1.call-start = ((), (), s32[]{:S(2)}) async-start(), calls=%async_computation.10 | async-start | bytes 1351680 | tf_op jit(solution)/shard_map/reduce_scatter | solution.py:270
  94.4 25.3 %copy-start.2 = (bf16[168,192]{1,0:T(8,128)(2,1)S(1)}, bf16[168,192]{1,0:T(8,128)(2,1)}, u32[]{:S(2)}) copy-start(bf16[168,192]{1,0:T(8,128)(2,1)} %constant.97.clone.pick_ref) | copy-start | bytes 193540
  94.4 15.4 %collective-permute-start.7 = (bf16[512,768]{1,0:T(8,128)(2,1)S(1)}, bf16[512,768]{1,0:T(8,128)(2,1)S(1)}, u32[]{:S(2)}, u32[]{:S(2)}) collective-permute-start(bf16[512,768]{1,0:T(8,128)(2,1)S(1)} %pad_maximum_fusion.1), channel_id=1, source_target_pairs={{0,1},{1,0},{2,3},{3,2},{4,5},{5,4},{6,7},{7,6},{8,9},{9,8},{10,11... | collective-permute-start | bytes 2359304 | tf_op jit(solution)/shard_map/ppermute | solution.py:37
  96.5 5.7 %collective-permute-start.6 = (f32[128,24]{0,1:T(8,128)S(1)}, f32[128,24]{0,1:T(8,128)S(1)}, u32[]{:S(2)}, u32[]{:S(2)}) collective-permute-start(f32[128,24]{0,1:T(8,128)S(1)} %get-tuple-element.82), channel_id=1, source_target_pairs={{0,8},{8,0},{1,9},{9,1},{2,10},{10,2},{3,11},{11,3},{4,12},{12,4},... | collective-permute-start | bytes 36872 | tf_op jit(solution)/shard_map/ppermute | solution.py:37
  100.0 6.2 %collective-permute-start.8 = (f32[1,512]{1,0:T(1,128)S(1)}, f32[1,512]{1,0:T(1,128)S(1)}, u32[]{:S(2)}, u32[]{:S(2)}) collective-permute-start(f32[1,512]{1,0:T(1,128)S(1)} %bitcast.155), channel_id=1, source_target_pairs={{0,1},{1,0},{2,3},{3,2},{4,5},{5,4},{6,7},{7,6},{8,9},{9,8},{10,11... | collective-permute-start | bytes 6152 | tf_op jit(solution)/shard_map/ppermute | solution.py:37
  102.2 7.6 %collective-permute-start.5 = (bf16[128,512]{1,0:T(8,128)(2,1)S(1)}, bf16[128,512]{1,0:T(8,128)(2,1)S(1)}, u32[]{:S(2)}, u32[]{:S(2)}) collective-permute-start(bf16[128,512]{1,0:T(8,128)(2,1)S(1)} %get-tuple-element.54), channel_id=1, source_target_pairs={{0,8},{8,0},{1,9},{9,1},{2,10},{10,2},{3,11},{11,3},{4,12},{12,4},... | collective-permute-start | bytes 393224 | tf_op jit(solution)/shard_map/ppermute | solution.py:37
  115.5 4.2 %collective-permute-start.9 = (bf16[768,512]{1,0:T(8,128)(2,1)S(1)}, bf16[768,512]{1,0:T(8,128)(2,1)S(1)}, u32[]{:S(2)}, u32[]{:S(2)}) collective-permute-start(bf16[768,512]{1,0:T(8,128)(2,1)S(1)} %bitcast.151), channel_id=1, source_target_pairs={{0,1},{1,0},{2,3},{3,2},{4,5},{5,4},{6,7},{7,6},{8,9},{9,8},{10,11... | collective-permute-start | bytes 2359304 | tf_op jit(solution)/shard_map/ppermute | solution.py:37
  123.1 76.3 %reduce-scatter.5.cloned.1.call-start = ((), (), s32[]{:S(2)}) async-start(), calls=%async_computation.11 | async-start | bytes 1351680 | tf_op jit(solution)/shard_map/reduce_scatter | solution.py:270
  155.2 4.2 %collective-permute-start.11 = (bf16[768,512]{1,0:T(8,128)(2,1)S(1)}, bf16[768,512]{1,0:T(8,128)(2,1)S(1)}, u32[]{:S(2)}, u32[]{:S(2)}) collective-permute-start(bf16[768,512]{1,0:T(8,128)(2,1)S(1)} %bitcast.153), channel_id=1, source_target_pairs={{0,1},{1,0},{2,3},{3,2},{4,5},{5,4},{6,7},{7,6},{8,9},{9,8},{10,11... | collective-permute-start | bytes 2359304 | tf_op jit(solution)/shard_map/ppermute | solution.py:37
  180.8 3.8 %collective-permute-start.10 = (bf16[672,384]{1,0:T(8,128)(2,1)S(1)}, bf16[672,384]{1,0:T(8,128)(2,1)S(1)}, u32[]{:S(2)}, u32[]{:S(2)}) collective-permute-start(bf16[672,384]{1,0:T(8,128)(2,1)S(1)} %all_gather.10.own_ref), channel_id=1, source_target_pairs={{0,1},{1,0},{2,3},{3,2},{4,5},{5,4},{6,7},{7,6},{8,9},{9,8},{10,11... | collective-permute-start | bytes 1548296 | tf_op jit(solution)/shard_map/ppermute | solution.py:37
  186.7 34.7 %all-to-all-start.5 = ((bf16[32,24,512]{2,1,0:T(8,128)(2,1)}), bf16[32,24,512]{2,1,0:T(8,128)(2,1)S(1)}, u32[]{:S(2)}, u32[]{:S(2)}) async-start(bf16[32,24,512]{2,1,0:T(8,128)(2,1)} %bitcast.50), calls=%async_computation.6 | async-start | bytes 1572864 | tf_op jit(solution)/shard_map/all_to_all | solution.py:41
  221.4 3.8 %collective-permute-start.12 = (bf16[672,384]{1,0:T(8,128)(2,1)S(1)}, bf16[672,384]{1,0:T(8,128)(2,1)S(1)}, u32[]{:S(2)}, u32[]{:S(2)}) collective-permute-start(bf16[672,384]{1,0:T(8,128)(2,1)S(1)} %all_gather.11.own_ref), channel_id=1, source_target_pairs={{0,1},{1,0},{2,3},{3,2},{4,5},{5,4},{6,7},{7,6},{8,9},{9,8},{10,11... | collective-permute-start | bytes 1548296 | tf_op jit(solution)/shard_map/ppermute | solution.py:37
  256.1 6.9 %collective-permute-start.13 = (bf16[128,512]{1,0:T(8,128)(2,1)S(1)}, bf16[128,512]{1,0:T(8,128)(2,1)S(1)}, u32[]{:S(2)}, u32[]{:S(2)}) collective-permute-start(bf16[128,512]{1,0:T(8,128)(2,1)S(1)} %convolution_convert_fusion.2), channel_id=1, source_target_pairs={{0,8},{8,0},{1,9},{9,1},{2,10},{10,2},{3,11},{11,3},{4,12},{12,4},... | collective-permute-start | bytes 393224 | tf_op jit(solution)/shard_map/ppermute | solution.py:37
  (11 other events, 76.2 us)
Sparse Core Ops, SparseCore 0:
  29.1 41.0 all-gather.1
  123.2 31.8 reduce-scatter.2
  162.9 36.4 reduce-scatter.4

commit v10 on v9

--- a/solution.py
+++ b/solution.py
@@ -1,3 +1,5 @@
+import functools
+
 import jax
 import jax.numpy as jnp
 import numpy as np
@@ -14,18 +16,11 @@
 FF = 768
 FIX = 32
 TOK = 128
-SLOTS = 21
-GROUP = 24
 NX, NY, NL, NH, NC = 4, 8, 2, 4, 2
 N_CTX = NX * NY * NL
-GRID = NX * NY
-SENT = GRID * GROUP
-ROWS = GRID * SLOTS
-SHARE = ROWS // NH
-LANES = 256
+PEERS = 8
 EXTRA = 8
-PACK = 8 * SLOTS
-PACK_SENT = 8 * GROUP
+PARTS = ((0, 8, 8), (8, 13, 16))
 SLICE = D // (NH * NC)
 CTX = ("x", "y", "l")
 f32, bf16 = jnp.float32, jnp.bfloat16
@@ -97,87 +92,97 @@
     return ids.astype(f32), rank
 
 
-def row_slots(table, side):
-    ids, rank, gates = table[:TOPK], table[TOPK : 2 * TOPK], table[2 * TOPK :]
-    column = jnp.floor(ids * 0.5)
-    return jnp.where(ids - 2.0 * column == side, column * GROUP + rank, -1.0), gates
-
-
-def spread(slots, values):
-    row_ids = jnp.arange(SENT, dtype=f32)[:, None]
-    total = jnp.zeros((SENT, slots.shape[1]), f32)
+def spread(slots, values, sent):
+    row_ids = jnp.arange(sent, dtype=f32)[:, None]
+    total = jnp.zeros((sent, slots.shape[1]), f32)
     for k in range(TOPK):
         total = total + jnp.where(slots[k][None, :] == row_ids, values[k][None, :], 0.0)
     return total.astype(bf16)
 
 
-def packing():
-    place = np.arange(PACK)
-    return (place // SLOTS * GROUP + place % SLOTS)[:, None] == np.arange(PACK_SENT)[None, :]
+def packing(used, group):
+    place = np.arange(PEERS * used)
+    return (place // used * group + place % used)[:, None] == np.arange(PEERS * group)[None, :]
 
 
 def products_kernel(
-    own_ref, other_ref, w_own_ref, w_other_ref, inv_own_ref, inv_other_ref, pick_ref, part_ref
+    used, group, own_ref, other_ref, w_own_ref, w_other_ref, inv_own_ref, inv_other_ref, pick_ref, part_ref
 ):
-    pick = pick_ref[...]
+    share, pack = 2 * PEERS * used, PEERS * group
+    lanes = -(-share // 128) * 128
     ones = jnp.ones((8, SLICE), bf16)
-    blank = jnp.zeros((LANES - SHARE, SLICE), bf16)
     row = lax.broadcasted_iota(jnp.int32, (EXTRA, FF), 0)
+
+    def packed(ref, h):
+        if used == group:
+            return ref[h * share : (h + 1) * share].astype(f32)
+        pick = pick_ref[...]
+        halves = [
+            jnp.dot(
+                pick,
+                ref[(2 * h + i) * pack : (2 * h + i + 1) * pack],
+                preferred_element_type=f32,
+            )
+            for i in range(2)
+        ]
+        return jnp.concatenate(halves, axis=0)
 
     def squares(rows, inverse_ref):
         weighted = (rows * rows * inverse_ref[...]).astype(bf16)
+        if lanes > share:
+            weighted = jnp.concatenate(
+                [weighted, jnp.zeros((lanes - share, SLICE), bf16)], axis=0
+            )
         return lax.dot_general(
-            ones,
-            jnp.concatenate([weighted, blank], axis=0),
-            (((1,), (1,)), ((), ())),
-            preferred_element_type=f32,
+            ones, weighted, (((1,), (1,)), ((), ())), preferred_element_type=f32
         )
 
     for h in range(NH):
-        taken = slice(h * PACK_SENT, (h + 1) * PACK_SENT)
-        own = jnp.dot(pick, own_ref[taken], preferred_element_type=f32)
-        other = jnp.dot(pick, other_ref[taken], preferred_element_type=f32)
+        own, other = packed(own_ref, h), packed(other_ref, h)
         part = jnp.dot(own.astype(bf16), w_own_ref[...], preferred_element_type=f32) + jnp.dot(
             other.astype(bf16), w_other_ref[...], preferred_element_type=f32
         )
         total = squares(own, inv_own_ref) + squares(other, inv_other_ref)
-        total = jnp.concatenate([total, jnp.zeros((8, FF - LANES), f32)], axis=1)
+        total = jnp.concatenate([total, jnp.zeros((8, FF - lanes), f32)], axis=1)
         high = total.astype(bf16).astype(f32)
         tail = jnp.where(row == 0, high, jnp.where(row == 1, total - high, 0.0))
         part_ref[h] = jnp.concatenate([part, tail], axis=0).astype(bf16)
 
 
-def products(own, other, w_own, w_other, inv_own, inv_other):
+def products(used, group, own, other, w_own, w_other, inv_own, inv_other):
     return pl.pallas_call(
-        products_kernel,
-        out_shape=jax.ShapeDtypeStruct((NH, SHARE + EXTRA, FF), bf16),
+        functools.partial(products_kernel, used, group),
+        out_shape=jax.ShapeDtypeStruct((NH, 2 * PEERS * used + EXTRA, FF), bf16),
         compiler_params=pltpu.CompilerParams(vmem_limit_bytes=48 * 1024 * 1024),
         cost_estimate=pl.CostEstimate(flops=100_000_000, bytes_accessed=500_000, transcendentals=0),
-    )(own, other, w_own, w_other, inv_own, inv_other, jnp.asarray(packing(), bf16))
-
-
-def results_kernel(own_ref, other_ref, down_own_ref, down_other_ref, place_ref, out_ref):
-    place = place_ref[...]
-    for i in range(NH // 2):
-        rows = slice(2 * i * SHARE, 2 * (i + 1) * SHARE)
+    )(own, other, w_own, w_other, inv_own, inv_other, jnp.asarray(packing(used, group), bf16))
+
+
+def results_kernel(used, group, own_ref, other_ref, down_own_ref, down_other_ref, place_ref, out_ref):
+    share, pack = 2 * PEERS * used, PEERS * group
+    for h in range(NH):
+        rows = slice(h * share, (h + 1) * share)
         part = jnp.dot(own_ref[rows], down_own_ref[...], preferred_element_type=f32) + jnp.dot(
             other_ref[rows], down_other_ref[...], preferred_element_type=f32
         )
-        for j in range(2):
-            rows = part[j * PACK : (j + 1) * PACK].astype(bf16)
-            start = (2 * i + j) * PACK_SENT
-            out_ref[start : start + PACK_SENT] = jnp.dot(
-                place, rows, preferred_element_type=f32
+        if used == group:
+            out_ref[rows] = part.astype(bf16)
+            continue
+        for i in range(2):
+            rows = part[i * PEERS * used : (i + 1) * PEERS * used].astype(bf16)
+            start = (2 * h + i) * pack
+            out_ref[start : start + pack] = jnp.dot(
+                place_ref[...], rows, preferred_element_type=f32
             ).astype(bf16)
 
 
-def expert_results(own, other, down_own, down_other):
+def expert_results(used, group, own, other, down_own, down_other):
     return pl.pallas_call(
-        results_kernel,
-        out_shape=jax.ShapeDtypeStruct((SENT, SLICE), bf16),
+        functools.partial(results_kernel, used, group),
+        out_shape=jax.ShapeDtypeStruct((N_CTX * group, SLICE), bf16),
         compiler_params=pltpu.CompilerParams(vmem_limit_bytes=48 * 1024 * 1024),
         cost_estimate=pl.CostEstimate(flops=100_000_000, bytes_accessed=500_000, transcendentals=0),
-    )(own, other, down_own, down_other, jnp.asarray(packing().T, bf16))
+    )(own, other, down_own, down_other, jnp.asarray(packing(used, group).T, bf16))
 
 
 def body(
@@ -222,14 +227,19 @@
         lax.dynamic_slice_in_dim(quarter, (1 - core) * SLICE, SLICE, 0),
         preferred_element_type=f32,
     )
-    partial, pred_ids, fix_pair, w_gate, w_up, norm_gain = lax.optimization_barrier(
-        (partial.astype(bf16), pred_ids, fix_pair, w_gate, w_up, norm_gain)
+    partial, pred_ids, fix_pair, fix_count, w_gate, w_up, norm_gain = lax.optimization_barrier(
+        (partial.astype(bf16), pred_ids, fix_pair, fix_count, w_gate, w_up, norm_gain)
     )
 
     ids, rank = slots_of(pred_ids, fix_pair, fix_expert, fix_count)
-    table = jnp.concatenate([ids, rank, route_gates.astype(f32)], axis=1)
-    slots, gates = row_slots(table.T, side.astype(f32))
-    pick = spread(slots, jnp.ones_like(slots))
+    ids, rank, gates = ids.T, rank.T, route_gates.astype(f32).T
+    lists = [
+        jnp.where((rank >= first) & (rank < first + used), ids * group + rank - first, -1.0)
+        for first, used, group in PARTS
+    ]
+    picks = [
+        spread(slots, jnp.ones_like(slots), N_CTX * part[2]) for slots, part in zip(lists, PARTS)
+    ]
 
     def columns(which):
         return jnp.concatenate(
@@ -248,55 +258,56 @@
     other_inverse = swap(inverse, "c")
 
     terms = exchange(partial.reshape(NX, tokens, SLICE), "x")
-    other_slots, other_gates = row_slots(swap(table, "l").T, side.astype(f32))
-    other_pick = spread(other_slots, jnp.ones_like(other_slots))
-    terms, pick = lax.optimization_barrier((terms, pick))
+    terms, pick = lax.optimization_barrier((terms, picks[0]))
     stream = residual.astype(f32) + jnp.sum(terms.astype(f32), axis=0)
 
     scaled = (stream * gain).astype(bf16)
-    beside = swap(scaled, "l")
-
-    def through(rows):
-        return exchange(rows.reshape(GRID, GROUP, SLICE), ("x", "y")).reshape(SENT, SLICE)
-
-    def sent(pick, rows):
-        return through(jnp.dot(pick, rows, preferred_element_type=f32).astype(bf16))
-
-    def share_products(rows):
-        return products(rows, swap(rows, "c"), gate_up, other_gate_up, inverse, other_inverse)
-
-    def reduced(part):
-        flat = part.reshape(NH * (SHARE + EXTRA), FF)
-        return lax.psum_scatter(flat, "h", scatter_dimension=0, tiled=True)
-
-    def gathered(sums):
+
+    def through(part, rows):
+        group = PARTS[part][2]
+        return exchange(rows.reshape(N_CTX, group, SLICE), CTX).reshape(N_CTX * group, SLICE)
+
+    def sent(part, pick):
+        return through(part, jnp.dot(pick, scaled, preferred_element_type=f32).astype(bf16))
+
+    def reduced(part, rows):
+        sums = products(
+            *PARTS[part][1:], rows, swap(rows, "c"), gate_up, other_gate_up, inverse, other_inverse
+        )
+        return lax.psum_scatter(
+            sums.reshape(-1, FF), "h", scatter_dimension=0, tiled=True
+        )
+
+    def gathered(part, sums):
+        share = 2 * PEERS * PARTS[part][1]
         sums = sums.astype(f32)
-        total = (sums[SHARE] + sums[SHARE + 1])[:SHARE]
-        sums = sums[:SHARE] * lax.rsqrt(total / D + epsilon)[:, None]
+        total = (sums[share] + sums[share + 1])[:share]
+        sums = sums[:share] * lax.rsqrt(total / D + epsilon)[:, None]
         hidden = (jax.nn.silu(sums[:, :half]) * sums[:, half:]).astype(bf16)
         return lax.all_gather(hidden, "h", axis=0, tiled=True)
 
-    def finished(hidden):
-        return expert_results(hidden, swap(hidden, "c"), down, other_down)
-
-    first = sent(pick, scaled)
-    first, beside, other_pick, gate_up, other_gate_up, inverse, other_inverse = (
-        lax.optimization_barrier(
-            (first, beside, other_pick, gate_up, other_gate_up, inverse, other_inverse)
-        )
-    )
-    first = reduced(share_products(first))
-    second = sent(other_pick, beside)
+    def finished(part, hidden):
+        rows = expert_results(*PARTS[part][1:], hidden, swap(hidden, "c"), down, other_down)
+        return through(part, rows)
+
+    def combined(combine, rows):
+        return jnp.einsum("rt,rd->td", combine, rows, preferred_element_type=f32)
+
+    first = sent(0, pick)
+    first, other_pick, gate_up, other_gate_up, inverse, other_inverse = lax.optimization_barrier(
+        (first, picks[1], gate_up, other_gate_up, inverse, other_inverse)
+    )
+    first = reduced(0, first)
+    second = sent(1, other_pick)
     first, second = lax.optimization_barrier((first, second))
-    second = reduced(share_products(second))
-    first = through(finished(gathered(first)))
-    hidden = gathered(second)
-    combine = spread(other_slots, other_gates)
+    second = reduced(1, second)
+    first = finished(0, gathered(0, first))
+    hidden = gathered(1, second)
+    combine = spread(lists[1], gates, N_CTX * PARTS[1][2])
     first, hidden, combine = lax.optimization_barrier((first, hidden, combine))
-    second = through(finished(hidden))
-    mixed = jnp.einsum("rt,rd->td", spread(slots, gates), first, preferred_element_type=f32)
-    other_mixed = jnp.einsum("rt,rd->td", combine, second, preferred_element_type=f32)
-    expert_out = mixed + swap(other_mixed.astype(bf16), "l").astype(f32)
+    second = finished(1, hidden)
+    expert_out = combined(spread(lists[0], gates, N_CTX * PARTS[0][2]), first)
+    expert_out = expert_out + combined(combine, second)
     return stream.astype(bf16), expert_out.astype(bf16)
 
 

time: 272 us -> 285 us (1.048)
  the two profiles are of different devices: /device:TPU:8 before, /device:TPU:128 now
where the time goes in v10:
time: 285 us; the launch traced here: 284 us
  waiting for transfers between devices  119 us (42%)
  starting transfers between devices  86 us (30%)
  blocking collectives  34.8 us (12%)
  between operations  15.1 us (5%)
  Pallas kernels  11.2 us (4%)
  matrix products  8.18 us (3%)
  other arithmetic  6.37 us (2%)
  local copies, waits for them, and re-layouts  3.87 us (1%)
    all_to_all x7, waiting for transfers between devices, exchange(): return lax.all_to_all(blocks, axes, split_axis=0, concat_axis=0, tiled=True)  91.7 us
    all_to_all x7, starting transfers between devices, exchange(): return lax.all_to_all(blocks, axes, split_axis=0, concat_axis=0, tiled=True)  56.2 us
    all_gather x2, blocking collectives, gathered(): return lax.all_gather(hidden, 'h', axis=0, tiled=True)  34.8 us
    ppermute x8, starting transfers between devices, swap(): return lax.ppermute(block, axis, [(0, 1), (1, 0)])  18.3 us
    reduce_scatter x2, waiting for transfers between devices, reduced(): lax.psum_scatter(sums.reshape(-1, FF), 'h', scatter_dimension=0, tiled=True)  15.4 us
    ppermute x3, starting transfers between devices, from_behind(): return lax.ppermute(block, CTX, route)  11.4 us
    ppermute x8, waiting for transfers between devices, swap(): return lax.ppermute(block, axis, [(0, 1), (1, 0)])  8.87 us
    pallas_call x2, Pallas kernels, products(): pl.pallas_call(functools.partial(products_kernel, used, group), out_shape...  7.01 us
  transfers between devices with their start and end apart: 21, of which 13 were waited for; matrix products, arithmetic and copies ran while one was open for 4% of the time, Pallas kernels for 2%

profile of v10, /device:TPU:128, one launch (start us, length us, event | category | flops | bytes accessed | tf_op | source)
XLA Modules:
  0.0 284.3 jit_solution(12756103881996658822)
XLA Ops:
  8.0 5.3 %collective-permute-start = (bf16[128,256]{1,0:T(8,128)(2,1)S(1)}, bf16[128,256]{1,0:T(8,128)(2,1)S(1)}, u32[]{:S(2)}, u32[]{:S(2)}) collective-permute-start(bf16[128,256]{1,0:T(8,128)(2,1)S(1)} %pad_maximum_fusion.2), channel_id=1, source_target_pairs={{0,24},{8,32},{16,40},{24,48},{32,56},{40,64},{48,72},{56,80},{64,... | collective-permute-start | bytes 196616 | tf_op jit(solution)/shard_map/ppermute | solution.py:41
  13.3 3.5 %collective-permute-start.1 = (bf16[128,256]{1,0:T(8,128)(2,1)S(1)}, bf16[128,256]{1,0:T(8,128)(2,1)S(1)}, u32[]{:S(2)}, u32[]{:S(2)}) collective-permute-start(bf16[128,256]{1,0:T(8,128)(2,1)S(1)} %pad_maximum_fusion.2), channel_id=1, source_target_pairs={{0,16},{8,24},{16,32},{24,40},{32,48},{40,56},{48,64},{56,72},{64,... | collective-permute-start | bytes 196616 | tf_op jit(solution)/shard_map/ppermute | solution.py:41
  19.4 4.3 %collective-permute-start.3 = (bf16[64,512]{1,0:T(8,128)(2,1)}, bf16[64,512]{1,0:T(8,128)(2,1)S(1)}, u32[]{:S(2)}, u32[]{:S(2)}) collective-permute-start(bf16[64,512]{1,0:T(8,128)(2,1)} %param.21), channel_id=1, source_target_pairs={{0,8},{8,0},{1,9},{9,1},{2,10},{10,2},{3,11},{11,3},{4,12},{12,4},... | collective-permute-start | bytes 196616 | tf_op jit(solution)/shard_map/ppermute | solution.py:32
  24.0 2.8 collective-permute-done.3
  30.7 8.1 %all-to-all-start = ((bf16[4,128,512]{2,1,0:T(8,128)(2,1)}), bf16[4,128,512]{2,1,0:T(8,128)(2,1)}, u32[]{:S(2)}, u32[]{:S(2)}) async-start(bf16[4,128,512]{2,1,0:T(8,128)(2,1)} %broadcast_in_dim.266), calls=%async_computation | async-start | bytes 1048576 | tf_op jit(solution)/shard_map/all_to_all | solution.py:36
  39.5 9.7 %all-to-all-done = bf16[4,128,512]{2,1,0:T(8,128)(2,1)} async-done(((bf16[4,128,512]{2,1,0:T(8,128)(2,1)}), bf16[4,128,512]{2,1,0:T(8,128)(2,1)}, u32[]{:S(2)}, u32[]{:S(2)}) %all-to-all-start) | async-done | bytes 524320 | tf_op jit(solution)/shard_map/all_to_all | solution.py:36
  49.3 6.2 %all-to-all-start.1 = ((bf16[4,128,512]{2,1,0:T(8,128)(2,1)}), bf16[4,128,512]{2,1,0:T(8,128)(2,1)S(1)}, u32[]{:S(2)}, u32[]{:S(2)}) async-start(bf16[4,128,512]{2,1,0:T(8,128)(2,1)} %all-to-all-done), calls=%async_computation.1 | async-start | bytes 1048576 | tf_op jit(solution)/shard_map/all_to_all | solution.py:36
  55.5 8.8 %all-to-all-done.1 = bf16[4,128,512]{2,1,0:T(8,128)(2,1)S(1)} async-done(((bf16[4,128,512]{2,1,0:T(8,128)(2,1)}), bf16[4,128,512]{2,1,0:T(8,128)(2,1)S(1)}, u32[]{:S(2)}, u32[]{:S(2)}) %all-to-all-start.1) | async-done | bytes 524320 | tf_op jit(solution)/shard_map/all_to_all | solution.py:36
  66.2 2.7 all-gather.2.cloned.1.call-done
  72.4 4.4 %all-to-all-start.2 = ((bf16[4,128,512]{2,1,0:T(8,128)(2,1)}), bf16[4,128,512]{2,1,0:T(8,128)(2,1)S(1)}, u32[]{:S(2)}, u32[]{:S(2)}) async-start(bf16[4,128,512]{2,1,0:T(8,128)(2,1)} %bitcast.7), calls=%async_computation.2 | async-start | bytes 1048576 | tf_op jit(solution)/shard_map/all_to_all | solution.py:36
  77.3 7.6 %all-to-all-done.2 = bf16[4,128,512]{2,1,0:T(8,128)(2,1)S(1)} async-done(((bf16[4,128,512]{2,1,0:T(8,128)(2,1)}), bf16[4,128,512]{2,1,0:T(8,128)(2,1)S(1)}, u32[]{:S(2)}, u32[]{:S(2)}) %all-to-all-start.2) | async-done | bytes 524320 | tf_op jit(solution)/shard_map/all_to_all | solution.py:36
  86.8 7.0 %all-to-all-start.3 = ((bf16[64,8,512]{2,1,0:T(8,128)(2,1)}), bf16[64,8,512]{2,1,0:T(8,128)(2,1)S(1)}, u32[]{:S(2)}, u32[]{:S(2)}) async-start(bf16[64,8,512]{2,1,0:T(8,128)(2,1)} %fusion.7), calls=%async_computation.3 | async-start | bytes 1048576 | tf_op jit(solution)/shard_map/all_to_all | solution.py:36
  100.1 10.4 %all-to-all-done.3 = bf16[64,8,512]{2,1,0:T(8,128)(2,1)S(1)} async-done(((bf16[64,8,512]{2,1,0:T(8,128)(2,1)}), bf16[64,8,512]{2,1,0:T(8,128)(2,1)S(1)}, u32[]{:S(2)}, u32[]{:S(2)}) %all-to-all-start.3) | async-done | bytes 524320 | tf_op jit(solution)/shard_map/all_to_all | solution.py:36
  113.8 6.1 %all-to-all-start.4 = ((bf16[64,16,512]{2,1,0:T(8,128)(2,1)}), bf16[64,16,512]{2,1,0:T(8,128)(2,1)S(1)}, u32[]{:S(2)}, u32[]{:S(2)}) async-start(bf16[64,16,512]{2,1,0:T(8,128)(2,1)} %bitcast.146), calls=%async_computation.5 | async-start | bytes 2097152 | tf_op jit(solution)/shard_map/all_to_all | solution.py:36
  120.0 3.3 %shard_map.185 = bf16[4,136,768]{2,1,0:T(8,128)(2,1)} custom-call(bf16[512,512]{1,0:T(8,128)(2,1)S(1)} %bitcast.142, bf16[512,512]{1,0:T(8,128)(2,1)} %collective-permute-done.7.other_ref, bf16[512,768]{1,0:T(8,128)(2,1)S(1)} %pad_maximum_fusion.w_own_ref, bf16[512,768]{1,0:T(8,128)(2,1)S(1)} %collective-permute-done.5.w_other_ref, f32[1,512]{1,0:T(1,128)S(1)} %bitcast.144, ...), custom_call_target="tpu_custom_call" | custom-call | flops 100000000 | bytes 500000 | tf_op jit(solution)/shard_map/pallas_call | solution.py:153
  123.3 26.4 %all-to-all-done.4 = bf16[64,16,512]{2,1,0:T(8,128)(2,1)S(1)} async-done(((bf16[64,16,512]{2,1,0:T(8,128)(2,1)}), bf16[64,16,512]{2,1,0:T(8,128)(2,1)S(1)}, u32[]{:S(2)}, u32[]{:S(2)}) %all-to-all-start.4) | async-done | bytes 1048608 | tf_op jit(solution)/shard_map/all_to_all | solution.py:36
  149.7 8.9 %reduce-scatter.3.cloned.1.call-done = bf16[136,768]{1,0:T(8,128)(2,1)} async-done(((bf16[544,768]{1,0:T(8,128)(2,1)}), bf16[136,768]{1,0:T(8,128)(2,1)}) %reduce-scatter.3.cloned.1.call-update) | async-done | bytes 208912 | tf_op jit(solution)/shard_map/reduce_scatter | solution.py:277
  163.2 3.7 %shard_map.187 = bf16[4,216,768]{2,1,0:T(8,128)(2,1)} custom-call(bf16[1024,512]{1,0:T(8,128)(2,1)S(1)} %bitcast.140, bf16[1024,512]{1,0:T(8,128)(2,1)S(1)} %collective-permute-done.9.other_ref, bf16[512,768]{1,0:T(8,128)(2,1)S(1)} %pad_maximum_fusion.w_own_ref, bf16[512,768]{1,0:T(8,128)(2,1)S(1)} %collective-permute-done.5.w_other_ref, ...), custom_call_target="tpu_custom_call" | custom-call | flops 100000000 | bytes 500000 | tf_op jit(solution)/shard_map/pallas_call | solution.py:153
  168.1 15.2 %all_gather.10.own_ref = bf16[512,384]{1,0:T(8,128)(2,1)S(1)} all-gather(bf16[128,384]{1,0:T(8,128)(2,1)S(1)} %fusion.16), channel_id=1, replica_groups=mesh['x'=4,'y'=8,'l'=2,'h'=4,'c'=2] {'h'}, dimensions={0}, use_global_device_ids=true | all-gather | bytes 491520 | tf_op jit(solution)/shard_map/all_gather | solution.py:287
  188.4 13.3 %all-to-all-start.5 = ((bf16[64,8,512]{2,1,0:T(8,128)(2,1)}), bf16[64,8,512]{2,1,0:T(8,128)(2,1)S(1)}, u32[]{:S(2)}, u32[]{:S(2)}) async-start(bf16[64,8,512]{2,1,0:T(8,128)(2,1)} %bitcast.51), calls=%async_computation.6 | async-start | bytes 1048576 | tf_op jit(solution)/shard_map/all_to_all | solution.py:36
  201.7 6.5 %reduce-scatter.5.cloned.1.call-done = bf16[216,768]{1,0:T(8,128)(2,1)} async-done(((bf16[864,768]{1,0:T(8,128)(2,1)}), bf16[216,768]{1,0:T(8,128)(2,1)}) %reduce-scatter.5.cloned.1.call-update) | async-done | bytes 331792 | tf_op jit(solution)/shard_map/reduce_scatter | solution.py:277
  210.3 19.6 %all_gather.11.own_ref = bf16[832,384]{1,0:T(8,128)(2,1)S(1)} all-gather(bf16[208,384]{1,0:T(8,128)(2,1)S(1)} %fusion.15), channel_id=1, replica_groups=mesh['x'=4,'y'=8,'l'=2,'h'=4,'c'=2] {'h'}, dimensions={0}, use_global_device_ids=true | all-gather | bytes 798720 | tf_op jit(solution)/shard_map/all_gather | solution.py:287
  236.5 11.0 %all-to-all-start.6 = ((bf16[64,16,512]{2,1,0:T(8,128)(2,1)}), bf16[64,16,512]{2,1,0:T(8,128)(2,1)S(1)}, u32[]{:S(2)}, u32[]{:S(2)}) async-start(bf16[64,16,512]{2,1,0:T(8,128)(2,1)} %bitcast.55), calls=%async_computation.8 | async-start | bytes 2097152 | tf_op jit(solution)/shard_map/all_to_all | solution.py:36
  248.0 28.8 %all-to-all-done.6 = bf16[64,16,512]{2,1,0:T(8,128)(2,1)S(1)} async-done(((bf16[64,16,512]{2,1,0:T(8,128)(2,1)}), bf16[64,16,512]{2,1,0:T(8,128)(2,1)S(1)}, u32[]{:S(2)}, u32[]{:S(2)}) %all-to-all-start.6) | async-done | bytes 1048608 | tf_op jit(solution)/shard_map/all_to_all | solution.py:36
  (115 shorter events, 45.6 us)
Async XLA Ops:
  7.2 61.8 %all-gather.2.cloned.1.call-start = ((), (), s32[]{:S(2)}) async-start(), calls=%async_computation.9 | async-start | bytes 1179648 | tf_op jit(solution)/shard_map/all_gather | solution.py:215
  8.0 20.3 %collective-permute-start = (bf16[128,256]{1,0:T(8,128)(2,1)S(1)}, bf16[128,256]{1,0:T(8,128)(2,1)S(1)}, u32[]{:S(2)}, u32[]{:S(2)}) collective-permute-start(bf16[128,256]{1,0:T(8,128)(2,1)S(1)} %pad_maximum_fusion.2), channel_id=1, source_target_pairs={{0,24},{8,32},{16,40},{24,48},{32,56},{40,64},{48,72},{56,80},{64,... | collective-permute-start | bytes 196616 | tf_op jit(solution)/shard_map/ppermute | solution.py:41
  13.3 15.0 %collective-permute-start.1 = (bf16[128,256]{1,0:T(8,128)(2,1)S(1)}, bf16[128,256]{1,0:T(8,128)(2,1)S(1)}, u32[]{:S(2)}, u32[]{:S(2)}) collective-permute-start(bf16[128,256]{1,0:T(8,128)(2,1)S(1)} %pad_maximum_fusion.2), channel_id=1, source_target_pairs={{0,16},{8,24},{16,32},{24,40},{32,48},{40,56},{48,64},{56,72},{64,... | collective-permute-start | bytes 196616 | tf_op jit(solution)/shard_map/ppermute | solution.py:41
  16.8 11.6 %collective-permute-start.2 = (bf16[128,256]{1,0:T(8,128)(2,1)S(1)}, bf16[128,256]{1,0:T(8,128)(2,1)S(1)}, u32[]{:S(2)}, u32[]{:S(2)}) collective-permute-start(bf16[128,256]{1,0:T(8,128)(2,1)S(1)} %pad_maximum_fusion.2), channel_id=1, source_target_pairs={{0,8},{8,16},{16,24},{24,32},{32,40},{40,48},{48,56},{56,64},{64,7... | collective-permute-start | bytes 196616 | tf_op jit(solution)/shard_map/ppermute | solution.py:41
  19.4 7.3 %collective-permute-start.3 = (bf16[64,512]{1,0:T(8,128)(2,1)}, bf16[64,512]{1,0:T(8,128)(2,1)S(1)}, u32[]{:S(2)}, u32[]{:S(2)}) collective-permute-start(bf16[64,512]{1,0:T(8,128)(2,1)} %param.21), channel_id=1, source_target_pairs={{0,8},{8,0},{1,9},{9,1},{2,10},{10,2},{3,11},{11,3},{4,12},{12,4},... | collective-permute-start | bytes 196616 | tf_op jit(solution)/shard_map/ppermute | solution.py:32
  29.9 25.6 %copy-start.13 = (bf16[128,8]{0,1:T(8,128)(2,1)S(1)}, bf16[128,8]{0,1:T(8,128)(2,1)}, u32[]{:S(2)}) copy-start(bf16[128,8]{0,1:T(8,128)(2,1)} %param.28) | copy-start | bytes 6148
  30.7 18.5 %all-to-all-start = ((bf16[4,128,512]{2,1,0:T(8,128)(2,1)}), bf16[4,128,512]{2,1,0:T(8,128)(2,1)}, u32[]{:S(2)}, u32[]{:S(2)}) async-start(bf16[4,128,512]{2,1,0:T(8,128)(2,1)} %broadcast_in_dim.266), calls=%async_computation | async-start | bytes 1048576 | tf_op jit(solution)/shard_map/all_to_all | solution.py:36
  49.3 15.0 %all-to-all-start.1 = ((bf16[4,128,512]{2,1,0:T(8,128)(2,1)}), bf16[4,128,512]{2,1,0:T(8,128)(2,1)S(1)}, u32[]{:S(2)}, u32[]{:S(2)}) async-start(bf16[4,128,512]{2,1,0:T(8,128)(2,1)} %all-to-all-done), calls=%async_computation.1 | async-start | bytes 1048576 | tf_op jit(solution)/shard_map/all_to_all | solution.py:36
  64.2 6.3 %collective-permute-start.4 = (bf16[512,512]{1,0:T(8,128)(2,1)S(1)}, bf16[512,512]{1,0:T(8,128)(2,1)S(1)}, u32[]{:S(2)}, u32[]{:S(2)}) collective-permute-start(bf16[512,512]{1,0:T(8,128)(2,1)S(1)} %bitcast.148), channel_id=1, source_target_pairs={{0,1},{1,0},{2,3},{3,2},{4,5},{5,4},{6,7},{7,6},{8,9},{9,8},{10,11... | collective-permute-start | bytes 1572872 | tf_op jit(solution)/shard_map/ppermute | solution.py:32
  72.4 12.5 %all-to-all-start.2 = ((bf16[4,128,512]{2,1,0:T(8,128)(2,1)}), bf16[4,128,512]{2,1,0:T(8,128)(2,1)S(1)}, u32[]{:S(2)}, u32[]{:S(2)}) async-start(bf16[4,128,512]{2,1,0:T(8,128)(2,1)} %bitcast.7), calls=%async_computation.2 | async-start | bytes 1048576 | tf_op jit(solution)/shard_map/all_to_all | solution.py:36
  86.8 23.6 %all-to-all-start.3 = ((bf16[64,8,512]{2,1,0:T(8,128)(2,1)}), bf16[64,8,512]{2,1,0:T(8,128)(2,1)S(1)}, u32[]{:S(2)}, u32[]{:S(2)}) async-start(bf16[64,8,512]{2,1,0:T(8,128)(2,1)} %fusion.7), calls=%async_computation.3 | async-start | bytes 1048576 | tf_op jit(solution)/shard_map/all_to_all | solution.py:36
  94.1 6.0 %collective-permute-start.5 = (bf16[512,768]{1,0:T(8,128)(2,1)S(1)}, bf16[512,768]{1,0:T(8,128)(2,1)S(1)}, u32[]{:S(2)}, u32[]{:S(2)}) collective-permute-start(bf16[512,768]{1,0:T(8,128)(2,1)S(1)} %pad_maximum_fusion.1), channel_id=1, source_target_pairs={{0,1},{1,0},{2,3},{3,2},{4,5},{5,4},{6,7},{7,6},{8,9},{9,8},{10,11... | collective-permute-start | bytes 2359304 | tf_op jit(solution)/shard_map/ppermute | solution.py:32
  96.0 4.0 %collective-permute-start.6 = (f32[1,512]{1,0:T(1,128)S(1)}, f32[1,512]{1,0:T(1,128)S(1)}, u32[]{:S(2)}, u32[]{:S(2)}) collective-permute-start(f32[1,512]{1,0:T(1,128)S(1)} %bitcast.143), channel_id=1, source_target_pairs={{0,1},{1,0},{2,3},{3,2},{4,5},{5,4},{6,7},{7,6},{8,9},{9,8},{10,11... | collective-permute-start | bytes 6152 | tf_op jit(solution)/shard_map/ppermute | solution.py:32
  110.5 9.5 %collective-permute-start.7 = (bf16[512,512]{1,0:T(8,128)(2,1)S(1)}, bf16[512,512]{1,0:T(8,128)(2,1)}, u32[]{:S(2)}, u32[]{:S(2)}) collective-permute-start(bf16[512,512]{1,0:T(8,128)(2,1)S(1)} %bitcast.141), channel_id=1, source_target_pairs={{0,1},{1,0},{2,3},{3,2},{4,5},{5,4},{6,7},{7,6},{8,9},{9,8},{10,11... | collective-permute-start | bytes 1572872 | tf_op jit(solution)/shard_map/ppermute | solution.py:32
  113.8 35.9 %all-to-all-start.4 = ((bf16[64,16,512]{2,1,0:T(8,128)(2,1)}), bf16[64,16,512]{2,1,0:T(8,128)(2,1)S(1)}, u32[]{:S(2)}, u32[]{:S(2)}) async-start(bf16[64,16,512]{2,1,0:T(8,128)(2,1)} %bitcast.146), calls=%async_computation.5 | async-start | bytes 2097152 | tf_op jit(solution)/shard_map/all_to_all | solution.py:36
  119.9 43.3 %copy-start.3 = (bf16[104,128]{1,0:T(8,128)(2,1)S(1)}, bf16[104,128]{1,0:T(8,128)(2,1)}, u32[]{:S(2)}) copy-start(bf16[104,128]{1,0:T(8,128)(2,1)} %constant.106.clone.pick_ref) | copy-start | bytes 79876
  119.9 38.7 %reduce-scatter.3.cloned.1.call-start = ((), (), s32[]{:S(2)}) async-start(), calls=%async_computation.10 | async-start | bytes 1044480 | tf_op jit(solution)/shard_map/reduce_scatter | solution.py:277
  123.3 84.9 %reduce-scatter.5.cloned.1.call-start = ((), (), s32[]{:S(2)}) async-start(), calls=%async_computation.11 | async-start | bytes 1658880 | tf_op jit(solution)/shard_map/reduce_scatter | solution.py:277
  158.6 4.5 %collective-permute-start.9 = (bf16[1024,512]{1,0:T(8,128)(2,1)S(1)}, bf16[1024,512]{1,0:T(8,128)(2,1)S(1)}, u32[]{:S(2)}, u32[]{:S(2)}) collective-permute-start(bf16[1024,512]{1,0:T(8,128)(2,1)S(1)} %bitcast.139), channel_id=1, source_target_pairs={{0,1},{1,0},{2,3},{3,2},{4,5},{5,4},{6,7},{7,6},{8,9},{9,8},{10,11... | collective-permute-start | bytes 3145736 | tf_op jit(solution)/shard_map/ppermute | solution.py:32
  183.3 3.6 %collective-permute-start.8 = (bf16[512,384]{1,0:T(8,128)(2,1)S(1)}, bf16[512,384]{1,0:T(8,128)(2,1)S(1)}, u32[]{:S(2)}, u32[]{:S(2)}) collective-permute-start(bf16[512,384]{1,0:T(8,128)(2,1)S(1)} %all_gather.10.own_ref), channel_id=1, source_target_pairs={{0,1},{1,0},{2,3},{3,2},{4,5},{5,4},{6,7},{7,6},{8,9},{9,8},{10,11... | collective-permute-start | bytes 1179656 | tf_op jit(solution)/shard_map/ppermute | solution.py:32
  188.4 41.4 %all-to-all-start.5 = ((bf16[64,8,512]{2,1,0:T(8,128)(2,1)}), bf16[64,8,512]{2,1,0:T(8,128)(2,1)S(1)}, u32[]{:S(2)}, u32[]{:S(2)}) async-start(bf16[64,8,512]{2,1,0:T(8,128)(2,1)} %bitcast.51), calls=%async_computation.6 | async-start | bytes 1048576 | tf_op jit(solution)/shard_map/all_to_all | solution.py:36
  229.8 4.0 %collective-permute-start.10 = (bf16[832,384]{1,0:T(8,128)(2,1)S(1)}, bf16[832,384]{1,0:T(8,128)(2,1)S(1)}, u32[]{:S(2)}, u32[]{:S(2)}) collective-permute-start(bf16[832,384]{1,0:T(8,128)(2,1)S(1)} %all_gather.11.own_ref), channel_id=1, source_target_pairs={{0,1},{1,0},{2,3},{3,2},{4,5},{5,4},{6,7},{7,6},{8,9},{9,8},{10,11... | collective-permute-start | bytes 1916936 | tf_op jit(solution)/shard_map/ppermute | solution.py:32
  236.5 40.3 %all-to-all-start.6 = ((bf16[64,16,512]{2,1,0:T(8,128)(2,1)}), bf16[64,16,512]{2,1,0:T(8,128)(2,1)S(1)}, u32[]{:S(2)}, u32[]{:S(2)}) async-start(bf16[64,16,512]{2,1,0:T(8,128)(2,1)} %bitcast.55), calls=%async_computation.8 | async-start | bytes 2097152 | tf_op jit(solution)/shard_map/all_to_all | solution.py:36
  247.5 29.3 %copy-start.5 = (bf16[1024,128]{1,0:T(8,128)(2,1)S(1)}, bf16[1024,128]{1,0:T(8,128)(2,1)}, u32[]{:S(2)}) copy-start(bf16[1024,128]{1,0:T(8,128)(2,1)} %get-tuple-element.44) | copy-start | bytes 786436
  (13 other events, 107.1 us)
Sparse Core Ops, SparseCore 0:
  28.5 40.4 all-gather.1
  123.6 34.9 reduce-scatter.2
  167.0 41.0 reduce-scatter.4

commit v11 on v9

--- a/solution.py
+++ b/solution.py
@@ -200,18 +200,28 @@
     tokens = queries.shape[0]
     half = FF // 2
 
+    attended = attention(queries, key_rows, value_rows)
+
     other_strip = swap(out_weight, "l")
+    attended, other_strip = lax.optimization_barrier((attended, other_strip))
     strips = jnp.where(
         side == 0,
         jnp.concatenate([out_weight, other_strip], axis=0),
         jnp.concatenate([other_strip, out_weight], axis=0),
     )
-    strips, queries = lax.optimization_barrier((strips, queries))
+    strips, attended = lax.optimization_barrier((strips, attended))
     quarter = lax.all_gather(strips, "y", axis=0, tiled=True)
 
-    attended = attention(queries, key_rows, value_rows)
+    attended, pred_ids, fix_pair = lax.optimization_barrier((attended, pred_ids, fix_pair))
+    ids, rank = slots_of(pred_ids, fix_pair, fix_expert, fix_count)
+    table = jnp.concatenate([ids, rank, route_gates.astype(f32)], axis=1)
+    slots, gates = row_slots(table.T, side.astype(f32))
+    pick = spread(slots, jnp.ones_like(slots))
+
     heads = exchange(jnp.broadcast_to(attended[None], (NH, *attended.shape)), "h")
+    other_slots, other_gates = row_slots(swap(table, "l").T, side.astype(f32))
     heads = exchange(heads, "x").reshape(NX * tokens, SLICE)
+    heads, other_slots = lax.optimization_barrier((heads, other_slots))
     other_heads = swap(heads, "c")
     partial = jnp.dot(
         heads,
@@ -222,14 +232,9 @@
         lax.dynamic_slice_in_dim(quarter, (1 - core) * SLICE, SLICE, 0),
         preferred_element_type=f32,
     )
-    partial, pred_ids, fix_pair, w_gate, w_up, norm_gain = lax.optimization_barrier(
-        (partial.astype(bf16), pred_ids, fix_pair, w_gate, w_up, norm_gain)
-    )
-
-    ids, rank = slots_of(pred_ids, fix_pair, fix_expert, fix_count)
-    table = jnp.concatenate([ids, rank, route_gates.astype(f32)], axis=1)
-    slots, gates = row_slots(table.T, side.astype(f32))
-    pick = spread(slots, jnp.ones_like(slots))
+    partial, w_gate, w_up, norm_gain = lax.optimization_barrier(
+        (partial.astype(bf16), w_gate, w_up, norm_gain)
+    )
 
     def columns(which):
         return jnp.concatenate(
@@ -248,9 +253,8 @@
     other_inverse = swap(inverse, "c")
 
     terms = exchange(partial.reshape(NX, tokens, SLICE), "x")
-    other_slots, other_gates = row_slots(swap(table, "l").T, side.astype(f32))
     other_pick = spread(other_slots, jnp.ones_like(other_slots))
-    terms, pick = lax.optimization_barrier((terms, pick))
+    terms, other_pick = lax.optimization_barrier((terms, other_pick))
     stream = residual.astype(f32) + jnp.sum(terms.astype(f32), axis=0)
 
     scaled = (stream * gain).astype(bf16)
@@ -279,23 +283,23 @@
     def finished(hidden):
         return expert_results(hidden, swap(hidden, "c"), down, other_down)
 
-    first = sent(pick, scaled)
-    first, beside, other_pick, gate_up, other_gate_up, inverse, other_inverse = (
-        lax.optimization_barrier(
-            (first, beside, other_pick, gate_up, other_gate_up, inverse, other_inverse)
-        )
+    first = sent(other_pick, beside)
+    first, pick, gate_up, other_gate_up, inverse, other_inverse = lax.optimization_barrier(
+        (first, pick, gate_up, other_gate_up, inverse, other_inverse)
     )
     first = reduced(share_products(first))
-    second = sent(other_pick, beside)
+    second = sent(pick, scaled)
     first, second = lax.optimization_barrier((first, second))
     second = reduced(share_products(second))
     first = through(finished(gathered(first)))
     hidden = gathered(second)
-    combine = spread(other_slots, other_gates)
+    combine = spread(slots, gates)
     first, hidden, combine = lax.optimization_barrier((first, hidden, combine))
     second = through(finished(hidden))
-    mixed = jnp.einsum("rt,rd->td", spread(slots, gates), first, preferred_element_type=f32)
-    other_mixed = jnp.einsum("rt,rd->td", combine, second, preferred_element_type=f32)
+    other_mixed = jnp.einsum(
+        "rt,rd->td", spread(other_slots, other_gates), first, preferred_element_type=f32
+    )
+    mixed = jnp.einsum("rt,rd->td", combine, second, preferred_element_type=f32)
     expert_out = mixed + swap(other_mixed.astype(bf16), "l").astype(f32)
     return stream.astype(bf16), expert_out.astype(bf16)
 

time: 272 us -> 269 us (0.989)
  blocking collectives: 115 us -> 61.6 us
  waiting for transfers between devices: 49 us -> 80.3 us
  starting transfers between devices: 65.4 us -> 81.9 us
    all_to_all x3 -> x1, blocking collectives: 82.4 us -> 28 us  [exchange(): return lax.all_to_all(blocks, axes, split_axis=0, concat_axis=0, tiled=True)]
    all_to_all x4 -> x6, waiting for transfers between devices: 26.1 us -> 55 us  [exchange(): return lax.all_to_all(blocks, axes, split_axis=0, concat_axis=0, tiled=True)]
    all_to_all x4 -> x6, starting transfers between devices: 24.8 us -> 41.1 us  [exchange(): return lax.all_to_all(blocks, axes, split_axis=0, concat_axis=0, tiled=True)]
  transfers between devices with their start and end apart: 21 -> 23, of which waited for: 14 -> 17; matrix products, arithmetic and copies ran while one was open for 3% -> 4% of each run, Pallas kernels for 1% -> 1%
where the time goes in v11:
time: 269 us; the launch traced here: 268 us
  starting transfers between devices  81.9 us (30%)
  waiting for transfers between devices  80.3 us (30%)
  blocking collectives  61.6 us (23%)
  between operations  15 us (6%)
  Pallas kernels  11.1 us (4%)
  matrix products  7.37 us (3%)
  other arithmetic  5.34 us (2%)
  local copies, waits for them, and re-layouts  5.19 us (2%)
    all_to_all x6, waiting for transfers between devices, exchange(): return lax.all_to_all(blocks, axes, split_axis=0, concat_axis=0, tiled=True)  55 us
    all_to_all x6, starting transfers between devices, exchange(): return lax.all_to_all(blocks, axes, split_axis=0, concat_axis=0, tiled=True)  41.1 us
    all_gather x2, blocking collectives, gathered(): return lax.all_gather(hidden, 'h', axis=0, tiled=True)  33.6 us
    ppermute x11, starting transfers between devices, swap(): return lax.ppermute(block, axis, [(0, 1), (1, 0)])  28.1 us
    all_to_all x1, blocking collectives, exchange(): return lax.all_to_all(blocks, axes, split_axis=0, concat_axis=0, tiled=True)  28 us
    ppermute x11, waiting for transfers between devices, swap(): return lax.ppermute(block, axis, [(0, 1), (1, 0)])  18.7 us
    ppermute x3, starting transfers between devices, from_behind(): return lax.ppermute(block, CTX, route)  12.6 us
    pallas_call x2, Pallas kernels, products(): pl.pallas_call(products_kernel, out_shape=jax.ShapeDtypeStruct((NH, SHARE...  6.81 us
  transfers between devices with their start and end apart: 23, of which 17 were waited for; matrix products, arithmetic and copies ran while one was open for 4% of the time, Pallas kernels for 1%

profile of v11, /device:TPU:8, one launch (start us, length us, event | category | flops | bytes accessed | tf_op | source)
XLA Modules:
  0.0 267.8 jit_solution(2127287291859352347)
XLA Ops:
  8.0 5.3 %collective-permute-start = (bf16[128,256]{1,0:T(8,128)(2,1)S(1)}, bf16[128,256]{1,0:T(8,128)(2,1)S(1)}, u32[]{:S(2)}, u32[]{:S(2)}) collective-permute-start(bf16[128,256]{1,0:T(8,128)(2,1)S(1)} %pad_maximum_fusion.2), channel_id=1, source_target_pairs={{0,24},{8,32},{16,40},{24,48},{32,56},{40,64},{48,72},{56,80},{64,... | collective-permute-start | bytes 196616 | tf_op jit(solution)/shard_map/ppermute | solution.py:46
  13.3 3.5 %collective-permute-start.1 = (bf16[128,256]{1,0:T(8,128)(2,1)S(1)}, bf16[128,256]{1,0:T(8,128)(2,1)S(1)}, u32[]{:S(2)}, u32[]{:S(2)}) collective-permute-start(bf16[128,256]{1,0:T(8,128)(2,1)S(1)} %pad_maximum_fusion.2), channel_id=1, source_target_pairs={{0,16},{8,24},{16,32},{24,40},{32,48},{40,56},{48,64},{56,72},{64,... | collective-permute-start | bytes 196616 | tf_op jit(solution)/shard_map/ppermute | solution.py:46
  16.8 3.8 %collective-permute-start.2 = (bf16[128,256]{1,0:T(8,128)(2,1)S(1)}, bf16[128,256]{1,0:T(8,128)(2,1)S(1)}, u32[]{:S(2)}, u32[]{:S(2)}) collective-permute-start(bf16[128,256]{1,0:T(8,128)(2,1)S(1)} %pad_maximum_fusion.2), channel_id=1, source_target_pairs={{0,8},{8,16},{16,24},{24,32},{32,40},{40,48},{48,56},{56,64},{64,7... | collective-permute-start | bytes 196616 | tf_op jit(solution)/shard_map/ppermute | solution.py:46
  20.6 4.3 %collective-permute-start.3 = (bf16[64,512]{1,0:T(8,128)(2,1)}, bf16[64,512]{1,0:T(8,128)(2,1)S(1)}, u32[]{:S(2)}, u32[]{:S(2)}) collective-permute-start(bf16[64,512]{1,0:T(8,128)(2,1)} %param.21), channel_id=1, source_target_pairs={{0,8},{8,0},{1,9},{9,1},{2,10},{10,2},{3,11},{11,3},{4,12},{12,4},... | collective-permute-start | bytes 196616 | tf_op jit(solution)/shard_map/ppermute | solution.py:37
  30.0 9.4 %all-to-all-start = ((bf16[4,128,512]{2,1,0:T(8,128)(2,1)}), bf16[4,128,512]{2,1,0:T(8,128)(2,1)}, u32[]{:S(2)}, u32[]{:S(2)}) async-start(bf16[4,128,512]{2,1,0:T(8,128)(2,1)} %broadcast_in_dim.274), calls=%async_computation | async-start | bytes 1048576 | tf_op jit(solution)/shard_map/all_to_all | solution.py:41
  39.9 13.6 %all-to-all-done = bf16[4,128,512]{2,1,0:T(8,128)(2,1)} async-done(((bf16[4,128,512]{2,1,0:T(8,128)(2,1)}), bf16[4,128,512]{2,1,0:T(8,128)(2,1)}, u32[]{:S(2)}, u32[]{:S(2)}) %all-to-all-start) | async-done | bytes 524320 | tf_op jit(solution)/shard_map/all_to_all | solution.py:41
  53.5 4.4 %all-to-all-start.1 = ((bf16[4,128,512]{2,1,0:T(8,128)(2,1)}), bf16[4,128,512]{2,1,0:T(8,128)(2,1)S(1)}, u32[]{:S(2)}, u32[]{:S(2)}) async-start(bf16[4,128,512]{2,1,0:T(8,128)(2,1)} %all-to-all-done), calls=%async_computation.1 | async-start | bytes 1048576 | tf_op jit(solution)/shard_map/all_to_all | solution.py:41
  60.1 3.5 %collective-permute-done.4 = f32[128,24]{0,1:T(8,128)S(1)} collective-permute-done((f32[128,24]{0,1:T(8,128)S(1)}, f32[128,24]{0,1:T(8,128)S(1)}, u32[]{:S(2)}, u32[]{:S(2)}) %collective-permute-start.4) | collective-permute-done | bytes 12320 | tf_op jit(solution)/shard_map/ppermute | solution.py:37
  73.0 4.5 %all-to-all-start.2 = ((bf16[4,128,512]{2,1,0:T(8,128)(2,1)}), bf16[4,128,512]{2,1,0:T(8,128)(2,1)S(1)}, u32[]{:S(2)}, u32[]{:S(2)}) async-start(bf16[4,128,512]{2,1,0:T(8,128)(2,1)} %bitcast.11), calls=%async_computation.2 | async-start | bytes 1048576 | tf_op jit(solution)/shard_map/all_to_all | solution.py:41
  77.9 7.7 %all-to-all-done.2 = bf16[4,128,512]{2,1,0:T(8,128)(2,1)S(1)} async-done(((bf16[4,128,512]{2,1,0:T(8,128)(2,1)}), bf16[4,128,512]{2,1,0:T(8,128)(2,1)S(1)}, u32[]{:S(2)}, u32[]{:S(2)}) %all-to-all-start.2) | async-done | bytes 524320 | tf_op jit(solution)/shard_map/all_to_all | solution.py:41
  86.4 3.5 %collective-permute-start.6 = (bf16[128,512]{1,0:T(8,128)(2,1)S(1)}, bf16[128,512]{1,0:T(8,128)(2,1)S(1)}, u32[]{:S(2)}, u32[]{:S(2)}) collective-permute-start(bf16[128,512]{1,0:T(8,128)(2,1)S(1)} %get-tuple-element.62), channel_id=1, source_target_pairs={{0,8},{8,0},{1,9},{9,1},{2,10},{10,2},{3,11},{11,3},{4,12},{12,4},... | collective-permute-start | bytes 393224 | tf_op jit(solution)/shard_map/ppermute | solution.py:37
  94.5 5.9 %all-to-all-start.3 = ((bf16[32,24,512]{2,1,0:T(8,128)(2,1)}), bf16[32,24,512]{2,1,0:T(8,128)(2,1)S(1)}, u32[]{:S(2)}, u32[]{:S(2)}) async-start(bf16[32,24,512]{2,1,0:T(8,128)(2,1)} %bitcast.20), calls=%async_computation.3 | async-start | bytes 1572864 | tf_op jit(solution)/shard_map/all_to_all | solution.py:41
  107.7 10.5 %all-to-all-done.3 = bf16[32,24,512]{2,1,0:T(8,128)(2,1)S(1)} async-done(((bf16[32,24,512]{2,1,0:T(8,128)(2,1)}), bf16[32,24,512]{2,1,0:T(8,128)(2,1)S(1)}, u32[]{:S(2)}, u32[]{:S(2)}) %all-to-all-start.3) | async-done | bytes 786464 | tf_op jit(solution)/shard_map/all_to_all | solution.py:41
  122.3 3.4 %shard_map.185 = bf16[4,176,768]{2,1,0:T(8,128)(2,1)} custom-call(bf16[768,512]{1,0:T(8,128)(2,1)S(1)} %bitcast.151, bf16[768,512]{1,0:T(8,128)(2,1)S(1)} %collective-permute-done.9.other_ref, bf16[512,768]{1,0:T(8,128)(2,1)S(1)} %pad_maximum_fusion.w_own_ref, bf16[512,768]{1,0:T(8,128)(2,1)S(1)} %collective-permute-done.7.w_other_ref, ...), custom_call_target="tpu_custom_call" | custom-call | flops 100000000 | bytes 500000 | tf_op jit(solution)/shard_map/pallas_call | solution.py:151
  126.2 28.0 %all_to_all.35 = bf16[32,24,512]{2,1,0:T(8,128)(2,1)S(1)} all-to-all(bf16[32,24,512]{2,1,0:T(8,128)(2,1)S(1)} %bitcast.158), channel_id=1, replica_groups=mesh['x'=4,'y'=8,'l'=2,'h'=4,'c'=2] {'x','y'}, dimensions={0} | all-to-all | bytes 1572864 | tf_op jit(solution)/shard_map/all_to_all | solution.py:41
  154.2 4.2 %reduce-scatter.3.cloned.1.call-done = bf16[176,768]{1,0:T(8,128)(2,1)} async-done(((bf16[704,768]{1,0:T(8,128)(2,1)}), bf16[176,768]{1,0:T(8,128)(2,1)}) %reduce-scatter.3.cloned.1.call-update) | async-done | bytes 270352 | tf_op jit(solution)/shard_map/reduce_scatter | solution.py:274
  162.6 3.4 %shard_map.187 = bf16[4,176,768]{2,1,0:T(8,128)(2,1)} custom-call(bf16[768,512]{1,0:T(8,128)(2,1)S(1)} %bitcast.153, bf16[768,512]{1,0:T(8,128)(2,1)S(1)} %collective-permute-done.11.other_ref, bf16[512,768]{1,0:T(8,128)(2,1)S(1)} %pad_maximum_fusion.w_own_ref, bf16[512,768]{1,0:T(8,128)(2,1)S(1)} %collective-permute-done.7.w_other_ref, ...), custom_call_target="tpu_custom_call" | custom-call | flops 100000000 | bytes 500000 | tf_op jit(solution)/shard_map/pallas_call | solution.py:151
  167.2 17.8 %all_gather.10.own_ref = bf16[672,384]{1,0:T(8,128)(2,1)S(1)} all-gather(bf16[168,384]{1,0:T(8,128)(2,1)S(1)} %fusion.15), channel_id=1, replica_groups=mesh['x'=4,'y'=8,'l'=2,'h'=4,'c'=2] {'h'}, dimensions={0}, use_global_device_ids=true | all-gather | bytes 645120 | tf_op jit(solution)/shard_map/all_gather | solution.py:281
  191.0 9.9 %all-to-all-start.5 = ((bf16[32,24,512]{2,1,0:T(8,128)(2,1)}), bf16[32,24,512]{2,1,0:T(8,128)(2,1)S(1)}, u32[]{:S(2)}, u32[]{:S(2)}) async-start(bf16[32,24,512]{2,1,0:T(8,128)(2,1)} %bitcast.42), calls=%async_computation.6 | async-start | bytes 1572864 | tf_op jit(solution)/shard_map/all_to_all | solution.py:41
  203.7 15.8 %all_gather.11.own_ref = bf16[672,384]{1,0:T(8,128)(2,1)S(1)} all-gather(bf16[168,384]{1,0:T(8,128)(2,1)S(1)} %fusion.14), channel_id=1, replica_groups=mesh['x'=4,'y'=8,'l'=2,'h'=4,'c'=2] {'h'}, dimensions={0}, use_global_device_ids=true | all-gather | bytes 645120 | tf_op jit(solution)/shard_map/all_gather | solution.py:281
  219.6 4.6 %all-to-all-done.5 = bf16[32,24,512]{2,1,0:T(8,128)(2,1)S(1)} async-done(((bf16[32,24,512]{2,1,0:T(8,128)(2,1)}), bf16[32,24,512]{2,1,0:T(8,128)(2,1)S(1)}, u32[]{:S(2)}, u32[]{:S(2)}) %all-to-all-start.5) | async-done | bytes 786464 | tf_op jit(solution)/shard_map/all_to_all | solution.py:41
  230.1 6.9 %all-to-all-start.6 = ((bf16[32,24,512]{2,1,0:T(8,128)(2,1)}), bf16[32,24,512]{2,1,0:T(8,128)(2,1)S(1)}, u32[]{:S(2)}, u32[]{:S(2)}) async-start(bf16[32,24,512]{2,1,0:T(8,128)(2,1)} %bitcast.54), calls=%async_computation.8 | async-start | bytes 1572864 | tf_op jit(solution)/shard_map/all_to_all | solution.py:41
  237.7 4.1 %collective-permute-start.13 = (bf16[128,512]{1,0:T(8,128)(2,1)S(1)}, bf16[128,512]{1,0:T(8,128)(2,1)S(1)}, u32[]{:S(2)}, u32[]{:S(2)}) collective-permute-start(bf16[128,512]{1,0:T(8,128)(2,1)S(1)} %convolution_convert_fusion.2), channel_id=1, source_target_pairs={{0,8},{8,0},{1,9},{9,1},{2,10},{10,2},{3,11},{11,3},{4,12},{12,4},... | collective-permute-start | bytes 393224 | tf_op jit(solution)/shard_map/ppermute | solution.py:37
  245.0 15.4 %all-to-all-done.6 = bf16[32,24,512]{2,1,0:T(8,128)(2,1)S(1)} async-done(((bf16[32,24,512]{2,1,0:T(8,128)(2,1)}), bf16[32,24,512]{2,1,0:T(8,128)(2,1)S(1)}, u32[]{:S(2)}, u32[]{:S(2)}) %all-to-all-start.6) | async-done | bytes 786464 | tf_op jit(solution)/shard_map/all_to_all | solution.py:41
  (120 shorter events, 59.4 us)
Async XLA Ops:
  7.2 63.0 %all-gather.2.cloned.1.call-start = ((), (), s32[]{:S(2)}) async-start(), calls=%async_computation.9 | async-start | bytes 1179648 | tf_op jit(solution)/shard_map/all_gather | solution.py:213
  8.0 18.5 %collective-permute-start = (bf16[128,256]{1,0:T(8,128)(2,1)S(1)}, bf16[128,256]{1,0:T(8,128)(2,1)S(1)}, u32[]{:S(2)}, u32[]{:S(2)}) collective-permute-start(bf16[128,256]{1,0:T(8,128)(2,1)S(1)} %pad_maximum_fusion.2), channel_id=1, source_target_pairs={{0,24},{8,32},{16,40},{24,48},{32,56},{40,64},{48,72},{56,80},{64,... | collective-permute-start | bytes 196616 | tf_op jit(solution)/shard_map/ppermute | solution.py:46
  13.3 13.2 %collective-permute-start.1 = (bf16[128,256]{1,0:T(8,128)(2,1)S(1)}, bf16[128,256]{1,0:T(8,128)(2,1)S(1)}, u32[]{:S(2)}, u32[]{:S(2)}) collective-permute-start(bf16[128,256]{1,0:T(8,128)(2,1)S(1)} %pad_maximum_fusion.2), channel_id=1, source_target_pairs={{0,16},{8,24},{16,32},{24,40},{32,48},{40,56},{48,64},{56,72},{64,... | collective-permute-start | bytes 196616 | tf_op jit(solution)/shard_map/ppermute | solution.py:46
  16.8 9.7 %collective-permute-start.2 = (bf16[128,256]{1,0:T(8,128)(2,1)S(1)}, bf16[128,256]{1,0:T(8,128)(2,1)S(1)}, u32[]{:S(2)}, u32[]{:S(2)}) collective-permute-start(bf16[128,256]{1,0:T(8,128)(2,1)S(1)} %pad_maximum_fusion.2), channel_id=1, source_target_pairs={{0,8},{8,16},{16,24},{24,32},{32,40},{40,48},{48,56},{56,64},{64,7... | collective-permute-start | bytes 196616 | tf_op jit(solution)/shard_map/ppermute | solution.py:46
  20.6 7.3 %collective-permute-start.3 = (bf16[64,512]{1,0:T(8,128)(2,1)}, bf16[64,512]{1,0:T(8,128)(2,1)S(1)}, u32[]{:S(2)}, u32[]{:S(2)}) collective-permute-start(bf16[64,512]{1,0:T(8,128)(2,1)} %param.21), channel_id=1, source_target_pairs={{0,8},{8,0},{1,9},{9,1},{2,10},{10,2},{3,11},{11,3},{4,12},{12,4},... | collective-permute-start | bytes 196616 | tf_op jit(solution)/shard_map/ppermute | solution.py:37
  30.0 23.5 %all-to-all-start = ((bf16[4,128,512]{2,1,0:T(8,128)(2,1)}), bf16[4,128,512]{2,1,0:T(8,128)(2,1)}, u32[]{:S(2)}, u32[]{:S(2)}) async-start(bf16[4,128,512]{2,1,0:T(8,128)(2,1)} %broadcast_in_dim.274), calls=%async_computation | async-start | bytes 1048576 | tf_op jit(solution)/shard_map/all_to_all | solution.py:41
  53.5 13.4 %all-to-all-start.1 = ((bf16[4,128,512]{2,1,0:T(8,128)(2,1)}), bf16[4,128,512]{2,1,0:T(8,128)(2,1)S(1)}, u32[]{:S(2)}, u32[]{:S(2)}) async-start(bf16[4,128,512]{2,1,0:T(8,128)(2,1)} %all-to-all-done), calls=%async_computation.1 | async-start | bytes 1048576 | tf_op jit(solution)/shard_map/all_to_all | solution.py:41
  58.0 5.6 %collective-permute-start.4 = (f32[128,24]{0,1:T(8,128)S(1)}, f32[128,24]{0,1:T(8,128)S(1)}, u32[]{:S(2)}, u32[]{:S(2)}) collective-permute-start(f32[128,24]{0,1:T(8,128)S(1)} %get-tuple-element.91), channel_id=1, source_target_pairs={{0,8},{8,0},{1,9},{9,1},{2,10},{10,2},{3,11},{11,3},{4,12},{12,4},... | collective-permute-start | bytes 36872 | tf_op jit(solution)/shard_map/ppermute | solution.py:37
  66.8 4.9 %collective-permute-start.5 = (bf16[512,512]{1,0:T(8,128)(2,1)S(1)}, bf16[512,512]{1,0:T(8,128)(2,1)S(1)}, u32[]{:S(2)}, u32[]{:S(2)}) collective-permute-start(bf16[512,512]{1,0:T(8,128)(2,1)S(1)} %bitcast.159), channel_id=1, source_target_pairs={{0,1},{1,0},{2,3},{3,2},{4,5},{5,4},{6,7},{7,6},{8,9},{9,8},{10,11... | collective-permute-start | bytes 1572872 | tf_op jit(solution)/shard_map/ppermute | solution.py:37
  73.0 12.6 %all-to-all-start.2 = ((bf16[4,128,512]{2,1,0:T(8,128)(2,1)}), bf16[4,128,512]{2,1,0:T(8,128)(2,1)S(1)}, u32[]{:S(2)}, u32[]{:S(2)}) async-start(bf16[4,128,512]{2,1,0:T(8,128)(2,1)} %bitcast.11), calls=%async_computation.2 | async-start | bytes 1048576 | tf_op jit(solution)/shard_map/all_to_all | solution.py:41
  86.4 6.8 %collective-permute-start.6 = (bf16[128,512]{1,0:T(8,128)(2,1)S(1)}, bf16[128,512]{1,0:T(8,128)(2,1)S(1)}, u32[]{:S(2)}, u32[]{:S(2)}) collective-permute-start(bf16[128,512]{1,0:T(8,128)(2,1)S(1)} %get-tuple-element.62), channel_id=1, source_target_pairs={{0,8},{8,0},{1,9},{9,1},{2,10},{10,2},{3,11},{11,3},{4,12},{12,4},... | collective-permute-start | bytes 393224 | tf_op jit(solution)/shard_map/ppermute | solution.py:37
  94.5 23.6 %all-to-all-start.3 = ((bf16[32,24,512]{2,1,0:T(8,128)(2,1)}), bf16[32,24,512]{2,1,0:T(8,128)(2,1)S(1)}, u32[]{:S(2)}, u32[]{:S(2)}) async-start(bf16[32,24,512]{2,1,0:T(8,128)(2,1)} %bitcast.20), calls=%async_computation.3 | async-start | bytes 1572864 | tf_op jit(solution)/shard_map/all_to_all | solution.py:41
  100.5 57.9 %reduce-scatter.3.cloned.1.call-start = ((), (), s32[]{:S(2)}) async-start(), calls=%async_computation.10 | async-start | bytes 1351680 | tf_op jit(solution)/shard_map/reduce_scatter | solution.py:274
  101.8 5.9 %collective-permute-start.7 = (bf16[512,768]{1,0:T(8,128)(2,1)S(1)}, bf16[512,768]{1,0:T(8,128)(2,1)S(1)}, u32[]{:S(2)}, u32[]{:S(2)}) collective-permute-start(bf16[512,768]{1,0:T(8,128)(2,1)S(1)} %pad_maximum_fusion.1), channel_id=1, source_target_pairs={{0,1},{1,0},{2,3},{3,2},{4,5},{5,4},{6,7},{7,6},{8,9},{9,8},{10,11... | collective-permute-start | bytes 2359304 | tf_op jit(solution)/shard_map/ppermute | solution.py:37
  104.5 3.2 %collective-permute-start.8 = (f32[1,512]{1,0:T(1,128)S(1)}, f32[1,512]{1,0:T(1,128)S(1)}, u32[]{:S(2)}, u32[]{:S(2)}) collective-permute-start(f32[1,512]{1,0:T(1,128)S(1)} %bitcast.154), channel_id=1, source_target_pairs={{0,1},{1,0},{2,3},{3,2},{4,5},{5,4},{6,7},{7,6},{8,9},{9,8},{10,11... | collective-permute-start | bytes 6152 | tf_op jit(solution)/shard_map/ppermute | solution.py:37
  118.2 4.2 %collective-permute-start.9 = (bf16[768,512]{1,0:T(8,128)(2,1)S(1)}, bf16[768,512]{1,0:T(8,128)(2,1)S(1)}, u32[]{:S(2)}, u32[]{:S(2)}) collective-permute-start(bf16[768,512]{1,0:T(8,128)(2,1)S(1)} %bitcast.150), channel_id=1, source_target_pairs={{0,1},{1,0},{2,3},{3,2},{4,5},{5,4},{6,7},{7,6},{8,9},{9,8},{10,11... | collective-permute-start | bytes 2359304 | tf_op jit(solution)/shard_map/ppermute | solution.py:37
  125.8 76.0 %reduce-scatter.5.cloned.1.call-start = ((), (), s32[]{:S(2)}) async-start(), calls=%async_computation.11 | async-start | bytes 1351680 | tf_op jit(solution)/shard_map/reduce_scatter | solution.py:274
  158.4 4.2 %collective-permute-start.11 = (bf16[768,512]{1,0:T(8,128)(2,1)S(1)}, bf16[768,512]{1,0:T(8,128)(2,1)S(1)}, u32[]{:S(2)}, u32[]{:S(2)}) collective-permute-start(bf16[768,512]{1,0:T(8,128)(2,1)S(1)} %bitcast.152), channel_id=1, source_target_pairs={{0,1},{1,0},{2,3},{3,2},{4,5},{5,4},{6,7},{7,6},{8,9},{9,8},{10,11... | collective-permute-start | bytes 2359304 | tf_op jit(solution)/shard_map/ppermute | solution.py:37
  167.2 21.6 %copy-start.1 = (bf16[192,168]{1,0:T(8,128)(2,1)S(1)}, bf16[192,168]{1,0:T(8,128)(2,1)}, u32[]{:S(2)}) copy-start(bf16[192,168]{1,0:T(8,128)(2,1)} %constant.98.clone.place_ref) | copy-start | bytes 193540
  185.0 3.8 %collective-permute-start.10 = (bf16[672,384]{1,0:T(8,128)(2,1)S(1)}, bf16[672,384]{1,0:T(8,128)(2,1)S(1)}, u32[]{:S(2)}, u32[]{:S(2)}) collective-permute-start(bf16[672,384]{1,0:T(8,128)(2,1)S(1)} %all_gather.10.own_ref), channel_id=1, source_target_pairs={{0,1},{1,0},{2,3},{3,2},{4,5},{5,4},{6,7},{7,6},{8,9},{9,8},{10,11... | collective-permute-start | bytes 1548296 | tf_op jit(solution)/shard_map/ppermute | solution.py:37
  191.0 33.2 %all-to-all-start.5 = ((bf16[32,24,512]{2,1,0:T(8,128)(2,1)}), bf16[32,24,512]{2,1,0:T(8,128)(2,1)S(1)}, u32[]{:S(2)}, u32[]{:S(2)}) async-start(bf16[32,24,512]{2,1,0:T(8,128)(2,1)} %bitcast.42), calls=%async_computation.6 | async-start | bytes 1572864 | tf_op jit(solution)/shard_map/all_to_all | solution.py:41
  224.2 3.8 %collective-permute-start.12 = (bf16[672,384]{1,0:T(8,128)(2,1)S(1)}, bf16[672,384]{1,0:T(8,128)(2,1)S(1)}, u32[]{:S(2)}, u32[]{:S(2)}) collective-permute-start(bf16[672,384]{1,0:T(8,128)(2,1)S(1)} %all_gather.11.own_ref), channel_id=1, source_target_pairs={{0,1},{1,0},{2,3},{3,2},{4,5},{5,4},{6,7},{7,6},{8,9},{9,8},{10,11... | collective-permute-start | bytes 1548296 | tf_op jit(solution)/shard_map/ppermute | solution.py:37
  230.1 30.2 %all-to-all-start.6 = ((bf16[32,24,512]{2,1,0:T(8,128)(2,1)}), bf16[32,24,512]{2,1,0:T(8,128)(2,1)S(1)}, u32[]{:S(2)}, u32[]{:S(2)}) async-start(bf16[32,24,512]{2,1,0:T(8,128)(2,1)} %bitcast.54), calls=%async_computation.8 | async-start | bytes 1572864 | tf_op jit(solution)/shard_map/all_to_all | solution.py:41
  237.7 7.3 %collective-permute-start.13 = (bf16[128,512]{1,0:T(8,128)(2,1)S(1)}, bf16[128,512]{1,0:T(8,128)(2,1)S(1)}, u32[]{:S(2)}, u32[]{:S(2)}) collective-permute-start(bf16[128,512]{1,0:T(8,128)(2,1)S(1)} %convolution_convert_fusion.2), channel_id=1, source_target_pairs={{0,8},{8,0},{1,9},{9,1},{2,10},{10,2},{3,11},{11,3},{4,12},{12,4},... | collective-permute-start | bytes 393224 | tf_op jit(solution)/shard_map/ppermute | solution.py:37
  (13 other events, 132.0 us)
Sparse Core Ops, SparseCore 0:
  29.2 40.9 all-gather.1
  125.9 32.4 reduce-scatter.2
  166.1 35.5 reduce-scatter.4

commit v12 on v11

--- a/solution.py
+++ b/solution.py
@@ -180,6 +180,26 @@
     )(own, other, down_own, down_other, jnp.asarray(packing().T, bf16))
 
 
+def activation_kernel(sums_ref, hidden_ref):
+    sums = sums_ref[...].astype(f32)
+    total = sums[SHARE : SHARE + 1, :LANES] + sums[SHARE + 1 : SHARE + 2, :LANES]
+    scale = lax.rsqrt(total / D + epsilon)
+    at = lax.broadcasted_iota(jnp.int32, (SHARE, LANES), 0)
+    lane = lax.broadcasted_iota(jnp.int32, (SHARE, LANES), 1)
+    scale = jnp.sum(jnp.where(at == lane, scale, 0.0), axis=1, keepdims=True)
+    gate, up = sums[:SHARE, : FF // 2] * scale, sums[:SHARE, FF // 2 :] * scale
+    hidden_ref[...] = (gate / (1.0 + jnp.exp(-gate)) * up).astype(bf16)
+
+
+def activated(sums):
+    return pl.pallas_call(
+        activation_kernel,
+        out_shape=jax.ShapeDtypeStruct((SHARE, FF // 2), bf16),
+        compiler_params=pltpu.CompilerParams(vmem_limit_bytes=32 * 1024 * 1024),
+        cost_estimate=pl.CostEstimate(flops=1_000_000, bytes_accessed=100_000, transcendentals=0),
+    )(sums)
+
+
 def body(
     queries,
     key_rows,
@@ -218,7 +238,7 @@
     slots, gates = row_slots(table.T, side.astype(f32))
     pick = spread(slots, jnp.ones_like(slots))
 
-    heads = exchange(jnp.broadcast_to(attended[None], (NH, *attended.shape)), "h")
+    heads = lax.all_gather(attended, "h", axis=0, tiled=True).reshape(NH, tokens, SLICE)
     other_slots, other_gates = row_slots(swap(table, "l").T, side.astype(f32))
     heads = exchange(heads, "x").reshape(NX * tokens, SLICE)
     heads, other_slots = lax.optimization_barrier((heads, other_slots))
@@ -274,11 +294,7 @@
         return lax.psum_scatter(flat, "h", scatter_dimension=0, tiled=True)
 
     def gathered(sums):
-        sums = sums.astype(f32)
-        total = (sums[SHARE] + sums[SHARE + 1])[:SHARE]
-        sums = sums[:SHARE] * lax.rsqrt(total / D + epsilon)[:, None]
-        hidden = (jax.nn.silu(sums[:, :half]) * sums[:, half:]).astype(bf16)
-        return lax.all_gather(hidden, "h", axis=0, tiled=True)
+        return lax.all_gather(activated(sums), "h", axis=0, tiled=True)
 
     def finished(hidden):
         return expert_results(hidden, swap(hidden, "c"), down, other_down)

time: 269 us -> 269 us (level)
  the two profiles are of different devices: /device:TPU:8 before, /device:TPU:72 now
where the time goes in v12:
time: 269 us; the launch traced here: 268 us
  blocking collectives  83.3 us (31%)
  waiting for transfers between devices  73 us (27%)
  starting transfers between devices  68.2 us (25%)
  between operations  15 us (6%)
  Pallas kernels  11.5 us (4%)
  matrix products  7.4 us (3%)
  local copies, waits for them, and re-layouts  5.33 us (2%)
  other arithmetic  3.93 us (1%)
    all_to_all x5, waiting for transfers between devices, exchange(): return lax.all_to_all(blocks, axes, split_axis=0, concat_axis=0, tiled=True)  38.8 us
    all_gather x2, blocking collectives, gathered(): return lax.all_gather(activated(sums), 'h', axis=0, tiled=True)  34.6 us
    all_to_all x5, starting transfers between devices, exchange(): return lax.all_to_all(blocks, axes, split_axis=0, concat_axis=0, tiled=True)  31.5 us
    all_to_all x1, blocking collectives, exchange(): return lax.all_to_all(blocks, axes, split_axis=0, concat_axis=0, tiled=True)  27.8 us
    ppermute x11, starting transfers between devices, swap(): return lax.ppermute(block, axis, [(0, 1), (1, 0)])  24 us
    ppermute x11, waiting for transfers between devices, swap(): return lax.ppermute(block, axis, [(0, 1), (1, 0)])  21.5 us
    all_gather x1, blocking collectives, body(): lax.all_gather(attended, 'h', axis=0, tiled=True).reshape(NH, tokens, SLICE)  21 us
    ppermute x3, starting transfers between devices, from_behind(): return lax.ppermute(block, CTX, route)  12.6 us
  transfers between devices with their start and end apart: 22, of which 17 were waited for; matrix products, arithmetic and copies ran while one was open for 3% of the time, Pallas kernels for 1%

profile of v12, /device:TPU:72, one launch (start us, length us, event | category | flops | bytes accessed | tf_op | source)
XLA Modules:
  0.0 267.7 jit_solution(11507508658281969183)
XLA Ops:
  8.0 3.6 %collective-permute-start = (bf16[128,256]{1,0:T(8,128)(2,1)S(1)}, bf16[128,256]{1,0:T(8,128)(2,1)S(1)}, u32[]{:S(2)}, u32[]{:S(2)}) collective-permute-start(bf16[128,256]{1,0:T(8,128)(2,1)S(1)} %pad_maximum_fusion.2), channel_id=1, source_target_pairs={{0,24},{8,32},{16,40},{24,48},{32,56},{40,64},{48,72},{56,80},{64,... | collective-permute-start | bytes 196616 | tf_op jit(solution)/shard_map/ppermute | solution.py:46
  11.6 4.7 %collective-permute-start.1 = (bf16[128,256]{1,0:T(8,128)(2,1)S(1)}, bf16[128,256]{1,0:T(8,128)(2,1)S(1)}, u32[]{:S(2)}, u32[]{:S(2)}) collective-permute-start(bf16[128,256]{1,0:T(8,128)(2,1)S(1)} %pad_maximum_fusion.2), channel_id=1, source_target_pairs={{0,16},{8,24},{16,32},{24,40},{32,48},{40,56},{48,64},{56,72},{64,... | collective-permute-start | bytes 196616 | tf_op jit(solution)/shard_map/ppermute | solution.py:46
  16.3 4.3 %collective-permute-start.2 = (bf16[128,256]{1,0:T(8,128)(2,1)S(1)}, bf16[128,256]{1,0:T(8,128)(2,1)S(1)}, u32[]{:S(2)}, u32[]{:S(2)}) collective-permute-start(bf16[128,256]{1,0:T(8,128)(2,1)S(1)} %pad_maximum_fusion.2), channel_id=1, source_target_pairs={{0,8},{8,16},{16,24},{24,32},{32,40},{40,48},{48,56},{56,64},{64,7... | collective-permute-start | bytes 196616 | tf_op jit(solution)/shard_map/ppermute | solution.py:46
  27.8 21.0 %all_gather.12 = bf16[512,512]{1,0:T(8,128)(2,1)S(1)} all-gather(bf16[128,512]{1,0:T(8,128)(2,1)S(1)} %copy.47), channel_id=1, replica_groups=mesh['x'=4,'y'=8,'l'=2,'h'=4,'c'=2] {'h'}, dimensions={0}, use_global_device_ids=true | all-gather | bytes 655360 | tf_op jit(solution)/shard_map/all_gather | solution.py:241
  49.8 4.3 %all-to-all-start = ((bf16[4,128,512]{1,2,0:T(8,128)(2,1)}), bf16[4,128,512]{1,2,0:T(8,128)(2,1)S(1)}, u32[]{:S(2)}, u32[]{:S(2)}) async-start(bf16[4,128,512]{1,2,0:T(8,128)(2,1)} %copy.48), calls=%async_computation | async-start | bytes 1048576 | tf_op jit(solution)/shard_map/all_to_all | solution.py:41
  54.7 3.7 %collective-permute-start.4 = (f32[128,24]{0,1:T(8,128)S(1)}, f32[128,24]{0,1:T(8,128)S(1)}, u32[]{:S(2)}, u32[]{:S(2)}) collective-permute-start(f32[128,24]{0,1:T(8,128)S(1)} %get-tuple-element.87), channel_id=1, source_target_pairs={{0,8},{8,0},{1,9},{9,1},{2,10},{10,2},{3,11},{11,3},{4,12},{12,4},... | collective-permute-start | bytes 36872 | tf_op jit(solution)/shard_map/ppermute | solution.py:37
  64.4 5.2 %all-gather.2.cloned.1.call-done = bf16[1024,512]{1,0:T(8,128)(2,1)} async-done(((bf16[128,512]{1,0:T(8,128)(2,1)}), bf16[1024,512]{1,0:T(8,128)(2,1)}) %all-gather.2.cloned.1.call-update) | async-done | bytes 1048592 | tf_op jit(solution)/shard_map/all_gather | solution.py:233
  72.4 4.4 %all-to-all-start.1 = ((bf16[4,128,512]{2,1,0:T(8,128)(2,1)}), bf16[4,128,512]{2,1,0:T(8,128)(2,1)S(1)}, u32[]{:S(2)}, u32[]{:S(2)}) async-start(bf16[4,128,512]{2,1,0:T(8,128)(2,1)} %bitcast.12), calls=%async_computation.1 | async-start | bytes 1048576 | tf_op jit(solution)/shard_map/all_to_all | solution.py:41
  77.2 7.7 %all-to-all-done.1 = bf16[4,128,512]{2,1,0:T(8,128)(2,1)S(1)} async-done(((bf16[4,128,512]{2,1,0:T(8,128)(2,1)}), bf16[4,128,512]{2,1,0:T(8,128)(2,1)S(1)}, u32[]{:S(2)}, u32[]{:S(2)}) %all-to-all-start.1) | async-done | bytes 524320 | tf_op jit(solution)/shard_map/all_to_all | solution.py:41
  88.0 4.5 %collective-permute-done.6 = bf16[128,512]{1,0:T(8,128)(2,1)S(1)} collective-permute-done((bf16[128,512]{1,0:T(8,128)(2,1)S(1)}, bf16[128,512]{1,0:T(8,128)(2,1)S(1)}, u32[]{:S(2)}, u32[]{:S(2)}) %collective-permute-start.6) | collective-permute-done | bytes 131104 | tf_op jit(solution)/shard_map/ppermute | solution.py:37
  93.8 5.9 %all-to-all-start.2 = ((bf16[32,24,512]{2,1,0:T(8,128)(2,1)}), bf16[32,24,512]{2,1,0:T(8,128)(2,1)S(1)}, u32[]{:S(2)}, u32[]{:S(2)}) async-start(bf16[32,24,512]{2,1,0:T(8,128)(2,1)} %bitcast.21), calls=%async_computation.2 | async-start | bytes 1572864 | tf_op jit(solution)/shard_map/all_to_all | solution.py:41
  103.7 2.4 collective-permute-start.8
  107.0 9.7 %all-to-all-done.2 = bf16[32,24,512]{2,1,0:T(8,128)(2,1)S(1)} async-done(((bf16[32,24,512]{2,1,0:T(8,128)(2,1)}), bf16[32,24,512]{2,1,0:T(8,128)(2,1)S(1)}, u32[]{:S(2)}, u32[]{:S(2)}) %all-to-all-start.2) | async-done | bytes 786464 | tf_op jit(solution)/shard_map/all_to_all | solution.py:41
  120.8 3.4 %shard_map.185 = bf16[4,176,768]{2,1,0:T(8,128)(2,1)} custom-call(bf16[768,512]{1,0:T(8,128)(2,1)S(1)} %bitcast.150, bf16[768,512]{1,0:T(8,128)(2,1)S(1)} %collective-permute-done.9.other_ref, bf16[512,768]{1,0:T(8,128)(2,1)S(1)} %pad_maximum_fusion.w_own_ref, bf16[512,768]{1,0:T(8,128)(2,1)S(1)} %collective-permute-done.7.w_other_ref, ...), custom_call_target="tpu_custom_call" | custom-call | flops 100000000 | bytes 500000 | tf_op jit(solution)/shard_map/pallas_call | solution.py:151
  124.6 27.8 %all_to_all.30 = bf16[32,24,512]{2,1,0:T(8,128)(2,1)S(1)} all-to-all(bf16[32,24,512]{2,1,0:T(8,128)(2,1)S(1)} %bitcast.157), channel_id=1, replica_groups=mesh['x'=4,'y'=8,'l'=2,'h'=4,'c'=2] {'x','y'}, dimensions={0} | all-to-all | bytes 1572864 | tf_op jit(solution)/shard_map/all_to_all | solution.py:41
  152.4 5.4 %reduce-scatter.3.cloned.1.call-done.sums_ref = bf16[176,768]{1,0:T(8,128)(2,1)} async-done(((bf16[704,768]{1,0:T(8,128)(2,1)}), bf16[176,768]{1,0:T(8,128)(2,1)}) %reduce-scatter.3.cloned.1.call-update) | async-done | bytes 270352 | tf_op jit(solution)/shard_map/reduce_scatter | solution.py:294
  161.9 3.4 %shard_map.188 = bf16[4,176,768]{2,1,0:T(8,128)(2,1)} custom-call(bf16[768,512]{1,0:T(8,128)(2,1)S(1)} %bitcast.152, bf16[768,512]{1,0:T(8,128)(2,1)S(1)} %collective-permute-done.11.other_ref, bf16[512,768]{1,0:T(8,128)(2,1)S(1)} %pad_maximum_fusion.w_own_ref, bf16[512,768]{1,0:T(8,128)(2,1)S(1)} %collective-permute-done.7.w_other_ref, ...), custom_call_target="tpu_custom_call" | custom-call | flops 100000000 | bytes 500000 | tf_op jit(solution)/shard_map/pallas_call | solution.py:151
  166.5 18.3 %all_gather.14.own_ref = bf16[672,384]{1,0:T(8,128)(2,1)S(1)} all-gather(bf16[168,384]{1,0:T(8,128)(2,1)S(1)} %shard_map.186), channel_id=1, replica_groups=mesh['x'=4,'y'=8,'l'=2,'h'=4,'c'=2] {'h'}, dimensions={0}, use_global_device_ids=true | all-gather | bytes 645120 | tf_op jit(solution)/shard_map/all_gather | solution.py:297
  190.7 9.7 %all-to-all-start.4 = ((bf16[32,24,512]{2,1,0:T(8,128)(2,1)}), bf16[32,24,512]{2,1,0:T(8,128)(2,1)S(1)}, u32[]{:S(2)}, u32[]{:S(2)}) async-start(bf16[32,24,512]{2,1,0:T(8,128)(2,1)} %bitcast.42), calls=%async_computation.5 | async-start | bytes 1572864 | tf_op jit(solution)/shard_map/all_to_all | solution.py:41
  203.7 16.3 %all_gather.15.own_ref = bf16[672,384]{1,0:T(8,128)(2,1)S(1)} all-gather(bf16[168,384]{1,0:T(8,128)(2,1)S(1)} %shard_map.189), channel_id=1, replica_groups=mesh['x'=4,'y'=8,'l'=2,'h'=4,'c'=2] {'h'}, dimensions={0}, use_global_device_ids=true | all-gather | bytes 645120 | tf_op jit(solution)/shard_map/all_gather | solution.py:297
  220.0 3.7 %all-to-all-done.4 = bf16[32,24,512]{2,1,0:T(8,128)(2,1)S(1)} async-done(((bf16[32,24,512]{2,1,0:T(8,128)(2,1)}), bf16[32,24,512]{2,1,0:T(8,128)(2,1)S(1)}, u32[]{:S(2)}, u32[]{:S(2)}) %all-to-all-start.4) | async-done | bytes 786464 | tf_op jit(solution)/shard_map/all_to_all | solution.py:41
  229.7 7.2 %all-to-all-start.5 = ((bf16[32,24,512]{2,1,0:T(8,128)(2,1)}), bf16[32,24,512]{2,1,0:T(8,128)(2,1)S(1)}, u32[]{:S(2)}, u32[]{:S(2)}) async-start(bf16[32,24,512]{2,1,0:T(8,128)(2,1)} %bitcast.53), calls=%async_computation.7 | async-start | bytes 1572864 | tf_op jit(solution)/shard_map/all_to_all | solution.py:41
  239.5 4.9 %collective-permute-done.13 = bf16[128,512]{1,0:T(8,128)(2,1)S(1)} collective-permute-done((bf16[128,512]{1,0:T(8,128)(2,1)S(1)}, bf16[128,512]{1,0:T(8,128)(2,1)S(1)}, u32[]{:S(2)}, u32[]{:S(2)}) %collective-permute-start.13) | collective-permute-done | bytes 131104 | tf_op jit(solution)/shard_map/ppermute | solution.py:37
  244.4 15.8 %all-to-all-done.5 = bf16[32,24,512]{2,1,0:T(8,128)(2,1)S(1)} async-done(((bf16[32,24,512]{2,1,0:T(8,128)(2,1)}), bf16[32,24,512]{2,1,0:T(8,128)(2,1)S(1)}, u32[]{:S(2)}, u32[]{:S(2)}) %all-to-all-start.5) | async-done | bytes 786464 | tf_op jit(solution)/shard_map/all_to_all | solution.py:41
  (114 shorter events, 55.5 us)
Async XLA Ops:
  7.2 62.4 %all-gather.2.cloned.1.call-start = ((), (), s32[]{:S(2)}) async-start(), calls=%async_computation.8 | async-start | bytes 1179648 | tf_op jit(solution)/shard_map/all_gather | solution.py:233
  8.0 16.2 %collective-permute-start = (bf16[128,256]{1,0:T(8,128)(2,1)S(1)}, bf16[128,256]{1,0:T(8,128)(2,1)S(1)}, u32[]{:S(2)}, u32[]{:S(2)}) collective-permute-start(bf16[128,256]{1,0:T(8,128)(2,1)S(1)} %pad_maximum_fusion.2), channel_id=1, source_target_pairs={{0,24},{8,32},{16,40},{24,48},{32,56},{40,64},{48,72},{56,80},{64,... | collective-permute-start | bytes 196616 | tf_op jit(solution)/shard_map/ppermute | solution.py:46
  11.6 12.6 %collective-permute-start.1 = (bf16[128,256]{1,0:T(8,128)(2,1)S(1)}, bf16[128,256]{1,0:T(8,128)(2,1)S(1)}, u32[]{:S(2)}, u32[]{:S(2)}) collective-permute-start(bf16[128,256]{1,0:T(8,128)(2,1)S(1)} %pad_maximum_fusion.2), channel_id=1, source_target_pairs={{0,16},{8,24},{16,32},{24,40},{32,48},{40,56},{48,64},{56,72},{64,... | collective-permute-start | bytes 196616 | tf_op jit(solution)/shard_map/ppermute | solution.py:46
  16.3 7.9 %collective-permute-start.2 = (bf16[128,256]{1,0:T(8,128)(2,1)S(1)}, bf16[128,256]{1,0:T(8,128)(2,1)S(1)}, u32[]{:S(2)}, u32[]{:S(2)}) collective-permute-start(bf16[128,256]{1,0:T(8,128)(2,1)S(1)} %pad_maximum_fusion.2), channel_id=1, source_target_pairs={{0,8},{8,16},{16,24},{24,32},{32,40},{40,48},{48,56},{56,64},{64,7... | collective-permute-start | bytes 196616 | tf_op jit(solution)/shard_map/ppermute | solution.py:46
  20.6 6.4 %collective-permute-start.3 = (bf16[64,512]{1,0:T(8,128)(2,1)}, bf16[64,512]{1,0:T(8,128)(2,1)S(1)}, u32[]{:S(2)}, u32[]{:S(2)}) collective-permute-start(bf16[64,512]{1,0:T(8,128)(2,1)} %param.21), channel_id=1, source_target_pairs={{0,8},{8,0},{1,9},{9,1},{2,10},{10,2},{3,11},{11,3},{4,12},{12,4},... | collective-permute-start | bytes 196616 | tf_op jit(solution)/shard_map/ppermute | solution.py:37
  49.8 12.4 %all-to-all-start = ((bf16[4,128,512]{1,2,0:T(8,128)(2,1)}), bf16[4,128,512]{1,2,0:T(8,128)(2,1)S(1)}, u32[]{:S(2)}, u32[]{:S(2)}) async-start(bf16[4,128,512]{1,2,0:T(8,128)(2,1)} %copy.48), calls=%async_computation | async-start | bytes 1048576 | tf_op jit(solution)/shard_map/all_to_all | solution.py:41
  54.7 5.6 %collective-permute-start.4 = (f32[128,24]{0,1:T(8,128)S(1)}, f32[128,24]{0,1:T(8,128)S(1)}, u32[]{:S(2)}, u32[]{:S(2)}) collective-permute-start(f32[128,24]{0,1:T(8,128)S(1)} %get-tuple-element.87), channel_id=1, source_target_pairs={{0,8},{8,0},{1,9},{9,1},{2,10},{10,2},{3,11},{11,3},{4,12},{12,4},... | collective-permute-start | bytes 36872 | tf_op jit(solution)/shard_map/ppermute | solution.py:37
  62.4 8.7 %collective-permute-start.5 = (bf16[512,512]{1,0:T(8,128)(2,1)S(1)}, bf16[512,512]{1,0:T(8,128)(2,1)S(1)}, u32[]{:S(2)}, u32[]{:S(2)}) collective-permute-start(bf16[512,512]{1,0:T(8,128)(2,1)S(1)} %bitcast.158), channel_id=1, source_target_pairs={{0,1},{1,0},{2,3},{3,2},{4,5},{5,4},{6,7},{7,6},{8,9},{9,8},{10,11... | collective-permute-start | bytes 1572872 | tf_op jit(solution)/shard_map/ppermute | solution.py:37
  72.4 12.5 %all-to-all-start.1 = ((bf16[4,128,512]{2,1,0:T(8,128)(2,1)}), bf16[4,128,512]{2,1,0:T(8,128)(2,1)S(1)}, u32[]{:S(2)}, u32[]{:S(2)}) async-start(bf16[4,128,512]{2,1,0:T(8,128)(2,1)} %bitcast.12), calls=%async_computation.1 | async-start | bytes 1048576 | tf_op jit(solution)/shard_map/all_to_all | solution.py:41
  85.7 6.8 %collective-permute-start.6 = (bf16[128,512]{1,0:T(8,128)(2,1)S(1)}, bf16[128,512]{1,0:T(8,128)(2,1)S(1)}, u32[]{:S(2)}, u32[]{:S(2)}) collective-permute-start(bf16[128,512]{1,0:T(8,128)(2,1)S(1)} %get-tuple-element.62), channel_id=1, source_target_pairs={{0,8},{8,0},{1,9},{9,1},{2,10},{10,2},{3,11},{11,3},{4,12},{12,4},... | collective-permute-start | bytes 393224 | tf_op jit(solution)/shard_map/ppermute | solution.py:37
  93.8 22.9 %all-to-all-start.2 = ((bf16[32,24,512]{2,1,0:T(8,128)(2,1)}), bf16[32,24,512]{2,1,0:T(8,128)(2,1)S(1)}, u32[]{:S(2)}, u32[]{:S(2)}) async-start(bf16[32,24,512]{2,1,0:T(8,128)(2,1)} %bitcast.21), calls=%async_computation.2 | async-start | bytes 1572864 | tf_op jit(solution)/shard_map/all_to_all | solution.py:41
  99.7 58.0 %reduce-scatter.3.cloned.1.call-start = ((), (), s32[]{:S(2)}) async-start(), calls=%async_computation.9 | async-start | bytes 1351680 | tf_op jit(solution)/shard_map/reduce_scatter | solution.py:294
  101.0 5.9 %collective-permute-start.7 = (bf16[512,768]{1,0:T(8,128)(2,1)S(1)}, bf16[512,768]{1,0:T(8,128)(2,1)S(1)}, u32[]{:S(2)}, u32[]{:S(2)}) collective-permute-start(bf16[512,768]{1,0:T(8,128)(2,1)S(1)} %pad_maximum_fusion.1), channel_id=1, source_target_pairs={{0,1},{1,0},{2,3},{3,2},{4,5},{5,4},{6,7},{7,6},{8,9},{9,8},{10,11... | collective-permute-start | bytes 2359304 | tf_op jit(solution)/shard_map/ppermute | solution.py:37
  103.7 3.2 %collective-permute-start.8 = (f32[1,512]{1,0:T(1,128)S(1)}, f32[1,512]{1,0:T(1,128)S(1)}, u32[]{:S(2)}, u32[]{:S(2)}) collective-permute-start(f32[1,512]{1,0:T(1,128)S(1)} %bitcast.153), channel_id=1, source_target_pairs={{0,1},{1,0},{2,3},{3,2},{4,5},{5,4},{6,7},{7,6},{8,9},{9,8},{10,11... | collective-permute-start | bytes 6152 | tf_op jit(solution)/shard_map/ppermute | solution.py:37
  116.7 4.2 %collective-permute-start.9 = (bf16[768,512]{1,0:T(8,128)(2,1)S(1)}, bf16[768,512]{1,0:T(8,128)(2,1)S(1)}, u32[]{:S(2)}, u32[]{:S(2)}) collective-permute-start(bf16[768,512]{1,0:T(8,128)(2,1)S(1)} %bitcast.149), channel_id=1, source_target_pairs={{0,1},{1,0},{2,3},{3,2},{4,5},{5,4},{6,7},{7,6},{8,9},{9,8},{10,11... | collective-permute-start | bytes 2359304 | tf_op jit(solution)/shard_map/ppermute | solution.py:37
  124.3 78.3 %reduce-scatter.5.cloned.1.call-start = ((), (), s32[]{:S(2)}) async-start(), calls=%async_computation.10 | async-start | bytes 1351680 | tf_op jit(solution)/shard_map/reduce_scatter | solution.py:294
  157.8 4.2 %collective-permute-start.11 = (bf16[768,512]{1,0:T(8,128)(2,1)S(1)}, bf16[768,512]{1,0:T(8,128)(2,1)S(1)}, u32[]{:S(2)}, u32[]{:S(2)}) collective-permute-start(bf16[768,512]{1,0:T(8,128)(2,1)S(1)} %bitcast.151), channel_id=1, source_target_pairs={{0,1},{1,0},{2,3},{3,2},{4,5},{5,4},{6,7},{7,6},{8,9},{9,8},{10,11... | collective-permute-start | bytes 2359304 | tf_op jit(solution)/shard_map/ppermute | solution.py:37
  165.3 21.6 %copy-start.8 = (bf16[1,768,512]{2,1,0:T(8,128)(2,1)S(1)}, bf16[1,768,512]{2,1,0:T(8,128)(2,1)}, u32[]{:S(2)}) copy-start(bf16[1,768,512]{2,1,0:T(8,128)(2,1)} %param.26) | copy-start | bytes 2359300
  166.5 22.1 %copy-start.1 = (bf16[192,168]{1,0:T(8,128)(2,1)S(1)}, bf16[192,168]{1,0:T(8,128)(2,1)}, u32[]{:S(2)}) copy-start(bf16[192,168]{1,0:T(8,128)(2,1)} %constant.89.clone.place_ref) | copy-start | bytes 193540
  184.8 3.8 %collective-permute-start.10 = (bf16[672,384]{1,0:T(8,128)(2,1)S(1)}, bf16[672,384]{1,0:T(8,128)(2,1)S(1)}, u32[]{:S(2)}, u32[]{:S(2)}) collective-permute-start(bf16[672,384]{1,0:T(8,128)(2,1)S(1)} %all_gather.14.own_ref), channel_id=1, source_target_pairs={{0,1},{1,0},{2,3},{3,2},{4,5},{5,4},{6,7},{7,6},{8,9},{9,8},{10,11... | collective-permute-start | bytes 1548296 | tf_op jit(solution)/shard_map/ppermute | solution.py:37
  190.7 33.0 %all-to-all-start.4 = ((bf16[32,24,512]{2,1,0:T(8,128)(2,1)}), bf16[32,24,512]{2,1,0:T(8,128)(2,1)S(1)}, u32[]{:S(2)}, u32[]{:S(2)}) async-start(bf16[32,24,512]{2,1,0:T(8,128)(2,1)} %bitcast.42), calls=%async_computation.5 | async-start | bytes 1572864 | tf_op jit(solution)/shard_map/all_to_all | solution.py:41
  223.7 3.8 %collective-permute-start.12 = (bf16[672,384]{1,0:T(8,128)(2,1)S(1)}, bf16[672,384]{1,0:T(8,128)(2,1)S(1)}, u32[]{:S(2)}, u32[]{:S(2)}) collective-permute-start(bf16[672,384]{1,0:T(8,128)(2,1)S(1)} %all_gather.15.own_ref), channel_id=1, source_target_pairs={{0,1},{1,0},{2,3},{3,2},{4,5},{5,4},{6,7},{7,6},{8,9},{9,8},{10,11... | collective-permute-start | bytes 1548296 | tf_op jit(solution)/shard_map/ppermute | solution.py:37
  229.7 30.5 %all-to-all-start.5 = ((bf16[32,24,512]{2,1,0:T(8,128)(2,1)}), bf16[32,24,512]{2,1,0:T(8,128)(2,1)S(1)}, u32[]{:S(2)}, u32[]{:S(2)}) async-start(bf16[32,24,512]{2,1,0:T(8,128)(2,1)} %bitcast.53), calls=%async_computation.7 | async-start | bytes 1572864 | tf_op jit(solution)/shard_map/all_to_all | solution.py:41
  237.5 6.9 %collective-permute-start.13 = (bf16[128,512]{1,0:T(8,128)(2,1)S(1)}, bf16[128,512]{1,0:T(8,128)(2,1)S(1)}, u32[]{:S(2)}, u32[]{:S(2)}) collective-permute-start(bf16[128,512]{1,0:T(8,128)(2,1)S(1)} %convolution_convert_fusion.2), channel_id=1, source_target_pairs={{0,8},{8,0},{1,9},{9,1},{2,10},{10,2},{3,11},{11,3},{4,12},{12,4},... | collective-permute-start | bytes 393224 | tf_op jit(solution)/shard_map/ppermute | solution.py:37
  (13 other events, 96.6 us)
Sparse Core Ops, SparseCore 0:
  27.9 41.5 all-gather.1
  124.4 33.3 reduce-scatter.2
  165.5 37.0 reduce-scatter.4

commit v13 on v12

--- a/solution.py
+++ b/solution.py
@@ -46,7 +46,7 @@
     return lax.ppermute(block, CTX, route)
 
 
-def attention(queries, key_rows, value_rows):
+def attention(queries, key_rows, value_rows, strips):
     tokens = queries.shape[0]
     block = lax.axis_index(CTX)
     kv_first = lax.axis_index("h") // 2 * HD
@@ -57,7 +57,9 @@
         ],
         axis=1,
     )
-    pairs = [from_behind(own, 3), from_behind(own, 2), from_behind(own, 1), own]
+    near = [from_behind(own, 2), from_behind(own, 1), own]
+    sent, strips = lax.optimization_barrier((own, strips))
+    pairs = [from_behind(sent, 3), *near]
     keys = jnp.concatenate([pair[:, :HD] for pair in pairs], axis=0)
     values = jnp.concatenate([pair[:, HD:] for pair in pairs], axis=0)
     q_view = queries.reshape(tokens, -1, HD)
@@ -73,7 +75,7 @@
         jnp.einsum("gts,sd->gtd", weights.astype(bf16), values, preferred_element_type=f32)
         / denominators
     )
-    return jnp.transpose(mixed, (1, 0, 2)).reshape(tokens, -1).astype(bf16)
+    return jnp.transpose(mixed, (1, 0, 2)).reshape(tokens, -1).astype(bf16), strips
 
 
 def slots_of(pred_ids, fix_pair, fix_expert, fix_count):
@@ -220,16 +222,13 @@
     tokens = queries.shape[0]
     half = FF // 2
 
-    attended = attention(queries, key_rows, value_rows)
-
     other_strip = swap(out_weight, "l")
-    attended, other_strip = lax.optimization_barrier((attended, other_strip))
     strips = jnp.where(
         side == 0,
         jnp.concatenate([out_weight, other_strip], axis=0),
         jnp.concatenate([other_strip, out_weight], axis=0),
     )
-    strips, attended = lax.optimization_barrier((strips, attended))
+    attended, strips = attention(queries, key_rows, value_rows, strips)
     quarter = lax.all_gather(strips, "y", axis=0, tiled=True)
 
     attended, pred_ids, fix_pair = lax.optimization_barrier((attended, pred_ids, fix_pair))

time: 269 us -> 272 us (1.011)
  starting transfers between devices: 68.2 us -> 73.2 us
  waiting for transfers between devices: 73 us -> 70.2 us
    all_to_all x5, waiting for transfers between devices: 38.8 us -> 44.9 us  [exchange(): return lax.all_to_all(blocks, axes, split_axis=0, concat_axis=0, tiled=True)]
    all_gather x1, waiting for transfers between devices: 5.18 us -> 0.29 us  [body(): quarter = lax.all_gather(strips, 'y', axis=0, tiled=True)]
    ppermute x11, starting transfers between devices: 24 us -> 28.4 us  [swap(): return lax.ppermute(block, axis, [(0, 1), (1, 0)])]
    reduce_scatter x2, waiting for transfers between devices: 7.45 us -> 3.21 us  [reduced(): return lax.psum_scatter(flat, 'h', scatter_dimension=0, tiled=True)]
  transfers between devices with their start and end apart: 22 -> 22, of which waited for: 17 -> 18; matrix products, arithmetic and copies ran while one was open for 3% -> 4% of each run, Pallas kernels for 1% -> 1%
where the time goes in v13:
time: 272 us; the launch traced here: 271 us
  blocking collectives  83.9 us (31%)
  starting transfers between devices  73.2 us (27%)
  waiting for transfers between devices  70.2 us (26%)
  between operations  15 us (6%)
  Pallas kernels  11.5 us (4%)
  matrix products  7.38 us (3%)
  local copies, waits for them, and re-layouts  5.31 us (2%)
  other arithmetic  4.85 us (2%)
    all_to_all x5, waiting for transfers between devices, exchange(): return lax.all_to_all(blocks, axes, split_axis=0, concat_axis=0, tiled=True)  44.9 us
    all_gather x2, blocking collectives, gathered(): return lax.all_gather(activated(sums), 'h', axis=0, tiled=True)  34.4 us
    all_to_all x5, starting transfers between devices, exchange(): return lax.all_to_all(blocks, axes, split_axis=0, concat_axis=0, tiled=True)  32.1 us
    ppermute x11, starting transfers between devices, swap(): return lax.ppermute(block, axis, [(0, 1), (1, 0)])  28.4 us
    all_to_all x1, blocking collectives, exchange(): return lax.all_to_all(blocks, axes, split_axis=0, concat_axis=0, tiled=True)  28 us
    all_gather x1, blocking collectives, body(): lax.all_gather(attended, 'h', axis=0, tiled=True).reshape(NH, tokens, SLICE)  21.5 us
    ppermute x11, waiting for transfers between devices, swap(): return lax.ppermute(block, axis, [(0, 1), (1, 0)])  19.9 us
    ppermute x3, starting transfers between devices, from_behind(): return lax.ppermute(block, CTX, route)  12.6 us
  transfers between devices with their start and end apart: 22, of which 18 were waited for; matrix products, arithmetic and copies ran while one was open for 4% of the time, Pallas kernels for 1%

profile of v13, /device:TPU:72, one launch (start us, length us, event | category | flops | bytes accessed | tf_op | source)
XLA Modules:
  0.0 271.2 jit_solution(10327490669776750547)
XLA Ops:
  8.0 3.5 %collective-permute-start.2 = (bf16[128,256]{1,0:T(8,128)(2,1)S(1)}, bf16[128,256]{1,0:T(8,128)(2,1)S(1)}, u32[]{:S(2)}, u32[]{:S(2)}) collective-permute-start(bf16[128,256]{1,0:T(8,128)(2,1)S(1)} %pad_maximum_fusion.2), channel_id=1, source_target_pairs={{0,16},{8,24},{16,32},{24,40},{32,48},{40,56},{48,64},{56,72},{64,... | collective-permute-start | bytes 196616 | tf_op jit(solution)/shard_map/ppermute | solution.py:46
  11.5 2.6 collective-permute-start.3
  14.1 3.3 %collective-permute-start = (bf16[64,512]{1,0:T(8,128)(2,1)}, bf16[64,512]{1,0:T(8,128)(2,1)S(1)}, u32[]{:S(2)}, u32[]{:S(2)}) collective-permute-start(bf16[64,512]{1,0:T(8,128)(2,1)} %param.21), channel_id=1, source_target_pairs={{0,8},{8,0},{1,9},{9,1},{2,10},{10,2},{3,11},{11,3},{4,12},{12,4},... | collective-permute-start | bytes 196616 | tf_op jit(solution)/shard_map/ppermute | solution.py:37
  22.1 6.5 %collective-permute-start.1 = (bf16[128,256]{1,0:T(8,128)(2,1)S(1)}, bf16[128,256]{1,0:T(8,128)(2,1)S(1)}, u32[]{:S(2)}, u32[]{:S(2)}) collective-permute-start(bf16[128,256]{1,0:T(8,128)(2,1)S(1)} %pad_maximum_fusion.2), channel_id=1, source_target_pairs={{0,24},{8,32},{16,40},{24,48},{32,56},{40,64},{48,72},{56,80},{64,... | collective-permute-start | bytes 196616 | tf_op jit(solution)/shard_map/ppermute | solution.py:46
  31.9 21.5 %all_gather.12 = bf16[512,512]{1,0:T(8,128)(2,1)S(1)} all-gather(bf16[128,512]{1,0:T(8,128)(2,1)S(1)} %copy.47), channel_id=1, replica_groups=mesh['x'=4,'y'=8,'l'=2,'h'=4,'c'=2] {'h'}, dimensions={0}, use_global_device_ids=true | all-gather | bytes 655360 | tf_op jit(solution)/shard_map/all_gather | solution.py:240
  54.4 4.5 %all-to-all-start = ((bf16[4,128,512]{1,2,0:T(8,128)(2,1)}), bf16[4,128,512]{1,2,0:T(8,128)(2,1)S(1)}, u32[]{:S(2)}, u32[]{:S(2)}) async-start(bf16[4,128,512]{1,2,0:T(8,128)(2,1)} %copy.48), calls=%async_computation | async-start | bytes 1048576 | tf_op jit(solution)/shard_map/all_to_all | solution.py:41
  59.4 4.5 %collective-permute-start.4 = (f32[128,24]{0,1:T(8,128)S(1)}, f32[128,24]{0,1:T(8,128)S(1)}, u32[]{:S(2)}, u32[]{:S(2)}) collective-permute-start(f32[128,24]{0,1:T(8,128)S(1)} %get-tuple-element.83), channel_id=1, source_target_pairs={{0,8},{8,0},{1,9},{9,1},{2,10},{10,2},{3,11},{11,3},{4,12},{12,4},... | collective-permute-start | bytes 36872 | tf_op jit(solution)/shard_map/ppermute | solution.py:37
  72.2 4.3 %all-to-all-start.1 = ((bf16[4,128,512]{2,1,0:T(8,128)(2,1)}), bf16[4,128,512]{2,1,0:T(8,128)(2,1)S(1)}, u32[]{:S(2)}, u32[]{:S(2)}) async-start(bf16[4,128,512]{2,1,0:T(8,128)(2,1)} %bitcast.12), calls=%async_computation.1 | async-start | bytes 1048576 | tf_op jit(solution)/shard_map/all_to_all | solution.py:41
  76.9 9.0 %all-to-all-done.1 = bf16[4,128,512]{2,1,0:T(8,128)(2,1)S(1)} async-done(((bf16[4,128,512]{2,1,0:T(8,128)(2,1)}), bf16[4,128,512]{2,1,0:T(8,128)(2,1)S(1)}, u32[]{:S(2)}, u32[]{:S(2)}) %all-to-all-start.1) | async-done | bytes 524320 | tf_op jit(solution)/shard_map/all_to_all | solution.py:41
  86.7 4.5 %collective-permute-start.6 = (bf16[128,512]{1,0:T(8,128)(2,1)S(1)}, bf16[128,512]{1,0:T(8,128)(2,1)S(1)}, u32[]{:S(2)}, u32[]{:S(2)}) collective-permute-start(bf16[128,512]{1,0:T(8,128)(2,1)S(1)} %get-tuple-element.58), channel_id=1, source_target_pairs={{0,8},{8,0},{1,9},{9,1},{2,10},{10,2},{3,11},{11,3},{4,12},{12,4},... | collective-permute-start | bytes 393224 | tf_op jit(solution)/shard_map/ppermute | solution.py:37
  91.2 3.1 %collective-permute-done.6 = bf16[128,512]{1,0:T(8,128)(2,1)S(1)} collective-permute-done((bf16[128,512]{1,0:T(8,128)(2,1)S(1)}, bf16[128,512]{1,0:T(8,128)(2,1)S(1)}, u32[]{:S(2)}, u32[]{:S(2)}) %collective-permute-start.6) | collective-permute-done | bytes 131104 | tf_op jit(solution)/shard_map/ppermute | solution.py:37
  95.6 6.4 %all-to-all-start.2 = ((bf16[32,24,512]{2,1,0:T(8,128)(2,1)}), bf16[32,24,512]{2,1,0:T(8,128)(2,1)S(1)}, u32[]{:S(2)}, u32[]{:S(2)}) async-start(bf16[32,24,512]{2,1,0:T(8,128)(2,1)} %bitcast.21), calls=%async_computation.2 | async-start | bytes 1572864 | tf_op jit(solution)/shard_map/all_to_all | solution.py:41
  106.0 2.4 collective-permute-start.8
  109.2 14.9 %all-to-all-done.2 = bf16[32,24,512]{2,1,0:T(8,128)(2,1)S(1)} async-done(((bf16[32,24,512]{2,1,0:T(8,128)(2,1)}), bf16[32,24,512]{2,1,0:T(8,128)(2,1)S(1)}, u32[]{:S(2)}, u32[]{:S(2)}) %all-to-all-start.2) | async-done | bytes 786464 | tf_op jit(solution)/shard_map/all_to_all | solution.py:41
  128.3 3.4 %shard_map.185 = bf16[4,176,768]{2,1,0:T(8,128)(2,1)} custom-call(bf16[768,512]{1,0:T(8,128)(2,1)S(1)} %bitcast.150, bf16[768,512]{1,0:T(8,128)(2,1)S(1)} %collective-permute-done.9.other_ref, bf16[512,768]{1,0:T(8,128)(2,1)S(1)} %pad_maximum_fusion.w_own_ref, bf16[512,768]{1,0:T(8,128)(2,1)S(1)} %collective-permute-done.7.w_other_ref, ...), custom_call_target="tpu_custom_call" | custom-call | flops 100000000 | bytes 500000 | tf_op jit(solution)/shard_map/pallas_call | solution.py:153
  132.2 28.0 %all_to_all.30 = bf16[32,24,512]{2,1,0:T(8,128)(2,1)S(1)} all-to-all(bf16[32,24,512]{2,1,0:T(8,128)(2,1)S(1)} %bitcast.157), channel_id=1, replica_groups=mesh['x'=4,'y'=8,'l'=2,'h'=4,'c'=2] {'x','y'}, dimensions={0} | all-to-all | bytes 1572864 | tf_op jit(solution)/shard_map/all_to_all | solution.py:41
  166.0 3.4 %shard_map.188 = bf16[4,176,768]{2,1,0:T(8,128)(2,1)} custom-call(bf16[768,512]{1,0:T(8,128)(2,1)S(1)} %bitcast.152, bf16[768,512]{1,0:T(8,128)(2,1)S(1)} %collective-permute-done.11.other_ref, bf16[512,768]{1,0:T(8,128)(2,1)S(1)} %pad_maximum_fusion.w_own_ref, bf16[512,768]{1,0:T(8,128)(2,1)S(1)} %collective-permute-done.7.w_other_ref, ...), custom_call_target="tpu_custom_call" | custom-call | flops 100000000 | bytes 500000 | tf_op jit(solution)/shard_map/pallas_call | solution.py:153
  170.5 17.8 %all_gather.14.own_ref = bf16[672,384]{1,0:T(8,128)(2,1)S(1)} all-gather(bf16[168,384]{1,0:T(8,128)(2,1)S(1)} %shard_map.186), channel_id=1, replica_groups=mesh['x'=4,'y'=8,'l'=2,'h'=4,'c'=2] {'h'}, dimensions={0}, use_global_device_ids=true | all-gather | bytes 645120 | tf_op jit(solution)/shard_map/all_gather | solution.py:296
  194.2 10.0 %all-to-all-start.4 = ((bf16[32,24,512]{2,1,0:T(8,128)(2,1)}), bf16[32,24,512]{2,1,0:T(8,128)(2,1)S(1)}, u32[]{:S(2)}, u32[]{:S(2)}) async-start(bf16[32,24,512]{2,1,0:T(8,128)(2,1)} %bitcast.42), calls=%async_computation.5 | async-start | bytes 1572864 | tf_op jit(solution)/shard_map/all_to_all | solution.py:41
  206.9 16.6 %all_gather.15.own_ref = bf16[672,384]{1,0:T(8,128)(2,1)S(1)} all-gather(bf16[168,384]{1,0:T(8,128)(2,1)S(1)} %shard_map.189), channel_id=1, replica_groups=mesh['x'=4,'y'=8,'l'=2,'h'=4,'c'=2] {'h'}, dimensions={0}, use_global_device_ids=true | all-gather | bytes 645120 | tf_op jit(solution)/shard_map/all_gather | solution.py:296
  223.6 3.9 %all-to-all-done.4 = bf16[32,24,512]{2,1,0:T(8,128)(2,1)S(1)} async-done(((bf16[32,24,512]{2,1,0:T(8,128)(2,1)}), bf16[32,24,512]{2,1,0:T(8,128)(2,1)S(1)}, u32[]{:S(2)}, u32[]{:S(2)}) %all-to-all-start.4) | async-done | bytes 786464 | tf_op jit(solution)/shard_map/all_to_all | solution.py:41
  233.4 7.0 %all-to-all-start.5 = ((bf16[32,24,512]{2,1,0:T(8,128)(2,1)}), bf16[32,24,512]{2,1,0:T(8,128)(2,1)S(1)}, u32[]{:S(2)}, u32[]{:S(2)}) async-start(bf16[32,24,512]{2,1,0:T(8,128)(2,1)} %bitcast.53), calls=%async_computation.7 | async-start | bytes 1572864 | tf_op jit(solution)/shard_map/all_to_all | solution.py:41
  243.0 4.9 %collective-permute-done.13 = bf16[128,512]{1,0:T(8,128)(2,1)S(1)} collective-permute-done((bf16[128,512]{1,0:T(8,128)(2,1)S(1)}, bf16[128,512]{1,0:T(8,128)(2,1)S(1)}, u32[]{:S(2)}, u32[]{:S(2)}) %collective-permute-start.13) | collective-permute-done | bytes 131104 | tf_op jit(solution)/shard_map/ppermute | solution.py:37
  247.9 15.8 %all-to-all-done.5 = bf16[32,24,512]{2,1,0:T(8,128)(2,1)S(1)} async-done(((bf16[32,24,512]{2,1,0:T(8,128)(2,1)}), bf16[32,24,512]{2,1,0:T(8,128)(2,1)S(1)}, u32[]{:S(2)}, u32[]{:S(2)}) %all-to-all-start.5) | async-done | bytes 786464 | tf_op jit(solution)/shard_map/all_to_all | solution.py:41
  (112 shorter events, 54.6 us)
Async XLA Ops:
  7.2 23.3 %copy-start = (bf16[128,512]{1,0:T(8,128)(2,1)S(1)}, bf16[128,512]{1,0:T(8,128)(2,1)}, u32[]{:S(2)}) copy-start(bf16[128,512]{1,0:T(8,128)(2,1)} %param.18) | copy-start | bytes 393220
  7.2 62.2 %all-gather.2.cloned.1.call-start = ((), (), s32[]{:S(2)}) async-start(), calls=%async_computation.8 | async-start | bytes 1179648 | tf_op jit(solution)/shard_map/all_gather | solution.py:232
  8.0 20.6 %collective-permute-start.2 = (bf16[128,256]{1,0:T(8,128)(2,1)S(1)}, bf16[128,256]{1,0:T(8,128)(2,1)S(1)}, u32[]{:S(2)}, u32[]{:S(2)}) collective-permute-start(bf16[128,256]{1,0:T(8,128)(2,1)S(1)} %pad_maximum_fusion.2), channel_id=1, source_target_pairs={{0,16},{8,24},{16,32},{24,40},{32,48},{40,56},{48,64},{56,72},{64,... | collective-permute-start | bytes 196616 | tf_op jit(solution)/shard_map/ppermute | solution.py:46
  11.5 17.1 %collective-permute-start.3 = (bf16[128,256]{1,0:T(8,128)(2,1)S(1)}, bf16[128,256]{1,0:T(8,128)(2,1)S(1)}, u32[]{:S(2)}, u32[]{:S(2)}) collective-permute-start(bf16[128,256]{1,0:T(8,128)(2,1)S(1)} %pad_maximum_fusion.2), channel_id=1, source_target_pairs={{0,8},{8,16},{16,24},{24,32},{32,40},{40,48},{48,56},{56,64},{64,7... | collective-permute-start | bytes 196616 | tf_op jit(solution)/shard_map/ppermute | solution.py:46
  14.1 6.4 %collective-permute-start = (bf16[64,512]{1,0:T(8,128)(2,1)}, bf16[64,512]{1,0:T(8,128)(2,1)S(1)}, u32[]{:S(2)}, u32[]{:S(2)}) collective-permute-start(bf16[64,512]{1,0:T(8,128)(2,1)} %param.21), channel_id=1, source_target_pairs={{0,8},{8,0},{1,9},{9,1},{2,10},{10,2},{3,11},{11,3},{4,12},{12,4},... | collective-permute-start | bytes 196616 | tf_op jit(solution)/shard_map/ppermute | solution.py:37
  22.1 8.4 %collective-permute-start.1 = (bf16[128,256]{1,0:T(8,128)(2,1)S(1)}, bf16[128,256]{1,0:T(8,128)(2,1)S(1)}, u32[]{:S(2)}, u32[]{:S(2)}) collective-permute-start(bf16[128,256]{1,0:T(8,128)(2,1)S(1)} %pad_maximum_fusion.2), channel_id=1, source_target_pairs={{0,24},{8,32},{16,40},{24,48},{32,56},{40,64},{48,72},{56,80},{64,... | collective-permute-start | bytes 196616 | tf_op jit(solution)/shard_map/ppermute | solution.py:46
  54.4 12.6 %all-to-all-start = ((bf16[4,128,512]{1,2,0:T(8,128)(2,1)}), bf16[4,128,512]{1,2,0:T(8,128)(2,1)S(1)}, u32[]{:S(2)}, u32[]{:S(2)}) async-start(bf16[4,128,512]{1,2,0:T(8,128)(2,1)} %copy.48), calls=%async_computation | async-start | bytes 1048576 | tf_op jit(solution)/shard_map/all_to_all | solution.py:41
  59.4 6.2 %collective-permute-start.4 = (f32[128,24]{0,1:T(8,128)S(1)}, f32[128,24]{0,1:T(8,128)S(1)}, u32[]{:S(2)}, u32[]{:S(2)}) collective-permute-start(f32[128,24]{0,1:T(8,128)S(1)} %get-tuple-element.83), channel_id=1, source_target_pairs={{0,8},{8,0},{1,9},{9,1},{2,10},{10,2},{3,11},{11,3},{4,12},{12,4},... | collective-permute-start | bytes 36872 | tf_op jit(solution)/shard_map/ppermute | solution.py:37
  67.1 3.8 %collective-permute-start.5 = (bf16[512,512]{1,0:T(8,128)(2,1)S(1)}, bf16[512,512]{1,0:T(8,128)(2,1)S(1)}, u32[]{:S(2)}, u32[]{:S(2)}) collective-permute-start(bf16[512,512]{1,0:T(8,128)(2,1)S(1)} %bitcast.158), channel_id=1, source_target_pairs={{0,1},{1,0},{2,3},{3,2},{4,5},{5,4},{6,7},{7,6},{8,9},{9,8},{10,11... | collective-permute-start | bytes 1572872 | tf_op jit(solution)/shard_map/ppermute | solution.py:37
  72.2 13.7 %all-to-all-start.1 = ((bf16[4,128,512]{2,1,0:T(8,128)(2,1)}), bf16[4,128,512]{2,1,0:T(8,128)(2,1)S(1)}, u32[]{:S(2)}, u32[]{:S(2)}) async-start(bf16[4,128,512]{2,1,0:T(8,128)(2,1)} %bitcast.12), calls=%async_computation.1 | async-start | bytes 1048576 | tf_op jit(solution)/shard_map/all_to_all | solution.py:41
  86.7 7.6 %collective-permute-start.6 = (bf16[128,512]{1,0:T(8,128)(2,1)S(1)}, bf16[128,512]{1,0:T(8,128)(2,1)S(1)}, u32[]{:S(2)}, u32[]{:S(2)}) collective-permute-start(bf16[128,512]{1,0:T(8,128)(2,1)S(1)} %get-tuple-element.58), channel_id=1, source_target_pairs={{0,8},{8,0},{1,9},{9,1},{2,10},{10,2},{3,11},{11,3},{4,12},{12,4},... | collective-permute-start | bytes 393224 | tf_op jit(solution)/shard_map/ppermute | solution.py:37
  95.6 28.6 %all-to-all-start.2 = ((bf16[32,24,512]{2,1,0:T(8,128)(2,1)}), bf16[32,24,512]{2,1,0:T(8,128)(2,1)S(1)}, u32[]{:S(2)}, u32[]{:S(2)}) async-start(bf16[32,24,512]{2,1,0:T(8,128)(2,1)} %bitcast.21), calls=%async_computation.2 | async-start | bytes 1572864 | tf_op jit(solution)/shard_map/all_to_all | solution.py:41
  102.0 59.8 %reduce-scatter.3.cloned.1.call-start = ((), (), s32[]{:S(2)}) async-start(), calls=%async_computation.9 | async-start | bytes 1351680 | tf_op jit(solution)/shard_map/reduce_scatter | solution.py:293
  103.3 25.0 %copy-start.2 = (bf16[168,192]{1,0:T(8,128)(2,1)S(1)}, bf16[168,192]{1,0:T(8,128)(2,1)}, u32[]{:S(2)}) copy-start(bf16[168,192]{1,0:T(8,128)(2,1)} %constant.88.clone.pick_ref) | copy-start | bytes 193540
  103.3 5.9 %collective-permute-start.7 = (bf16[512,768]{1,0:T(8,128)(2,1)S(1)}, bf16[512,768]{1,0:T(8,128)(2,1)S(1)}, u32[]{:S(2)}, u32[]{:S(2)}) collective-permute-start(bf16[512,768]{1,0:T(8,128)(2,1)S(1)} %pad_maximum_fusion.1), channel_id=1, source_target_pairs={{0,1},{1,0},{2,3},{3,2},{4,5},{5,4},{6,7},{7,6},{8,9},{9,8},{10,11... | collective-permute-start | bytes 2359304 | tf_op jit(solution)/shard_map/ppermute | solution.py:37
  106.0 3.2 %collective-permute-start.8 = (f32[1,512]{1,0:T(1,128)S(1)}, f32[1,512]{1,0:T(1,128)S(1)}, u32[]{:S(2)}, u32[]{:S(2)}) collective-permute-start(f32[1,512]{1,0:T(1,128)S(1)} %bitcast.153), channel_id=1, source_target_pairs={{0,1},{1,0},{2,3},{3,2},{4,5},{5,4},{6,7},{7,6},{8,9},{9,8},{10,11... | collective-permute-start | bytes 6152 | tf_op jit(solution)/shard_map/ppermute | solution.py:37
  124.2 4.2 %collective-permute-start.9 = (bf16[768,512]{1,0:T(8,128)(2,1)S(1)}, bf16[768,512]{1,0:T(8,128)(2,1)S(1)}, u32[]{:S(2)}, u32[]{:S(2)}) collective-permute-start(bf16[768,512]{1,0:T(8,128)(2,1)S(1)} %bitcast.149), channel_id=1, source_target_pairs={{0,1},{1,0},{2,3},{3,2},{4,5},{5,4},{6,7},{7,6},{8,9},{9,8},{10,11... | collective-permute-start | bytes 2359304 | tf_op jit(solution)/shard_map/ppermute | solution.py:37
  131.8 74.0 %reduce-scatter.5.cloned.1.call-start = ((), (), s32[]{:S(2)}) async-start(), calls=%async_computation.10 | async-start | bytes 1351680 | tf_op jit(solution)/shard_map/reduce_scatter | solution.py:293
  161.8 4.2 %collective-permute-start.11 = (bf16[768,512]{1,0:T(8,128)(2,1)S(1)}, bf16[768,512]{1,0:T(8,128)(2,1)S(1)}, u32[]{:S(2)}, u32[]{:S(2)}) collective-permute-start(bf16[768,512]{1,0:T(8,128)(2,1)S(1)} %bitcast.151), channel_id=1, source_target_pairs={{0,1},{1,0},{2,3},{3,2},{4,5},{5,4},{6,7},{7,6},{8,9},{9,8},{10,11... | collective-permute-start | bytes 2359304 | tf_op jit(solution)/shard_map/ppermute | solution.py:37
  188.3 3.8 %collective-permute-start.10 = (bf16[672,384]{1,0:T(8,128)(2,1)S(1)}, bf16[672,384]{1,0:T(8,128)(2,1)S(1)}, u32[]{:S(2)}, u32[]{:S(2)}) collective-permute-start(bf16[672,384]{1,0:T(8,128)(2,1)S(1)} %all_gather.14.own_ref), channel_id=1, source_target_pairs={{0,1},{1,0},{2,3},{3,2},{4,5},{5,4},{6,7},{7,6},{8,9},{9,8},{10,11... | collective-permute-start | bytes 1548296 | tf_op jit(solution)/shard_map/ppermute | solution.py:37
  194.2 33.3 %all-to-all-start.4 = ((bf16[32,24,512]{2,1,0:T(8,128)(2,1)}), bf16[32,24,512]{2,1,0:T(8,128)(2,1)S(1)}, u32[]{:S(2)}, u32[]{:S(2)}) async-start(bf16[32,24,512]{2,1,0:T(8,128)(2,1)} %bitcast.42), calls=%async_computation.5 | async-start | bytes 1572864 | tf_op jit(solution)/shard_map/all_to_all | solution.py:41
  227.5 3.8 %collective-permute-start.12 = (bf16[672,384]{1,0:T(8,128)(2,1)S(1)}, bf16[672,384]{1,0:T(8,128)(2,1)S(1)}, u32[]{:S(2)}, u32[]{:S(2)}) collective-permute-start(bf16[672,384]{1,0:T(8,128)(2,1)S(1)} %all_gather.15.own_ref), channel_id=1, source_target_pairs={{0,1},{1,0},{2,3},{3,2},{4,5},{5,4},{6,7},{7,6},{8,9},{9,8},{10,11... | collective-permute-start | bytes 1548296 | tf_op jit(solution)/shard_map/ppermute | solution.py:37
  233.4 30.2 %all-to-all-start.5 = ((bf16[32,24,512]{2,1,0:T(8,128)(2,1)}), bf16[32,24,512]{2,1,0:T(8,128)(2,1)S(1)}, u32[]{:S(2)}, u32[]{:S(2)}) async-start(bf16[32,24,512]{2,1,0:T(8,128)(2,1)} %bitcast.53), calls=%async_computation.7 | async-start | bytes 1572864 | tf_op jit(solution)/shard_map/all_to_all | solution.py:41
  241.0 6.9 %collective-permute-start.13 = (bf16[128,512]{1,0:T(8,128)(2,1)S(1)}, bf16[128,512]{1,0:T(8,128)(2,1)S(1)}, u32[]{:S(2)}, u32[]{:S(2)}) collective-permute-start(bf16[128,512]{1,0:T(8,128)(2,1)S(1)} %convolution_convert_fusion.2), channel_id=1, source_target_pairs={{0,8},{8,0},{1,9},{9,1},{2,10},{10,2},{3,11},{11,3},{4,12},{12,4},... | collective-permute-start | bytes 393224 | tf_op jit(solution)/shard_map/ppermute | solution.py:37
  (12 other events, 102.5 us)
Sparse Core Ops, SparseCore 0:
  28.7 40.5 all-gather.1
  131.9 29.8 reduce-scatter.2
  169.5 36.2 reduce-scatter.4

commit v14 on v12

--- a/solution.py
+++ b/solution.py
@@ -238,7 +238,7 @@
     slots, gates = row_slots(table.T, side.astype(f32))
     pick = spread(slots, jnp.ones_like(slots))
 
-    heads = lax.all_gather(attended, "h", axis=0, tiled=True).reshape(NH, tokens, SLICE)
+    heads = exchange(jnp.broadcast_to(attended[None], (NH, *attended.shape)), "h")
     other_slots, other_gates = row_slots(swap(table, "l").T, side.astype(f32))
     heads = exchange(heads, "x").reshape(NX * tokens, SLICE)
     heads, other_slots = lax.optimization_barrier((heads, other_slots))

time: 269 us -> 267 us (level)
  blocking collectives: 83.3 us -> 62.2 us
  waiting for transfers between devices: 73 us -> 84.3 us
  starting transfers between devices: 68.2 us -> 76.5 us
    all_gather x1 -> x0, blocking collectives: 21 us -> none  [body(): lax.all_gather(attended, 'h', axis=0, tiled=True).reshape(NH, tokens, SLICE)]
    all_to_all x5 -> x6, waiting for transfers between devices: 38.8 us -> 51.7 us  [exchange(): return lax.all_to_all(blocks, axes, split_axis=0, concat_axis=0, tiled=True)]
    all_to_all x5 -> x6, starting transfers between devices: 31.5 us -> 39.7 us  [exchange(): return lax.all_to_all(blocks, axes, split_axis=0, concat_axis=0, tiled=True)]
  transfers between devices with their start and end apart: 22 -> 23, of which waited for: 17 -> 18; matrix products, arithmetic and copies ran while one was open for 3% -> 3% of each run, Pallas kernels for 1% -> 1%
where the time goes in v14:
time: 267 us; the launch traced here: 266 us
  waiting for transfers between devices  84.3 us (32%)
  starting transfers between devices  76.5 us (29%)
  blocking collectives  62.2 us (23%)
  between operations  15 us (6%)
  Pallas kernels  11.5 us (4%)
  matrix products  7.39 us (3%)
  local copies, waits for them, and re-layouts  4.93 us (2%)
  other arithmetic  3.93 us (1%)
    all_to_all x6, waiting for transfers between devices, exchange(): return lax.all_to_all(blocks, axes, split_axis=0, concat_axis=0, tiled=True)  51.7 us
    all_to_all x6, starting transfers between devices, exchange(): return lax.all_to_all(blocks, axes, split_axis=0, concat_axis=0, tiled=True)  39.7 us
    all_gather x2, blocking collectives, gathered(): return lax.all_gather(activated(sums), 'h', axis=0, tiled=True)  34.5 us
    all_to_all x1, blocking collectives, exchange(): return lax.all_to_all(blocks, axes, split_axis=0, concat_axis=0, tiled=True)  27.8 us
    ppermute x11, starting transfers between devices, swap(): return lax.ppermute(block, axis, [(0, 1), (1, 0)])  24.1 us
    ppermute x11, waiting for transfers between devices, swap(): return lax.ppermute(block, axis, [(0, 1), (1, 0)])  21.4 us
    ppermute x3, starting transfers between devices, from_behind(): return lax.ppermute(block, CTX, route)  12.6 us
    reduce_scatter x2, waiting for transfers between devices, reduced(): return lax.psum_scatter(flat, 'h', scatter_dimension=0, tiled=True)  7.28 us
  transfers between devices with their start and end apart: 23, of which 18 were waited for; matrix products, arithmetic and copies ran while one was open for 3% of the time, Pallas kernels for 1%

profile of v14, /device:TPU:72, one launch (start us, length us, event | category | flops | bytes accessed | tf_op | source)
XLA Modules:
  0.0 265.9 jit_solution(12466687306362531888)
XLA Ops:
  8.0 3.6 %collective-permute-start = (bf16[128,256]{1,0:T(8,128)(2,1)S(1)}, bf16[128,256]{1,0:T(8,128)(2,1)S(1)}, u32[]{:S(2)}, u32[]{:S(2)}) collective-permute-start(bf16[128,256]{1,0:T(8,128)(2,1)S(1)} %pad_maximum_fusion.2), channel_id=1, source_target_pairs={{0,24},{8,32},{16,40},{24,48},{32,56},{40,64},{48,72},{56,80},{64,... | collective-permute-start | bytes 196616 | tf_op jit(solution)/shard_map/ppermute | solution.py:46
  11.6 4.7 %collective-permute-start.1 = (bf16[128,256]{1,0:T(8,128)(2,1)S(1)}, bf16[128,256]{1,0:T(8,128)(2,1)S(1)}, u32[]{:S(2)}, u32[]{:S(2)}) collective-permute-start(bf16[128,256]{1,0:T(8,128)(2,1)S(1)} %pad_maximum_fusion.2), channel_id=1, source_target_pairs={{0,16},{8,24},{16,32},{24,40},{32,48},{40,56},{48,64},{56,72},{64,... | collective-permute-start | bytes 196616 | tf_op jit(solution)/shard_map/ppermute | solution.py:46
  16.3 4.3 %collective-permute-start.2 = (bf16[128,256]{1,0:T(8,128)(2,1)S(1)}, bf16[128,256]{1,0:T(8,128)(2,1)S(1)}, u32[]{:S(2)}, u32[]{:S(2)}) collective-permute-start(bf16[128,256]{1,0:T(8,128)(2,1)S(1)} %pad_maximum_fusion.2), channel_id=1, source_target_pairs={{0,8},{8,16},{16,24},{24,32},{32,40},{40,48},{48,56},{56,64},{64,7... | collective-permute-start | bytes 196616 | tf_op jit(solution)/shard_map/ppermute | solution.py:46
  28.7 9.4 %all-to-all-start = ((bf16[4,128,512]{2,1,0:T(8,128)(2,1)}), bf16[4,128,512]{2,1,0:T(8,128)(2,1)}, u32[]{:S(2)}, u32[]{:S(2)}) async-start(bf16[4,128,512]{2,1,0:T(8,128)(2,1)} %broadcast_in_dim.272), calls=%async_computation | async-start | bytes 1048576 | tf_op jit(solution)/shard_map/all_to_all | solution.py:41
  38.6 12.8 %all-to-all-done = bf16[4,128,512]{2,1,0:T(8,128)(2,1)} async-done(((bf16[4,128,512]{2,1,0:T(8,128)(2,1)}), bf16[4,128,512]{2,1,0:T(8,128)(2,1)}, u32[]{:S(2)}, u32[]{:S(2)}) %all-to-all-start) | async-done | bytes 524320 | tf_op jit(solution)/shard_map/all_to_all | solution.py:41
  51.4 4.3 %all-to-all-start.1 = ((bf16[4,128,512]{2,1,0:T(8,128)(2,1)}), bf16[4,128,512]{2,1,0:T(8,128)(2,1)S(1)}, u32[]{:S(2)}, u32[]{:S(2)}) async-start(bf16[4,128,512]{2,1,0:T(8,128)(2,1)} %all-to-all-done), calls=%async_computation.1 | async-start | bytes 1048576 | tf_op jit(solution)/shard_map/all_to_all | solution.py:41
  55.8 3.8 %collective-permute-start.4 = (f32[128,24]{0,1:T(8,128)S(1)}, f32[128,24]{0,1:T(8,128)S(1)}, u32[]{:S(2)}, u32[]{:S(2)}) collective-permute-start(f32[128,24]{0,1:T(8,128)S(1)} %get-tuple-element.87), channel_id=1, source_target_pairs={{0,8},{8,0},{1,9},{9,1},{2,10},{10,2},{3,11},{11,3},{4,12},{12,4},... | collective-permute-start | bytes 36872 | tf_op jit(solution)/shard_map/ppermute | solution.py:37
  65.7 3.9 %all-gather.2.cloned.1.call-done = bf16[1024,512]{1,0:T(8,128)(2,1)} async-done(((bf16[128,512]{1,0:T(8,128)(2,1)}), bf16[1024,512]{1,0:T(8,128)(2,1)}) %all-gather.2.cloned.1.call-update) | async-done | bytes 1048592 | tf_op jit(solution)/shard_map/all_gather | solution.py:233
  72.4 4.4 %all-to-all-start.2 = ((bf16[4,128,512]{2,1,0:T(8,128)(2,1)}), bf16[4,128,512]{2,1,0:T(8,128)(2,1)S(1)}, u32[]{:S(2)}, u32[]{:S(2)}) async-start(bf16[4,128,512]{2,1,0:T(8,128)(2,1)} %bitcast.11), calls=%async_computation.2 | async-start | bytes 1048576 | tf_op jit(solution)/shard_map/all_to_all | solution.py:41
  77.2 7.7 %all-to-all-done.2 = bf16[4,128,512]{2,1,0:T(8,128)(2,1)S(1)} async-done(((bf16[4,128,512]{2,1,0:T(8,128)(2,1)}), bf16[4,128,512]{2,1,0:T(8,128)(2,1)S(1)}, u32[]{:S(2)}, u32[]{:S(2)}) %all-to-all-start.2) | async-done | bytes 524320 | tf_op jit(solution)/shard_map/all_to_all | solution.py:41
  88.0 4.5 %collective-permute-done.6 = bf16[128,512]{1,0:T(8,128)(2,1)S(1)} collective-permute-done((bf16[128,512]{1,0:T(8,128)(2,1)S(1)}, bf16[128,512]{1,0:T(8,128)(2,1)S(1)}, u32[]{:S(2)}, u32[]{:S(2)}) %collective-permute-start.6) | collective-permute-done | bytes 131104 | tf_op jit(solution)/shard_map/ppermute | solution.py:37
  93.8 5.9 %all-to-all-start.3 = ((bf16[32,24,512]{2,1,0:T(8,128)(2,1)}), bf16[32,24,512]{2,1,0:T(8,128)(2,1)S(1)}, u32[]{:S(2)}, u32[]{:S(2)}) async-start(bf16[32,24,512]{2,1,0:T(8,128)(2,1)} %bitcast.20), calls=%async_computation.3 | async-start | bytes 1572864 | tf_op jit(solution)/shard_map/all_to_all | solution.py:41
  107.0 9.7 %all-to-all-done.3 = bf16[32,24,512]{2,1,0:T(8,128)(2,1)S(1)} async-done(((bf16[32,24,512]{2,1,0:T(8,128)(2,1)}), bf16[32,24,512]{2,1,0:T(8,128)(2,1)S(1)}, u32[]{:S(2)}, u32[]{:S(2)}) %all-to-all-start.3) | async-done | bytes 786464 | tf_op jit(solution)/shard_map/all_to_all | solution.py:41
  120.8 3.4 %shard_map.185 = bf16[4,176,768]{2,1,0:T(8,128)(2,1)} custom-call(bf16[768,512]{1,0:T(8,128)(2,1)S(1)} %bitcast.149, bf16[768,512]{1,0:T(8,128)(2,1)S(1)} %collective-permute-done.9.other_ref, bf16[512,768]{1,0:T(8,128)(2,1)S(1)} %pad_maximum_fusion.w_own_ref, bf16[512,768]{1,0:T(8,128)(2,1)S(1)} %collective-permute-done.7.w_other_ref, ...), custom_call_target="tpu_custom_call" | custom-call | flops 100000000 | bytes 500000 | tf_op jit(solution)/shard_map/pallas_call | solution.py:151
  124.7 27.8 %all_to_all.35 = bf16[32,24,512]{2,1,0:T(8,128)(2,1)S(1)} all-to-all(bf16[32,24,512]{2,1,0:T(8,128)(2,1)S(1)} %bitcast.156), channel_id=1, replica_groups=mesh['x'=4,'y'=8,'l'=2,'h'=4,'c'=2] {'x','y'}, dimensions={0} | all-to-all | bytes 1572864 | tf_op jit(solution)/shard_map/all_to_all | solution.py:41
  152.4 4.8 %reduce-scatter.3.cloned.1.call-done.sums_ref = bf16[176,768]{1,0:T(8,128)(2,1)} async-done(((bf16[704,768]{1,0:T(8,128)(2,1)}), bf16[176,768]{1,0:T(8,128)(2,1)}) %reduce-scatter.3.cloned.1.call-update) | async-done | bytes 270352 | tf_op jit(solution)/shard_map/reduce_scatter | solution.py:294
  161.4 3.4 %shard_map.188 = bf16[4,176,768]{2,1,0:T(8,128)(2,1)} custom-call(bf16[768,512]{1,0:T(8,128)(2,1)S(1)} %bitcast.151, bf16[768,512]{1,0:T(8,128)(2,1)S(1)} %collective-permute-done.11.other_ref, bf16[512,768]{1,0:T(8,128)(2,1)S(1)} %pad_maximum_fusion.w_own_ref, bf16[512,768]{1,0:T(8,128)(2,1)S(1)} %collective-permute-done.7.w_other_ref, ...), custom_call_target="tpu_custom_call" | custom-call | flops 100000000 | bytes 500000 | tf_op jit(solution)/shard_map/pallas_call | solution.py:151
  166.0 18.2 %all_gather.10.own_ref = bf16[672,384]{1,0:T(8,128)(2,1)S(1)} all-gather(bf16[168,384]{1,0:T(8,128)(2,1)S(1)} %shard_map.186), channel_id=1, replica_groups=mesh['x'=4,'y'=8,'l'=2,'h'=4,'c'=2] {'h'}, dimensions={0}, use_global_device_ids=true | all-gather | bytes 645120 | tf_op jit(solution)/shard_map/all_gather | solution.py:297
  190.1 9.4 %all-to-all-start.5 = ((bf16[32,24,512]{2,1,0:T(8,128)(2,1)}), bf16[32,24,512]{2,1,0:T(8,128)(2,1)S(1)}, u32[]{:S(2)}, u32[]{:S(2)}) async-start(bf16[32,24,512]{2,1,0:T(8,128)(2,1)} %bitcast.41), calls=%async_computation.6 | async-start | bytes 1572864 | tf_op jit(solution)/shard_map/all_to_all | solution.py:41
  203.1 16.3 %all_gather.11.own_ref = bf16[672,384]{1,0:T(8,128)(2,1)S(1)} all-gather(bf16[168,384]{1,0:T(8,128)(2,1)S(1)} %shard_map.189), channel_id=1, replica_groups=mesh['x'=4,'y'=8,'l'=2,'h'=4,'c'=2] {'h'}, dimensions={0}, use_global_device_ids=true | all-gather | bytes 645120 | tf_op jit(solution)/shard_map/all_gather | solution.py:297
  219.4 3.4 %all-to-all-done.5 = bf16[32,24,512]{2,1,0:T(8,128)(2,1)S(1)} async-done(((bf16[32,24,512]{2,1,0:T(8,128)(2,1)}), bf16[32,24,512]{2,1,0:T(8,128)(2,1)S(1)}, u32[]{:S(2)}, u32[]{:S(2)}) %all-to-all-start.5) | async-done | bytes 786464 | tf_op jit(solution)/shard_map/all_to_all | solution.py:41
  228.7 6.3 %all-to-all-start.6 = ((bf16[32,24,512]{2,1,0:T(8,128)(2,1)}), bf16[32,24,512]{2,1,0:T(8,128)(2,1)S(1)}, u32[]{:S(2)}, u32[]{:S(2)}) async-start(bf16[32,24,512]{2,1,0:T(8,128)(2,1)} %bitcast.52), calls=%async_computation.8 | async-start | bytes 1572864 | tf_op jit(solution)/shard_map/all_to_all | solution.py:41
  237.6 4.9 %collective-permute-done.13 = bf16[128,512]{1,0:T(8,128)(2,1)S(1)} collective-permute-done((bf16[128,512]{1,0:T(8,128)(2,1)S(1)}, bf16[128,512]{1,0:T(8,128)(2,1)S(1)}, u32[]{:S(2)}, u32[]{:S(2)}) %collective-permute-start.13) | collective-permute-done | bytes 131104 | tf_op jit(solution)/shard_map/ppermute | solution.py:37
  242.6 15.8 %all-to-all-done.6 = bf16[32,24,512]{2,1,0:T(8,128)(2,1)S(1)} async-done(((bf16[32,24,512]{2,1,0:T(8,128)(2,1)}), bf16[32,24,512]{2,1,0:T(8,128)(2,1)S(1)}, u32[]{:S(2)}, u32[]{:S(2)}) %all-to-all-start.6) | async-done | bytes 786464 | tf_op jit(solution)/shard_map/all_to_all | solution.py:41
  (114 shorter events, 58.2 us)
Async XLA Ops:
  7.2 62.4 %all-gather.2.cloned.1.call-start = ((), (), s32[]{:S(2)}) async-start(), calls=%async_computation.9 | async-start | bytes 1179648 | tf_op jit(solution)/shard_map/all_gather | solution.py:233
  8.0 16.1 %collective-permute-start = (bf16[128,256]{1,0:T(8,128)(2,1)S(1)}, bf16[128,256]{1,0:T(8,128)(2,1)S(1)}, u32[]{:S(2)}, u32[]{:S(2)}) collective-permute-start(bf16[128,256]{1,0:T(8,128)(2,1)S(1)} %pad_maximum_fusion.2), channel_id=1, source_target_pairs={{0,24},{8,32},{16,40},{24,48},{32,56},{40,64},{48,72},{56,80},{64,... | collective-permute-start | bytes 196616 | tf_op jit(solution)/shard_map/ppermute | solution.py:46
  11.6 12.6 %collective-permute-start.1 = (bf16[128,256]{1,0:T(8,128)(2,1)S(1)}, bf16[128,256]{1,0:T(8,128)(2,1)S(1)}, u32[]{:S(2)}, u32[]{:S(2)}) collective-permute-start(bf16[128,256]{1,0:T(8,128)(2,1)S(1)} %pad_maximum_fusion.2), channel_id=1, source_target_pairs={{0,16},{8,24},{16,32},{24,40},{32,48},{40,56},{48,64},{56,72},{64,... | collective-permute-start | bytes 196616 | tf_op jit(solution)/shard_map/ppermute | solution.py:46
  16.3 7.9 %collective-permute-start.2 = (bf16[128,256]{1,0:T(8,128)(2,1)S(1)}, bf16[128,256]{1,0:T(8,128)(2,1)S(1)}, u32[]{:S(2)}, u32[]{:S(2)}) collective-permute-start(bf16[128,256]{1,0:T(8,128)(2,1)S(1)} %pad_maximum_fusion.2), channel_id=1, source_target_pairs={{0,8},{8,16},{16,24},{24,32},{32,40},{40,48},{48,56},{56,64},{64,7... | collective-permute-start | bytes 196616 | tf_op jit(solution)/shard_map/ppermute | solution.py:46
  20.6 6.4 %collective-permute-start.3 = (bf16[64,512]{1,0:T(8,128)(2,1)}, bf16[64,512]{1,0:T(8,128)(2,1)S(1)}, u32[]{:S(2)}, u32[]{:S(2)}) collective-permute-start(bf16[64,512]{1,0:T(8,128)(2,1)} %param.21), channel_id=1, source_target_pairs={{0,8},{8,0},{1,9},{9,1},{2,10},{10,2},{3,11},{11,3},{4,12},{12,4},... | collective-permute-start | bytes 196616 | tf_op jit(solution)/shard_map/ppermute | solution.py:37
  28.7 22.7 %all-to-all-start = ((bf16[4,128,512]{2,1,0:T(8,128)(2,1)}), bf16[4,128,512]{2,1,0:T(8,128)(2,1)}, u32[]{:S(2)}, u32[]{:S(2)}) async-start(bf16[4,128,512]{2,1,0:T(8,128)(2,1)} %broadcast_in_dim.272), calls=%async_computation | async-start | bytes 1048576 | tf_op jit(solution)/shard_map/all_to_all | solution.py:41
  51.4 12.4 %all-to-all-start.1 = ((bf16[4,128,512]{2,1,0:T(8,128)(2,1)}), bf16[4,128,512]{2,1,0:T(8,128)(2,1)S(1)}, u32[]{:S(2)}, u32[]{:S(2)}) async-start(bf16[4,128,512]{2,1,0:T(8,128)(2,1)} %all-to-all-done), calls=%async_computation.1 | async-start | bytes 1048576 | tf_op jit(solution)/shard_map/all_to_all | solution.py:41
  55.8 5.6 %collective-permute-start.4 = (f32[128,24]{0,1:T(8,128)S(1)}, f32[128,24]{0,1:T(8,128)S(1)}, u32[]{:S(2)}, u32[]{:S(2)}) collective-permute-start(f32[128,24]{0,1:T(8,128)S(1)} %get-tuple-element.87), channel_id=1, source_target_pairs={{0,8},{8,0},{1,9},{9,1},{2,10},{10,2},{3,11},{11,3},{4,12},{12,4},... | collective-permute-start | bytes 36872 | tf_op jit(solution)/shard_map/ppermute | solution.py:37
  63.8 7.4 %collective-permute-start.5 = (bf16[512,512]{1,0:T(8,128)(2,1)S(1)}, bf16[512,512]{1,0:T(8,128)(2,1)S(1)}, u32[]{:S(2)}, u32[]{:S(2)}) collective-permute-start(bf16[512,512]{1,0:T(8,128)(2,1)S(1)} %bitcast.157), channel_id=1, source_target_pairs={{0,1},{1,0},{2,3},{3,2},{4,5},{5,4},{6,7},{7,6},{8,9},{9,8},{10,11... | collective-permute-start | bytes 1572872 | tf_op jit(solution)/shard_map/ppermute | solution.py:37
  72.4 12.5 %all-to-all-start.2 = ((bf16[4,128,512]{2,1,0:T(8,128)(2,1)}), bf16[4,128,512]{2,1,0:T(8,128)(2,1)S(1)}, u32[]{:S(2)}, u32[]{:S(2)}) async-start(bf16[4,128,512]{2,1,0:T(8,128)(2,1)} %bitcast.11), calls=%async_computation.2 | async-start | bytes 1048576 | tf_op jit(solution)/shard_map/all_to_all | solution.py:41
  85.7 6.8 %collective-permute-start.6 = (bf16[128,512]{1,0:T(8,128)(2,1)S(1)}, bf16[128,512]{1,0:T(8,128)(2,1)S(1)}, u32[]{:S(2)}, u32[]{:S(2)}) collective-permute-start(bf16[128,512]{1,0:T(8,128)(2,1)S(1)} %get-tuple-element.62), channel_id=1, source_target_pairs={{0,8},{8,0},{1,9},{9,1},{2,10},{10,2},{3,11},{11,3},{4,12},{12,4},... | collective-permute-start | bytes 393224 | tf_op jit(solution)/shard_map/ppermute | solution.py:37
  93.8 22.9 %all-to-all-start.3 = ((bf16[32,24,512]{2,1,0:T(8,128)(2,1)}), bf16[32,24,512]{2,1,0:T(8,128)(2,1)S(1)}, u32[]{:S(2)}, u32[]{:S(2)}) async-start(bf16[32,24,512]{2,1,0:T(8,128)(2,1)} %bitcast.20), calls=%async_computation.3 | async-start | bytes 1572864 | tf_op jit(solution)/shard_map/all_to_all | solution.py:41
  99.8 57.5 %reduce-scatter.3.cloned.1.call-start = ((), (), s32[]{:S(2)}) async-start(), calls=%async_computation.10 | async-start | bytes 1351680 | tf_op jit(solution)/shard_map/reduce_scatter | solution.py:294
  101.1 5.9 %collective-permute-start.7 = (bf16[512,768]{1,0:T(8,128)(2,1)S(1)}, bf16[512,768]{1,0:T(8,128)(2,1)S(1)}, u32[]{:S(2)}, u32[]{:S(2)}) collective-permute-start(bf16[512,768]{1,0:T(8,128)(2,1)S(1)} %pad_maximum_fusion.1), channel_id=1, source_target_pairs={{0,1},{1,0},{2,3},{3,2},{4,5},{5,4},{6,7},{7,6},{8,9},{9,8},{10,11... | collective-permute-start | bytes 2359304 | tf_op jit(solution)/shard_map/ppermute | solution.py:37
  103.8 3.2 %collective-permute-start.8 = (f32[1,512]{1,0:T(1,128)S(1)}, f32[1,512]{1,0:T(1,128)S(1)}, u32[]{:S(2)}, u32[]{:S(2)}) collective-permute-start(f32[1,512]{1,0:T(1,128)S(1)} %bitcast.152), channel_id=1, source_target_pairs={{0,1},{1,0},{2,3},{3,2},{4,5},{5,4},{6,7},{7,6},{8,9},{9,8},{10,11... | collective-permute-start | bytes 6152 | tf_op jit(solution)/shard_map/ppermute | solution.py:37
  116.7 4.2 %collective-permute-start.9 = (bf16[768,512]{1,0:T(8,128)(2,1)S(1)}, bf16[768,512]{1,0:T(8,128)(2,1)S(1)}, u32[]{:S(2)}, u32[]{:S(2)}) collective-permute-start(bf16[768,512]{1,0:T(8,128)(2,1)S(1)} %bitcast.148), channel_id=1, source_target_pairs={{0,1},{1,0},{2,3},{3,2},{4,5},{5,4},{6,7},{7,6},{8,9},{9,8},{10,11... | collective-permute-start | bytes 2359304 | tf_op jit(solution)/shard_map/ppermute | solution.py:37
  124.3 77.7 %reduce-scatter.5.cloned.1.call-start = ((), (), s32[]{:S(2)}) async-start(), calls=%async_computation.11 | async-start | bytes 1351680 | tf_op jit(solution)/shard_map/reduce_scatter | solution.py:294
  157.3 4.2 %collective-permute-start.11 = (bf16[768,512]{1,0:T(8,128)(2,1)S(1)}, bf16[768,512]{1,0:T(8,128)(2,1)S(1)}, u32[]{:S(2)}, u32[]{:S(2)}) collective-permute-start(bf16[768,512]{1,0:T(8,128)(2,1)S(1)} %bitcast.150), channel_id=1, source_target_pairs={{0,1},{1,0},{2,3},{3,2},{4,5},{5,4},{6,7},{7,6},{8,9},{9,8},{10,11... | collective-permute-start | bytes 2359304 | tf_op jit(solution)/shard_map/ppermute | solution.py:37
  166.0 22.0 %copy-start.1 = (bf16[192,168]{1,0:T(8,128)(2,1)S(1)}, bf16[192,168]{1,0:T(8,128)(2,1)}, u32[]{:S(2)}) copy-start(bf16[192,168]{1,0:T(8,128)(2,1)} %constant.89.clone.place_ref) | copy-start | bytes 193540
  184.2 3.8 %collective-permute-start.10 = (bf16[672,384]{1,0:T(8,128)(2,1)S(1)}, bf16[672,384]{1,0:T(8,128)(2,1)S(1)}, u32[]{:S(2)}, u32[]{:S(2)}) collective-permute-start(bf16[672,384]{1,0:T(8,128)(2,1)S(1)} %all_gather.10.own_ref), channel_id=1, source_target_pairs={{0,1},{1,0},{2,3},{3,2},{4,5},{5,4},{6,7},{7,6},{8,9},{9,8},{10,11... | collective-permute-start | bytes 1548296 | tf_op jit(solution)/shard_map/ppermute | solution.py:37
  190.1 32.7 %all-to-all-start.5 = ((bf16[32,24,512]{2,1,0:T(8,128)(2,1)}), bf16[32,24,512]{2,1,0:T(8,128)(2,1)S(1)}, u32[]{:S(2)}, u32[]{:S(2)}) async-start(bf16[32,24,512]{2,1,0:T(8,128)(2,1)} %bitcast.41), calls=%async_computation.6 | async-start | bytes 1572864 | tf_op jit(solution)/shard_map/all_to_all | solution.py:41
  222.8 3.8 %collective-permute-start.12 = (bf16[672,384]{1,0:T(8,128)(2,1)S(1)}, bf16[672,384]{1,0:T(8,128)(2,1)S(1)}, u32[]{:S(2)}, u32[]{:S(2)}) collective-permute-start(bf16[672,384]{1,0:T(8,128)(2,1)S(1)} %all_gather.11.own_ref), channel_id=1, source_target_pairs={{0,1},{1,0},{2,3},{3,2},{4,5},{5,4},{6,7},{7,6},{8,9},{9,8},{10,11... | collective-permute-start | bytes 1548296 | tf_op jit(solution)/shard_map/ppermute | solution.py:37
  228.7 29.6 %all-to-all-start.6 = ((bf16[32,24,512]{2,1,0:T(8,128)(2,1)}), bf16[32,24,512]{2,1,0:T(8,128)(2,1)S(1)}, u32[]{:S(2)}, u32[]{:S(2)}) async-start(bf16[32,24,512]{2,1,0:T(8,128)(2,1)} %bitcast.52), calls=%async_computation.8 | async-start | bytes 1572864 | tf_op jit(solution)/shard_map/all_to_all | solution.py:41
  235.7 6.9 %collective-permute-start.13 = (bf16[128,512]{1,0:T(8,128)(2,1)S(1)}, bf16[128,512]{1,0:T(8,128)(2,1)S(1)}, u32[]{:S(2)}, u32[]{:S(2)}) collective-permute-start(bf16[128,512]{1,0:T(8,128)(2,1)S(1)} %convolution_convert_fusion.2), channel_id=1, source_target_pairs={{0,8},{8,0},{1,9},{9,1},{2,10},{10,2},{3,11},{11,3},{4,12},{12,4},... | collective-permute-start | bytes 393224 | tf_op jit(solution)/shard_map/ppermute | solution.py:37
  (14 other events, 133.2 us)
Sparse Core Ops, SparseCore 0:
  27.8 41.7 all-gather.1
  124.4 32.8 reduce-scatter.2
  165.0 36.8 reduce-scatter.4
